TPU v7x, 32 devices: a whole 2x2x4 slice. The times are simulated.
32 devices in a mesh: frames: 8 (over z, y), tiles: 4 (over x, core).
Axes of the slice: x: 2, y: 2, z: 4, core: 2. Of those that a mesh axis runs over, the one named last changes fastest.
Arguments:
- frames: bfloat16 [32, 3, 128, 1024], P(('frames', 'tiles')), may hold values from -6 to 6
- weight_map: bfloat16 [32, 128, 1024], P(('frames', 'tiles')), may hold values from 0.049804688 to 1
- seam_mask: int32 [32, 128, 64], P(('frames', 'tiles')), may hold values 0 or 1
- strip_cell: int32 [32], P(('frames', 'tiles')), may hold values from 0 to 60
- partner: int32 [32], P(('frames', 'tiles')), may hold values from 0 to 31, as said below
- tile_group: int32 [32, 32, 1], P(('frames', 'tiles')), may hold values from 0 to 7; in each aligned block of 32 rows (0 to 31, 32 to 63, ..., all dimensions but the last counted through in order) at most 8 rows name the same one
- tile_position_in_group: int32 [32, 32], P(('frames', 'tiles')), may hold values from 0 to 15
Outputs:
- panorama: float32 [128, 3, 4096], P(('frames', 'tiles'))
Inputs may be any that keep to these rules, and one draw needn't show every extreme that they name: partner[partner[f]] = f. Writing f = (g * 4 + t) + j with t < 4 and j < 1, partner[f] = ((g XOR m_(t,j)) * 4 + t) + j, with one nonzero m_(t,j) below 8 for each pair t, j; among these masks are 4 and 1. `tile_group`: within the rows of one device (32 rows), no value occurs more than 8 times, and some value occurs exactly 8 times.
All inputs are finite; a program needn't handle non-finite values. No bound on the sum of `seam_mask` on one device may be relied on, other than what follows from the above.
Results may differ from a plain program's by a relative error of at most 0.0028.
Values may be sent and summed in bfloat16 or wider, within the bound.
No kernel may reach another device: no remote copies, remote signals or barrier semaphores. Data moves between devices by JAX's collectives and lax.ppermute only.
A program may use at most 128 MiB of HBM per device.

v0:
```python
import functools

import jax
import jax.numpy as jnp
import numpy as np
from jax import lax
from jax.experimental import pallas as pl
from jax.experimental.pallas import tpu as pltpu
from jax.sharding import PartitionSpec as P

COLOURS = 3
FH = 128
FW = 1024
QB = 32
WIN = 256
TILE_DEV = 4
F32 = jnp.float32
BF16 = jnp.bfloat16


def shrink_matrix(n):
    m = np.zeros((n // 2, n), np.float32)
    for i in range(n // 2):
        for d, tap in zip(range(-2, 3), (1, 4, 6, 4, 1)):
            m[i, min(max(2 * i + d, 0), n - 1)] += tap / 16.0
    return m


def grow_matrix(n):
    m = np.zeros((2 * n, n), np.float32)
    for i in range(n):
        lo, hi = max(i - 1, 0), min(i + 1, n - 1)
        m[2 * i, lo] += 1 / 8
        m[2 * i, i] += 6 / 8
        m[2 * i, hi] += 1 / 8
        m[2 * i + 1, i] += 1 / 2
        m[2 * i + 1, hi] += 1 / 2
    return m


def padded(m, rows, cols):
    return np.pad(m, ((0, rows - m.shape[0]), (0, cols - m.shape[1])))


def row_order():
    m = np.zeros((FH, FH), np.float32)
    for r in range(2):
        for par in range(2):
            for i in range(32):
                m[r * 64 + par * 32 + i, r * 64 + 2 * i + par] = 1
    return m


def vertical():
    v = {1: shrink_matrix(128), 2: shrink_matrix(64), 3: shrink_matrix(32)}
    spread = np.zeros((16, 8), np.float32)
    for r in range(2):
        for i in range(4):
            spread[r * 8 + i, r * 4 + i] = 1
    v[4] = spread @ shrink_matrix(16)
    g = {0: row_order() @ grow_matrix(64), 1: grow_matrix(32), 2: grow_matrix(16)}
    g[3] = grow_matrix(8) @ spread.T
    return v, g


def horizontal(width, pad_last):
    s = {k: shrink_matrix(width >> (k - 1)).T for k in range(1, 5)}
    g = {k: grow_matrix(width >> (k + 1)).T for k in range(4)}
    if pad_last:
        s[4] = padded(s[4], s[4].shape[0], pad_last)
        g[3] = padded(g[3], pad_last, g[3].shape[1])
    return s, g


def const(m):
    return jnp.asarray(m, BF16)


def mm(a, b):
    return jnp.dot(a, b, preferred_element_type=F32)


def split(v):
    hi = v.astype(BF16)
    return hi, (v - hi.astype(F32)).astype(BF16)


def rdot(v, m):
    hi, lo = split(v)
    return mm(hi, m) + mm(lo, m)


def ldot(m, v):
    hi, lo = split(v)
    return mm(m, hi) + mm(m, lo)


def pyramid(planes, v, s):
    n = len(planes)
    t = jnp.concatenate([mm(v[1], p) for p in planes], axis=0)
    levels = {1: rdot(t, s[1])}
    for k in range(2, 5):
        prev = levels[k - 1]
        rows = prev.shape[0] // n
        t = jnp.concatenate([ldot(v[k], prev[i * rows : (i + 1) * rows]) for i in range(n)], axis=0)
        levels[k] = rdot(t, s[k])
    return levels


def grown(level, n, gv, gh):
    h = rdot(level, gh)
    rows = level.shape[0] // n
    return [ldot(gv, h[i * rows : (i + 1) * rows]) for i in range(n)]


def place(rows, cols, base, width, offset):
    i = lax.broadcasted_iota(jnp.int32, (rows, cols), 0)
    c = lax.broadcasted_iota(jnp.int32, (rows, cols), 1)
    hit = (i >= base) & (i < base + width) & (c - i == offset - base)
    return jnp.where(hit, 1.0, 0.0).astype(BF16)


def strips_kernel(cell, xa, xb, *refs):
    mats, (out, acc) = refs[:-2], refs[-2:]
    v = {k: mats[k - 1][...] for k in range(1, 5)}
    gv = {k: mats[4 + k][...] for k in range(4)}
    s = {k: mats[7 + k][...] for k in range(1, 5)}
    gh = {k: mats[12 + k][...] for k in range(4)}
    order = mats[16][...]
    first = window_tile(cell[0]) * 128
    planes = [jnp.concatenate([xa[0, c], xb[0, c]], axis=1) for c in range(COLOURS)]
    levels = pyramid(planes, v, s)
    back = grown(levels[1], COLOURS, gv[0], gh[0])
    b0 = jnp.concatenate([mm(order, planes[c]) - back[c] for c in range(COLOURS)], axis=0)
    bands = [b0.astype(BF16)]
    for k in range(1, 4):
        back = grown(levels[k + 1], COLOURS, gv[k], gh[k])
        bands.append((levels[k] - jnp.concatenate(back, axis=0)).astype(BF16))
    bands.append(levels[4].astype(BF16))
    start = cell[0] * 16 - first

    def pick(band, base, k):
        i = lax.broadcasted_iota(jnp.int32, (band.shape[1], 128), 0)
        c = lax.broadcasted_iota(jnp.int32, (band.shape[1], 128), 1)
        hit = (c >= base) & (c < base + (64 >> k)) & (i - c == (start >> k) - base)
        return mm(band, jnp.where(hit, 1.0, 0.0).astype(BF16))

    out[0:192, :] = (pick(bands[0][0:192], 0, 0) + pick(bands[0][192:384], 64, 0)).astype(BF16)
    acc[...] = pick(bands[1][0:96], 0, 1) + pick(bands[1][96:192], 32, 1) + pick(bands[2], 64, 2)
    acc[0:48, :] = acc[0:48, :] + pick(bands[3], 80, 3) + pick(bands[4], 88, 4)
    out[192:288, :] = acc[...].astype(BF16)


def window_tile(cell):
    return jnp.clip((cell - 3) >> 3, 0, (FW - WIN) // 128)


def full_spec(a):
    return pl.BlockSpec(a.shape, lambda *_: (0,) * a.ndim)


def strips_of(frames, cell):
    v, g = vertical()
    s, gh = horizontal(WIN, 0)
    mats = [const(v[k]) for k in range(1, 5)] + [const(g[k]) for k in range(4)]
    mats += [const(s[k]) for k in range(1, 5)] + [const(gh[k]) for k in range(4)]
    mats.append(const(row_order()))
    grid_spec = pltpu.PrefetchScalarGridSpec(
        num_scalar_prefetch=1,
        grid=(1,),
        in_specs=[
            pl.BlockSpec((1, COLOURS, FH, 128), lambda i, c: (0, 0, 0, window_tile(c[0]))),
            pl.BlockSpec((1, COLOURS, FH, 128), lambda i, c: (0, 0, 0, window_tile(c[0]) + 1)),
        ]
        + [full_spec(m) for m in mats],
        out_specs=pl.BlockSpec((288, 128), lambda i, c: (0, 0)),
        scratch_shapes=[pltpu.VMEM((96, 128), F32)],
    )
    return pl.pallas_call(
        strips_kernel,
        grid_spec=grid_spec,
        out_shape=jax.ShapeDtypeStruct((288, 128), BF16),
        compiler_params=pltpu.CompilerParams(vmem_limit_bytes=48 << 20),
        cost_estimate=pl.CostEstimate(flops=2 * 10**9, bytes_accessed=10**6, transcendentals=0),
        name="strips",
    )(cell, frames, frames, *mats)


def lane_index():
    return lax.broadcasted_iota(jnp.int32, (1, 128), 1)


def fold_level0(p, store):
    left = lane_index() < 64
    for r in range(2):
        for j in range(8):
            even = p[r * 64 : r * 64 + 32, j * 128 : j * 128 + 128]
            odd = p[r * 64 + 32 : r * 64 + 64, j * 128 : j * 128 + 128]
            store(r * 16 + 2 * j, jnp.where(left, even, pltpu.roll(odd, 64, 1)))
            store(r * 16 + 2 * j + 1, jnp.where(left, pltpu.roll(even, 64, 1), odd))


def gather_channels(parts, width, cc, base):
    groups = 128 // width
    group = lane_index() // width
    out = jnp.zeros_like(parts[0])
    for ch in range(4):
        out = jnp.where(group == (cc + ch) % groups, parts[ch], out)
    return pltpu.roll(out, (base - cc * width) % 128, 1)


def bands_kernel(x, w, m, *refs):
    mats, outs = refs[:21], refs[21:]
    v = {k: mats[k - 1][...] for k in range(1, 5)}
    gv = {k: mats[4 + k][...] for k in range(4)}
    s = {k: mats[7 + k][...] for k in range(1, 5)}
    gh = {k: mats[12 + k][...] for k in range(4)}
    order = mats[16][...]
    sm = {k: mats[16 + k][...] for k in range(1, 5)}
    wblocks, b0, b1, b2, b3, b4, wp, w1, w2, w3, w4, n0, n1, n2, n3, n4 = outs
    planes = [x[0, c] for c in range(COLOURS)] + [w[0]]
    weights = mm(order, planes[3])
    wp[...] = weights.astype(BF16)

    def store(q, piece):
        wblocks[q] = piece.astype(BF16)

    fold_level0(weights, store)
    levels = pyramid(planes, v, s)
    bands, wl = (b1, b2, b3), (w1, w2, w3, w4)
    for k in range(1, 5):
        rows = levels[k].shape[0] // 4
        wl[k - 1][...] = levels[k][3 * rows :]
    back = grown(levels[1][: 3 * 64], COLOURS, gv[0], gh[0])
    for c in range(COLOURS):
        b0[c] = mm(order, planes[c]) - back[c]
    for k in range(1, 4):
        rows = levels[k].shape[0] // 4
        below = levels[k + 1].shape[0] // 4
        back = grown(levels[k + 1][: 3 * below], COLOURS, gv[k], gh[k])
        for c in range(COLOURS):
            bands[k - 1][c] = levels[k][c * rows : (c + 1) * rows] - back[c]
    for c in range(COLOURS):
        b4[c] = levels[4][c * 16 : (c + 1) * 16]
    other = (1.0 - m[0].astype(F32)).astype(BF16)
    n0[...] = mm(order, other)
    masks = pyramid([other], v, sm)
    for k, ref in enumerate((n1, n2, n3, n4)):
        ref[...] = masks[k + 1]


def bands_of(frames, weight_map, seam_mask):
    v, g = vertical()
    s, gh = horizontal(FW, 128)
    sm, _ = horizontal(64, 0)
    mats = [const(v[k]) for k in range(1, 5)] + [const(g[k]) for k in range(4)]
    mats += [const(s[k]) for k in range(1, 5)] + [const(gh[k]) for k in range(4)]
    mats.append(const(row_order()))
    mats += [const(sm[k]) for k in range(1, 5)]
    out_shape = [jax.ShapeDtypeStruct((QB, 32, 128), BF16)]
    shapes = [(128, 1024), (64, 512), (32, 256), (16, 128), (16, 128)]
    out_shape += [jax.ShapeDtypeStruct((COLOURS,) + sh, F32) for sh in shapes]
    out_shape += [jax.ShapeDtypeStruct(shapes[0], BF16)]
    out_shape += [jax.ShapeDtypeStruct(sh, F32) for sh in shapes[1:]]
    out_shape += [jax.ShapeDtypeStruct(sh, F32) for sh in ((128, 64), (64, 32), (32, 16), (16, 8), (16, 4))]
    return pl.pallas_call(
        bands_kernel,
        out_shape=out_shape,
        compiler_params=pltpu.CompilerParams(vmem_limit_bytes=48 << 20),
        cost_estimate=pl.CostEstimate(flops=8 * 10**9, bytes_accessed=6 * 10**6, transcendentals=0),
        name="bands",
    )(frames, weight_map, seam_mask, *mats)


def blend_kernel(cell, strips, b0, b1, b2, b3, b4, wp, w1, w2, w3, w4, n0, n1, n2, n3, n4, first, second):
    start = cell[0] * 16
    low = strips[192:288]

    def mixed(band, remote, share):
        return band + share * (remote - band)

    widths = (1024, 512, 256, 128, 128)
    share0 = mm(n0[...].astype(BF16), place(64, 1024, 0, 64, start))
    share = [share0]
    for k, ref in enumerate((n1, n2, n3, n4)):
        share.append(rdot(ref[...], place(64 >> (k + 1), widths[k + 1], 0, 64 >> (k + 1), start >> (k + 1))))
    top = strips[0:192]
    remote0 = [mm(top, place(128, 1024, 0, 64, start)), mm(top, place(128, 1024, 64, 64, start))]
    remote0 = jnp.concatenate(remote0, axis=0)
    weights = wp[...].astype(F32)
    for c in range(COLOURS):
        p = weights * mixed(b0[c], remote0[c * 128 : (c + 1) * 128], share[0])
        out, row = (first, 0) if c == 0 else (second, 32 * (c - 1))

        def store(q, piece, out=out, row=row):
            out[q, row : row + 32, :] = piece.astype(BF16)

        fold_level0(p, store)
    remote1 = [mm(low, place(128, 512, 0, 32, start >> 1)), mm(low, place(128, 512, 32, 32, start >> 1))]
    remote1 = jnp.concatenate(remote1, axis=0)
    parts = [w1[...] * mixed(b1[c], remote1[c * 64 : (c + 1) * 64], share[1]) for c in range(COLOURS)] + [w1[...]]
    for r in range(2):
        for j in range(4):
            turned = [parts[ch][r * 32 : r * 32 + 32, j * 128 : j * 128 + 128] for ch in range(4)]
            turned = [turned[0]] + [pltpu.roll(turned[ch], 32 * ch, 1) for ch in range(1, 4)]
            for cc in range(4):
                first[r * 16 + 4 * j + cc, 32:64, :] = gather_channels(turned, 32, cc, 0).astype(BF16)
    remote2 = mm(low, place(128, 256, 64, 16, start >> 2))
    remote3 = mm(low[0:48], place(128, 128, 80, 8, start >> 3))
    remote4 = mm(low[0:48], place(128, 128, 88, 4, start >> 4))
    parts2 = [w2[...] * mixed(b2[c], remote2[c * 32 : (c + 1) * 32], share[2]) for c in range(COLOURS)] + [w2[...]]
    parts3 = [w3[...] * mixed(b3[c], remote3[c * 16 : (c + 1) * 16], share[3]) for c in range(COLOURS)] + [w3[...]]
    parts4 = [w4[...] * mixed(b4[c], remote4[c * 16 : (c + 1) * 16], share[4]) for c in range(COLOURS)] + [w4[...]]
    lane = lane_index()
    for r in range(2):
        turned3 = [pltpu.roll(parts3[ch][r * 8 : r * 8 + 8], 8 * ch, 1) for ch in range(4)]
        turned4 = [pltpu.roll(parts4[ch][r * 8 : r * 8 + 8], 4 * ch, 1) for ch in range(4)]
        for j in range(2):
            turned2 = [parts2[ch][r * 16 : r * 16 + 16, j * 128 : j * 128 + 128] for ch in range(4)]
            turned2 = [pltpu.roll(turned2[ch], 16 * ch, 1) for ch in range(4)]
            for cc in range(8):
                c = j * 8 + cc
                two = gather_channels(turned2, 16, cc, 0)
                three = gather_channels(turned3, 8, c, 64)
                four = gather_channels(turned4, 4, c, 96)
                head = jnp.where(lane < 64, two[0:8], jnp.where(lane < 96, three, four))
                tail = jnp.where(lane < 64, two[8:16], 0.0)
                first[r * 16 + c, 64:80, :] = jnp.concatenate([head, tail], axis=0).astype(BF16)


def blend(cell, strips, parts):
    vmem = pl.BlockSpec(memory_space=pltpu.VMEM)
    return pl.pallas_call(
        blend_kernel,
        in_specs=[pl.BlockSpec(memory_space=pltpu.SMEM)] + [vmem] * 16,
        out_shape=[jax.ShapeDtypeStruct((QB, 80, 128), BF16), jax.ShapeDtypeStruct((QB, 64, 128), BF16)],
        compiler_params=pltpu.CompilerParams(vmem_limit_bytes=48 << 20),
        cost_estimate=pl.CostEstimate(flops=4 * 10**9, bytes_accessed=4 * 10**6, transcendentals=0),
        name="blend",
    )(cell, strips, *parts)


def gather_kernel(spot, a, b, c, d, out, acc):
    acc[...] = jnp.zeros_like(acc)
    for source, ref in enumerate((a, b, c, d)):

        def body(q, carry, source=source, ref=ref):
            at = spot[source, q]

            @pl.when(at >= 0)
            def _():
                acc[at] = acc[at] + ref[q].astype(F32)

            return carry

        lax.fori_loop(0, QB, body, 0)
    out[...] = acc[...].astype(BF16)


def gather_rows(spot, rows, tiles):
    height = rows[0].shape[1]
    vmem = pl.BlockSpec(memory_space=pltpu.VMEM)
    return pl.pallas_call(
        gather_kernel,
        in_specs=[pl.BlockSpec(memory_space=pltpu.SMEM)] + [vmem] * 4,
        out_shape=jax.ShapeDtypeStruct((tiles, height, 128), BF16),
        scratch_shapes=[pltpu.VMEM((tiles, height, 128), F32)],
        compiler_params=pltpu.CompilerParams(vmem_limit_bytes=48 << 20),
        cost_estimate=pl.CostEstimate(flops=10**9, bytes_accessed=4 * 10**6, transcendentals=0),
        name="gather_rows",
    )(spot, *rows)


def collapse_matrices():
    def across(src, dst, width, copies=1):
        g = grow_matrix(width).T
        m = np.zeros((128, 128), np.float32)
        for ch in range(COLOURS):
            m[src + ch * width : src + (ch + 1) * width, dst + ch * 2 * width : dst + (ch + 1) * 2 * width] = g
        return m

    last = np.zeros((128, 384), np.float32)
    g = grow_matrix(32).T
    for ch in range(COLOURS):
        for half in range(2):
            last[ch * 32 : ch * 32 + 32, ch * 128 + half * 64 : ch * 128 + half * 64 + 64] = g

    def down(n, rows_in, rows_out, pick=None):
        g = grow_matrix(n)
        g = g if pick is None else g[pick::2]
        m = np.zeros((TILE_DEV * rows_out, TILE_DEV * rows_in), np.float32)
        for t in range(TILE_DEV):
            m[t * rows_out : t * rows_out + g.shape[0], t * rows_in : t * rows_in + n] = g
        return m

    return [
        across(96, 64, 4),
        across(64, 0, 8),
        across(0, 0, 16),
        last,
        down(4, 16, 16),
        down(8, 16, 16),
        down(16, 16, 32),
        down(32, 32, 32, 0),
        down(32, 32, 32, 1),
    ]


def collapse_kernel(a, b, c, m43, m32, m21, m10, d43, d32, d21, even, odd, out, level0):
    def total(ref, lo, hi):
        acc = ref[0, :, lo:hi, :].astype(F32)
        for source in range(1, ref.shape[0]):
            acc = acc + ref[source, :, lo:hi, :].astype(F32)
        return acc.reshape(TILE_DEV * (hi - lo), 128)

    lane = lane_index()
    small = total(b, 64, 80)
    bottom = small
    for lo, width, chans in ((0, 16, 3), (64, 8, 3), (96, 4, 3)):
        for ch in range(chans):
            inside = (lane >= lo + ch * width) & (lane < lo + (ch + 1) * width)
            bottom = jnp.where(inside, pltpu.roll(small, (128 - (3 - ch) * width) % 128, 1), bottom)
    small = small / jnp.maximum(bottom, 1.0)
    three = small + ldot(d43[...], rdot(small, m43[...]))
    two = small + ldot(d32[...], rdot(three, m32[...]))
    one = total(b, 32, 64)
    bottom = one
    for ch in range(3):
        inside = (lane >= ch * 32) & (lane < (ch + 1) * 32)
        bottom = jnp.where(inside, pltpu.roll(one, (128 - (3 - ch) * 32) % 128, 1), bottom)
    one = one / jnp.maximum(bottom, 1.0) + ldot(d21[...], rdot(two, m21[...]))
    wide = rdot(one, m10[...])
    hi, lo = split(wide)
    up = mm(even[...], hi) + mm(even[...], lo)
    down = mm(odd[...], hi) + mm(odd[...], lo)
    bottom = jnp.maximum(total(a, 0, 32), 1.0)
    for ch in range(COLOURS):
        own = total(b, 0, 32) if ch == 0 else total(c, 32 * (ch - 1), 32 * ch)
        back = jnp.where(lane < 64, up[:, ch * 128 : ch * 128 + 128], down[:, ch * 128 : ch * 128 + 128])
        level0[ch * 128 : ch * 128 + 128, :] = own / bottom + back
    for t in range(TILE_DEV):
        for row in range(32):
            out[t, :, row * 128 : row * 128 + 128] = level0[pl.ds(t * 32 + row, COLOURS, stride=128), :]


def collapse(a, b, c):
    mats = [const(m) for m in collapse_matrices()]
    return pl.pallas_call(
        collapse_kernel,
        out_shape=jax.ShapeDtypeStruct((TILE_DEV, COLOURS, 4096), F32),
        scratch_shapes=[pltpu.VMEM((COLOURS * 128, 128), F32)],
        compiler_params=pltpu.CompilerParams(vmem_limit_bytes=56 << 20),
        cost_estimate=pl.CostEstimate(flops=10**9, bytes_accessed=3 * 10**6, transcendentals=0),
        name="collapse",
    )(a, b, c, *mats)


def swap(value, axis, bit):
    size = lax.axis_size(axis)
    return lax.ppermute(value, axis, [(i, i ^ bit) for i in range(size)])


def local(frames, weight_map, seam_mask, strip_cell, partner, tile_group, tile_position_in_group):
    groups = lax.axis_size("frames")
    parts = lax.axis_size("tiles")
    mine = lax.axis_index("tiles")
    mask = lax.bitwise_xor(partner[0] // parts, lax.axis_index("frames"))

    ids = tile_group.reshape(QB) * (parts * TILE_DEV) + tile_position_in_group.reshape(QB)
    ids_core = swap(ids, "tiles", 1)
    ids_far = swap(ids, "tiles", 2)
    ids_far_core = swap(ids_far, "tiles", 1)
    ids = jnp.stack([ids, ids_core, ids_far, ids_far_core])
    group_size = parts * TILE_DEV
    owner = ids % group_size // TILE_DEV
    spot = jnp.where(owner == mine, ids // group_size * TILE_DEV + ids % TILE_DEV, -1)

    strips = strips_of(frames, strip_cell)
    bit = 1
    while bit < groups:
        strips = jnp.where((mask & bit) != 0, swap(strips, "frames", bit), strips)
        bit *= 2

    bands = bands_of(frames, weight_map, seam_mask)
    weights = bands[0]

    def send(rows):
        far = swap(rows, "tiles", 2)
        near = swap(rows, "tiles", 1)
        far_near = swap(far, "tiles", 1)
        sums = gather_rows(spot, (rows, near, far, far_near), groups * TILE_DEV)
        sums = sums.reshape(groups, TILE_DEV, rows.shape[1], 128)
        return lax.all_to_all(sums, "frames", split_axis=0, concat_axis=0, tiled=True)

    got_weights = send(weights)
    first, second = blend(strip_cell, strips, bands[1:])
    got_first = send(first)
    got_second = send(second)
    return collapse(got_weights, got_first, got_second)


def solution(mesh):
    in_specs = (
        P(("frames", "tiles"), None, None, None),
        P(("frames", "tiles"), None, None),
        P(("frames", "tiles"), None, None),
        P(("frames", "tiles")),
        P(("frames", "tiles")),
        P(("frames", "tiles"), None, None),
        P(("frames", "tiles"), None),
    )
    out_specs = P(("frames", "tiles"), None, None)
    return jax.shard_map(local, mesh=mesh, in_specs=in_specs, out_specs=out_specs, check_vma=False)
```

profile of v0, /device:TPU:0, one launch (start us, length us, event | category | flops | bytes accessed | tf_op | source)
XLA Modules:
  0.0 154.7 jit_solution(14487326530562941678)
XLA Ops:
  14.2 1.9 %strips.1 = bf16[288,128]{1,0:T(8,128)(2,1)S(1)} custom-call(s32[1]{0:T(128)S(6)} %copy.57.cell, bf16[1,3,128,1024]{3,2,1,0:T(8,128)(2,1)S(1)} %copy-done, bf16[1,3,128,1024]{3,2,1,0:T(8,128)(2,1)S(1)} %copy-done, bf16[64,128]{1,0:T(8,128)(2,1)S(1)} %copy-done.18, bf16[32,64]{1,0:T(8,128)(2,1)S(1)} %copy-done.25, bf16[16,32]{1,0:T(8,128)(2,1)S(1)} %copy-done.32, ...), custom_call_target="tpu_custom_call" | custom-call | flops 2000000000 | bytes 1000000 | tf_op jit(solution)/shard_map/strips/pallas_call | solution.py:179
  16.1 3.0 %collective-permute-start.6 = (bf16[288,128]{1,0:T(8,128)(2,1)S(1)}, bf16[288,128]{1,0:T(8,128)(2,1)}, u32[]{:S(2)}, u32[]{:S(2)}) collective-permute-start(bf16[288,128]{1,0:T(8,128)(2,1)S(1)} %strips.1), channel_id=1, source_target_pairs={{0,4},{4,0},{8,12},{12,8},{16,20},{20,16},{24,28},{28,24},{1,5},{5... | collective-permute-start | bytes 221192 | tf_op jit(solution)/shard_map/ppermute | solution.py:460
  19.8 1.8 %collective-permute-done.6 = bf16[288,128]{1,0:T(8,128)(2,1)} collective-permute-done((bf16[288,128]{1,0:T(8,128)(2,1)S(1)}, bf16[288,128]{1,0:T(8,128)(2,1)}, u32[]{:S(2)}, u32[]{:S(2)}) %collective-permute-start.6) | collective-permute-done | bytes 73760 | tf_op jit(solution)/shard_map/ppermute | solution.py:460
  22.2 2.1 %collective-permute-start.7 = (bf16[288,128]{1,0:T(8,128)(2,1)}, bf16[288,128]{1,0:T(8,128)(2,1)}, u32[]{:S(2)}, u32[]{:S(2)}) collective-permute-start(bf16[288,128]{1,0:T(8,128)(2,1)} %broadcast_select_fusion), channel_id=1, source_target_pairs={{0,8},{4,12},{8,0},{12,4},{16,24},{20,28},{24,16},{28,20},{1,9},{5... | collective-permute-start | bytes 221192 | tf_op jit(solution)/shard_map/ppermute | solution.py:460
  25.1 1.8 %collective-permute-done.7 = bf16[288,128]{1,0:T(8,128)(2,1)} collective-permute-done((bf16[288,128]{1,0:T(8,128)(2,1)}, bf16[288,128]{1,0:T(8,128)(2,1)}, u32[]{:S(2)}, u32[]{:S(2)}) %collective-permute-start.7) | collective-permute-done | bytes 73760 | tf_op jit(solution)/shard_map/ppermute | solution.py:460
  26.9 1.5 broadcast_select_fusion.1
  28.4 3.0 %collective-permute-start.8 = (bf16[288,128]{1,0:T(8,128)(2,1)}, bf16[288,128]{1,0:T(8,128)(2,1)}, u32[]{:S(2)}, u32[]{:S(2)}) collective-permute-start(bf16[288,128]{1,0:T(8,128)(2,1)} %broadcast_select_fusion.1), channel_id=1, source_target_pairs={{0,16},{4,20},{8,24},{12,28},{16,0},{20,4},{24,8},{28,12},{1,17},{... | collective-permute-start | bytes 221192 | tf_op jit(solution)/shard_map/ppermute | solution.py:460
  43.3 5.2 %bands.1 = (bf16[32,32,128]{2,1,0:T(8,128)(2,1)}, f32[3,128,1024]{2,1,0:T(8,128)}, f32[3,64,512]{2,1,0:T(8,128)S(1)}, f32[3,32,256]{2,1,0:T(8,128)S(1)}, f32[3,1...) custom-call(bf16[1,3,128,1024]{3,2,1,0:T(8,128)(2,1)S(1)} %copy-done, ...), custom_call_target="tpu_custom_call" | custom-call | flops 8000000000 | bytes 6000000 | tf_op jit(solution)/shard_map/bands/pallas_call | solution.py:266
  70.6 1.5 blend.1
  72.1 1.6 %collective-permute-start.13 = (bf16[32,64,128]{2,1,0:T(8,128)(2,1)S(1)}, bf16[32,64,128]{2,1,0:T(8,128)(2,1)S(1)}, u32[]{:S(2)}, u32[]{:S(2)}) collective-permute-start(bf16[32,64,128]{2,1,0:T(8,128)(2,1)S(1)} %get-tuple-element.40.a), channel_id=1, source_target_pairs={{0,2},{1,3},{2,0},{3,1},{4,6},{5,7},{6,4},{7,5},{8,10},{9,11},{10,... | collective-permute-start | bytes 1572872 | tf_op jit(solution)/shard_map/ppermute | solution.py:460
  74.2 1.6 %collective-permute-start.1 = (s32[32]{0:T(128)S(1)}, s32[32]{0:T(128)S(1)}, u32[]{:S(2)}, u32[]{:S(2)}) collective-permute-start(s32[32]{0:T(128)S(1)} %bitcast_add_fusion), channel_id=1, source_target_pairs={{0,2},{1,3},{2,0},{3,1},{4,6},{5,7},{6,4},{7,5},{8,10},{9,11},{10,... | collective-permute-start | bytes 392 | tf_op jit(solution)/shard_map/ppermute | solution.py:460
  76.2 13.6 %collective-permute-done.4.c = bf16[32,32,128]{2,1,0:T(8,128)(2,1)} collective-permute-done((bf16[32,32,128]{2,1,0:T(8,128)(2,1)}, bf16[32,32,128]{2,1,0:T(8,128)(2,1)}, u32[]{:S(2)}, u32[]{:S(2)}) %collective-permute-start.4) | collective-permute-done | bytes 262176 | tf_op jit(solution)/shard_map/ppermute | solution.py:460
  91.4 1.5 collective-permute-start.10
  92.9 4.0 %gather_rows.3 = bf16[32,32,128]{2,1,0:T(8,128)(2,1)} custom-call(s32[4,32]{1,0:T(4,128)S(1)} %fusion.4.spot, bf16[32,32,128]{2,1,0:T(8,128)(2,1)} %get-tuple-element.23.a, bf16[32,32,128]{2,1,0:T(8,128)(2,1)} %collective-permute-done.3.b, bf16[32,32,128]{2,1,0:T(8,128)(2,1)} %collective-permute-done.4.c, bf16[32,32,128]{2,1,0:T(8,128)(2,1)} %collective-permute-done.5.d), custom_call_target="tpu_custom_call" | custom-call | flops 1000000000 | bytes 4000000 | tf_op jit(solution)/shard_map/gather_rows/pallas_call | solution.py:363
  96.9 4.0 %all-to-all-start = ((bf16[8,4,32,128]{3,2,1,0:T(8,128)(2,1)}), bf16[8,4,32,128]{3,2,1,0:T(8,128)(2,1)}, u32[]{:S(2)}, u32[]{:S(2)}) async-start(bf16[8,4,32,128]{3,2,1,0:T(8,128)(2,1)} %bitcast.6), calls=%async_computation | async-start | bytes 524288 | tf_op jit(solution)/shard_map/all_to_all | solution.py:493
  101.0 3.6 %gather_rows.5 = bf16[32,64,128]{2,1,0:T(8,128)(2,1)} custom-call(s32[4,32]{1,0:T(4,128)S(1)} %fusion.4.spot, bf16[32,64,128]{2,1,0:T(8,128)(2,1)S(1)} %get-tuple-element.40.a, bf16[32,64,128]{2,1,0:T(8,128)(2,1)S(1)} %collective-permute-done.12.b, bf16[32,64,128]{2,1,0:T(8,128)(2,1)S(1)} %collective-permute-done.13.c, ...), custom_call_target="tpu_custom_call" | custom-call | flops 1000000000 | bytes 4000000 | tf_op jit(solution)/shard_map/gather_rows/pallas_call | solution.py:363
  104.6 5.7 %all-to-all-done.a = bf16[8,4,32,128]{3,2,1,0:T(8,128)(2,1)} async-done(((bf16[8,4,32,128]{3,2,1,0:T(8,128)(2,1)}), bf16[8,4,32,128]{3,2,1,0:T(8,128)(2,1)}, u32[]{:S(2)}, u32[]{:S(2)}) %all-to-all-start) | async-done | bytes 262176 | tf_op jit(solution)/shard_map/all_to_all | solution.py:493
  110.3 3.6 %all-to-all-start.2 = ((bf16[8,4,64,128]{3,2,1,0:T(8,128)(2,1)}), bf16[8,4,64,128]{3,2,1,0:T(8,128)(2,1)S(1)}, u32[]{:S(2)}, u32[]{:S(2)}) async-start(bf16[8,4,64,128]{3,2,1,0:T(8,128)(2,1)} %bitcast.9), calls=%async_computation.2 | async-start | bytes 1048576 | tf_op jit(solution)/shard_map/all_to_all | solution.py:493
  114.4 1.6 %collective-permute-done.9.b = bf16[32,80,128]{2,1,0:T(8,128)(2,1)S(1)} collective-permute-done((bf16[32,80,128]{2,1,0:T(8,128)(2,1)S(1)}, bf16[32,80,128]{2,1,0:T(8,128)(2,1)S(1)}, u32[]{:S(2)}, u32[]{:S(2)}) %collective-permute-start.9) | collective-permute-done | bytes 655392 | tf_op jit(solution)/shard_map/ppermute | solution.py:460
  116.9 2.8 %gather_rows.4 = bf16[32,80,128]{2,1,0:T(8,128)(2,1)S(1)} custom-call(s32[4,32]{1,0:T(4,128)S(1)} %fusion.4.spot, bf16[32,80,128]{2,1,0:T(8,128)(2,1)S(1)} %get-tuple-element.39.a, bf16[32,80,128]{2,1,0:T(8,128)(2,1)S(1)} %collective-permute-done.9.b, bf16[32,80,128]{2,1,0:T(8,128)(2,1)S(1)} %collective-permute-done.10.c, ...), custom_call_target="tpu_custom_call" | custom-call | flops 1000000000 | bytes 4000000 | tf_op jit(solution)/shard_map/gather_rows/pallas_call | solution.py:363
  119.7 8.3 %all-to-all-done.2.c = bf16[8,4,64,128]{3,2,1,0:T(8,128)(2,1)S(1)} async-done(((bf16[8,4,64,128]{3,2,1,0:T(8,128)(2,1)}), bf16[8,4,64,128]{3,2,1,0:T(8,128)(2,1)S(1)}, u32[]{:S(2)}, u32[]{:S(2)}) %all-to-all-start.2) | async-done | bytes 524320 | tf_op jit(solution)/shard_map/all_to_all | solution.py:493
  128.0 21.2 %all_to_all.15.b = bf16[8,4,80,128]{3,2,1,0:T(8,128)(2,1)} all-to-all(bf16[8,4,80,128]{3,2,1,0:T(8,128)(2,1)S(1)} %bitcast.17), channel_id=1, replica_groups=mesh['frames'=8,'tiles'=4] {'frames'}, dimensions={0} | all-to-all | bytes 1310720 | tf_op jit(solution)/shard_map/all_to_all | solution.py:493
  149.3 3.6 %collapse.1 = f32[4,3,4096]{2,1,0:T(4,128)} custom-call(bf16[8,4,32,128]{3,2,1,0:T(8,128)(2,1)} %all-to-all-done.a, bf16[8,4,80,128]{3,2,1,0:T(8,128)(2,1)} %all_to_all.15.b, bf16[8,4,64,128]{3,2,1,0:T(8,128)(2,1)} %copy-done.70, bf16[128,128]{1,0:T(8,128)(2,1)} %constant.164.clone.m43, bf16[128,128]{1,0:T(8,128)(2,1)} %constant.165.clone.m32, ...), custom_call_target="tpu_custom_call" | custom-call | flops 1000000000 | bytes 3000000 | tf_op jit(solution)/shard_map/collapse/pallas_call | solution.py:448
  152.9 1.8 %copy.56 = f32[4,3,4096]{2,0,1:T(4,128)} copy(f32[4,3,4096]{2,1,0:T(4,128)} %collapse.1) | data formatting | bytes 393216 | tf_op jit(solution)/shard_map/collapse/pallas_call | solution.py:448
  (172 shorter events, 52.9 us)
Async XLA Ops:
  14.2 17.3 %copy-start.1 = (bf16[1,3,128,1024]{3,2,1,0:T(8,128)(2,1)S(1)}, bf16[1,3,128,1024]{3,2,1,0:T(8,128)(2,1)}, u32[]{:S(2)}) copy-start(bf16[1,3,128,1024]{3,2,1,0:T(8,128)(2,1)} %xb.1) | copy-start | bytes 2359300
  14.2 17.3 %copy-start.2 = (bf16[1,128,1024]{2,1,0:T(8,128)(2,1)S(1)}, bf16[1,128,1024]{2,1,0:T(8,128)(2,1)}, u32[]{:S(2)}) copy-start(bf16[1,128,1024]{2,1,0:T(8,128)(2,1)} %w.1) | copy-start | bytes 786436
  14.2 17.3 %copy-start.3 = (bf16[1024,512]{1,0:T(8,128)(2,1)S(1)}, bf16[1024,512]{1,0:T(8,128)(2,1)}, u32[]{:S(2)}) copy-start(bf16[1024,512]{1,0:T(8,128)(2,1)} %constant.156.clone.refs_8_) | copy-start | bytes 3145732
  14.2 17.3 %copy-start.4 = (bf16[512,1024]{1,0:T(8,128)(2,1)S(1)}, bf16[512,1024]{1,0:T(8,128)(2,1)}, u32[]{:S(2)}) copy-start(bf16[512,1024]{1,0:T(8,128)(2,1)} %constant.159.clone.refs_12_) | copy-start | bytes 3145732
  14.2 17.3 %copy-start.5 = (bf16[512,256]{1,0:T(8,128)(2,1)S(1)}, bf16[512,256]{1,0:T(8,128)(2,1)}, u32[]{:S(2)}) copy-start(bf16[512,256]{1,0:T(8,128)(2,1)} %constant.157.clone.refs_9_) | copy-start | bytes 786436
  14.2 17.3 %copy-start.8 = (bf16[256,128]{1,0:T(8,128)(2,1)S(1)}, bf16[256,128]{1,0:T(8,128)(2,1)}, u32[]{:S(2)}) copy-start(bf16[256,128]{1,0:T(8,128)(2,1)} %constant.147.clone.refs_10_.refs_8_) | copy-start | bytes 196612
  16.1 5.5 %collective-permute-start.6 = (bf16[288,128]{1,0:T(8,128)(2,1)S(1)}, bf16[288,128]{1,0:T(8,128)(2,1)}, u32[]{:S(2)}, u32[]{:S(2)}) collective-permute-start(bf16[288,128]{1,0:T(8,128)(2,1)S(1)} %strips.1), channel_id=1, source_target_pairs={{0,4},{4,0},{8,12},{12,8},{16,20},{20,16},{24,28},{28,24},{1,5},{5... | collective-permute-start | bytes 221192 | tf_op jit(solution)/shard_map/ppermute | solution.py:460
  22.2 4.7 %collective-permute-start.7 = (bf16[288,128]{1,0:T(8,128)(2,1)}, bf16[288,128]{1,0:T(8,128)(2,1)}, u32[]{:S(2)}, u32[]{:S(2)}) collective-permute-start(bf16[288,128]{1,0:T(8,128)(2,1)} %broadcast_select_fusion), channel_id=1, source_target_pairs={{0,8},{4,12},{8,0},{12,4},{16,24},{20,28},{24,16},{28,20},{1,9},{5... | collective-permute-start | bytes 221192 | tf_op jit(solution)/shard_map/ppermute | solution.py:460
  28.4 28.8 %collective-permute-start.8 = (bf16[288,128]{1,0:T(8,128)(2,1)}, bf16[288,128]{1,0:T(8,128)(2,1)}, u32[]{:S(2)}, u32[]{:S(2)}) collective-permute-start(bf16[288,128]{1,0:T(8,128)(2,1)} %broadcast_select_fusion.1), channel_id=1, source_target_pairs={{0,16},{4,20},{8,24},{12,28},{16,0},{20,4},{24,8},{28,12},{1,17},{... | collective-permute-start | bytes 221192 | tf_op jit(solution)/shard_map/ppermute | solution.py:460
  72.1 18.4 %collective-permute-start.13 = (bf16[32,64,128]{2,1,0:T(8,128)(2,1)S(1)}, bf16[32,64,128]{2,1,0:T(8,128)(2,1)S(1)}, u32[]{:S(2)}, u32[]{:S(2)}) collective-permute-start(bf16[32,64,128]{2,1,0:T(8,128)(2,1)S(1)} %get-tuple-element.40.a), channel_id=1, source_target_pairs={{0,2},{1,3},{2,0},{3,1},{4,6},{5,7},{6,4},{7,5},{8,10},{9,11},{10,... | collective-permute-start | bytes 1572872 | tf_op jit(solution)/shard_map/ppermute | solution.py:460
  73.6 16.2 %collective-permute-start.4 = (bf16[32,32,128]{2,1,0:T(8,128)(2,1)}, bf16[32,32,128]{2,1,0:T(8,128)(2,1)}, u32[]{:S(2)}, u32[]{:S(2)}) collective-permute-start(bf16[32,32,128]{2,1,0:T(8,128)(2,1)} %get-tuple-element.23.a), channel_id=1, source_target_pairs={{0,2},{1,3},{2,0},{3,1},{4,6},{5,7},{6,4},{7,5},{8,10},{9,11},{10,... | collective-permute-start | bytes 786440 | tf_op jit(solution)/shard_map/ppermute | solution.py:460
  74.2 15.7 %collective-permute-start.1 = (s32[32]{0:T(128)S(1)}, s32[32]{0:T(128)S(1)}, u32[]{:S(2)}, u32[]{:S(2)}) collective-permute-start(s32[32]{0:T(128)S(1)} %bitcast_add_fusion), channel_id=1, source_target_pairs={{0,2},{1,3},{2,0},{3,1},{4,6},{5,7},{6,4},{7,5},{8,10},{9,11},{10,... | collective-permute-start | bytes 392 | tf_op jit(solution)/shard_map/ppermute | solution.py:460
  75.7 14.6 %collective-permute-start = (s32[32]{0:T(128)S(1)}, s32[32]{0:T(128)S(1)}, u32[]{:S(2)}, u32[]{:S(2)}) collective-permute-start(s32[32]{0:T(128)S(1)} %bitcast_add_fusion), channel_id=1, source_target_pairs={{0,1},{1,0},{2,3},{3,2},{4,5},{5,4},{6,7},{7,6},{8,9},{9,8},{10,11... | collective-permute-start | bytes 392 | tf_op jit(solution)/shard_map/ppermute | solution.py:460
  75.7 17.2 %collective-permute-start.3 = (bf16[32,32,128]{2,1,0:T(8,128)(2,1)}, bf16[32,32,128]{2,1,0:T(8,128)(2,1)}, u32[]{:S(2)}, u32[]{:S(2)}) collective-permute-start(bf16[32,32,128]{2,1,0:T(8,128)(2,1)} %get-tuple-element.23.a), channel_id=1, source_target_pairs={{0,1},{1,0},{2,3},{3,2},{4,5},{5,4},{6,7},{7,6},{8,9},{9,8},{10,11... | collective-permute-start | bytes 786440 | tf_op jit(solution)/shard_map/ppermute | solution.py:460
  89.9 3.1 %collective-permute-start.5 = (bf16[32,32,128]{2,1,0:T(8,128)(2,1)}, bf16[32,32,128]{2,1,0:T(8,128)(2,1)}, u32[]{:S(2)}, u32[]{:S(2)}) collective-permute-start(bf16[32,32,128]{2,1,0:T(8,128)(2,1)} %collective-permute-done.4.c), channel_id=1, source_target_pairs={{0,1},{1,0},{2,3},{3,2},{4,5},{5,4},{6,7},{7,6},{8,9},{9,8},{10,11... | collective-permute-start | bytes 786440 | tf_op jit(solution)/shard_map/ppermute | solution.py:460
  89.9 1.5 collective-permute-start.2
  90.4 10.6 %collective-permute-start.12 = (bf16[32,64,128]{2,1,0:T(8,128)(2,1)S(1)}, bf16[32,64,128]{2,1,0:T(8,128)(2,1)S(1)}, u32[]{:S(2)}, u32[]{:S(2)}) collective-permute-start(bf16[32,64,128]{2,1,0:T(8,128)(2,1)S(1)} %get-tuple-element.40.a), channel_id=1, source_target_pairs={{0,1},{1,0},{2,3},{3,2},{4,5},{5,4},{6,7},{7,6},{8,9},{9,8},{10,11... | collective-permute-start | bytes 1572872 | tf_op jit(solution)/shard_map/ppermute | solution.py:460
  90.5 10.5 %collective-permute-start.14 = (bf16[32,64,128]{2,1,0:T(8,128)(2,1)S(1)}, bf16[32,64,128]{2,1,0:T(8,128)(2,1)S(1)}, u32[]{:S(2)}, u32[]{:S(2)}) collective-permute-start(bf16[32,64,128]{2,1,0:T(8,128)(2,1)S(1)} %collective-permute-done.13.c), channel_id=1, source_target_pairs={{0,1},{1,0},{2,3},{3,2},{4,5},{5,4},{6,7},{7,6},{8,9},{9,8},{10,11... | collective-permute-start | bytes 1572872 | tf_op jit(solution)/shard_map/ppermute | solution.py:460
  91.4 22.5 %collective-permute-start.10 = (bf16[32,80,128]{2,1,0:T(8,128)(2,1)S(1)}, bf16[32,80,128]{2,1,0:T(8,128)(2,1)S(1)}, u32[]{:S(2)}, u32[]{:S(2)}) collective-permute-start(bf16[32,80,128]{2,1,0:T(8,128)(2,1)S(1)} %get-tuple-element.39.a), channel_id=1, source_target_pairs={{0,2},{1,3},{2,0},{3,1},{4,6},{5,7},{6,4},{7,5},{8,10},{9,11},{10,... | collective-permute-start | bytes 1966088 | tf_op jit(solution)/shard_map/ppermute | solution.py:460
  96.9 13.3 %all-to-all-start = ((bf16[8,4,32,128]{3,2,1,0:T(8,128)(2,1)}), bf16[8,4,32,128]{3,2,1,0:T(8,128)(2,1)}, u32[]{:S(2)}, u32[]{:S(2)}) async-start(bf16[8,4,32,128]{3,2,1,0:T(8,128)(2,1)} %bitcast.6), calls=%async_computation | async-start | bytes 524288 | tf_op jit(solution)/shard_map/all_to_all | solution.py:493
  110.3 17.8 %all-to-all-start.2 = ((bf16[8,4,64,128]{3,2,1,0:T(8,128)(2,1)}), bf16[8,4,64,128]{3,2,1,0:T(8,128)(2,1)S(1)}, u32[]{:S(2)}, u32[]{:S(2)}) async-start(bf16[8,4,64,128]{3,2,1,0:T(8,128)(2,1)} %bitcast.9), calls=%async_computation.2 | async-start | bytes 1048576 | tf_op jit(solution)/shard_map/all_to_all | solution.py:493
  113.8 2.1 %collective-permute-start.9 = (bf16[32,80,128]{2,1,0:T(8,128)(2,1)S(1)}, bf16[32,80,128]{2,1,0:T(8,128)(2,1)S(1)}, u32[]{:S(2)}, u32[]{:S(2)}) collective-permute-start(bf16[32,80,128]{2,1,0:T(8,128)(2,1)S(1)} %get-tuple-element.39.a), channel_id=1, source_target_pairs={{0,1},{1,0},{2,3},{3,2},{4,5},{5,4},{6,7},{7,6},{8,9},{9,8},{10,11... | collective-permute-start | bytes 1966088 | tf_op jit(solution)/shard_map/ppermute | solution.py:460
  113.9 3.0 %collective-permute-start.11 = (bf16[32,80,128]{2,1,0:T(8,128)(2,1)S(1)}, bf16[32,80,128]{2,1,0:T(8,128)(2,1)S(1)}, u32[]{:S(2)}, u32[]{:S(2)}) collective-permute-start(bf16[32,80,128]{2,1,0:T(8,128)(2,1)S(1)} %collective-permute-done.10.c), channel_id=1, source_target_pairs={{0,1},{1,0},{2,3},{3,2},{4,5},{5,4},{6,7},{7,6},{8,9},{9,8},{10,11... | collective-permute-start | bytes 1966088 | tf_op jit(solution)/shard_map/ppermute | solution.py:460
  128.0 21.2 %copy-start.70 = (bf16[8,4,64,128]{3,2,1,0:T(8,128)(2,1)}, bf16[8,4,64,128]{3,2,1,0:T(8,128)(2,1)S(1)}, u32[]{:S(2)}) copy-start(bf16[8,4,64,128]{3,2,1,0:T(8,128)(2,1)S(1)} %all-to-all-done.2.c) | copy-start | bytes 1572868
  (66 other events, 71.0 us)
where the time goes:
time: 158 us; the launch traced here: 155 us
  local copies, waits for them, and re-layouts  49.1 us (31%)
  waiting for transfers between devices  34.2 us (22%)
  starting transfers between devices  23 us (15%)
  Pallas kernels  22.5 us (14%)
  blocking collectives  21.2 us (13%)
  other arithmetic  3.09 us (2%)
    unnamed x147, local copies, waits for them, and re-layouts  47.3 us
    all_to_all x1, blocking collectives, send(): lax.all_to_all(sums, 'frames', split_axis=0, concat_axis=0, tiled=True)  21.2 us
    ppermute x15, waiting for transfers between devices, swap(): return lax.ppermute(value, axis, [(i, i ^ bit) for i in range(size)])  20.2 us
    ppermute x15, starting transfers between devices, swap(): return lax.ppermute(value, axis, [(i, i ^ bit) for i in range(size)])  15.4 us
    all_to_all x2, waiting for transfers between devices, send(): lax.all_to_all(sums, 'frames', split_axis=0, concat_axis=0, tiled=True)  14 us
    pallas_call x3, Pallas kernels, gather_rows(): pl.pallas_call(gather_kernel, in_specs=[pl.BlockSpec(memory_space=pltpu.S...  10.4 us
    all_to_all x2, starting transfers between devices, send(): lax.all_to_all(sums, 'frames', split_axis=0, concat_axis=0, tiled=True)  7.59 us
    pallas_call x1, Pallas kernels, bands_of(): pl.pallas_call(bands_kernel, out_shape=out_shape, compiler_params=pltpu.C...  5.15 us
  transfers between devices with their start and end apart: 17, of which 8 were waited for; matrix products, arithmetic and copies ran while one was open for 1% of the time, Pallas kernels for 10%

commit v1 on v0

--- a/solution.py
+++ b/solution.py
@@ -14,6 +14,8 @@
 QB = 32
 WIN = 256
 TILE_DEV = 4
+VMEM = 30 << 20
+ROUTE = 4096
 F32 = jnp.float32
 BF16 = jnp.bfloat16
 
@@ -72,8 +74,44 @@
     return s, g
 
 
-def const(m):
-    return jnp.asarray(m, BF16)
+def pack(mats, width):
+    places, row, col, height = {}, 0, 0, 0
+    for name in sorted(mats, key=lambda n: (-mats[n].shape[0], -mats[n].shape[1], n)):
+        h, w = mats[name].shape
+        wide = -(-w // 128) * 128
+        if col + wide > width:
+            row, col, height = row + height, 0, 0
+        height = max(height, -(-h // 16) * 16)
+        places[name] = (row, col, h, w)
+        col += wide
+    out = np.zeros((row + height, width), np.float32)
+    for name, (r, c, h, w) in places.items():
+        out[r : r + h, c : c + w] = mats[name]
+    return jnp.asarray(out, BF16), places
+
+
+def unpack(ref, places):
+    return {name: ref[r : r + h, c : c + w] for name, (r, c, h, w) in places.items()}
+
+
+def small_matrices():
+    v, g = vertical()
+    s, gh = horizontal(WIN, 0)
+    sm, _ = horizontal(64, 0)
+    mats = {f"v{k}": m for k, m in v.items()} | {f"g{k}": m for k, m in g.items()}
+    mats |= {f"s{k}": m for k, m in s.items()} | {f"h{k}": m for k, m in gh.items()}
+    mats |= {f"m{k}": m for k, m in sm.items()} | {"order": row_order()}
+    return pack(mats, 512)
+
+
+def large_matrices():
+    s, gh = horizontal(FW, 128)
+    mats = {f"s{k}": m for k, m in s.items()} | {f"h{k}": m for k, m in gh.items()}
+    return pack(mats, 1024)
+
+
+def levels_of(mats, letter):
+    return {int(n[1:]): m for n, m in mats.items() if n[0] == letter and n[1:].isdigit()}
 
 
 def mm(a, b):
@@ -95,9 +133,13 @@
     return mm(m, hi) + mm(m, lo)
 
 
-def pyramid(planes, v, s):
+def mmt(a, b):
+    return lax.dot_general(a, b, (((1,), (1,)), ((), ())), preferred_element_type=F32)
+
+
+def pyramid(planes, v, s, product=mm):
     n = len(planes)
-    t = jnp.concatenate([mm(v[1], p) for p in planes], axis=0)
+    t = jnp.concatenate([product(v[1], p) for p in planes], axis=0)
     levels = {1: rdot(t, s[1])}
     for k in range(2, 5):
         prev = levels[k - 1]
@@ -120,13 +162,10 @@
     return jnp.where(hit, 1.0, 0.0).astype(BF16)
 
 
-def strips_kernel(cell, xa, xb, *refs):
-    mats, (out, acc) = refs[:-2], refs[-2:]
-    v = {k: mats[k - 1][...] for k in range(1, 5)}
-    gv = {k: mats[4 + k][...] for k in range(4)}
-    s = {k: mats[7 + k][...] for k in range(1, 5)}
-    gh = {k: mats[12 + k][...] for k in range(4)}
-    order = mats[16][...]
+def strips_kernel(places, cell, xa, xb, packed, out, acc):
+    mats = unpack(packed, places)
+    v, gv, s, gh = (levels_of(mats, letter) for letter in "vgsh")
+    order = mats["order"]
     first = window_tile(cell[0]) * 128
     planes = [jnp.concatenate([xa[0, c], xb[0, c]], axis=1) for c in range(COLOURS)]
     levels = pyramid(planes, v, s)
@@ -160,11 +199,7 @@
 
 
 def strips_of(frames, cell):
-    v, g = vertical()
-    s, gh = horizontal(WIN, 0)
-    mats = [const(v[k]) for k in range(1, 5)] + [const(g[k]) for k in range(4)]
-    mats += [const(s[k]) for k in range(1, 5)] + [const(gh[k]) for k in range(4)]
-    mats.append(const(row_order()))
+    packed, places = small_matrices()
     grid_spec = pltpu.PrefetchScalarGridSpec(
         num_scalar_prefetch=1,
         grid=(1,),
@@ -172,18 +207,18 @@
             pl.BlockSpec((1, COLOURS, FH, 128), lambda i, c: (0, 0, 0, window_tile(c[0]))),
             pl.BlockSpec((1, COLOURS, FH, 128), lambda i, c: (0, 0, 0, window_tile(c[0]) + 1)),
         ]
-        + [full_spec(m) for m in mats],
+        + [full_spec(packed)],
         out_specs=pl.BlockSpec((288, 128), lambda i, c: (0, 0)),
         scratch_shapes=[pltpu.VMEM((96, 128), F32)],
     )
     return pl.pallas_call(
-        strips_kernel,
+        functools.partial(strips_kernel, places),
         grid_spec=grid_spec,
         out_shape=jax.ShapeDtypeStruct((288, 128), BF16),
-        compiler_params=pltpu.CompilerParams(vmem_limit_bytes=48 << 20),
+        compiler_params=pltpu.CompilerParams(vmem_limit_bytes=VMEM),
         cost_estimate=pl.CostEstimate(flops=2 * 10**9, bytes_accessed=10**6, transcendentals=0),
         name="strips",
-    )(cell, frames, frames, *mats)
+    )(cell, frames, frames, packed)
 
 
 def lane_index():
@@ -209,70 +244,75 @@
     return pltpu.roll(out, (base - cc * width) % 128, 1)
 
 
-def bands_kernel(x, w, m, *refs):
-    mats, outs = refs[:21], refs[21:]
-    v = {k: mats[k - 1][...] for k in range(1, 5)}
-    gv = {k: mats[4 + k][...] for k in range(4)}
-    s = {k: mats[7 + k][...] for k in range(1, 5)}
-    gh = {k: mats[12 + k][...] for k in range(4)}
-    order = mats[16][...]
-    sm = {k: mats[16 + k][...] for k in range(1, 5)}
-    wblocks, b0, b1, b2, b3, b4, wp, w1, w2, w3, w4, n0, n1, n2, n3, n4 = outs
+STATE_ROWS = 816
+
+
+def state_views(state):
+    at = lambda r, h, c, w: (slice(r, r + h), slice(c, c + w))
+    b0 = [at(128 * c, 128, 0, 1024) for c in range(3)]
+    l1 = [at(384, 64, 0, 512), at(384, 64, 512, 512), at(448, 64, 0, 512), at(448, 64, 512, 512)]
+    l2 = [at(512, 32, 256 * c, 256) for c in range(4)]
+    l3 = [at(544, 16, 128 * c, 128) for c in range(4)]
+    l4 = [at(544, 16, 512 + 128 * c, 128) for c in range(4)]
+    levels = [b0 + [at(560, 128, 0, 1024)], l1, l2, l3, l4]
+    masks = [at(688, 128 >> k, 128 * k, 64 >> k) for k in range(4)] + [at(688, 16, 512, 4)]
+    return levels, masks
+
+
+def bands_kernel(small_places, large_places, x, w, m, small, large, wblocks, state):
+    mats = unpack(small, small_places)
+    v, gv, sm = (levels_of(mats, letter) for letter in "vgm")
+    order = mats["order"]
+    mats = unpack(large, large_places)
+    s, gh = (levels_of(mats, letter) for letter in "sh")
+    views, mask_views = state_views(state)
     planes = [x[0, c] for c in range(COLOURS)] + [w[0]]
     weights = mm(order, planes[3])
-    wp[...] = weights.astype(BF16)
+    state[views[0][3]] = weights
 
     def store(q, piece):
         wblocks[q] = piece.astype(BF16)
 
     fold_level0(weights, store)
     levels = pyramid(planes, v, s)
-    bands, wl = (b1, b2, b3), (w1, w2, w3, w4)
     for k in range(1, 5):
         rows = levels[k].shape[0] // 4
-        wl[k - 1][...] = levels[k][3 * rows :]
+        state[views[k][3]] = levels[k][3 * rows :]
     back = grown(levels[1][: 3 * 64], COLOURS, gv[0], gh[0])
     for c in range(COLOURS):
-        b0[c] = mm(order, planes[c]) - back[c]
+        state[views[0][c]] = mm(order, planes[c]) - back[c]
     for k in range(1, 4):
         rows = levels[k].shape[0] // 4
         below = levels[k + 1].shape[0] // 4
         back = grown(levels[k + 1][: 3 * below], COLOURS, gv[k], gh[k])
         for c in range(COLOURS):
-            bands[k - 1][c] = levels[k][c * rows : (c + 1) * rows] - back[c]
+            state[views[k][c]] = levels[k][c * rows : (c + 1) * rows] - back[c]
     for c in range(COLOURS):
-        b4[c] = levels[4][c * 16 : (c + 1) * 16]
+        state[views[4][c]] = levels[4][c * 16 : (c + 1) * 16]
     other = (1.0 - m[0].astype(F32)).astype(BF16)
-    n0[...] = mm(order, other)
-    masks = pyramid([other], v, sm)
-    for k, ref in enumerate((n1, n2, n3, n4)):
-        ref[...] = masks[k + 1]
+    state[mask_views[0]] = mmt(order, other)
+    masks = pyramid([other], v, sm, mmt)
+    for k in range(1, 5):
+        state[mask_views[k]] = masks[k]
 
 
 def bands_of(frames, weight_map, seam_mask):
-    v, g = vertical()
-    s, gh = horizontal(FW, 128)
-    sm, _ = horizontal(64, 0)
-    mats = [const(v[k]) for k in range(1, 5)] + [const(g[k]) for k in range(4)]
-    mats += [const(s[k]) for k in range(1, 5)] + [const(gh[k]) for k in range(4)]
-    mats.append(const(row_order()))
-    mats += [const(sm[k]) for k in range(1, 5)]
-    out_shape = [jax.ShapeDtypeStruct((QB, 32, 128), BF16)]
-    shapes = [(128, 1024), (64, 512), (32, 256), (16, 128), (16, 128)]
-    out_shape += [jax.ShapeDtypeStruct((COLOURS,) + sh, F32) for sh in shapes]
-    out_shape += [jax.ShapeDtypeStruct(shapes[0], BF16)]
-    out_shape += [jax.ShapeDtypeStruct(sh, F32) for sh in shapes[1:]]
-    out_shape += [jax.ShapeDtypeStruct(sh, F32) for sh in ((128, 64), (64, 32), (32, 16), (16, 8), (16, 4))]
+    small, small_places = small_matrices()
+    large, large_places = large_matrices()
     return pl.pallas_call(
-        bands_kernel,
-        out_shape=out_shape,
-        compiler_params=pltpu.CompilerParams(vmem_limit_bytes=48 << 20),
+        functools.partial(bands_kernel, small_places, large_places),
+        out_shape=[jax.ShapeDtypeStruct((QB, 32, 128), BF16), jax.ShapeDtypeStruct((STATE_ROWS, FW), F32)],
+        compiler_params=pltpu.CompilerParams(vmem_limit_bytes=VMEM),
         cost_estimate=pl.CostEstimate(flops=8 * 10**9, bytes_accessed=6 * 10**6, transcendentals=0),
         name="bands",
-    )(frames, weight_map, seam_mask, *mats)
-
-
-def blend_kernel(cell, strips, b0, b1, b2, b3, b4, wp, w1, w2, w3, w4, n0, n1, n2, n3, n4, first, second):
+    )(frames, weight_map, jnp.swapaxes(seam_mask, 1, 2), small, large)
+
+
+def blend_kernel(cell, strips, state, first, second):
+    views, mask_views = state_views(state)
+    (b0, b1, b2, b3, b4) = [[state[view] for view in views[k][:3]] for k in range(5)]
+    (wp, w1, w2, w3, w4) = [state[views[k][3]] for k in range(5)]
+    (n0, n1, n2, n3, n4) = [state[view] for view in mask_views]
     start = cell[0] * 16
     low = strips[192:288]
 
@@ -280,14 +320,14 @@
         return band + share * (remote - band)
 
     widths = (1024, 512, 256, 128, 128)
-    share0 = mm(n0[...].astype(BF16), place(64, 1024, 0, 64, start))
+    share0 = mm(n0.astype(BF16), place(64, 1024, 0, 64, start))
     share = [share0]
     for k, ref in enumerate((n1, n2, n3, n4)):
-        share.append(rdot(ref[...], place(64 >> (k + 1), widths[k + 1], 0, 64 >> (k + 1), start >> (k + 1))))
+        share.append(rdot(ref, place(64 >> (k + 1), widths[k + 1], 0, 64 >> (k + 1), start >> (k + 1))))
     top = strips[0:192]
     remote0 = [mm(top, place(128, 1024, 0, 64, start)), mm(top, place(128, 1024, 64, 64, start))]
     remote0 = jnp.concatenate(remote0, axis=0)
-    weights = wp[...].astype(F32)
+    weights = wp
     for c in range(COLOURS):
         p = weights * mixed(b0[c], remote0[c * 128 : (c + 1) * 128], share[0])
         out, row = (first, 0) if c == 0 else (second, 32 * (c - 1))
@@ -298,7 +338,7 @@
         fold_level0(p, store)
     remote1 = [mm(low, place(128, 512, 0, 32, start >> 1)), mm(low, place(128, 512, 32, 32, start >> 1))]
     remote1 = jnp.concatenate(remote1, axis=0)
-    parts = [w1[...] * mixed(b1[c], remote1[c * 64 : (c + 1) * 64], share[1]) for c in range(COLOURS)] + [w1[...]]
+    parts = [w1 * mixed(b1[c], remote1[c * 64 : (c + 1) * 64], share[1]) for c in range(COLOURS)] + [w1]
     for r in range(2):
         for j in range(4):
             turned = [parts[ch][r * 32 : r * 32 + 32, j * 128 : j * 128 + 128] for ch in range(4)]
@@ -308,9 +348,9 @@
     remote2 = mm(low, place(128, 256, 64, 16, start >> 2))
     remote3 = mm(low[0:48], place(128, 128, 80, 8, start >> 3))
     remote4 = mm(low[0:48], place(128, 128, 88, 4, start >> 4))
-    parts2 = [w2[...] * mixed(b2[c], remote2[c * 32 : (c + 1) * 32], share[2]) for c in range(COLOURS)] + [w2[...]]
-    parts3 = [w3[...] * mixed(b3[c], remote3[c * 16 : (c + 1) * 16], share[3]) for c in range(COLOURS)] + [w3[...]]
-    parts4 = [w4[...] * mixed(b4[c], remote4[c * 16 : (c + 1) * 16], share[4]) for c in range(COLOURS)] + [w4[...]]
+    parts2 = [w2 * mixed(b2[c], remote2[c * 32 : (c + 1) * 32], share[2]) for c in range(COLOURS)] + [w2]
+    parts3 = [w3 * mixed(b3[c], remote3[c * 16 : (c + 1) * 16], share[3]) for c in range(COLOURS)] + [w3]
+    parts4 = [w4 * mixed(b4[c], remote4[c * 16 : (c + 1) * 16], share[4]) for c in range(COLOURS)] + [w4]
     lane = lane_index()
     for r in range(2):
         turned3 = [pltpu.roll(parts3[ch][r * 8 : r * 8 + 8], 8 * ch, 1) for ch in range(4)]
@@ -328,51 +368,70 @@
                 first[r * 16 + c, 64:80, :] = jnp.concatenate([head, tail], axis=0).astype(BF16)
 
 
-def blend(cell, strips, parts):
+def blend(cell, strips, state):
     vmem = pl.BlockSpec(memory_space=pltpu.VMEM)
     return pl.pallas_call(
         blend_kernel,
-        in_specs=[pl.BlockSpec(memory_space=pltpu.SMEM)] + [vmem] * 16,
+        in_specs=[pl.BlockSpec(memory_space=pltpu.SMEM)] + [vmem] * 2,
         out_shape=[jax.ShapeDtypeStruct((QB, 80, 128), BF16), jax.ShapeDtypeStruct((QB, 64, 128), BF16)],
-        compiler_params=pltpu.CompilerParams(vmem_limit_bytes=48 << 20),
+        compiler_params=pltpu.CompilerParams(vmem_limit_bytes=VMEM),
         cost_estimate=pl.CostEstimate(flops=4 * 10**9, bytes_accessed=4 * 10**6, transcendentals=0),
         name="blend",
-    )(cell, strips, *parts)
-
-
-def gather_kernel(spot, a, b, c, d, out, acc):
+    )(cell, strips, state)
+
+
+def routes_kernel(spot, lists, counts):
+    for source in range(4):
+
+        def body(q, count, source=source):
+            at = spot[source, q]
+            lists[source, count] = q * ROUTE + at
+            return jnp.where(at >= 0, count + 1, count)
+
+        counts[source] = lax.fori_loop(0, QB, body, 0)
+
+
+def routes_of(spot):
+    smem = pl.BlockSpec(memory_space=pltpu.SMEM)
+    return pl.pallas_call(
+        routes_kernel,
+        in_specs=[smem],
+        out_specs=[smem, smem],
+        out_shape=[jax.ShapeDtypeStruct((4, QB + 1), jnp.int32), jax.ShapeDtypeStruct((4,), jnp.int32)],
+        name="routes",
+    )(spot)
+
+
+def gather_kernel(lists, counts, a, b, c, d, out, acc):
     acc[...] = jnp.zeros_like(acc)
     for source, ref in enumerate((a, b, c, d)):
 
-        def body(q, carry, source=source, ref=ref):
-            at = spot[source, q]
-
-            @pl.when(at >= 0)
-            def _():
-                acc[at] = acc[at] + ref[q].astype(F32)
-
+        def body(i, carry, source=source, ref=ref):
+            entry = lists[source, i]
+            q, at = entry // ROUTE, entry % ROUTE
+            acc[at] = acc[at] + ref[q].astype(F32)
             return carry
 
-        lax.fori_loop(0, QB, body, 0)
+        lax.fori_loop(0, counts[source], body, 0)
     out[...] = acc[...].astype(BF16)
 
 
-def gather_rows(spot, rows, tiles):
+def gather_rows(routes, rows, tiles):
     height = rows[0].shape[1]
     vmem = pl.BlockSpec(memory_space=pltpu.VMEM)
     return pl.pallas_call(
         gather_kernel,
-        in_specs=[pl.BlockSpec(memory_space=pltpu.SMEM)] + [vmem] * 4,
+        in_specs=[pl.BlockSpec(memory_space=pltpu.SMEM)] * 2 + [vmem] * 4,
         out_shape=jax.ShapeDtypeStruct((tiles, height, 128), BF16),
         scratch_shapes=[pltpu.VMEM((tiles, height, 128), F32)],
-        compiler_params=pltpu.CompilerParams(vmem_limit_bytes=48 << 20),
+        compiler_params=pltpu.CompilerParams(vmem_limit_bytes=VMEM),
         cost_estimate=pl.CostEstimate(flops=10**9, bytes_accessed=4 * 10**6, transcendentals=0),
         name="gather_rows",
-    )(spot, *rows)
+    )(*routes, *rows)
 
 
 def collapse_matrices():
-    def across(src, dst, width, copies=1):
+    def across(src, dst, width):
         g = grow_matrix(width).T
         m = np.zeros((128, 128), np.float32)
         for ch in range(COLOURS):
@@ -393,20 +452,15 @@
             m[t * rows_out : t * rows_out + g.shape[0], t * rows_in : t * rows_in + n] = g
         return m
 
-    return [
-        across(96, 64, 4),
-        across(64, 0, 8),
-        across(0, 0, 16),
-        last,
-        down(4, 16, 16),
-        down(8, 16, 16),
-        down(16, 16, 32),
-        down(32, 32, 32, 0),
-        down(32, 32, 32, 1),
-    ]
-
-
-def collapse_kernel(a, b, c, m43, m32, m21, m10, d43, d32, d21, even, odd, out, level0):
+    mats = {"m43": across(96, 64, 4), "m32": across(64, 0, 8), "m21": across(0, 0, 16), "m10": last}
+    mats |= {"d43": down(4, 16, 16), "d32": down(8, 16, 16), "d21": down(16, 16, 32)}
+    mats |= {"even": down(32, 32, 32, 0), "odd": down(32, 32, 32, 1)}
+    return pack(mats, 1280)
+
+
+def collapse_kernel(places, a, b, c, packed, out, level0):
+    mats = unpack(packed, places)
+
     def total(ref, lo, hi):
         acc = ref[0, :, lo:hi, :].astype(F32)
         for source in range(1, ref.shape[0]):
@@ -421,38 +475,39 @@
             inside = (lane >= lo + ch * width) & (lane < lo + (ch + 1) * width)
             bottom = jnp.where(inside, pltpu.roll(small, (128 - (3 - ch) * width) % 128, 1), bottom)
     small = small / jnp.maximum(bottom, 1.0)
-    three = small + ldot(d43[...], rdot(small, m43[...]))
-    two = small + ldot(d32[...], rdot(three, m32[...]))
+    three = small + ldot(mats["d43"], rdot(small, mats["m43"]))
+    two = small + ldot(mats["d32"], rdot(three, mats["m32"]))
     one = total(b, 32, 64)
     bottom = one
     for ch in range(3):
         inside = (lane >= ch * 32) & (lane < (ch + 1) * 32)
         bottom = jnp.where(inside, pltpu.roll(one, (128 - (3 - ch) * 32) % 128, 1), bottom)
-    one = one / jnp.maximum(bottom, 1.0) + ldot(d21[...], rdot(two, m21[...]))
-    wide = rdot(one, m10[...])
+    one = one / jnp.maximum(bottom, 1.0) + ldot(mats["d21"], rdot(two, mats["m21"]))
+    wide = rdot(one, mats["m10"])
     hi, lo = split(wide)
-    up = mm(even[...], hi) + mm(even[...], lo)
-    down = mm(odd[...], hi) + mm(odd[...], lo)
+    up = mm(mats["even"], hi) + mm(mats["even"], lo)
+    down = mm(mats["odd"], hi) + mm(mats["odd"], lo)
     bottom = jnp.maximum(total(a, 0, 32), 1.0)
     for ch in range(COLOURS):
         own = total(b, 0, 32) if ch == 0 else total(c, 32 * (ch - 1), 32 * ch)
         back = jnp.where(lane < 64, up[:, ch * 128 : ch * 128 + 128], down[:, ch * 128 : ch * 128 + 128])
         level0[ch * 128 : ch * 128 + 128, :] = own / bottom + back
-    for t in range(TILE_DEV):
+    for ch in range(COLOURS):
         for row in range(32):
-            out[t, :, row * 128 : row * 128 + 128] = level0[pl.ds(t * 32 + row, COLOURS, stride=128), :]
+            out[ch, :, row * 128 : row * 128 + 128] = level0[pl.ds(ch * 128 + row, TILE_DEV, stride=32), :]
 
 
 def collapse(a, b, c):
-    mats = [const(m) for m in collapse_matrices()]
-    return pl.pallas_call(
-        collapse_kernel,
-        out_shape=jax.ShapeDtypeStruct((TILE_DEV, COLOURS, 4096), F32),
+    packed, places = collapse_matrices()
+    tiles = pl.pallas_call(
+        functools.partial(collapse_kernel, places),
+        out_shape=jax.ShapeDtypeStruct((COLOURS, TILE_DEV, 4096), F32),
         scratch_shapes=[pltpu.VMEM((COLOURS * 128, 128), F32)],
-        compiler_params=pltpu.CompilerParams(vmem_limit_bytes=56 << 20),
+        compiler_params=pltpu.CompilerParams(vmem_limit_bytes=VMEM),
         cost_estimate=pl.CostEstimate(flops=10**9, bytes_accessed=3 * 10**6, transcendentals=0),
         name="collapse",
-    )(a, b, c, *mats)
+    )(a, b, c, packed)
+    return jnp.swapaxes(tiles, 0, 1)
 
 
 def swap(value, axis, bit):
@@ -481,21 +536,26 @@
         strips = jnp.where((mask & bit) != 0, swap(strips, "frames", bit), strips)
         bit *= 2
 
-    bands = bands_of(frames, weight_map, seam_mask)
-    weights = bands[0]
-
-    def send(rows):
+    weights, state = bands_of(frames, weight_map, seam_mask)
+    routes = routes_of(spot)
+
+    def spread(rows):
         far = swap(rows, "tiles", 2)
-        near = swap(rows, "tiles", 1)
-        far_near = swap(far, "tiles", 1)
-        sums = gather_rows(spot, (rows, near, far, far_near), groups * TILE_DEV)
+        return rows, swap(rows, "tiles", 1), far
+
+    def send(rows, near, far):
+        sums = gather_rows(routes, (rows, near, far, swap(far, "tiles", 1)), groups * TILE_DEV)
         sums = sums.reshape(groups, TILE_DEV, rows.shape[1], 128)
         return lax.all_to_all(sums, "frames", split_axis=0, concat_axis=0, tiled=True)
 
-    got_weights = send(weights)
-    first, second = blend(strip_cell, strips, bands[1:])
-    got_first = send(first)
-    got_second = send(second)
+    weight_rows = spread(weights)
+    weight_rows, routes, strips = lax.optimization_barrier((weight_rows, routes, strips))
+    first, second = blend(strip_cell, strips, state)
+    first_rows = spread(first)
+    second_rows = spread(second)
+    got_weights = send(*weight_rows)
+    got_first = send(*first_rows)
+    got_second = send(*second_rows)
     return collapse(got_weights, got_first, got_second)
 
 

time: 158 us -> 106 us (0.67); the launches traced: 155 us -> 105 us
  local copies, waits for them, and re-layouts: 49.1 us -> 8.1 us
  Pallas kernels: 22.5 us -> 18.5 us
  starting transfers between devices: 23 us -> 20.5 us
  other arithmetic: 3.09 us -> 0.65 us
    unnamed x147 -> x24, local copies, waits for them, and re-layouts: 47.3 us -> 8.1 us
    pallas_call x3, Pallas kernels: 10.4 us -> 6.24 us  [gather_rows(): pl.pallas_call(gather_kernel, in_specs=[pl.BlockSpec(memory_space=pltpu.S...]
    ppermute x15, starting transfers between devices: 15.4 us -> 12.3 us  [swap(): return lax.ppermute(value, axis, [(i, i ^ bit) for i in range(size)])]
    select_n x3, other arithmetic: 3.06 us -> 0.04 us  [local(): strips = jnp.where(mask & bit != 0, swap(strips, 'frames', bit), strips)]
    all_to_all x2, waiting for transfers between devices: 14 us -> 16.9 us  [send(): lax.all_to_all(sums, 'frames', split_axis=0, concat_axis=0, tiled=True)]
    ppermute x15, waiting for transfers between devices: 20.2 us -> 17.6 us  [swap(): return lax.ppermute(value, axis, [(i, i ^ bit) for i in range(size)])]
    pallas_call x1 -> x0, local copies, waits for them, and re-layouts: 1.75 us -> none  [collapse(): pl.pallas_call(collapse_kernel, out_shape=jax.ShapeDtypeStruct((TILE_DEV,...]
    pallas_call x3 -> x4, Pallas kernels: 10.7 us -> 10.9 us  [the longest x1 4.39 us: bands_of(): pl.pallas_call(functools.partial(bands_kernel, small_places, large_places...]
  transfers between devices with their start and end apart: 17 -> 17, of which waited for: 8 -> 7; matrix products, arithmetic and copies ran while one was open for 1% -> 1% of each run, Pallas kernels for 10% -> 10%
where the time goes in v1:
time: 106 us; the launch traced here: 105 us
  waiting for transfers between devices  34.4 us (32%)
  blocking collectives  21.3 us (20%)
  starting transfers between devices  20.5 us (19%)
  Pallas kernels  18.5 us (17%)
  local copies, waits for them, and re-layouts  8.1 us (8%)
  between operations  1.48 us (1%)
    all_to_all x1, blocking collectives, send(): lax.all_to_all(sums, 'frames', split_axis=0, concat_axis=0, tiled=True)  21.3 us
    ppermute x15, waiting for transfers between devices, swap(): return lax.ppermute(value, axis, [(i, i ^ bit) for i in range(size)])  17.6 us
    all_to_all x2, waiting for transfers between devices, send(): lax.all_to_all(sums, 'frames', split_axis=0, concat_axis=0, tiled=True)  16.9 us
    ppermute x15, starting transfers between devices, swap(): return lax.ppermute(value, axis, [(i, i ^ bit) for i in range(size)])  12.3 us
    all_to_all x2, starting transfers between devices, send(): lax.all_to_all(sums, 'frames', split_axis=0, concat_axis=0, tiled=True)  8.21 us
    unnamed x24, local copies, waits for them, and re-layouts  8.1 us
    pallas_call x3, Pallas kernels, gather_rows(): pl.pallas_call(gather_kernel, in_specs=[pl.BlockSpec(memory_space=pltpu.S...  6.24 us
    pallas_call x1, Pallas kernels, bands_of(): pl.pallas_call(functools.partial(bands_kernel, small_places, large_places...  4.39 us
  transfers between devices with their start and end apart: 17, of which 7 were waited for; matrix products, arithmetic and copies ran while one was open for 1% of the time, Pallas kernels for 10%

profile of v1, /device:TPU:0, one launch (start us, length us, event | category | flops | bytes accessed | tf_op | source)
XLA Modules:
  0.0 104.9 jit_solution(7066479419059595335)
XLA Ops:
  0.0 1.1 %copy-done = bf16[1,3,128,1024]{3,2,1,0:T(8,128)(2,1)S(1)} copy-done((bf16[1,3,128,1024]{3,2,1,0:T(8,128)(2,1)S(1)}, bf16[1,3,128,1024]{3,2,1,0:T(8,128)(2,1)}, u32[]{:S(2)}) %copy-start) | copy-done | bytes 786456
  2.8 2.3 %copy-done.5 = bf16[2176,1024]{1,0:T(8,128)(2,1)S(1)} copy-done((bf16[2176,1024]{1,0:T(8,128)(2,1)S(1)}, bf16[2176,1024]{1,0:T(8,128)(2,1)}, u32[]{:S(2)}) %copy-start.5) | copy-done | bytes 4456472
  6.1 4.4 %bands.1 = (bf16[32,32,128]{2,1,0:T(8,128)(2,1)S(1)}, f32[816,1024]{1,0:T(8,128)S(1)}) custom-call(bf16[1,3,128,1024]{3,2,1,0:T(8,128)(2,1)S(1)} %copy-done, bf16[1,128,1024]{2,1,0:T(8,128)(2,1)S(1)} %copy-done.1, s32[1,64,128]{2,1,0:T(8,128)S(1)} %bitcast.20, bf16[512,512]{1,0:T(8,128)(2,1)S(1)} %copy-done.6, bf16[2176,1024]{1,0:T(8,128)(2,1)S(1)} %copy-done.5), custom_call_target="tpu_custom_call" | custom-call | flops 8000000000 | bytes 6000000 | tf_op jit(solution)/shard_map/bands/pallas_call | solution.py:302
  11.0 2.6 %collective-permute-start.1 = (bf16[32,32,128]{2,1,0:T(8,128)(2,1)S(1)}, bf16[32,32,128]{2,1,0:T(8,128)(2,1)}, u32[]{:S(2)}, u32[]{:S(2)}) collective-permute-start(bf16[32,32,128]{2,1,0:T(8,128)(2,1)S(1)} %get-tuple-element.22.a), channel_id=1, source_target_pairs={{0,2},{1,3},{2,0},{3,1},{4,6},{5,7},{6,4},{7,5},{8,10},{9,11},{10,... | collective-permute-start | bytes 786440 | tf_op jit(solution)/shard_map/ppermute | solution.py:515
  14.3 1.9 %strips.1 = bf16[288,128]{1,0:T(8,128)(2,1)S(1)} custom-call(s32[1]{0:T(128)S(6)} %copy.12.cell, bf16[1,3,128,1024]{3,2,1,0:T(8,128)(2,1)S(1)} %copy-done, bf16[1,3,128,1024]{3,2,1,0:T(8,128)(2,1)S(1)} %copy-done, bf16[512,512]{1,0:T(8,128)(2,1)S(1)} %copy-done.6), custom_call_target="tpu_custom_call" | custom-call | flops 2000000000 | bytes 1000000 | tf_op jit(solution)/shard_map/strips/pallas_call | solution.py:214
  16.1 1.6 %collective-permute-start.5 = (bf16[288,128]{1,0:T(8,128)(2,1)S(1)}, bf16[288,128]{1,0:T(8,128)(2,1)S(1)}, u32[]{:S(2)}, u32[]{:S(2)}) collective-permute-start(bf16[288,128]{1,0:T(8,128)(2,1)S(1)} %strips.1), channel_id=1, source_target_pairs={{0,4},{4,0},{8,12},{12,8},{16,20},{20,16},{24,28},{28,24},{1,5},{5... | collective-permute-start | bytes 221192 | tf_op jit(solution)/shard_map/ppermute | solution.py:515
  19.0 1.5 %collective-permute-done.5 = bf16[288,128]{1,0:T(8,128)(2,1)S(1)} collective-permute-done((bf16[288,128]{1,0:T(8,128)(2,1)S(1)}, bf16[288,128]{1,0:T(8,128)(2,1)S(1)}, u32[]{:S(2)}, u32[]{:S(2)}) %collective-permute-start.5) | collective-permute-done | bytes 73760 | tf_op jit(solution)/shard_map/ppermute | solution.py:515
  20.6 1.6 %collective-permute-start.6 = (bf16[288,128]{1,0:T(8,128)(2,1)S(1)}, bf16[288,128]{1,0:T(8,128)(2,1)S(1)}, u32[]{:S(2)}, u32[]{:S(2)}) collective-permute-start(bf16[288,128]{1,0:T(8,128)(2,1)S(1)} %broadcast_select_fusion), channel_id=1, source_target_pairs={{0,8},{4,12},{8,0},{12,4},{16,24},{20,28},{24,16},{28,20},{1,9},{5... | collective-permute-start | bytes 221192 | tf_op jit(solution)/shard_map/ppermute | solution.py:515
  22.2 2.8 %collective-permute-done.6 = bf16[288,128]{1,0:T(8,128)(2,1)S(1)} collective-permute-done((bf16[288,128]{1,0:T(8,128)(2,1)S(1)}, bf16[288,128]{1,0:T(8,128)(2,1)S(1)}, u32[]{:S(2)}, u32[]{:S(2)}) %collective-permute-start.6) | collective-permute-done | bytes 73760 | tf_op jit(solution)/shard_map/ppermute | solution.py:515
  25.0 2.7 %collective-permute-start.7 = (bf16[288,128]{1,0:T(8,128)(2,1)S(1)}, bf16[288,128]{1,0:T(8,128)(2,1)S(1)}, u32[]{:S(2)}, u32[]{:S(2)}) collective-permute-start(bf16[288,128]{1,0:T(8,128)(2,1)S(1)} %broadcast_select_fusion.1), channel_id=1, source_target_pairs={{0,16},{4,20},{8,24},{12,28},{16,0},{20,4},{24,8},{28,12},{1,17},{... | collective-permute-start | bytes 221192 | tf_op jit(solution)/shard_map/ppermute | solution.py:515
  28.3 2.4 %routes.1 = (s32[4,33]{1,0:T(4,128)}, s32[4]{0:T(128)}) custom-call(s32[4,32]{1,0:T(4,128)} %fusion.4.spot), custom_call_target="tpu_custom_call" | custom-call | tf_op jit(solution)/shard_map/routes/pallas_call | solution.py:396
  30.8 1.9 %copy-done.9 = f32[816,1024]{1,0:T(8,128)S(1)} copy-done((f32[816,1024]{1,0:T(8,128)S(1)}, f32[816,1024]{1,0:T(8,128)}, u32[]{:S(2)}) %copy-start.9) | copy-done | bytes 3342360
  32.7 1.4 %blend.1 = (bf16[32,80,128]{2,1,0:T(8,128)(2,1)S(1)}, bf16[32,64,128]{2,1,0:T(8,128)(2,1)S(1)}) custom-call(s32[1]{0:T(128)S(6)} %copy.12.cell, bf16[288,128]{1,0:T(8,128)(2,1)S(1)} %broadcast_select_fusion.2.strips, f32[816,1024]{1,0:T(8,128)S(1)} %copy-done.9), custom_call_target="tpu_custom_call" | custom-call | flops 4000000000 | bytes 4000000 | tf_op jit(solution)/shard_map/blend/pallas_call | solution.py:373
  35.3 10.7 %collective-permute-done.13.c = bf16[32,64,128]{2,1,0:T(8,128)(2,1)S(1)} collective-permute-done((bf16[32,64,128]{2,1,0:T(8,128)(2,1)S(1)}, bf16[32,64,128]{2,1,0:T(8,128)(2,1)S(1)}, u32[]{:S(2)}, u32[]{:S(2)}) %collective-permute-start.13) | collective-permute-done | bytes 524320 | tf_op jit(solution)/shard_map/ppermute | solution.py:515
  47.1 2.3 %gather_rows.3 = bf16[32,32,128]{2,1,0:T(8,128)(2,1)} custom-call(s32[4,33]{1,0:T(4,128)S(1)} %copy-done.3, s32[4]{0:T(128)S(1)} %copy-done.4, bf16[32,32,128]{2,1,0:T(8,128)(2,1)S(1)} %get-tuple-element.22.a, bf16[32,32,128]{2,1,0:T(8,128)(2,1)S(1)} %collective-permute-done.b, bf16[32,32,128]{2,1,0:T(8,128)(2,1)} %collective-permute-done.1.c, ...), custom_call_target="tpu_custom_call" | custom-call | flops 1000000000 | bytes 4000000 | tf_op jit(solution)/shard_map/gather_rows/pallas_call | solution.py:422
  49.3 4.6 %all-to-all-start = ((bf16[8,4,32,128]{3,2,1,0:T(8,128)(2,1)}), bf16[8,4,32,128]{3,2,1,0:T(8,128)(2,1)S(1)}, u32[]{:S(2)}, u32[]{:S(2)}) async-start(bf16[8,4,32,128]{3,2,1,0:T(8,128)(2,1)} %bitcast.8), calls=%async_computation | async-start | bytes 524288 | tf_op jit(solution)/shard_map/all_to_all | solution.py:549
  54.0 2.6 %gather_rows.5 = bf16[32,64,128]{2,1,0:T(8,128)(2,1)} custom-call(s32[4,33]{1,0:T(4,128)S(1)} %copy-done.3, s32[4]{0:T(128)S(1)} %copy-done.4, bf16[32,64,128]{2,1,0:T(8,128)(2,1)S(1)} %get-tuple-element.28.a, bf16[32,64,128]{2,1,0:T(8,128)(2,1)S(1)} %collective-permute-done.12.b, bf16[32,64,128]{2,1,0:T(8,128)(2,1)S(1)} %collective-permute-done.13.c, ...), custom_call_target="tpu_custom_call" | custom-call | flops 1000000000 | bytes 4000000 | tf_op jit(solution)/shard_map/gather_rows/pallas_call | solution.py:422
  56.6 6.8 %all-to-all-done.a = bf16[8,4,32,128]{3,2,1,0:T(8,128)(2,1)S(1)} async-done(((bf16[8,4,32,128]{3,2,1,0:T(8,128)(2,1)}), bf16[8,4,32,128]{3,2,1,0:T(8,128)(2,1)S(1)}, u32[]{:S(2)}, u32[]{:S(2)}) %all-to-all-start) | async-done | bytes 262176 | tf_op jit(solution)/shard_map/all_to_all | solution.py:549
  63.4 3.6 %all-to-all-start.2 = ((bf16[8,4,64,128]{3,2,1,0:T(8,128)(2,1)}), bf16[8,4,64,128]{3,2,1,0:T(8,128)(2,1)S(1)}, u32[]{:S(2)}, u32[]{:S(2)}) async-start(bf16[8,4,64,128]{3,2,1,0:T(8,128)(2,1)} %bitcast.10), calls=%async_computation.2 | async-start | bytes 1048576 | tf_op jit(solution)/shard_map/all_to_all | solution.py:549
  67.5 1.6 %collective-permute-done.9.b = bf16[32,80,128]{2,1,0:T(8,128)(2,1)S(1)} collective-permute-done((bf16[32,80,128]{2,1,0:T(8,128)(2,1)S(1)}, bf16[32,80,128]{2,1,0:T(8,128)(2,1)S(1)}, u32[]{:S(2)}, u32[]{:S(2)}) %collective-permute-start.9) | collective-permute-done | bytes 655392 | tf_op jit(solution)/shard_map/ppermute | solution.py:515
  70.0 1.4 %gather_rows.4 = bf16[32,80,128]{2,1,0:T(8,128)(2,1)S(1)} custom-call(s32[4,33]{1,0:T(4,128)S(1)} %copy-done.3, s32[4]{0:T(128)S(1)} %copy-done.4, bf16[32,80,128]{2,1,0:T(8,128)(2,1)S(1)} %get-tuple-element.27.a, bf16[32,80,128]{2,1,0:T(8,128)(2,1)S(1)} %collective-permute-done.9.b, bf16[32,80,128]{2,1,0:T(8,128)(2,1)S(1)} %collective-permute-done.10.c, ...), custom_call_target="tpu_custom_call" | custom-call | flops 1000000000 | bytes 4000000 | tf_op jit(solution)/shard_map/gather_rows/pallas_call | solution.py:422
  71.4 10.1 %all-to-all-done.2.c = bf16[8,4,64,128]{3,2,1,0:T(8,128)(2,1)S(1)} async-done(((bf16[8,4,64,128]{3,2,1,0:T(8,128)(2,1)}), bf16[8,4,64,128]{3,2,1,0:T(8,128)(2,1)S(1)}, u32[]{:S(2)}, u32[]{:S(2)}) %all-to-all-start.2) | async-done | bytes 524320 | tf_op jit(solution)/shard_map/all_to_all | solution.py:549
  81.5 21.3 %all_to_all.15.b = bf16[8,4,80,128]{3,2,1,0:T(8,128)(2,1)S(1)} all-to-all(bf16[8,4,80,128]{3,2,1,0:T(8,128)(2,1)S(1)} %bitcast.19), channel_id=1, replica_groups=mesh['frames'=8,'tiles'=4] {'frames'}, dimensions={0} | all-to-all | bytes 1310720 | tf_op jit(solution)/shard_map/all_to_all | solution.py:549
  102.7 2.2 %collapse.1 = f32[3,4,4096]{2,1,0:T(4,128)} custom-call(bf16[8,4,32,128]{3,2,1,0:T(8,128)(2,1)S(1)} %all-to-all-done.a, bf16[8,4,80,128]{3,2,1,0:T(8,128)(2,1)S(1)} %all_to_all.15.b, bf16[8,4,64,128]{3,2,1,0:T(8,128)(2,1)S(1)} %all-to-all-done.2.c, bf16[192,1280]{1,0:T(8,128)(2,1)S(1)} %copy-done.7), custom_call_target="tpu_custom_call" | custom-call | flops 1000000000 | bytes 3000000 | tf_op jit(solution)/shard_map/collapse/pallas_call | solution.py:502
  (49 shorter events, 8.2 us)
Async XLA Ops:
  2.8 2.3 %copy-start.5 = (bf16[2176,1024]{1,0:T(8,128)(2,1)S(1)}, bf16[2176,1024]{1,0:T(8,128)(2,1)}, u32[]{:S(2)}) copy-start(bf16[2176,1024]{1,0:T(8,128)(2,1)} %constant.78.clone.large) | copy-start | bytes 13369348
  10.5 5.6 %copy-start.8 = (f32[816,1024]{1,0:T(8,128)}, f32[816,1024]{1,0:T(8,128)S(1)}, u32[]{:S(2)}) copy-start(f32[816,1024]{1,0:T(8,128)S(1)} %get-tuple-element.26.state) | copy-start | bytes 10027012
  10.5 7.2 %copy-start.10 = (s32[1,32]{1,0:T(1,128)S(1)}, s32[1,32]{1,0:T(1,128)}, u32[]{:S(2)}) copy-start(s32[1,32]{1,0:T(1,128)} %param.17) | copy-start | bytes 388
  10.5 7.2 %copy-start.11 = (s32[1,32,1]{1,2,0:T(1,128)S(1)}, s32[1,32,1]{1,2,0:T(1,128)}, u32[]{:S(2)}) copy-start(s32[1,32,1]{1,2,0:T(1,128)} %param.16) | copy-start | bytes 388
  10.5 20.2 %collective-permute-start = (bf16[32,32,128]{2,1,0:T(8,128)(2,1)S(1)}, bf16[32,32,128]{2,1,0:T(8,128)(2,1)S(1)}, u32[]{:S(2)}, u32[]{:S(2)}) collective-permute-start(bf16[32,32,128]{2,1,0:T(8,128)(2,1)S(1)} %get-tuple-element.22.a), channel_id=1, source_target_pairs={{0,1},{1,0},{2,3},{3,2},{4,5},{5,4},{6,7},{7,6},{8,9},{9,8},{10,11... | collective-permute-start | bytes 786440 | tf_op jit(solution)/shard_map/ppermute | solution.py:515
  11.0 19.7 %collective-permute-start.1 = (bf16[32,32,128]{2,1,0:T(8,128)(2,1)S(1)}, bf16[32,32,128]{2,1,0:T(8,128)(2,1)}, u32[]{:S(2)}, u32[]{:S(2)}) collective-permute-start(bf16[32,32,128]{2,1,0:T(8,128)(2,1)S(1)} %get-tuple-element.22.a), channel_id=1, source_target_pairs={{0,2},{1,3},{2,0},{3,1},{4,6},{5,7},{6,4},{7,5},{8,10},{9,11},{10,... | collective-permute-start | bytes 786440 | tf_op jit(solution)/shard_map/ppermute | solution.py:515
  16.1 4.4 %collective-permute-start.5 = (bf16[288,128]{1,0:T(8,128)(2,1)S(1)}, bf16[288,128]{1,0:T(8,128)(2,1)S(1)}, u32[]{:S(2)}, u32[]{:S(2)}) collective-permute-start(bf16[288,128]{1,0:T(8,128)(2,1)S(1)} %strips.1), channel_id=1, source_target_pairs={{0,4},{4,0},{8,12},{12,8},{16,20},{20,16},{24,28},{28,24},{1,5},{5... | collective-permute-start | bytes 221192 | tf_op jit(solution)/shard_map/ppermute | solution.py:515
  17.7 4.5 %collective-permute-start.3 = (s32[32]{0:T(128)S(1)}, s32[32]{0:T(128)S(1)}, u32[]{:S(2)}, u32[]{:S(2)}) collective-permute-start(s32[32]{0:T(128)S(1)} %bitcast_add_fusion), channel_id=1, source_target_pairs={{0,2},{1,3},{2,0},{3,1},{4,6},{5,7},{6,4},{7,5},{8,10},{9,11},{10,... | collective-permute-start | bytes 392 | tf_op jit(solution)/shard_map/ppermute | solution.py:515
  18.4 9.3 %collective-permute-start.2 = (s32[32]{0:T(128)S(1)}, s32[32]{0:T(128)S(1)}, u32[]{:S(2)}, u32[]{:S(2)}) collective-permute-start(s32[32]{0:T(128)S(1)} %bitcast_add_fusion), channel_id=1, source_target_pairs={{0,1},{1,0},{2,3},{3,2},{4,5},{5,4},{6,7},{7,6},{8,9},{9,8},{10,11... | collective-permute-start | bytes 392 | tf_op jit(solution)/shard_map/ppermute | solution.py:515
  20.6 4.4 %collective-permute-start.6 = (bf16[288,128]{1,0:T(8,128)(2,1)S(1)}, bf16[288,128]{1,0:T(8,128)(2,1)S(1)}, u32[]{:S(2)}, u32[]{:S(2)}) collective-permute-start(bf16[288,128]{1,0:T(8,128)(2,1)S(1)} %broadcast_select_fusion), channel_id=1, source_target_pairs={{0,8},{4,12},{8,0},{12,4},{16,24},{20,28},{24,16},{28,20},{1,9},{5... | collective-permute-start | bytes 221192 | tf_op jit(solution)/shard_map/ppermute | solution.py:515
  22.2 5.5 %collective-permute-start.4 = (s32[32]{0:T(128)S(1)}, s32[32]{0:T(128)S(1)}, u32[]{:S(2)}, u32[]{:S(2)}) collective-permute-start(s32[32]{0:T(128)S(1)} %collective-permute-done.3), channel_id=1, source_target_pairs={{0,1},{1,0},{2,3},{3,2},{4,5},{5,4},{6,7},{7,6},{8,9},{9,8},{10,11... | collective-permute-start | bytes 392 | tf_op jit(solution)/shard_map/ppermute | solution.py:515
  25.0 5.7 %collective-permute-start.7 = (bf16[288,128]{1,0:T(8,128)(2,1)S(1)}, bf16[288,128]{1,0:T(8,128)(2,1)S(1)}, u32[]{:S(2)}, u32[]{:S(2)}) collective-permute-start(bf16[288,128]{1,0:T(8,128)(2,1)S(1)} %broadcast_select_fusion.1), channel_id=1, source_target_pairs={{0,16},{4,20},{8,24},{12,28},{16,0},{20,4},{24,8},{28,12},{1,17},{... | collective-permute-start | bytes 221192 | tf_op jit(solution)/shard_map/ppermute | solution.py:515
  32.7 14.3 %copy-start.3 = (s32[4,33]{1,0:T(4,128)S(1)}, s32[4,33]{1,0:T(4,128)}, u32[]{:S(2)}) copy-start(s32[4,33]{1,0:T(4,128)} %get-tuple-element.20.lists) | copy-start | bytes 1588
  32.7 14.3 %copy-start.4 = (s32[4]{0:T(128)S(1)}, s32[4]{0:T(128)}, u32[]{:S(2)}) copy-start(s32[4]{0:T(128)} %get-tuple-element.21.counts) | copy-start | bytes 52
  34.1 11.9 %collective-permute-start.13 = (bf16[32,64,128]{2,1,0:T(8,128)(2,1)S(1)}, bf16[32,64,128]{2,1,0:T(8,128)(2,1)S(1)}, u32[]{:S(2)}, u32[]{:S(2)}) collective-permute-start(bf16[32,64,128]{2,1,0:T(8,128)(2,1)S(1)} %get-tuple-element.28.a), channel_id=1, source_target_pairs={{0,2},{1,3},{2,0},{3,1},{4,6},{5,7},{6,4},{7,5},{8,10},{9,11},{10,... | collective-permute-start | bytes 1572872 | tf_op jit(solution)/shard_map/ppermute | solution.py:515
  34.7 12.3 %collective-permute-start.8 = (bf16[32,32,128]{2,1,0:T(8,128)(2,1)}, bf16[32,32,128]{2,1,0:T(8,128)(2,1)S(1)}, u32[]{:S(2)}, u32[]{:S(2)}) collective-permute-start(bf16[32,32,128]{2,1,0:T(8,128)(2,1)} %collective-permute-done.1.c), channel_id=1, source_target_pairs={{0,1},{1,0},{2,3},{3,2},{4,5},{5,4},{6,7},{7,6},{8,9},{9,8},{10,11... | collective-permute-start | bytes 786440 | tf_op jit(solution)/shard_map/ppermute | solution.py:515
  34.8 19.2 %collective-permute-start.12 = (bf16[32,64,128]{2,1,0:T(8,128)(2,1)S(1)}, bf16[32,64,128]{2,1,0:T(8,128)(2,1)S(1)}, u32[]{:S(2)}, u32[]{:S(2)}) collective-permute-start(bf16[32,64,128]{2,1,0:T(8,128)(2,1)S(1)} %get-tuple-element.28.a), channel_id=1, source_target_pairs={{0,1},{1,0},{2,3},{3,2},{4,5},{5,4},{6,7},{7,6},{8,9},{9,8},{10,11... | collective-permute-start | bytes 1572872 | tf_op jit(solution)/shard_map/ppermute | solution.py:515
  46.0 8.0 %collective-permute-start.14 = (bf16[32,64,128]{2,1,0:T(8,128)(2,1)S(1)}, bf16[32,64,128]{2,1,0:T(8,128)(2,1)}, u32[]{:S(2)}, u32[]{:S(2)}) collective-permute-start(bf16[32,64,128]{2,1,0:T(8,128)(2,1)S(1)} %collective-permute-done.13.c), channel_id=1, source_target_pairs={{0,1},{1,0},{2,3},{3,2},{4,5},{5,4},{6,7},{7,6},{8,9},{9,8},{10,11... | collective-permute-start | bytes 1572872 | tf_op jit(solution)/shard_map/ppermute | solution.py:515
  46.0 21.0 %collective-permute-start.10 = (bf16[32,80,128]{2,1,0:T(8,128)(2,1)S(1)}, bf16[32,80,128]{2,1,0:T(8,128)(2,1)S(1)}, u32[]{:S(2)}, u32[]{:S(2)}) collective-permute-start(bf16[32,80,128]{2,1,0:T(8,128)(2,1)S(1)} %get-tuple-element.27.a), channel_id=1, source_target_pairs={{0,2},{1,3},{2,0},{3,1},{4,6},{5,7},{6,4},{7,5},{8,10},{9,11},{10,... | collective-permute-start | bytes 1966088 | tf_op jit(solution)/shard_map/ppermute | solution.py:515
  49.3 14.0 %all-to-all-start = ((bf16[8,4,32,128]{3,2,1,0:T(8,128)(2,1)}), bf16[8,4,32,128]{3,2,1,0:T(8,128)(2,1)S(1)}, u32[]{:S(2)}, u32[]{:S(2)}) async-start(bf16[8,4,32,128]{3,2,1,0:T(8,128)(2,1)} %bitcast.8), calls=%async_computation | async-start | bytes 524288 | tf_op jit(solution)/shard_map/all_to_all | solution.py:549
  56.6 46.2 %copy-start.7 = (bf16[192,1280]{1,0:T(8,128)(2,1)S(1)}, bf16[192,1280]{1,0:T(8,128)(2,1)}, u32[]{:S(2)}) copy-start(bf16[192,1280]{1,0:T(8,128)(2,1)} %constant.79.clone.packed) | copy-start | bytes 1474564
  63.4 18.1 %all-to-all-start.2 = ((bf16[8,4,64,128]{3,2,1,0:T(8,128)(2,1)}), bf16[8,4,64,128]{3,2,1,0:T(8,128)(2,1)S(1)}, u32[]{:S(2)}, u32[]{:S(2)}) async-start(bf16[8,4,64,128]{3,2,1,0:T(8,128)(2,1)} %bitcast.10), calls=%async_computation.2 | async-start | bytes 1048576 | tf_op jit(solution)/shard_map/all_to_all | solution.py:549
  66.9 2.1 %collective-permute-start.9 = (bf16[32,80,128]{2,1,0:T(8,128)(2,1)S(1)}, bf16[32,80,128]{2,1,0:T(8,128)(2,1)S(1)}, u32[]{:S(2)}, u32[]{:S(2)}) collective-permute-start(bf16[32,80,128]{2,1,0:T(8,128)(2,1)S(1)} %get-tuple-element.27.a), channel_id=1, source_target_pairs={{0,1},{1,0},{2,3},{3,2},{4,5},{5,4},{6,7},{7,6},{8,9},{9,8},{10,11... | collective-permute-start | bytes 1966088 | tf_op jit(solution)/shard_map/ppermute | solution.py:515
  67.0 3.0 %collective-permute-start.11 = (bf16[32,80,128]{2,1,0:T(8,128)(2,1)S(1)}, bf16[32,80,128]{2,1,0:T(8,128)(2,1)S(1)}, u32[]{:S(2)}, u32[]{:S(2)}) collective-permute-start(bf16[32,80,128]{2,1,0:T(8,128)(2,1)S(1)} %collective-permute-done.10.c), channel_id=1, source_target_pairs={{0,1},{1,0},{2,3},{3,2},{4,5},{5,4},{6,7},{7,6},{8,9},{9,8},{10,11... | collective-permute-start | bytes 1966088 | tf_op jit(solution)/shard_map/ppermute | solution.py:515
  (5 other events, 5.8 us)

commit v2 on v1

--- a/solution.py
+++ b/solution.py
@@ -65,13 +65,27 @@
     return v, g
 
 
-def horizontal(width, pad_last):
+def horizontal(width):
     s = {k: shrink_matrix(width >> (k - 1)).T for k in range(1, 5)}
     g = {k: grow_matrix(width >> (k + 1)).T for k in range(4)}
-    if pad_last:
-        s[4] = padded(s[4], s[4].shape[0], pad_last)
-        g[3] = padded(g[3], pad_last, g[3].shape[1])
     return s, g
+
+
+def shrink_window():
+    m = np.zeros((512, 128), np.float32)
+    for i in range(128):
+        for d, tap in zip(range(-2, 3), (1, 4, 6, 4, 1)):
+            m[128 + 2 * i + d, i] = tap / 16.0
+    return m
+
+
+def grow_window():
+    m = np.zeros((384, 256), np.float32)
+    for i in range(128):
+        for d, tap in zip(range(-1, 2), (1, 6, 1)):
+            m[128 + i + d, 2 * i] = tap / 8.0
+        m[128 + i, 2 * i + 1] = m[128 + i + 1, 2 * i + 1] = 0.5
+    return m
 
 
 def pack(mats, width):
@@ -96,8 +110,8 @@
 
 def small_matrices():
     v, g = vertical()
-    s, gh = horizontal(WIN, 0)
-    sm, _ = horizontal(64, 0)
+    s, gh = horizontal(WIN)
+    sm, _ = horizontal(64)
     mats = {f"v{k}": m for k, m in v.items()} | {f"g{k}": m for k, m in g.items()}
     mats |= {f"s{k}": m for k, m in s.items()} | {f"h{k}": m for k, m in gh.items()}
     mats |= {f"m{k}": m for k, m in sm.items()} | {"order": row_order()}
@@ -105,9 +119,10 @@
 
 
 def large_matrices():
-    s, gh = horizontal(FW, 128)
-    mats = {f"s{k}": m for k, m in s.items()} | {f"h{k}": m for k, m in gh.items()}
-    return pack(mats, 1024)
+    mats = {"shrink": shrink_window(), "grow": grow_window()}
+    mats["last"] = padded(shrink_matrix(128).T, 128, 128)
+    mats["least"] = padded(grow_matrix(64).T, 128, 128)
+    return pack(mats, 640)
 
 
 def levels_of(mats, letter):
@@ -137,20 +152,37 @@
     return lax.dot_general(a, b, (((1,), (1,)), ((), ())), preferred_element_type=F32)
 
 
-def pyramid(planes, v, s, product=mm):
+def windows(v, m, step):
+    rows, width = v.shape
+    both = jnp.concatenate(split(v), axis=0)
+    left = jnp.broadcast_to(both[:, :1], (2 * rows, 128))
+    right = jnp.broadcast_to(both[:, width - 1 :], (2 * rows, 128))
+    both = jnp.concatenate([left, both, right], axis=1)
+    pieces = []
+    for n in range(width // step):
+        piece = mm(both[:, n * step : n * step + step + 256], m)
+        pieces.append(piece[:rows] + piece[rows:])
+    return jnp.concatenate(pieces, axis=1)
+
+
+def right_of(m):
+    return lambda v: rdot(v, m)
+
+
+def pyramid(planes, v, shrinks, product=mm):
     n = len(planes)
     t = jnp.concatenate([product(v[1], p) for p in planes], axis=0)
-    levels = {1: rdot(t, s[1])}
+    levels = {1: shrinks[1](t)}
     for k in range(2, 5):
         prev = levels[k - 1]
         rows = prev.shape[0] // n
         t = jnp.concatenate([ldot(v[k], prev[i * rows : (i + 1) * rows]) for i in range(n)], axis=0)
-        levels[k] = rdot(t, s[k])
+        levels[k] = shrinks[k](t)
     return levels
 
 
-def grown(level, n, gv, gh):
-    h = rdot(level, gh)
+def grown(level, n, gv, grow):
+    h = grow(level)
     rows = level.shape[0] // n
     return [ldot(gv, h[i * rows : (i + 1) * rows]) for i in range(n)]
 
@@ -165,6 +197,7 @@
 def strips_kernel(places, cell, xa, xb, packed, out, acc):
     mats = unpack(packed, places)
     v, gv, s, gh = (levels_of(mats, letter) for letter in "vgsh")
+    s, gh = ({k: right_of(m) for k, m in each.items()} for each in (s, gh))
     order = mats["order"]
     first = window_tile(cell[0]) * 128
     planes = [jnp.concatenate([xa[0, c], xb[0, c]], axis=1) for c in range(COLOURS)]
@@ -263,8 +296,12 @@
     mats = unpack(small, small_places)
     v, gv, sm = (levels_of(mats, letter) for letter in "vgm")
     order = mats["order"]
+    sm = {k: right_of(each) for k, each in sm.items()}
     mats = unpack(large, large_places)
-    s, gh = (levels_of(mats, letter) for letter in "sh")
+    half = lambda each: windows(each, mats["shrink"], 256)
+    twice = lambda each: windows(each, mats["grow"], 128)
+    s = {1: half, 2: half, 3: half, 4: right_of(mats["last"])}
+    gh = {0: twice, 1: twice, 2: twice, 3: right_of(mats["least"])}
     views, mask_views = state_views(state)
     planes = [x[0, c] for c in range(COLOURS)] + [w[0]]
     weights = mm(order, planes[3])
@@ -402,7 +439,7 @@
     )(spot)
 
 
-def gather_kernel(lists, counts, a, b, c, d, out, acc):
+def gather_kernel(lists, counts, a, b, c, d, home, away, acc):
     acc[...] = jnp.zeros_like(acc)
     for source, ref in enumerate((a, b, c, d)):
 
@@ -413,21 +450,46 @@
             return carry
 
         lax.fori_loop(0, counts[source], body, 0)
-    out[...] = acc[...].astype(BF16)
+    tiles = home.shape[0]
+    home[...] = acc[0:tiles]
+    away[...] = acc[tiles : 2 * tiles].astype(BF16)
 
 
 def gather_rows(routes, rows, tiles):
     height = rows[0].shape[1]
     vmem = pl.BlockSpec(memory_space=pltpu.VMEM)
+    shape = (tiles // 2, height, 128)
     return pl.pallas_call(
         gather_kernel,
         in_specs=[pl.BlockSpec(memory_space=pltpu.SMEM)] * 2 + [vmem] * 4,
-        out_shape=jax.ShapeDtypeStruct((tiles, height, 128), BF16),
+        out_shape=[jax.ShapeDtypeStruct(shape, F32), jax.ShapeDtypeStruct(shape, BF16)],
         scratch_shapes=[pltpu.VMEM((tiles, height, 128), F32)],
         compiler_params=pltpu.CompilerParams(vmem_limit_bytes=VMEM),
         cost_estimate=pl.CostEstimate(flops=10**9, bytes_accessed=4 * 10**6, transcendentals=0),
         name="gather_rows",
     )(*routes, *rows)
+
+
+def add_kernel(home, got, own, *away):
+    for j in range(len(away) + 1):
+        lo = j * TILE_DEV
+        total = home[lo : lo + TILE_DEV] + got[lo : lo + TILE_DEV].astype(F32)
+        if j == 0:
+            own[...] = total
+        else:
+            away[j - 1][...] = total.astype(BF16)
+
+
+def add_halves(home, got):
+    shape = (TILE_DEV,) + home.shape[1:]
+    others = home.shape[0] // TILE_DEV - 1
+    return pl.pallas_call(
+        add_kernel,
+        out_shape=[jax.ShapeDtypeStruct(shape, F32)] + [jax.ShapeDtypeStruct(shape, BF16)] * others,
+        compiler_params=pltpu.CompilerParams(vmem_limit_bytes=VMEM),
+        cost_estimate=pl.CostEstimate(flops=10**8, bytes_accessed=2 * 10**6, transcendentals=0),
+        name="add_halves",
+    )(home, got)
 
 
 def collapse_matrices():
@@ -458,13 +520,15 @@
     return pack(mats, 1280)
 
 
-def collapse_kernel(places, a, b, c, packed, out, level0):
+def collapse_kernel(places, each, packed, *refs):
     mats = unpack(packed, places)
-
-    def total(ref, lo, hi):
-        acc = ref[0, :, lo:hi, :].astype(F32)
-        for source in range(1, ref.shape[0]):
-            acc = acc + ref[source, :, lo:hi, :].astype(F32)
+    a, b, c = (refs[i * each : (i + 1) * each] for i in range(3))
+    out, level0 = refs[3 * each :]
+
+    def total(sources, lo, hi):
+        acc = sources[0][:, lo:hi, :]
+        for source in sources[1:]:
+            acc = acc + source[:, lo:hi, :].astype(F32)
         return acc.reshape(TILE_DEV * (hi - lo), 128)
 
     lane = lane_index()
@@ -500,13 +564,13 @@
 def collapse(a, b, c):
     packed, places = collapse_matrices()
     tiles = pl.pallas_call(
-        functools.partial(collapse_kernel, places),
+        functools.partial(collapse_kernel, places, len(a)),
         out_shape=jax.ShapeDtypeStruct((COLOURS, TILE_DEV, 4096), F32),
         scratch_shapes=[pltpu.VMEM((COLOURS * 128, 128), F32)],
         compiler_params=pltpu.CompilerParams(vmem_limit_bytes=VMEM),
         cost_estimate=pl.CostEstimate(flops=10**9, bytes_accessed=3 * 10**6, transcendentals=0),
         name="collapse",
-    )(a, b, c, packed)
+    )(packed, *a, *b, *c)
     return jnp.swapaxes(tiles, 0, 1)
 
 
@@ -528,9 +592,12 @@
     ids = jnp.stack([ids, ids_core, ids_far, ids_far_core])
     group_size = parts * TILE_DEV
     owner = ids % group_size // TILE_DEV
-    spot = jnp.where(owner == mine, ids // group_size * TILE_DEV + ids % TILE_DEV, -1)
+    relative = lax.bitwise_xor(ids // group_size, lax.axis_index("frames"))
+    relative = (relative & 1) * (groups // 2) + (relative >> 1)
+    spot = jnp.where(owner == mine, relative * TILE_DEV + ids % TILE_DEV, -1)
 
     strips = strips_of(frames, strip_cell)
+    strips, frames = lax.optimization_barrier((strips, frames))
     bit = 1
     while bit < groups:
         strips = jnp.where((mask & bit) != 0, swap(strips, "frames", bit), strips)
@@ -544,9 +611,9 @@
         return rows, swap(rows, "tiles", 1), far
 
     def send(rows, near, far):
-        sums = gather_rows(routes, (rows, near, far, swap(far, "tiles", 1)), groups * TILE_DEV)
-        sums = sums.reshape(groups, TILE_DEV, rows.shape[1], 128)
-        return lax.all_to_all(sums, "frames", split_axis=0, concat_axis=0, tiled=True)
+        home, away = gather_rows(routes, (rows, near, far, swap(far, "tiles", 1)), groups * TILE_DEV)
+        own, *away = add_halves(home, swap(away, "frames", 1))
+        return [own] + [swap(part, "frames", 2 * (j + 1)) for j, part in enumerate(away)]
 
     weight_rows = spread(weights)
     weight_rows, routes, strips = lax.optimization_barrier((weight_rows, routes, strips))

time: 106 us -> 102 us (0.962)
  blocking collectives: 21.3 us -> 0 us
  waiting for transfers between devices: 34.4 us -> 47.5 us
  starting transfers between devices: 20.5 us -> 29.9 us
  local copies, waits for them, and re-layouts: 8.1 us -> 5.87 us
  Pallas kernels: 18.5 us -> 16.3 us
    ppermute x15 -> x27, waiting for transfers between devices: 17.6 us -> 47.5 us  [swap(): return lax.ppermute(value, axis, [(i, i ^ bit) for i in range(size)])]
    all_to_all x1 -> x0, blocking collectives: 21.3 us -> none  [send(): lax.all_to_all(sums, 'frames', split_axis=0, concat_axis=0, tiled=True)]
    ppermute x15 -> x27, starting transfers between devices: 12.3 us -> 29.9 us  [swap(): return lax.ppermute(value, axis, [(i, i ^ bit) for i in range(size)])]
    all_to_all x2 -> x0, waiting for transfers between devices: 16.9 us -> none  [send(): lax.all_to_all(sums, 'frames', split_axis=0, concat_axis=0, tiled=True)]
    all_to_all x2 -> x0, starting transfers between devices: 8.21 us -> none  [send(): lax.all_to_all(sums, 'frames', split_axis=0, concat_axis=0, tiled=True)]
    pallas_call x3, Pallas kernels: 6.24 us -> 3.69 us  [gather_rows(): pl.pallas_call(gather_kernel, in_specs=[pl.BlockSpec(memory_space=pltpu.S...]
    unnamed x24, local copies, waits for them, and re-layouts: 8.1 us -> 5.87 us
    pallas_call x1 -> x4, Pallas kernels: 2.19 us -> 2.31 us  [the longest x1 2.18 us: collapse(): pl.pallas_call(functools.partial(collapse_kernel, places, len(a)), out_sh...]
  transfers between devices with their start and end apart: 17 -> 27, of which waited for: 7 -> 8; matrix products, arithmetic and copies ran while one was open for 1% -> 1% of each run, Pallas kernels for 10% -> 6%
where the time goes in v2:
time: 102 us
  waiting for transfers between devices  47.5 us (47%)
  starting transfers between devices  29.9 us (29%)
  Pallas kernels  16.3 us (16%)
  local copies, waits for them, and re-layouts  5.87 us (6%)
  between operations  1.55 us (2%)
    ppermute x27, waiting for transfers between devices, swap(): return lax.ppermute(value, axis, [(i, i ^ bit) for i in range(size)])  47.5 us
    ppermute x27, starting transfers between devices, swap(): return lax.ppermute(value, axis, [(i, i ^ bit) for i in range(size)])  29.9 us
    unnamed x24, local copies, waits for them, and re-layouts  5.87 us
    pallas_call x1, Pallas kernels, bands_of(): pl.pallas_call(functools.partial(bands_kernel, small_places, large_places...  4.69 us
    pallas_call x3, Pallas kernels, gather_rows(): pl.pallas_call(gather_kernel, in_specs=[pl.BlockSpec(memory_space=pltpu.S...  3.69 us
    pallas_call x1, Pallas kernels, routes_of(): pl.pallas_call(routes_kernel, in_specs=[smem], out_specs=[smem, smem], ou...  2.45 us
    pallas_call x1, Pallas kernels, collapse(): pl.pallas_call(functools.partial(collapse_kernel, places, len(a)), out_sh...  2.18 us
  transfers between devices with their start and end apart: 27, of which 8 were waited for; matrix products, arithmetic and copies ran while one was open for 1% of the time, Pallas kernels for 6%

profile of v2, /device:TPU:0, one launch (start us, length us, event | category | flops | bytes accessed | tf_op | source)
XLA Modules:
  0.0 101.8 jit_solution(9939645945450654733)
XLA Ops:
  2.8 1.9 %strips.1 = bf16[288,128]{1,0:T(8,128)(2,1)S(1)} custom-call(s32[1]{0:T(128)S(6)} %copy.12.cell, bf16[1,3,128,1024]{3,2,1,0:T(8,128)(2,1)S(1)} %copy-done, bf16[1,3,128,1024]{3,2,1,0:T(8,128)(2,1)S(1)} %copy-done, bf16[512,512]{1,0:T(8,128)(2,1)S(1)} %copy-done.6), custom_call_target="tpu_custom_call" | custom-call | flops 2000000000 | bytes 1000000 | tf_op jit(solution)/shard_map/strips/pallas_call | solution.py:247
  4.7 4.7 %bands.1 = (bf16[32,32,128]{2,1,0:T(8,128)(2,1)S(1)}, f32[816,1024]{1,0:T(8,128)S(1)}) custom-call(bf16[1,3,128,1024]{3,2,1,0:T(8,128)(2,1)S(1)} %copy-done, bf16[1,128,1024]{2,1,0:T(8,128)(2,1)S(1)} %copy-done.1, s32[1,64,128]{2,1,0:T(8,128)S(1)} %bitcast.16, bf16[512,512]{1,0:T(8,128)(2,1)S(1)} %copy-done.6, bf16[512,640]{1,0:T(8,128)(2,1)S(1)} %copy-done.5), custom_call_target="tpu_custom_call" | custom-call | flops 8000000000 | bytes 6000000 | tf_op jit(solution)/shard_map/bands/pallas_call | solution.py:339
  9.4 1.7 %copy-done.8 = f32[816,1024]{1,0:T(8,128)} copy-done((f32[816,1024]{1,0:T(8,128)}, f32[816,1024]{1,0:T(8,128)S(1)}, u32[]{:S(2)}) %copy-start.8) | copy-done | bytes 3342360
  11.6 2.5 %collective-permute-start.1 = (bf16[32,32,128]{2,1,0:T(8,128)(2,1)S(1)}, bf16[32,32,128]{2,1,0:T(8,128)(2,1)S(1)}, u32[]{:S(2)}, u32[]{:S(2)}) collective-permute-start(bf16[32,32,128]{2,1,0:T(8,128)(2,1)S(1)} %get-tuple-element.44.a), channel_id=1, source_target_pairs={{0,2},{1,3},{2,0},{3,1},{4,6},{5,7},{6,4},{7,5},{8,10},{9,11},{10,... | collective-permute-start | bytes 786440 | tf_op jit(solution)/shard_map/ppermute | solution.py:579
  14.1 1.5 %collective-permute-start.5 = (bf16[288,128]{1,0:T(8,128)(2,1)S(1)}, bf16[288,128]{1,0:T(8,128)(2,1)S(1)}, u32[]{:S(2)}, u32[]{:S(2)}) collective-permute-start(bf16[288,128]{1,0:T(8,128)(2,1)S(1)} %strips.1), channel_id=1, source_target_pairs={{0,4},{4,0},{8,12},{12,8},{16,20},{20,16},{24,28},{28,24},{1,5},{5... | collective-permute-start | bytes 221192 | tf_op jit(solution)/shard_map/ppermute | solution.py:579
  16.9 1.6 %collective-permute-done.5 = bf16[288,128]{1,0:T(8,128)(2,1)S(1)} collective-permute-done((bf16[288,128]{1,0:T(8,128)(2,1)S(1)}, bf16[288,128]{1,0:T(8,128)(2,1)S(1)}, u32[]{:S(2)}, u32[]{:S(2)}) %collective-permute-start.5) | collective-permute-done | bytes 73760 | tf_op jit(solution)/shard_map/ppermute | solution.py:579
  18.5 1.6 %collective-permute-start.6 = (bf16[288,128]{1,0:T(8,128)(2,1)S(1)}, bf16[288,128]{1,0:T(8,128)(2,1)S(1)}, u32[]{:S(2)}, u32[]{:S(2)}) collective-permute-start(bf16[288,128]{1,0:T(8,128)(2,1)S(1)} %broadcast_select_fusion), channel_id=1, source_target_pairs={{0,8},{4,12},{8,0},{12,4},{16,24},{20,28},{24,16},{28,20},{1,9},{5... | collective-permute-start | bytes 221192 | tf_op jit(solution)/shard_map/ppermute | solution.py:579
  21.1 1.8 %collective-permute-done.6 = bf16[288,128]{1,0:T(8,128)(2,1)S(1)} collective-permute-done((bf16[288,128]{1,0:T(8,128)(2,1)S(1)}, bf16[288,128]{1,0:T(8,128)(2,1)S(1)}, u32[]{:S(2)}, u32[]{:S(2)}) %collective-permute-start.6) | collective-permute-done | bytes 73760 | tf_op jit(solution)/shard_map/ppermute | solution.py:579
  22.9 2.7 %collective-permute-start.7 = (bf16[288,128]{1,0:T(8,128)(2,1)S(1)}, bf16[288,128]{1,0:T(8,128)(2,1)S(1)}, u32[]{:S(2)}, u32[]{:S(2)}) collective-permute-start(bf16[288,128]{1,0:T(8,128)(2,1)S(1)} %broadcast_select_fusion.1), channel_id=1, source_target_pairs={{0,16},{4,20},{8,24},{12,28},{16,0},{20,4},{24,8},{28,12},{1,17},{... | collective-permute-start | bytes 221192 | tf_op jit(solution)/shard_map/ppermute | solution.py:579
  26.2 2.4 %routes.1 = (s32[4,33]{1,0:T(4,128)}, s32[4]{0:T(128)}) custom-call(s32[4,32]{1,0:T(4,128)} %fusion.4.spot), custom_call_target="tpu_custom_call" | custom-call | tf_op jit(solution)/shard_map/routes/pallas_call | solution.py:433
  28.7 1.9 %copy-done.9 = f32[816,1024]{1,0:T(8,128)S(1)} copy-done((f32[816,1024]{1,0:T(8,128)S(1)}, f32[816,1024]{1,0:T(8,128)}, u32[]{:S(2)}) %copy-start.9) | copy-done | bytes 3342360
  32.0 1.5 %collective-permute-start.14 = (bf16[32,80,128]{2,1,0:T(8,128)(2,1)S(1)}, bf16[32,80,128]{2,1,0:T(8,128)(2,1)S(1)}, u32[]{:S(2)}, u32[]{:S(2)}) collective-permute-start(bf16[32,80,128]{2,1,0:T(8,128)(2,1)S(1)} %get-tuple-element.55.a), channel_id=1, source_target_pairs={{0,2},{1,3},{2,0},{3,1},{4,6},{5,7},{6,4},{7,5},{8,10},{9,11},{10,... | collective-permute-start | bytes 1966088 | tf_op jit(solution)/shard_map/ppermute | solution.py:579
  34.1 15.6 %collective-permute-done.14.c = bf16[32,80,128]{2,1,0:T(8,128)(2,1)S(1)} collective-permute-done((bf16[32,80,128]{2,1,0:T(8,128)(2,1)S(1)}, bf16[32,80,128]{2,1,0:T(8,128)(2,1)S(1)}, u32[]{:S(2)}, u32[]{:S(2)}) %collective-permute-start.14) | collective-permute-done | bytes 655392 | tf_op jit(solution)/shard_map/ppermute | solution.py:579
  50.3 8.4 %collective-permute-done.21.c = bf16[32,64,128]{2,1,0:T(8,128)(2,1)S(1)} collective-permute-done((bf16[32,64,128]{2,1,0:T(8,128)(2,1)S(1)}, bf16[32,64,128]{2,1,0:T(8,128)(2,1)S(1)}, u32[]{:S(2)}, u32[]{:S(2)}) %collective-permute-start.21) | collective-permute-done | bytes 524320 | tf_op jit(solution)/shard_map/ppermute | solution.py:579
  60.5 1.4 %collective-permute-start.16 = (bf16[16,80,128]{2,1,0:T(8,128)(2,1)S(1)}, bf16[16,80,128]{2,1,0:T(8,128)(2,1)S(1)}, u32[]{:S(2)}, u32[]{:S(2)}) collective-permute-start(bf16[16,80,128]{2,1,0:T(8,128)(2,1)S(1)} %get-tuple-element.57), channel_id=1, source_target_pairs={{0,4},{4,0},{8,12},{12,8},{16,20},{20,16},{24,28},{28,24},{1,5},{5... | collective-permute-start | bytes 983048 | tf_op jit(solution)/shard_map/ppermute | solution.py:579
  65.0 1.5 %collective-permute-start.9 = (bf16[16,32,128]{2,1,0:T(8,128)(2,1)S(1)}, bf16[16,32,128]{2,1,0:T(8,128)(2,1)S(1)}, u32[]{:S(2)}, u32[]{:S(2)}) collective-permute-start(bf16[16,32,128]{2,1,0:T(8,128)(2,1)S(1)} %get-tuple-element.48), channel_id=1, source_target_pairs={{0,4},{4,0},{8,12},{12,8},{16,20},{20,16},{24,28},{28,24},{1,5},{5... | collective-permute-start | bytes 393224 | tf_op jit(solution)/shard_map/ppermute | solution.py:579
  66.5 10.3 %collective-permute-done.23.got = bf16[16,64,128]{2,1,0:T(8,128)(2,1)S(1)} collective-permute-done((bf16[16,64,128]{2,1,0:T(8,128)(2,1)S(1)}, bf16[16,64,128]{2,1,0:T(8,128)(2,1)S(1)}, u32[]{:S(2)}, u32[]{:S(2)}) %collective-permute-start.23) | collective-permute-done | bytes 262176 | tf_op jit(solution)/shard_map/ppermute | solution.py:579
  76.8 1.8 %collective-permute-start.24 = (bf16[4,64,128]{2,1,0:T(8,128)(2,1)S(1)}, bf16[4,64,128]{2,1,0:T(8,128)(2,1)S(1)}, u32[]{:S(2)}, u32[]{:S(2)}) collective-permute-start(bf16[4,64,128]{2,1,0:T(8,128)(2,1)S(1)} %get-tuple-element.66), channel_id=1, source_target_pairs={{0,8},{4,12},{8,0},{12,4},{16,24},{20,28},{24,16},{28,20},{1,9},{5... | collective-permute-start | bytes 196616 | tf_op jit(solution)/shard_map/ppermute | solution.py:579
  78.7 1.6 %collective-permute-start.10 = (bf16[4,32,128]{2,1,0:T(8,128)(2,1)S(1)}, bf16[4,32,128]{2,1,0:T(8,128)(2,1)S(1)}, u32[]{:S(2)}, u32[]{:S(2)}) collective-permute-start(bf16[4,32,128]{2,1,0:T(8,128)(2,1)S(1)} %get-tuple-element.50), channel_id=1, source_target_pairs={{0,8},{4,12},{8,0},{12,4},{16,24},{20,28},{24,16},{28,20},{1,9},{5... | collective-permute-start | bytes 98312 | tf_op jit(solution)/shard_map/ppermute | solution.py:579
  80.3 3.3 %collective-permute-start.11 = (bf16[4,32,128]{2,1,0:T(8,128)(2,1)S(1)}, bf16[4,32,128]{2,1,0:T(8,128)(2,1)S(1)}, u32[]{:S(2)}, u32[]{:S(2)}) collective-permute-start(bf16[4,32,128]{2,1,0:T(8,128)(2,1)S(1)} %get-tuple-element.51), channel_id=1, source_target_pairs={{0,16},{4,20},{8,24},{12,28},{16,0},{20,4},{24,8},{28,12},{1,17},{... | collective-permute-start | bytes 98312 | tf_op jit(solution)/shard_map/ppermute | solution.py:579
  84.3 3.8 %collective-permute-start.18 = (bf16[4,80,128]{2,1,0:T(8,128)(2,1)S(1)}, bf16[4,80,128]{2,1,0:T(8,128)(2,1)S(1)}, u32[]{:S(2)}, u32[]{:S(2)}) collective-permute-start(bf16[4,80,128]{2,1,0:T(8,128)(2,1)S(1)} %get-tuple-element.60), channel_id=1, source_target_pairs={{0,16},{4,20},{8,24},{12,28},{16,0},{20,4},{24,8},{28,12},{1,17},{... | collective-permute-start | bytes 245768 | tf_op jit(solution)/shard_map/ppermute | solution.py:579
  89.7 2.3 %collective-permute-start.26 = (bf16[4,64,128]{2,1,0:T(8,128)(2,1)S(1)}, bf16[4,64,128]{2,1,0:T(8,128)(2,1)S(1)}, u32[]{:S(2)}, u32[]{:S(2)}) collective-permute-start(bf16[4,64,128]{2,1,0:T(8,128)(2,1)S(1)} %get-tuple-element.68), channel_id=1, source_target_pairs={{0,24},{4,28},{8,16},{12,20},{16,8},{20,12},{24,0},{28,4},{1,25},{... | collective-permute-start | bytes 196616 | tf_op jit(solution)/shard_map/ppermute | solution.py:579
  92.1 7.5 %collective-permute-done.25.refs_10_ = bf16[4,64,128]{2,1,0:T(8,128)(2,1)S(1)} collective-permute-done((bf16[4,64,128]{2,1,0:T(8,128)(2,1)S(1)}, bf16[4,64,128]{2,1,0:T(8,128)(2,1)S(1)}, u32[]{:S(2)}, u32[]{:S(2)}) %collective-permute-start.25) | collective-permute-done | bytes 65568 | tf_op jit(solution)/shard_map/ppermute | solution.py:579
  99.6 2.2 %collapse.1 = f32[3,4,4096]{2,1,0:T(4,128)} custom-call(bf16[192,1280]{1,0:T(8,128)(2,1)S(1)} %copy-done.7, f32[4,32,128]{2,1,0:T(8,128)S(1)} %get-tuple-element.49.refs_0_, bf16[4,32,128]{2,1,0:T(8,128)(2,1)S(1)} %collective-permute-done.10.refs_1_, bf16[4,32,128]{2,1,0:T(8,128)(2,1)S(1)} %collective-permute-done.11.refs_2_, ...), custom_call_target="tpu_custom_call" | custom-call | flops 1000000000 | bytes 3000000 | tf_op jit(solution)/shard_map/collapse/pallas_call | solution.py:566
  (71 shorter events, 14.5 us)
Async XLA Ops:
  11.2 17.5 %collective-permute-start = (bf16[32,32,128]{2,1,0:T(8,128)(2,1)S(1)}, bf16[32,32,128]{2,1,0:T(8,128)(2,1)S(1)}, u32[]{:S(2)}, u32[]{:S(2)}) collective-permute-start(bf16[32,32,128]{2,1,0:T(8,128)(2,1)S(1)} %get-tuple-element.44.a), channel_id=1, source_target_pairs={{0,1},{1,0},{2,3},{3,2},{4,5},{5,4},{6,7},{7,6},{8,9},{9,8},{10,11... | collective-permute-start | bytes 786440 | tf_op jit(solution)/shard_map/ppermute | solution.py:579
  11.6 17.1 %collective-permute-start.1 = (bf16[32,32,128]{2,1,0:T(8,128)(2,1)S(1)}, bf16[32,32,128]{2,1,0:T(8,128)(2,1)S(1)}, u32[]{:S(2)}, u32[]{:S(2)}) collective-permute-start(bf16[32,32,128]{2,1,0:T(8,128)(2,1)S(1)} %get-tuple-element.44.a), channel_id=1, source_target_pairs={{0,2},{1,3},{2,0},{3,1},{4,6},{5,7},{6,4},{7,5},{8,10},{9,11},{10,... | collective-permute-start | bytes 786440 | tf_op jit(solution)/shard_map/ppermute | solution.py:579
  15.6 5.5 %collective-permute-start.3 = (s32[32]{0:T(128)S(1)}, s32[32]{0:T(128)S(1)}, u32[]{:S(2)}, u32[]{:S(2)}) collective-permute-start(s32[32]{0:T(128)S(1)} %bitcast_add_fusion), channel_id=1, source_target_pairs={{0,2},{1,3},{2,0},{3,1},{4,6},{5,7},{6,4},{7,5},{8,10},{9,11},{10,... | collective-permute-start | bytes 392 | tf_op jit(solution)/shard_map/ppermute | solution.py:579
  16.2 9.4 %collective-permute-start.2 = (s32[32]{0:T(128)S(1)}, s32[32]{0:T(128)S(1)}, u32[]{:S(2)}, u32[]{:S(2)}) collective-permute-start(s32[32]{0:T(128)S(1)} %bitcast_add_fusion), channel_id=1, source_target_pairs={{0,1},{1,0},{2,3},{3,2},{4,5},{5,4},{6,7},{7,6},{8,9},{9,8},{10,11... | collective-permute-start | bytes 392 | tf_op jit(solution)/shard_map/ppermute | solution.py:579
  21.1 4.5 %collective-permute-start.4 = (s32[32]{0:T(128)S(1)}, s32[32]{0:T(128)S(1)}, u32[]{:S(2)}, u32[]{:S(2)}) collective-permute-start(s32[32]{0:T(128)S(1)} %collective-permute-done.3), channel_id=1, source_target_pairs={{0,1},{1,0},{2,3},{3,2},{4,5},{5,4},{6,7},{7,6},{8,9},{9,8},{10,11... | collective-permute-start | bytes 392 | tf_op jit(solution)/shard_map/ppermute | solution.py:579
  22.9 5.7 %collective-permute-start.7 = (bf16[288,128]{1,0:T(8,128)(2,1)S(1)}, bf16[288,128]{1,0:T(8,128)(2,1)S(1)}, u32[]{:S(2)}, u32[]{:S(2)}) collective-permute-start(bf16[288,128]{1,0:T(8,128)(2,1)S(1)} %broadcast_select_fusion.1), channel_id=1, source_target_pairs={{0,16},{4,20},{8,24},{12,28},{16,0},{20,4},{24,8},{28,12},{1,17},{... | collective-permute-start | bytes 221192 | tf_op jit(solution)/shard_map/ppermute | solution.py:579
  32.0 17.7 %collective-permute-start.14 = (bf16[32,80,128]{2,1,0:T(8,128)(2,1)S(1)}, bf16[32,80,128]{2,1,0:T(8,128)(2,1)S(1)}, u32[]{:S(2)}, u32[]{:S(2)}) collective-permute-start(bf16[32,80,128]{2,1,0:T(8,128)(2,1)S(1)} %get-tuple-element.55.a), channel_id=1, source_target_pairs={{0,2},{1,3},{2,0},{3,1},{4,6},{5,7},{6,4},{7,5},{8,10},{9,11},{10,... | collective-permute-start | bytes 1966088 | tf_op jit(solution)/shard_map/ppermute | solution.py:579
  33.6 25.1 %collective-permute-start.21 = (bf16[32,64,128]{2,1,0:T(8,128)(2,1)S(1)}, bf16[32,64,128]{2,1,0:T(8,128)(2,1)S(1)}, u32[]{:S(2)}, u32[]{:S(2)}) collective-permute-start(bf16[32,64,128]{2,1,0:T(8,128)(2,1)S(1)} %get-tuple-element.62.a), channel_id=1, source_target_pairs={{0,2},{1,3},{2,0},{3,1},{4,6},{5,7},{6,4},{7,5},{8,10},{9,11},{10,... | collective-permute-start | bytes 1572872 | tf_op jit(solution)/shard_map/ppermute | solution.py:579
  34.1 25.1 %collective-permute-start.13 = (bf16[32,80,128]{2,1,0:T(8,128)(2,1)S(1)}, bf16[32,80,128]{2,1,0:T(8,128)(2,1)S(1)}, u32[]{:S(2)}, u32[]{:S(2)}) collective-permute-start(bf16[32,80,128]{2,1,0:T(8,128)(2,1)S(1)} %get-tuple-element.55.a), channel_id=1, source_target_pairs={{0,1},{1,0},{2,3},{3,2},{4,5},{5,4},{6,7},{7,6},{8,9},{9,8},{10,11... | collective-permute-start | bytes 1966088 | tf_op jit(solution)/shard_map/ppermute | solution.py:579
  49.8 9.4 %collective-permute-start.15 = (bf16[32,80,128]{2,1,0:T(8,128)(2,1)S(1)}, bf16[32,80,128]{2,1,0:T(8,128)(2,1)S(1)}, u32[]{:S(2)}, u32[]{:S(2)}) collective-permute-start(bf16[32,80,128]{2,1,0:T(8,128)(2,1)S(1)} %collective-permute-done.14.c), channel_id=1, source_target_pairs={{0,1},{1,0},{2,3},{3,2},{4,5},{5,4},{6,7},{7,6},{8,9},{9,8},{10,11... | collective-permute-start | bytes 1966088 | tf_op jit(solution)/shard_map/ppermute | solution.py:579
  49.8 12.2 %collective-permute-start.20 = (bf16[32,64,128]{2,1,0:T(8,128)(2,1)S(1)}, bf16[32,64,128]{2,1,0:T(8,128)(2,1)S(1)}, u32[]{:S(2)}, u32[]{:S(2)}) collective-permute-start(bf16[32,64,128]{2,1,0:T(8,128)(2,1)S(1)} %get-tuple-element.62.a), channel_id=1, source_target_pairs={{0,1},{1,0},{2,3},{3,2},{4,5},{5,4},{6,7},{7,6},{8,9},{9,8},{10,11... | collective-permute-start | bytes 1572872 | tf_op jit(solution)/shard_map/ppermute | solution.py:579
  58.7 5.2 %collective-permute-start.8 = (bf16[32,32,128]{2,1,0:T(8,128)(2,1)S(1)}, bf16[32,32,128]{2,1,0:T(8,128)(2,1)S(1)}, u32[]{:S(2)}, u32[]{:S(2)}) collective-permute-start(bf16[32,32,128]{2,1,0:T(8,128)(2,1)S(1)} %collective-permute-done.1.c), channel_id=1, source_target_pairs={{0,1},{1,0},{2,3},{3,2},{4,5},{5,4},{6,7},{7,6},{8,9},{9,8},{10,11... | collective-permute-start | bytes 786440 | tf_op jit(solution)/shard_map/ppermute | solution.py:579
  60.5 23.1 %collective-permute-start.16 = (bf16[16,80,128]{2,1,0:T(8,128)(2,1)S(1)}, bf16[16,80,128]{2,1,0:T(8,128)(2,1)S(1)}, u32[]{:S(2)}, u32[]{:S(2)}) collective-permute-start(bf16[16,80,128]{2,1,0:T(8,128)(2,1)S(1)} %get-tuple-element.57), channel_id=1, source_target_pairs={{0,4},{4,0},{8,12},{12,8},{16,20},{20,16},{24,28},{28,24},{1,5},{5... | collective-permute-start | bytes 983048 | tf_op jit(solution)/shard_map/ppermute | solution.py:579
  63.3 13.5 %collective-permute-start.23 = (bf16[16,64,128]{2,1,0:T(8,128)(2,1)S(1)}, bf16[16,64,128]{2,1,0:T(8,128)(2,1)S(1)}, u32[]{:S(2)}, u32[]{:S(2)}) collective-permute-start(bf16[16,64,128]{2,1,0:T(8,128)(2,1)S(1)} %get-tuple-element.64), channel_id=1, source_target_pairs={{0,4},{4,0},{8,12},{12,8},{16,20},{20,16},{24,28},{28,24},{1,5},{5... | collective-permute-start | bytes 786440 | tf_op jit(solution)/shard_map/ppermute | solution.py:579
  65.0 13.7 %collective-permute-start.9 = (bf16[16,32,128]{2,1,0:T(8,128)(2,1)S(1)}, bf16[16,32,128]{2,1,0:T(8,128)(2,1)S(1)}, u32[]{:S(2)}, u32[]{:S(2)}) collective-permute-start(bf16[16,32,128]{2,1,0:T(8,128)(2,1)S(1)} %get-tuple-element.48), channel_id=1, source_target_pairs={{0,4},{4,0},{8,12},{12,8},{16,20},{20,16},{24,28},{28,24},{1,5},{5... | collective-permute-start | bytes 393224 | tf_op jit(solution)/shard_map/ppermute | solution.py:579
  76.8 12.9 %collective-permute-start.24 = (bf16[4,64,128]{2,1,0:T(8,128)(2,1)S(1)}, bf16[4,64,128]{2,1,0:T(8,128)(2,1)S(1)}, u32[]{:S(2)}, u32[]{:S(2)}) collective-permute-start(bf16[4,64,128]{2,1,0:T(8,128)(2,1)S(1)} %get-tuple-element.66), channel_id=1, source_target_pairs={{0,8},{4,12},{8,0},{12,4},{16,24},{20,28},{24,16},{28,20},{1,9},{5... | collective-permute-start | bytes 196616 | tf_op jit(solution)/shard_map/ppermute | solution.py:579
  78.7 5.6 %collective-permute-start.10 = (bf16[4,32,128]{2,1,0:T(8,128)(2,1)S(1)}, bf16[4,32,128]{2,1,0:T(8,128)(2,1)S(1)}, u32[]{:S(2)}, u32[]{:S(2)}) collective-permute-start(bf16[4,32,128]{2,1,0:T(8,128)(2,1)S(1)} %get-tuple-element.50), channel_id=1, source_target_pairs={{0,8},{4,12},{8,0},{12,4},{16,24},{20,28},{24,16},{28,20},{1,9},{5... | collective-permute-start | bytes 98312 | tf_op jit(solution)/shard_map/ppermute | solution.py:579
  80.3 7.8 %collective-permute-start.11 = (bf16[4,32,128]{2,1,0:T(8,128)(2,1)S(1)}, bf16[4,32,128]{2,1,0:T(8,128)(2,1)S(1)}, u32[]{:S(2)}, u32[]{:S(2)}) collective-permute-start(bf16[4,32,128]{2,1,0:T(8,128)(2,1)S(1)} %get-tuple-element.51), channel_id=1, source_target_pairs={{0,16},{4,20},{8,24},{12,28},{16,0},{20,4},{24,8},{28,12},{1,17},{... | collective-permute-start | bytes 98312 | tf_op jit(solution)/shard_map/ppermute | solution.py:579
  83.6 5.7 %collective-permute-start.12 = (bf16[4,32,128]{2,1,0:T(8,128)(2,1)S(1)}, bf16[4,32,128]{2,1,0:T(8,128)(2,1)S(1)}, u32[]{:S(2)}, u32[]{:S(2)}) collective-permute-start(bf16[4,32,128]{2,1,0:T(8,128)(2,1)S(1)} %get-tuple-element.52), channel_id=1, source_target_pairs={{0,24},{4,28},{8,16},{12,20},{16,8},{20,12},{24,0},{28,4},{1,25},{... | collective-permute-start | bytes 98312 | tf_op jit(solution)/shard_map/ppermute | solution.py:579
  83.7 15.9 %collective-permute-start.17 = (bf16[4,80,128]{2,1,0:T(8,128)(2,1)S(1)}, bf16[4,80,128]{2,1,0:T(8,128)(2,1)S(1)}, u32[]{:S(2)}, u32[]{:S(2)}) collective-permute-start(bf16[4,80,128]{2,1,0:T(8,128)(2,1)S(1)} %get-tuple-element.59), channel_id=1, source_target_pairs={{0,8},{4,12},{8,0},{12,4},{16,24},{20,28},{24,16},{28,20},{1,9},{5... | collective-permute-start | bytes 245768 | tf_op jit(solution)/shard_map/ppermute | solution.py:579
  84.3 15.3 %collective-permute-start.18 = (bf16[4,80,128]{2,1,0:T(8,128)(2,1)S(1)}, bf16[4,80,128]{2,1,0:T(8,128)(2,1)S(1)}, u32[]{:S(2)}, u32[]{:S(2)}) collective-permute-start(bf16[4,80,128]{2,1,0:T(8,128)(2,1)S(1)} %get-tuple-element.60), channel_id=1, source_target_pairs={{0,16},{4,20},{8,24},{12,28},{16,0},{20,4},{24,8},{28,12},{1,17},{... | collective-permute-start | bytes 245768 | tf_op jit(solution)/shard_map/ppermute | solution.py:579
  88.2 11.5 %collective-permute-start.19 = (bf16[4,80,128]{2,1,0:T(8,128)(2,1)S(1)}, bf16[4,80,128]{2,1,0:T(8,128)(2,1)S(1)}, u32[]{:S(2)}, u32[]{:S(2)}) collective-permute-start(bf16[4,80,128]{2,1,0:T(8,128)(2,1)S(1)} %get-tuple-element.61), channel_id=1, source_target_pairs={{0,24},{4,28},{8,16},{12,20},{16,8},{20,12},{24,0},{28,4},{1,25},{... | collective-permute-start | bytes 245768 | tf_op jit(solution)/shard_map/ppermute | solution.py:579
  89.3 10.3 %collective-permute-start.25 = (bf16[4,64,128]{2,1,0:T(8,128)(2,1)S(1)}, bf16[4,64,128]{2,1,0:T(8,128)(2,1)S(1)}, u32[]{:S(2)}, u32[]{:S(2)}) collective-permute-start(bf16[4,64,128]{2,1,0:T(8,128)(2,1)S(1)} %get-tuple-element.67), channel_id=1, source_target_pairs={{0,16},{4,20},{8,24},{12,28},{16,0},{20,4},{24,8},{28,12},{1,17},{... | collective-permute-start | bytes 196616 | tf_op jit(solution)/shard_map/ppermute | solution.py:579
  89.7 9.9 %collective-permute-start.26 = (bf16[4,64,128]{2,1,0:T(8,128)(2,1)S(1)}, bf16[4,64,128]{2,1,0:T(8,128)(2,1)S(1)}, u32[]{:S(2)}, u32[]{:S(2)}) collective-permute-start(bf16[4,64,128]{2,1,0:T(8,128)(2,1)S(1)} %get-tuple-element.68), channel_id=1, source_target_pairs={{0,24},{4,28},{8,16},{12,20},{16,8},{20,12},{24,0},{28,4},{1,25},{... | collective-permute-start | bytes 196616 | tf_op jit(solution)/shard_map/ppermute | solution.py:579
  (15 other events, 138.8 us)

commit v3 on v2

--- a/solution.py
+++ b/solution.py
@@ -596,33 +596,48 @@
     relative = (relative & 1) * (groups // 2) + (relative >> 1)
     spot = jnp.where(owner == mine, relative * TILE_DEV + ids % TILE_DEV, -1)
 
+    routes = routes_of(spot)
     strips = strips_of(frames, strip_cell)
     strips, frames = lax.optimization_barrier((strips, frames))
+    weights, state = bands_of(frames, weight_map, seam_mask)
     bit = 1
     while bit < groups:
-        strips = jnp.where((mask & bit) != 0, swap(strips, "frames", bit), strips)
+        got = swap(strips, "frames", bit)
+        if bit == 1:
+            got, weights, state = lax.optimization_barrier((got, weights, state))
+        strips = jnp.where((mask & bit) != 0, got, strips)
         bit *= 2
 
-    weights, state = bands_of(frames, weight_map, seam_mask)
-    routes = routes_of(spot)
-
-    def spread(rows):
-        far = swap(rows, "tiles", 2)
-        return rows, swap(rows, "tiles", 1), far
-
-    def send(rows, near, far):
-        home, away = gather_rows(routes, (rows, near, far, swap(far, "tiles", 1)), groups * TILE_DEV)
-        own, *away = add_halves(home, swap(away, "frames", 1))
+    tie = lax.optimization_barrier
+
+    def gather(rows, near, far, far_near):
+        return gather_rows(routes, (rows, near, far, far_near), groups * TILE_DEV)
+
+    def along(own, *away):
         return [own] + [swap(part, "frames", 2 * (j + 1)) for j, part in enumerate(away)]
 
-    weight_rows = spread(weights)
-    weight_rows, routes, strips = lax.optimization_barrier((weight_rows, routes, strips))
+    far = swap(weights, "tiles", 2)
+    home, away = gather(weights, swap(weights, "tiles", 1), far, swap(far, "tiles", 1))
+    home, away, strips = tie((home, away, strips))
     first, second = blend(strip_cell, strips, state)
-    first_rows = spread(first)
-    second_rows = spread(second)
-    got_weights = send(*weight_rows)
-    got_first = send(*first_rows)
-    got_second = send(*second_rows)
+    far = swap(first, "tiles", 2)
+    near = swap(first, "tiles", 1)
+    sums = add_halves(home, swap(away, "frames", 1))
+    far, near, sums, second = tie((far, near, sums, second))
+    got_weights = along(*sums)
+    far_second = swap(second, "tiles", 2)
+    near_second = swap(second, "tiles", 1)
+    home, away = gather(first, near, far, swap(far, "tiles", 1))
+    got = swap(away, "frames", 1)
+    far_second, got, got_weights = tie((far_second, got, got_weights))
+    far_near = swap(far_second, "tiles", 1)
+    sums = add_halves(home, got)
+    far_near, sums = tie((far_near, sums))
+    got_first = along(*sums)
+    home, away = gather(second, near_second, far_second, far_near)
+    got = swap(away, "frames", 1)
+    got, got_first = tie((got, got_first))
+    got_second = along(*add_halves(home, got))
     return collapse(got_weights, got_first, got_second)
 
 

time: 102 us -> 93 us (0.912)
  waiting for transfers between devices: 47.5 us -> 40.1 us
  starting transfers between devices: 29.9 us -> 27.6 us
    ppermute x27, waiting for transfers between devices: 47.5 us -> 40.1 us  [swap(): return lax.ppermute(value, axis, [(i, i ^ bit) for i in range(size)])]
    ppermute x27, starting transfers between devices: 29.9 us -> 27.6 us  [swap(): return lax.ppermute(value, axis, [(i, i ^ bit) for i in range(size)])]
    unnamed x24 -> x28, local copies, waits for them, and re-layouts: 5.87 us -> 6.08 us
  transfers between devices with their start and end apart: 27 -> 27, of which waited for: 8 -> 14; matrix products, arithmetic and copies ran while one was open for 1% -> 1% of each run, Pallas kernels for 6% -> 11%
where the time goes in v3:
time: 93 us; the launch traced here: 92.8 us
  waiting for transfers between devices  40.1 us (43%)
  starting transfers between devices  27.6 us (30%)
  Pallas kernels  16 us (17%)
  local copies, waits for them, and re-layouts  6.08 us (7%)
  between operations  1.55 us (2%)
  other arithmetic  1.32 us (1%)
    ppermute x27, waiting for transfers between devices, swap(): return lax.ppermute(value, axis, [(i, i ^ bit) for i in range(size)])  40.1 us
    ppermute x27, starting transfers between devices, swap(): return lax.ppermute(value, axis, [(i, i ^ bit) for i in range(size)])  27.6 us
    unnamed x28, local copies, waits for them, and re-layouts  6.08 us
    pallas_call x1, Pallas kernels, bands_of(): pl.pallas_call(functools.partial(bands_kernel, small_places, large_places...  4.68 us
    pallas_call x3, Pallas kernels, gather_rows(): pl.pallas_call(gather_kernel, in_specs=[pl.BlockSpec(memory_space=pltpu.S...  3.34 us
    pallas_call x1, Pallas kernels, routes_of(): pl.pallas_call(routes_kernel, in_specs=[smem], out_specs=[smem, smem], ou...  2.45 us
    pallas_call x1, Pallas kernels, collapse(): pl.pallas_call(functools.partial(collapse_kernel, places, len(a)), out_sh...  2.18 us
  transfers between devices with their start and end apart: 27, of which 14 were waited for; matrix products, arithmetic and copies ran while one was open for 1% of the time, Pallas kernels for 11%

profile of v3, /device:TPU:0, one launch (start us, length us, event | category | flops | bytes accessed | tf_op | source)
XLA Modules:
  0.0 92.8 jit_solution(6477008828102605682)
XLA Ops:
  0.7 2.9 %collective-permute-start.1 = (s32[32]{0:T(128)S(1)}, s32[32]{0:T(128)S(1)}, u32[]{:S(2)}, u32[]{:S(2)}) collective-permute-start(s32[32]{0:T(128)S(1)} %bitcast_add_fusion), channel_id=1, source_target_pairs={{0,2},{1,3},{2,0},{3,1},{4,6},{5,7},{6,4},{7,5},{8,10},{9,11},{10,... | collective-permute-start | bytes 392 | tf_op jit(solution)/shard_map/ppermute | solution.py:579
  6.5 1.9 %strips.1 = bf16[288,128]{1,0:T(8,128)(2,1)S(1)} custom-call(s32[1]{0:T(128)S(6)} %copy.12.cell, bf16[1,3,128,1024]{3,2,1,0:T(8,128)(2,1)S(1)} %copy-done, bf16[1,3,128,1024]{3,2,1,0:T(8,128)(2,1)S(1)} %copy-done, bf16[512,512]{1,0:T(8,128)(2,1)S(1)} %copy-done.8), custom_call_target="tpu_custom_call" | custom-call | flops 2000000000 | bytes 1000000 | tf_op jit(solution)/shard_map/strips/pallas_call | solution.py:247
  8.3 1.6 %collective-permute-start.3 = (bf16[288,128]{1,0:T(8,128)(2,1)S(1)}, bf16[288,128]{1,0:T(8,128)(2,1)S(1)}, u32[]{:S(2)}, u32[]{:S(2)}) collective-permute-start(bf16[288,128]{1,0:T(8,128)(2,1)S(1)} %strips.1), channel_id=1, source_target_pairs={{0,4},{4,0},{8,12},{12,8},{16,20},{20,16},{24,28},{28,24},{1,5},{5... | collective-permute-start | bytes 221192 | tf_op jit(solution)/shard_map/ppermute | solution.py:579
  9.9 4.7 %bands.1 = (bf16[32,32,128]{2,1,0:T(8,128)(2,1)S(1)}, f32[816,1024]{1,0:T(8,128)S(1)}) custom-call(bf16[1,3,128,1024]{3,2,1,0:T(8,128)(2,1)S(1)} %copy-done, bf16[1,128,1024]{2,1,0:T(8,128)(2,1)S(1)} %copy-done.1, s32[1,64,128]{2,1,0:T(8,128)S(1)} %bitcast.16, bf16[512,512]{1,0:T(8,128)(2,1)S(1)} %copy-done.8, bf16[512,640]{1,0:T(8,128)(2,1)S(1)} %copy-done.7), custom_call_target="tpu_custom_call" | custom-call | flops 8000000000 | bytes 6000000 | tf_op jit(solution)/shard_map/bands/pallas_call | solution.py:339
  14.6 1.7 %copy-done.10 = f32[816,1024]{1,0:T(8,128)} copy-done((f32[816,1024]{1,0:T(8,128)}, f32[816,1024]{1,0:T(8,128)S(1)}, u32[]{:S(2)}) %copy-start.10) | copy-done | bytes 3342360
  17.0 1.6 %collective-permute-start.7 = (bf16[288,128]{1,0:T(8,128)(2,1)S(1)}, bf16[288,128]{1,0:T(8,128)(2,1)S(1)}, u32[]{:S(2)}, u32[]{:S(2)}) collective-permute-start(bf16[288,128]{1,0:T(8,128)(2,1)S(1)} %broadcast_select_fusion), channel_id=1, source_target_pairs={{0,8},{4,12},{8,0},{12,4},{16,24},{20,28},{24,16},{28,20},{1,9},{5... | collective-permute-start | bytes 221192 | tf_op jit(solution)/shard_map/ppermute | solution.py:579
  19.8 1.7 %collective-permute-done.7 = bf16[288,128]{1,0:T(8,128)(2,1)S(1)} collective-permute-done((bf16[288,128]{1,0:T(8,128)(2,1)S(1)}, bf16[288,128]{1,0:T(8,128)(2,1)S(1)}, u32[]{:S(2)}, u32[]{:S(2)}) %collective-permute-start.7) | collective-permute-done | bytes 73760 | tf_op jit(solution)/shard_map/ppermute | solution.py:579
  21.5 2.7 %collective-permute-start.8 = (bf16[288,128]{1,0:T(8,128)(2,1)S(1)}, bf16[288,128]{1,0:T(8,128)(2,1)S(1)}, u32[]{:S(2)}, u32[]{:S(2)}) collective-permute-start(bf16[288,128]{1,0:T(8,128)(2,1)S(1)} %broadcast_select_fusion.1), channel_id=1, source_target_pairs={{0,16},{4,20},{8,24},{12,28},{16,0},{20,4},{24,8},{28,12},{1,17},{... | collective-permute-start | bytes 221192 | tf_op jit(solution)/shard_map/ppermute | solution.py:579
  24.2 2.7 %collective-permute-done.5.c = bf16[32,32,128]{2,1,0:T(8,128)(2,1)S(1)} collective-permute-done((bf16[32,32,128]{2,1,0:T(8,128)(2,1)S(1)}, bf16[32,32,128]{2,1,0:T(8,128)(2,1)S(1)}, u32[]{:S(2)}, u32[]{:S(2)}) %collective-permute-start.5) | collective-permute-done | bytes 262176 | tf_op jit(solution)/shard_map/ppermute | solution.py:579
  27.5 2.4 %routes.1 = (s32[4,33]{1,0:T(4,128)}, s32[4]{0:T(128)}) custom-call(s32[4,32]{1,0:T(4,128)} %fusion.4.spot), custom_call_target="tpu_custom_call" | custom-call | tf_op jit(solution)/shard_map/routes/pallas_call | solution.py:433
  36.2 4.7 %collective-permute-done.11.got = bf16[16,32,128]{2,1,0:T(8,128)(2,1)S(1)} collective-permute-done((bf16[16,32,128]{2,1,0:T(8,128)(2,1)S(1)}, bf16[16,32,128]{2,1,0:T(8,128)(2,1)S(1)}, u32[]{:S(2)}, u32[]{:S(2)}) %collective-permute-start.11) | collective-permute-done | bytes 131104 | tf_op jit(solution)/shard_map/ppermute | solution.py:579
  40.9 10.9 %collective-permute-done.9.c = bf16[32,80,128]{2,1,0:T(8,128)(2,1)S(1)} collective-permute-done((bf16[32,80,128]{2,1,0:T(8,128)(2,1)S(1)}, bf16[32,80,128]{2,1,0:T(8,128)(2,1)S(1)}, u32[]{:S(2)}, u32[]{:S(2)}) %collective-permute-start.9) | collective-permute-done | bytes 655392 | tf_op jit(solution)/shard_map/ppermute | solution.py:579
  52.4 1.6 %collective-permute-done.13.d = bf16[32,80,128]{2,1,0:T(8,128)(2,1)S(1)} collective-permute-done((bf16[32,80,128]{2,1,0:T(8,128)(2,1)S(1)}, bf16[32,80,128]{2,1,0:T(8,128)(2,1)S(1)}, u32[]{:S(2)}, u32[]{:S(2)}) %collective-permute-start.13) | collective-permute-done | bytes 655392 | tf_op jit(solution)/shard_map/ppermute | solution.py:579
  56.2 2.7 %collective-permute-start.16 = (bf16[4,32,128]{2,1,0:T(8,128)(2,1)S(1)}, bf16[4,32,128]{2,1,0:T(8,128)(2,1)S(1)}, u32[]{:S(2)}, u32[]{:S(2)}) collective-permute-start(bf16[4,32,128]{2,1,0:T(8,128)(2,1)S(1)} %get-tuple-element.86), channel_id=1, source_target_pairs={{0,16},{4,20},{8,24},{12,28},{16,0},{20,4},{24,8},{28,12},{1,17},{... | collective-permute-start | bytes 98312 | tf_op jit(solution)/shard_map/ppermute | solution.py:579
  61.3 3.3 %collective-permute-done.17.refs_3_ = bf16[4,32,128]{2,1,0:T(8,128)(2,1)S(1)} collective-permute-done((bf16[4,32,128]{2,1,0:T(8,128)(2,1)S(1)}, bf16[4,32,128]{2,1,0:T(8,128)(2,1)S(1)}, u32[]{:S(2)}, u32[]{:S(2)}) %collective-permute-start.17) | collective-permute-done | bytes 32800 | tf_op jit(solution)/shard_map/ppermute | solution.py:579
  64.6 1.6 %collective-permute-done.12.c = bf16[32,64,128]{2,1,0:T(8,128)(2,1)S(1)} collective-permute-done((bf16[32,64,128]{2,1,0:T(8,128)(2,1)S(1)}, bf16[32,64,128]{2,1,0:T(8,128)(2,1)S(1)}, u32[]{:S(2)}, u32[]{:S(2)}) %collective-permute-start.12) | collective-permute-done | bytes 524320 | tf_op jit(solution)/shard_map/ppermute | solution.py:579
  71.1 2.7 %collective-permute-start.22 = (bf16[4,80,128]{2,1,0:T(8,128)(2,1)S(1)}, bf16[4,80,128]{2,1,0:T(8,128)(2,1)S(1)}, u32[]{:S(2)}, u32[]{:S(2)}) collective-permute-start(bf16[4,80,128]{2,1,0:T(8,128)(2,1)S(1)} %get-tuple-element.103), channel_id=1, source_target_pairs={{0,16},{4,20},{8,24},{12,28},{16,0},{20,4},{24,8},{28,12},{1,17},{... | collective-permute-start | bytes 245768 | tf_op jit(solution)/shard_map/ppermute | solution.py:579
  75.0 1.4 %collective-permute-done.21.refs_5_ = bf16[4,80,128]{2,1,0:T(8,128)(2,1)S(1)} collective-permute-done((bf16[4,80,128]{2,1,0:T(8,128)(2,1)S(1)}, bf16[4,80,128]{2,1,0:T(8,128)(2,1)S(1)}, u32[]{:S(2)}, u32[]{:S(2)}) %collective-permute-start.21) | collective-permute-done | bytes 81952 | tf_op jit(solution)/shard_map/ppermute | solution.py:579
  77.7 2.6 %collective-permute-done.23.refs_7_ = bf16[4,80,128]{2,1,0:T(8,128)(2,1)S(1)} collective-permute-done((bf16[4,80,128]{2,1,0:T(8,128)(2,1)S(1)}, bf16[4,80,128]{2,1,0:T(8,128)(2,1)S(1)}, u32[]{:S(2)}, u32[]{:S(2)}) %collective-permute-start.23) | collective-permute-done | bytes 81952 | tf_op jit(solution)/shard_map/ppermute | solution.py:579
  80.5 1.9 %collective-permute-start.24 = (bf16[4,64,128]{2,1,0:T(8,128)(2,1)S(1)}, bf16[4,64,128]{2,1,0:T(8,128)(2,1)S(1)}, u32[]{:S(2)}, u32[]{:S(2)}) collective-permute-start(bf16[4,64,128]{2,1,0:T(8,128)(2,1)S(1)} %get-tuple-element.112), channel_id=1, source_target_pairs={{0,8},{4,12},{8,0},{12,4},{16,24},{20,28},{24,16},{28,20},{1,9},{5... | collective-permute-start | bytes 196616 | tf_op jit(solution)/shard_map/ppermute | solution.py:579
  82.4 1.6 %collective-permute-start.25 = (bf16[4,64,128]{2,1,0:T(8,128)(2,1)S(1)}, bf16[4,64,128]{2,1,0:T(8,128)(2,1)S(1)}, u32[]{:S(2)}, u32[]{:S(2)}) collective-permute-start(bf16[4,64,128]{2,1,0:T(8,128)(2,1)S(1)} %get-tuple-element.113), channel_id=1, source_target_pairs={{0,16},{4,20},{8,24},{12,28},{16,0},{20,4},{24,8},{28,12},{1,17},{... | collective-permute-start | bytes 196616 | tf_op jit(solution)/shard_map/ppermute | solution.py:579
  84.0 1.4 %collective-permute-start.26 = (bf16[4,64,128]{2,1,0:T(8,128)(2,1)S(1)}, bf16[4,64,128]{2,1,0:T(8,128)(2,1)S(1)}, u32[]{:S(2)}, u32[]{:S(2)}) collective-permute-start(bf16[4,64,128]{2,1,0:T(8,128)(2,1)S(1)} %get-tuple-element.114), channel_id=1, source_target_pairs={{0,24},{4,28},{8,16},{12,20},{16,8},{20,12},{24,0},{28,4},{1,25},{... | collective-permute-start | bytes 196616 | tf_op jit(solution)/shard_map/ppermute | solution.py:579
  85.4 5.2 %collective-permute-done.25.refs_10_ = bf16[4,64,128]{2,1,0:T(8,128)(2,1)S(1)} collective-permute-done((bf16[4,64,128]{2,1,0:T(8,128)(2,1)S(1)}, bf16[4,64,128]{2,1,0:T(8,128)(2,1)S(1)}, u32[]{:S(2)}, u32[]{:S(2)}) %collective-permute-start.25) | collective-permute-done | bytes 65568 | tf_op jit(solution)/shard_map/ppermute | solution.py:579
  90.6 2.2 %collapse.1 = f32[3,4,4096]{2,1,0:T(4,128)} custom-call(bf16[192,1280]{1,0:T(8,128)(2,1)S(1)} %copy-done.9, f32[4,32,128]{2,1,0:T(8,128)S(1)} %get-tuple-element.88.refs_0_, bf16[4,32,128]{2,1,0:T(8,128)(2,1)S(1)} %collective-permute-done.15.refs_1_, bf16[4,32,128]{2,1,0:T(8,128)(2,1)S(1)} %collective-permute-done.16.refs_2_, ...), custom_call_target="tpu_custom_call" | custom-call | flops 1000000000 | bytes 3000000 | tf_op jit(solution)/shard_map/collapse/pallas_call | solution.py:566
  (75 shorter events, 23.6 us)
Async XLA Ops:
  0.7 18.6 %collective-permute-start.1 = (s32[32]{0:T(128)S(1)}, s32[32]{0:T(128)S(1)}, u32[]{:S(2)}, u32[]{:S(2)}) collective-permute-start(s32[32]{0:T(128)S(1)} %bitcast_add_fusion), channel_id=1, source_target_pairs={{0,2},{1,3},{2,0},{3,1},{4,6},{5,7},{6,4},{7,5},{8,10},{9,11},{10,... | collective-permute-start | bytes 392 | tf_op jit(solution)/shard_map/ppermute | solution.py:579
  3.6 23.2 %collective-permute-start = (s32[32]{0:T(128)S(1)}, s32[32]{0:T(128)S(1)}, u32[]{:S(2)}, u32[]{:S(2)}) collective-permute-start(s32[32]{0:T(128)S(1)} %bitcast_add_fusion), channel_id=1, source_target_pairs={{0,1},{1,0},{2,3},{3,2},{4,5},{5,4},{6,7},{7,6},{8,9},{9,8},{10,11... | collective-permute-start | bytes 392 | tf_op jit(solution)/shard_map/ppermute | solution.py:579
  8.3 8.7 %collective-permute-start.3 = (bf16[288,128]{1,0:T(8,128)(2,1)S(1)}, bf16[288,128]{1,0:T(8,128)(2,1)S(1)}, u32[]{:S(2)}, u32[]{:S(2)}) collective-permute-start(bf16[288,128]{1,0:T(8,128)(2,1)S(1)} %strips.1), channel_id=1, source_target_pairs={{0,4},{4,0},{8,12},{12,8},{16,20},{20,16},{24,28},{28,24},{1,5},{5... | collective-permute-start | bytes 221192 | tf_op jit(solution)/shard_map/ppermute | solution.py:579
  17.0 4.5 %collective-permute-start.7 = (bf16[288,128]{1,0:T(8,128)(2,1)S(1)}, bf16[288,128]{1,0:T(8,128)(2,1)S(1)}, u32[]{:S(2)}, u32[]{:S(2)}) collective-permute-start(bf16[288,128]{1,0:T(8,128)(2,1)S(1)} %broadcast_select_fusion), channel_id=1, source_target_pairs={{0,8},{4,12},{8,0},{12,4},{16,24},{20,28},{24,16},{28,20},{1,9},{5... | collective-permute-start | bytes 221192 | tf_op jit(solution)/shard_map/ppermute | solution.py:579
  18.7 8.2 %collective-permute-start.5 = (bf16[32,32,128]{2,1,0:T(8,128)(2,1)S(1)}, bf16[32,32,128]{2,1,0:T(8,128)(2,1)S(1)}, u32[]{:S(2)}, u32[]{:S(2)}) collective-permute-start(bf16[32,32,128]{2,1,0:T(8,128)(2,1)S(1)} %get-tuple-element.66.a), channel_id=1, source_target_pairs={{0,2},{1,3},{2,0},{3,1},{4,6},{5,7},{6,4},{7,5},{8,10},{9,11},{10,... | collective-permute-start | bytes 786440 | tf_op jit(solution)/shard_map/ppermute | solution.py:579
  19.2 7.6 %collective-permute-start.2 = (s32[32]{0:T(128)S(1)}, s32[32]{0:T(128)S(1)}, u32[]{:S(2)}, u32[]{:S(2)}) collective-permute-start(s32[32]{0:T(128)S(1)} %collective-permute-done.1), channel_id=1, source_target_pairs={{0,1},{1,0},{2,3},{3,2},{4,5},{5,4},{6,7},{7,6},{8,9},{9,8},{10,11... | collective-permute-start | bytes 392 | tf_op jit(solution)/shard_map/ppermute | solution.py:579
  19.3 10.6 %collective-permute-start.4 = (bf16[32,32,128]{2,1,0:T(8,128)(2,1)S(1)}, bf16[32,32,128]{2,1,0:T(8,128)(2,1)S(1)}, u32[]{:S(2)}, u32[]{:S(2)}) collective-permute-start(bf16[32,32,128]{2,1,0:T(8,128)(2,1)S(1)} %get-tuple-element.66.a), channel_id=1, source_target_pairs={{0,1},{1,0},{2,3},{3,2},{4,5},{5,4},{6,7},{7,6},{8,9},{9,8},{10,11... | collective-permute-start | bytes 786440 | tf_op jit(solution)/shard_map/ppermute | solution.py:579
  21.5 8.4 %collective-permute-start.8 = (bf16[288,128]{1,0:T(8,128)(2,1)S(1)}, bf16[288,128]{1,0:T(8,128)(2,1)S(1)}, u32[]{:S(2)}, u32[]{:S(2)}) collective-permute-start(bf16[288,128]{1,0:T(8,128)(2,1)S(1)} %broadcast_select_fusion.1), channel_id=1, source_target_pairs={{0,16},{4,20},{8,24},{12,28},{16,0},{20,4},{24,8},{28,12},{1,17},{... | collective-permute-start | bytes 221192 | tf_op jit(solution)/shard_map/ppermute | solution.py:579
  26.8 3.1 %collective-permute-start.6 = (bf16[32,32,128]{2,1,0:T(8,128)(2,1)S(1)}, bf16[32,32,128]{2,1,0:T(8,128)(2,1)S(1)}, u32[]{:S(2)}, u32[]{:S(2)}) collective-permute-start(bf16[32,32,128]{2,1,0:T(8,128)(2,1)S(1)} %collective-permute-done.5.c), channel_id=1, source_target_pairs={{0,1},{1,0},{2,3},{3,2},{4,5},{5,4},{6,7},{7,6},{8,9},{9,8},{10,11... | collective-permute-start | bytes 786440 | tf_op jit(solution)/shard_map/ppermute | solution.py:579
  34.6 6.3 %collective-permute-start.10 = (bf16[32,80,128]{2,1,0:T(8,128)(2,1)S(1)}, bf16[32,80,128]{2,1,0:T(8,128)(2,1)S(1)}, u32[]{:S(2)}, u32[]{:S(2)}) collective-permute-start(bf16[32,80,128]{2,1,0:T(8,128)(2,1)S(1)} %get-tuple-element.72.a), channel_id=1, source_target_pairs={{0,1},{1,0},{2,3},{3,2},{4,5},{5,4},{6,7},{7,6},{8,9},{9,8},{10,11... | collective-permute-start | bytes 1966088 | tf_op jit(solution)/shard_map/ppermute | solution.py:579
  35.1 16.7 %collective-permute-start.9 = (bf16[32,80,128]{2,1,0:T(8,128)(2,1)S(1)}, bf16[32,80,128]{2,1,0:T(8,128)(2,1)S(1)}, u32[]{:S(2)}, u32[]{:S(2)}) collective-permute-start(bf16[32,80,128]{2,1,0:T(8,128)(2,1)S(1)} %get-tuple-element.72.a), channel_id=1, source_target_pairs={{0,2},{1,3},{2,0},{3,1},{4,6},{5,7},{6,4},{7,5},{8,10},{9,11},{10,... | collective-permute-start | bytes 1966088 | tf_op jit(solution)/shard_map/ppermute | solution.py:579
  35.7 5.2 %collective-permute-start.11 = (bf16[16,32,128]{2,1,0:T(8,128)(2,1)S(1)}, bf16[16,32,128]{2,1,0:T(8,128)(2,1)S(1)}, u32[]{:S(2)}, u32[]{:S(2)}) collective-permute-start(bf16[16,32,128]{2,1,0:T(8,128)(2,1)S(1)} %get-tuple-element.74), channel_id=1, source_target_pairs={{0,4},{4,0},{8,12},{12,8},{16,20},{20,16},{24,28},{28,24},{1,5},{5... | collective-permute-start | bytes 393224 | tf_op jit(solution)/shard_map/ppermute | solution.py:579
  51.8 14.3 %collective-permute-start.12 = (bf16[32,64,128]{2,1,0:T(8,128)(2,1)S(1)}, bf16[32,64,128]{2,1,0:T(8,128)(2,1)S(1)}, u32[]{:S(2)}, u32[]{:S(2)}) collective-permute-start(bf16[32,64,128]{2,1,0:T(8,128)(2,1)S(1)} %get-tuple-element.80.a), channel_id=1, source_target_pairs={{0,2},{1,3},{2,0},{3,1},{4,6},{5,7},{6,4},{7,5},{8,10},{9,11},{10,... | collective-permute-start | bytes 1572872 | tf_op jit(solution)/shard_map/ppermute | solution.py:579
  55.1 11.0 %collective-permute-start.14 = (bf16[16,80,128]{2,1,0:T(8,128)(2,1)S(1)}, bf16[16,80,128]{2,1,0:T(8,128)(2,1)S(1)}, u32[]{:S(2)}, u32[]{:S(2)}) collective-permute-start(bf16[16,80,128]{2,1,0:T(8,128)(2,1)S(1)} %get-tuple-element.83), channel_id=1, source_target_pairs={{0,4},{4,0},{8,12},{12,8},{16,20},{20,16},{24,28},{28,24},{1,5},{5... | collective-permute-start | bytes 983048 | tf_op jit(solution)/shard_map/ppermute | solution.py:579
  55.8 4.4 %collective-permute-start.15 = (bf16[4,32,128]{2,1,0:T(8,128)(2,1)S(1)}, bf16[4,32,128]{2,1,0:T(8,128)(2,1)S(1)}, u32[]{:S(2)}, u32[]{:S(2)}) collective-permute-start(bf16[4,32,128]{2,1,0:T(8,128)(2,1)S(1)} %get-tuple-element.85), channel_id=1, source_target_pairs={{0,8},{4,12},{8,0},{12,4},{16,24},{20,28},{24,16},{28,20},{1,9},{5... | collective-permute-start | bytes 98312 | tf_op jit(solution)/shard_map/ppermute | solution.py:579
  56.2 5.0 %collective-permute-start.16 = (bf16[4,32,128]{2,1,0:T(8,128)(2,1)S(1)}, bf16[4,32,128]{2,1,0:T(8,128)(2,1)S(1)}, u32[]{:S(2)}, u32[]{:S(2)}) collective-permute-start(bf16[4,32,128]{2,1,0:T(8,128)(2,1)S(1)} %get-tuple-element.86), channel_id=1, source_target_pairs={{0,16},{4,20},{8,24},{12,28},{16,0},{20,4},{24,8},{28,12},{1,17},{... | collective-permute-start | bytes 98312 | tf_op jit(solution)/shard_map/ppermute | solution.py:579
  58.9 5.7 %collective-permute-start.17 = (bf16[4,32,128]{2,1,0:T(8,128)(2,1)S(1)}, bf16[4,32,128]{2,1,0:T(8,128)(2,1)S(1)}, u32[]{:S(2)}, u32[]{:S(2)}) collective-permute-start(bf16[4,32,128]{2,1,0:T(8,128)(2,1)S(1)} %get-tuple-element.87), channel_id=1, source_target_pairs={{0,24},{4,28},{8,16},{12,20},{16,8},{20,12},{24,0},{28,4},{1,25},{... | collective-permute-start | bytes 98312 | tf_op jit(solution)/shard_map/ppermute | solution.py:579
  70.0 10.4 %collective-permute-start.20 = (bf16[16,64,128]{2,1,0:T(8,128)(2,1)S(1)}, bf16[16,64,128]{2,1,0:T(8,128)(2,1)S(1)}, u32[]{:S(2)}, u32[]{:S(2)}) collective-permute-start(bf16[16,64,128]{2,1,0:T(8,128)(2,1)S(1)} %get-tuple-element.100), channel_id=1, source_target_pairs={{0,4},{4,0},{8,12},{12,8},{16,20},{20,16},{24,28},{28,24},{1,5},{5... | collective-permute-start | bytes 786440 | tf_op jit(solution)/shard_map/ppermute | solution.py:579
  70.7 5.8 %collective-permute-start.21 = (bf16[4,80,128]{2,1,0:T(8,128)(2,1)S(1)}, bf16[4,80,128]{2,1,0:T(8,128)(2,1)S(1)}, u32[]{:S(2)}, u32[]{:S(2)}) collective-permute-start(bf16[4,80,128]{2,1,0:T(8,128)(2,1)S(1)} %get-tuple-element.102), channel_id=1, source_target_pairs={{0,8},{4,12},{8,0},{12,4},{16,24},{20,28},{24,16},{28,20},{1,9},{5... | collective-permute-start | bytes 245768 | tf_op jit(solution)/shard_map/ppermute | solution.py:579
  71.1 6.7 %collective-permute-start.22 = (bf16[4,80,128]{2,1,0:T(8,128)(2,1)S(1)}, bf16[4,80,128]{2,1,0:T(8,128)(2,1)S(1)}, u32[]{:S(2)}, u32[]{:S(2)}) collective-permute-start(bf16[4,80,128]{2,1,0:T(8,128)(2,1)S(1)} %get-tuple-element.103), channel_id=1, source_target_pairs={{0,16},{4,20},{8,24},{12,28},{16,0},{20,4},{24,8},{28,12},{1,17},{... | collective-permute-start | bytes 245768 | tf_op jit(solution)/shard_map/ppermute | solution.py:579
  73.7 6.7 %collective-permute-start.23 = (bf16[4,80,128]{2,1,0:T(8,128)(2,1)S(1)}, bf16[4,80,128]{2,1,0:T(8,128)(2,1)S(1)}, u32[]{:S(2)}, u32[]{:S(2)}) collective-permute-start(bf16[4,80,128]{2,1,0:T(8,128)(2,1)S(1)} %get-tuple-element.104), channel_id=1, source_target_pairs={{0,24},{4,28},{8,16},{12,20},{16,8},{20,12},{24,0},{28,4},{1,25},{... | collective-permute-start | bytes 245768 | tf_op jit(solution)/shard_map/ppermute | solution.py:579
  80.5 4.9 %collective-permute-start.24 = (bf16[4,64,128]{2,1,0:T(8,128)(2,1)S(1)}, bf16[4,64,128]{2,1,0:T(8,128)(2,1)S(1)}, u32[]{:S(2)}, u32[]{:S(2)}) collective-permute-start(bf16[4,64,128]{2,1,0:T(8,128)(2,1)S(1)} %get-tuple-element.112), channel_id=1, source_target_pairs={{0,8},{4,12},{8,0},{12,4},{16,24},{20,28},{24,16},{28,20},{1,9},{5... | collective-permute-start | bytes 196616 | tf_op jit(solution)/shard_map/ppermute | solution.py:579
  82.4 8.2 %collective-permute-start.25 = (bf16[4,64,128]{2,1,0:T(8,128)(2,1)S(1)}, bf16[4,64,128]{2,1,0:T(8,128)(2,1)S(1)}, u32[]{:S(2)}, u32[]{:S(2)}) collective-permute-start(bf16[4,64,128]{2,1,0:T(8,128)(2,1)S(1)} %get-tuple-element.113), channel_id=1, source_target_pairs={{0,16},{4,20},{8,24},{12,28},{16,0},{20,4},{24,8},{28,12},{1,17},{... | collective-permute-start | bytes 196616 | tf_op jit(solution)/shard_map/ppermute | solution.py:579
  84.0 6.6 %collective-permute-start.26 = (bf16[4,64,128]{2,1,0:T(8,128)(2,1)S(1)}, bf16[4,64,128]{2,1,0:T(8,128)(2,1)S(1)}, u32[]{:S(2)}, u32[]{:S(2)}) collective-permute-start(bf16[4,64,128]{2,1,0:T(8,128)(2,1)S(1)} %get-tuple-element.114), channel_id=1, source_target_pairs={{0,24},{4,28},{8,16},{12,20},{16,8},{20,12},{24,0},{28,4},{1,25},{... | collective-permute-start | bytes 196616 | tf_op jit(solution)/shard_map/ppermute | solution.py:579
  (17 other events, 119.7 us)

commit v4 on v3

--- a/solution.py
+++ b/solution.py
@@ -16,6 +16,9 @@
 TILE_DEV = 4
 VMEM = 30 << 20
 ROUTE = 4096
+FREE = 28
+PATCH = 144
+HALF = 96
 F32 = jnp.float32
 BF16 = jnp.bfloat16
 
@@ -249,13 +252,21 @@
         grid_spec=grid_spec,
         out_shape=jax.ShapeDtypeStruct((288, 128), BF16),
         compiler_params=pltpu.CompilerParams(vmem_limit_bytes=VMEM),
-        cost_estimate=pl.CostEstimate(flops=2 * 10**9, bytes_accessed=10**6, transcendentals=0),
+        cost_estimate=pl.CostEstimate(flops=10**6, bytes_accessed=10**4, transcendentals=0),
         name="strips",
     )(cell, frames, frames, packed)
 
 
 def lane_index():
     return lax.broadcasted_iota(jnp.int32, (1, 128), 1)
+
+
+def slot_of(c, left):
+    return jnp.where(c < left, c, jnp.where(c < left + 2, c - left + 14, c - 2))
+
+
+def left_column(cell):
+    return jnp.minimum(cell // 4, 14)
 
 
 def fold_level0(p, store):
@@ -264,8 +275,35 @@
         for j in range(8):
             even = p[r * 64 : r * 64 + 32, j * 128 : j * 128 + 128]
             odd = p[r * 64 + 32 : r * 64 + 64, j * 128 : j * 128 + 128]
-            store(r * 16 + 2 * j, jnp.where(left, even, pltpu.roll(odd, 64, 1)))
-            store(r * 16 + 2 * j + 1, jnp.where(left, pltpu.roll(even, 64, 1), odd))
+            store(r, 2 * j, jnp.where(left, even, pltpu.roll(odd, 64, 1)))
+            store(r, 2 * j + 1, jnp.where(left, pltpu.roll(even, 64, 1), odd))
+
+
+def cut(level0, parts1, parts2, parts3, parts4, put):
+    for ch in range(COLOURS):
+        row = (0, 32, 96)[ch]
+        fold_level0(level0(ch), lambda r, c, piece, row=row: put(r, c, row, piece))
+    for r in range(2):
+        for j in range(4):
+            turned = [parts1[ch][r * 32 : r * 32 + 32, j * 128 : j * 128 + 128] for ch in range(4)]
+            turned = [turned[0]] + [pltpu.roll(turned[ch], 32 * ch, 1) for ch in range(1, 4)]
+            for cc in range(4):
+                put(r, 4 * j + cc, 64, gather_channels(turned, 32, cc, 0))
+    lane = lane_index()
+    for r in range(2):
+        turned3 = [pltpu.roll(parts3[ch][r * 8 : r * 8 + 8], 8 * ch, 1) for ch in range(4)]
+        turned4 = [pltpu.roll(parts4[ch][r * 8 : r * 8 + 8], 4 * ch, 1) for ch in range(4)]
+        for j in range(2):
+            turned2 = [parts2[ch][r * 16 : r * 16 + 16, j * 128 : j * 128 + 128] for ch in range(4)]
+            turned2 = [pltpu.roll(turned2[ch], 16 * ch, 1) for ch in range(4)]
+            for cc in range(8):
+                c = j * 8 + cc
+                two = gather_channels(turned2, 16, cc, 0)
+                three = gather_channels(turned3, 8, c, 64)
+                four = gather_channels(turned4, 4, c, 96)
+                head = jnp.where(lane < 64, two[0:8], jnp.where(lane < 96, three, four))
+                tail = jnp.where(lane < 64, two[8:16], 0.0)
+                put(r, c, 128, jnp.concatenate([head, tail], axis=0))
 
 
 def gather_channels(parts, width, cc, base):
@@ -292,7 +330,7 @@
     return levels, masks
 
 
-def bands_kernel(small_places, large_places, x, w, m, small, large, wblocks, state):
+def bands_kernel(small_places, large_places, cell, x, w, m, small, large, wblocks, first, second, state):
     mats = unpack(small, small_places)
     v, gv, sm = (levels_of(mats, letter) for letter in "vgm")
     order = mats["order"]
@@ -307,8 +345,10 @@
     weights = mm(order, planes[3])
     state[views[0][3]] = weights
 
-    def store(q, piece):
-        wblocks[q] = piece.astype(BF16)
+    left = left_column(cell[0])
+
+    def store(r, c, piece):
+        wblocks[slot_of(c, left) * 2 + r] = piece.astype(BF16)
 
     fold_level0(weights, store)
     levels = pyramid(planes, v, s)
@@ -332,20 +372,40 @@
     for k in range(1, 5):
         state[mask_views[k]] = masks[k]
 
-
-def bands_of(frames, weight_map, seam_mask):
+    def put(r, c, row, piece):
+        slot = slot_of(c, left)
+        out, at = (first, row) if row < HALF else (second, row - HALF)
+
+        @pl.when(slot < 14)
+        def _():
+            out[slot * 2 + r, at : at + piece.shape[0], :] = piece.astype(BF16)
+
+    parts = [None]
+    for k in range(1, 5):
+        wk = state[views[k][3]]
+        parts.append([wk * state[views[k][c]] for c in range(COLOURS)] + [wk])
+    cut(lambda ch: weights * state[views[0][ch]], *parts[1:], put)
+
+
+def bands_of(cell, frames, weight_map, seam_mask):
     small, small_places = small_matrices()
     large, large_places = large_matrices()
     return pl.pallas_call(
         functools.partial(bands_kernel, small_places, large_places),
-        out_shape=[jax.ShapeDtypeStruct((QB, 32, 128), BF16), jax.ShapeDtypeStruct((STATE_ROWS, FW), F32)],
+        in_specs=[pl.BlockSpec(memory_space=pltpu.SMEM)] + [pl.BlockSpec(memory_space=pltpu.VMEM)] * 5,
+        out_shape=[
+            jax.ShapeDtypeStruct((QB, 32, 128), BF16),
+            jax.ShapeDtypeStruct((FREE, HALF, 128), BF16),
+            jax.ShapeDtypeStruct((FREE, PATCH - HALF, 128), BF16),
+            jax.ShapeDtypeStruct((STATE_ROWS, FW), F32),
+        ],
         compiler_params=pltpu.CompilerParams(vmem_limit_bytes=VMEM),
-        cost_estimate=pl.CostEstimate(flops=8 * 10**9, bytes_accessed=6 * 10**6, transcendentals=0),
+        cost_estimate=pl.CostEstimate(flops=10**6, bytes_accessed=10**4, transcendentals=0),
         name="bands",
-    )(frames, weight_map, jnp.swapaxes(seam_mask, 1, 2), small, large)
-
-
-def blend_kernel(cell, strips, state, first, second):
+    )(cell, frames, weight_map, jnp.swapaxes(seam_mask, 1, 2), small, large)
+
+
+def blend_kernel(cell, strips, state, patch):
     views, mask_views = state_views(state)
     (b0, b1, b2, b3, b4) = [[state[view] for view in views[k][:3]] for k in range(5)]
     (wp, w1, w2, w3, w4) = [state[views[k][3]] for k in range(5)]
@@ -364,45 +424,26 @@
     top = strips[0:192]
     remote0 = [mm(top, place(128, 1024, 0, 64, start)), mm(top, place(128, 1024, 64, 64, start))]
     remote0 = jnp.concatenate(remote0, axis=0)
-    weights = wp
-    for c in range(COLOURS):
-        p = weights * mixed(b0[c], remote0[c * 128 : (c + 1) * 128], share[0])
-        out, row = (first, 0) if c == 0 else (second, 32 * (c - 1))
-
-        def store(q, piece, out=out, row=row):
-            out[q, row : row + 32, :] = piece.astype(BF16)
-
-        fold_level0(p, store)
+
+    left = left_column(cell[0])
+
+    def put(r, c, row, piece):
+        slot = slot_of(c, left)
+
+        @pl.when(slot >= 14)
+        def _():
+            patch[(slot - 14) * 2 + r, row : row + piece.shape[0], :] = piece.astype(BF16)
+
     remote1 = [mm(low, place(128, 512, 0, 32, start >> 1)), mm(low, place(128, 512, 32, 32, start >> 1))]
     remote1 = jnp.concatenate(remote1, axis=0)
-    parts = [w1 * mixed(b1[c], remote1[c * 64 : (c + 1) * 64], share[1]) for c in range(COLOURS)] + [w1]
-    for r in range(2):
-        for j in range(4):
-            turned = [parts[ch][r * 32 : r * 32 + 32, j * 128 : j * 128 + 128] for ch in range(4)]
-            turned = [turned[0]] + [pltpu.roll(turned[ch], 32 * ch, 1) for ch in range(1, 4)]
-            for cc in range(4):
-                first[r * 16 + 4 * j + cc, 32:64, :] = gather_channels(turned, 32, cc, 0).astype(BF16)
+    parts1 = [w1 * mixed(b1[c], remote1[c * 64 : (c + 1) * 64], share[1]) for c in range(COLOURS)] + [w1]
     remote2 = mm(low, place(128, 256, 64, 16, start >> 2))
     remote3 = mm(low[0:48], place(128, 128, 80, 8, start >> 3))
     remote4 = mm(low[0:48], place(128, 128, 88, 4, start >> 4))
     parts2 = [w2 * mixed(b2[c], remote2[c * 32 : (c + 1) * 32], share[2]) for c in range(COLOURS)] + [w2]
     parts3 = [w3 * mixed(b3[c], remote3[c * 16 : (c + 1) * 16], share[3]) for c in range(COLOURS)] + [w3]
     parts4 = [w4 * mixed(b4[c], remote4[c * 16 : (c + 1) * 16], share[4]) for c in range(COLOURS)] + [w4]
-    lane = lane_index()
-    for r in range(2):
-        turned3 = [pltpu.roll(parts3[ch][r * 8 : r * 8 + 8], 8 * ch, 1) for ch in range(4)]
-        turned4 = [pltpu.roll(parts4[ch][r * 8 : r * 8 + 8], 4 * ch, 1) for ch in range(4)]
-        for j in range(2):
-            turned2 = [parts2[ch][r * 16 : r * 16 + 16, j * 128 : j * 128 + 128] for ch in range(4)]
-            turned2 = [pltpu.roll(turned2[ch], 16 * ch, 1) for ch in range(4)]
-            for cc in range(8):
-                c = j * 8 + cc
-                two = gather_channels(turned2, 16, cc, 0)
-                three = gather_channels(turned3, 8, c, 64)
-                four = gather_channels(turned4, 4, c, 96)
-                head = jnp.where(lane < 64, two[0:8], jnp.where(lane < 96, three, four))
-                tail = jnp.where(lane < 64, two[8:16], 0.0)
-                first[r * 16 + c, 64:80, :] = jnp.concatenate([head, tail], axis=0).astype(BF16)
+    cut(lambda c: wp * mixed(b0[c], remote0[c * 128 : (c + 1) * 128], share[0]), parts1, parts2, parts3, parts4, put)
 
 
 def blend(cell, strips, state):
@@ -410,9 +451,9 @@
     return pl.pallas_call(
         blend_kernel,
         in_specs=[pl.BlockSpec(memory_space=pltpu.SMEM)] + [vmem] * 2,
-        out_shape=[jax.ShapeDtypeStruct((QB, 80, 128), BF16), jax.ShapeDtypeStruct((QB, 64, 128), BF16)],
+        out_shape=jax.ShapeDtypeStruct((QB - FREE, PATCH, 128), BF16),
         compiler_params=pltpu.CompilerParams(vmem_limit_bytes=VMEM),
-        cost_estimate=pl.CostEstimate(flops=4 * 10**9, bytes_accessed=4 * 10**6, transcendentals=0),
+        cost_estimate=pl.CostEstimate(flops=10**6, bytes_accessed=10**4, transcendentals=0),
         name="blend",
     )(cell, strips, state)
 
@@ -425,7 +466,9 @@
             lists[source, count] = q * ROUTE + at
             return jnp.where(at >= 0, count + 1, count)
 
-        counts[source] = lax.fori_loop(0, QB, body, 0)
+        free = lax.fori_loop(0, FREE, body, 0)
+        counts[source] = free
+        counts[4 + source] = lax.fori_loop(FREE, QB, body, free)
 
 
 def routes_of(spot):
@@ -434,40 +477,53 @@
         routes_kernel,
         in_specs=[smem],
         out_specs=[smem, smem],
-        out_shape=[jax.ShapeDtypeStruct((4, QB + 1), jnp.int32), jax.ShapeDtypeStruct((4,), jnp.int32)],
+        out_shape=[jax.ShapeDtypeStruct((4, QB + 1), jnp.int32), jax.ShapeDtypeStruct((8,), jnp.int32)],
         name="routes",
     )(spot)
 
 
-def gather_kernel(lists, counts, a, b, c, d, home, away, acc):
+def gather_kernel(row, lists, counts, *refs):
+    home, away, acc = refs[-3:]
+    sources, patches = refs[:4], refs[4:-3]
+    height = acc.shape[1]
     acc[...] = jnp.zeros_like(acc)
-    for source, ref in enumerate((a, b, c, d)):
-
-        def body(i, carry, source=source, ref=ref):
+
+    def add(source, lo, hi, load):
+        def body(i, carry):
             entry = lists[source, i]
-            q, at = entry // ROUTE, entry % ROUTE
-            acc[at] = acc[at] + ref[q].astype(F32)
+            at = entry % ROUTE
+            acc[at] = acc[at] + load(entry // ROUTE).astype(F32)
             return carry
 
-        lax.fori_loop(0, counts[source], body, 0)
+        lax.fori_loop(lo, hi, body, 0)
+
+    for source in range(4):
+        ref = sources[source]
+        if patches:
+            patch = patches[source]
+            add(source, 0, counts[source], lambda q, ref=ref: ref[q])
+            load = lambda q, ref=patch: ref[q - FREE, row : row + height, :]
+            add(source, counts[source], counts[4 + source], load)
+        else:
+            add(source, 0, counts[4 + source], lambda q, ref=ref: ref[q])
     tiles = home.shape[0]
     home[...] = acc[0:tiles]
     away[...] = acc[tiles : 2 * tiles].astype(BF16)
 
 
-def gather_rows(routes, rows, tiles):
+def gather_rows(routes, rows, patches, row, tiles):
     height = rows[0].shape[1]
     vmem = pl.BlockSpec(memory_space=pltpu.VMEM)
     shape = (tiles // 2, height, 128)
     return pl.pallas_call(
-        gather_kernel,
-        in_specs=[pl.BlockSpec(memory_space=pltpu.SMEM)] * 2 + [vmem] * 4,
+        functools.partial(gather_kernel, row),
+        in_specs=[pl.BlockSpec(memory_space=pltpu.SMEM)] * 2 + [vmem] * len(rows + patches),
         out_shape=[jax.ShapeDtypeStruct(shape, F32), jax.ShapeDtypeStruct(shape, BF16)],
         scratch_shapes=[pltpu.VMEM((tiles, height, 128), F32)],
         compiler_params=pltpu.CompilerParams(vmem_limit_bytes=VMEM),
-        cost_estimate=pl.CostEstimate(flops=10**9, bytes_accessed=4 * 10**6, transcendentals=0),
+        cost_estimate=pl.CostEstimate(flops=10**6, bytes_accessed=10**4, transcendentals=0),
         name="gather_rows",
-    )(*routes, *rows)
+    )(*routes, *rows, *patches)
 
 
 def add_kernel(home, got, own, *away):
@@ -487,7 +543,7 @@
         add_kernel,
         out_shape=[jax.ShapeDtypeStruct(shape, F32)] + [jax.ShapeDtypeStruct(shape, BF16)] * others,
         compiler_params=pltpu.CompilerParams(vmem_limit_bytes=VMEM),
-        cost_estimate=pl.CostEstimate(flops=10**8, bytes_accessed=2 * 10**6, transcendentals=0),
+        cost_estimate=pl.CostEstimate(flops=10**6, bytes_accessed=10**4, transcendentals=0),
         name="add_halves",
     )(home, got)
 
@@ -532,7 +588,7 @@
         return acc.reshape(TILE_DEV * (hi - lo), 128)
 
     lane = lane_index()
-    small = total(b, 64, 80)
+    small = total(c, 32, 48)
     bottom = small
     for lo, width, chans in ((0, 16, 3), (64, 8, 3), (96, 4, 3)):
         for ch in range(chans):
@@ -541,7 +597,7 @@
     small = small / jnp.maximum(bottom, 1.0)
     three = small + ldot(mats["d43"], rdot(small, mats["m43"]))
     two = small + ldot(mats["d32"], rdot(three, mats["m32"]))
-    one = total(b, 32, 64)
+    one = total(b, 64, 96)
     bottom = one
     for ch in range(3):
         inside = (lane >= ch * 32) & (lane < (ch + 1) * 32)
@@ -553,7 +609,7 @@
     down = mm(mats["odd"], hi) + mm(mats["odd"], lo)
     bottom = jnp.maximum(total(a, 0, 32), 1.0)
     for ch in range(COLOURS):
-        own = total(b, 0, 32) if ch == 0 else total(c, 32 * (ch - 1), 32 * ch)
+        own = total(b, 32 * ch, 32 * ch + 32) if ch < 2 else total(c, 0, 32)
         back = jnp.where(lane < 64, up[:, ch * 128 : ch * 128 + 128], down[:, ch * 128 : ch * 128 + 128])
         level0[ch * 128 : ch * 128 + 128, :] = own / bottom + back
     for ch in range(COLOURS):
@@ -568,7 +624,7 @@
         out_shape=jax.ShapeDtypeStruct((COLOURS, TILE_DEV, 4096), F32),
         scratch_shapes=[pltpu.VMEM((COLOURS * 128, 128), F32)],
         compiler_params=pltpu.CompilerParams(vmem_limit_bytes=VMEM),
-        cost_estimate=pl.CostEstimate(flops=10**9, bytes_accessed=3 * 10**6, transcendentals=0),
+        cost_estimate=pl.CostEstimate(flops=10**6, bytes_accessed=10**4, transcendentals=0),
         name="collapse",
     )(packed, *a, *b, *c)
     return jnp.swapaxes(tiles, 0, 1)
@@ -585,11 +641,14 @@
     mine = lax.axis_index("tiles")
     mask = lax.bitwise_xor(partner[0] // parts, lax.axis_index("frames"))
 
+    strips = strips_of(frames, strip_cell)
     ids = tile_group.reshape(QB) * (parts * TILE_DEV) + tile_position_in_group.reshape(QB)
-    ids_core = swap(ids, "tiles", 1)
+    columns = jnp.arange(QB, dtype=jnp.int32) % 16
+    slots = slot_of(columns, left_column(strip_cell[0])) * 2 + jnp.arange(QB, dtype=jnp.int32) // 16
+    ids = jnp.sum(jnp.where(slots[None, :] == jnp.arange(QB, dtype=jnp.int32)[:, None], ids[None, :], 0), axis=1)
+    strips, frames, ids = lax.optimization_barrier((strips, frames, ids))
     ids_far = swap(ids, "tiles", 2)
-    ids_far_core = swap(ids_far, "tiles", 1)
-    ids = jnp.stack([ids, ids_core, ids_far, ids_far_core])
+    ids = jnp.stack([ids, swap(ids, "tiles", 1), ids_far, swap(ids_far, "tiles", 1)])
     group_size = parts * TILE_DEV
     owner = ids % group_size // TILE_DEV
     relative = lax.bitwise_xor(ids // group_size, lax.axis_index("frames"))
@@ -597,44 +656,50 @@
     spot = jnp.where(owner == mine, relative * TILE_DEV + ids % TILE_DEV, -1)
 
     routes = routes_of(spot)
-    strips = strips_of(frames, strip_cell)
-    strips, frames = lax.optimization_barrier((strips, frames))
-    weights, state = bands_of(frames, weight_map, seam_mask)
+    tie = lax.optimization_barrier
+    weights, first, second, state = bands_of(strip_cell, frames, weight_map, seam_mask)
     bit = 1
     while bit < groups:
         got = swap(strips, "frames", bit)
         if bit == 1:
-            got, weights, state = lax.optimization_barrier((got, weights, state))
+            got, weights, first, second, state = tie((got, weights, first, second, state))
+            far_weights, near_weights = swap(weights, "tiles", 2), swap(weights, "tiles", 1)
+        if bit == 2:
+            got, far_weights, near_weights, first = tie((got, far_weights, near_weights, first))
+        if bit == groups // 2:
+            got, routes = tie((got, routes))
         strips = jnp.where((mask & bit) != 0, got, strips)
         bit *= 2
 
-    tie = lax.optimization_barrier
-
-    def gather(rows, near, far, far_near):
-        return gather_rows(routes, (rows, near, far, far_near), groups * TILE_DEV)
+    def gather(rows, patches=(), row=0):
+        return gather_rows(routes, rows, patches, row, groups * TILE_DEV)
 
     def along(own, *away):
         return [own] + [swap(part, "frames", 2 * (j + 1)) for j, part in enumerate(away)]
 
-    far = swap(weights, "tiles", 2)
-    home, away = gather(weights, swap(weights, "tiles", 1), far, swap(far, "tiles", 1))
-    home, away, strips = tie((home, away, strips))
-    first, second = blend(strip_cell, strips, state)
-    far = swap(first, "tiles", 2)
-    near = swap(first, "tiles", 1)
-    sums = add_halves(home, swap(away, "frames", 1))
-    far, near, sums, second = tie((far, near, sums, second))
+    far_first, near_first = swap(first, "tiles", 2), swap(first, "tiles", 1)
+    patch = blend(strip_cell, strips, state)
+    far_patch, near_patch = swap(patch, "tiles", 2), swap(patch, "tiles", 1)
+    near_patch, second = tie((near_patch, second))
+    far_second, near_second = swap(second, "tiles", 2), swap(second, "tiles", 1)
+    home, away = gather((weights, near_weights, far_weights, swap(far_weights, "tiles", 1)))
+    away_got = swap(away, "frames", 1)
+    far_first, near_first, far_patch, near_patch, home, away_got = tie(
+        (far_first, near_first, far_patch, near_patch, home, away_got)
+    )
+    patches = (patch, near_patch, far_patch, swap(far_patch, "tiles", 1))
+    sums = add_halves(home, away_got)
+    far_near = swap(far_first, "tiles", 1)
+    far_near, sums = tie((far_near, sums))
     got_weights = along(*sums)
-    far_second = swap(second, "tiles", 2)
-    near_second = swap(second, "tiles", 1)
-    home, away = gather(first, near, far, swap(far, "tiles", 1))
+    home, away = gather((first, near_first, far_first, far_near), patches, 0)
     got = swap(away, "frames", 1)
-    far_second, got, got_weights = tie((far_second, got, got_weights))
+    far_second, home, got_weights = tie((far_second, home, got_weights))
     far_near = swap(far_second, "tiles", 1)
     sums = add_halves(home, got)
     far_near, sums = tie((far_near, sums))
     got_first = along(*sums)
-    home, away = gather(second, near_second, far_second, far_near)
+    home, away = gather((second, near_second, far_second, far_near), patches, HALF)
     got = swap(away, "frames", 1)
     got, got_first = tie((got, got_first))
     got_second = along(*add_halves(home, got))

time: 93 us -> 113 us (1.22)
  Pallas kernels: 16 us -> 41.8 us
  waiting for transfers between devices: 40.1 us -> 28 us
  starting transfers between devices: 27.6 us -> 30.8 us
  local copies, waits for them, and re-layouts: 6.08 us -> 8.77 us
    pallas_call x1, Pallas kernels: 4.68 us -> 17.5 us  [bands_of(): pl.pallas_call(functools.partial(bands_kernel, small_places, large_places...]
    ppermute x27 -> x30, waiting for transfers between devices: 40.1 us -> 28 us  [swap(): return lax.ppermute(value, axis, [(i, i ^ bit) for i in range(size)])]
    pallas_call x1, Pallas kernels: 1.37 us -> 12.6 us  [blend(): pl.pallas_call(blend_kernel, in_specs=[pl.BlockSpec(memory_space=pltpu.SM...]
    ppermute x27 -> x30, starting transfers between devices: 27.6 us -> 30.8 us  [swap(): return lax.ppermute(value, axis, [(i, i ^ bit) for i in range(size)])]
    unnamed x28 -> x32, local copies, waits for them, and re-layouts: 6.08 us -> 8.77 us
    pallas_call x3, Pallas kernels: 3.34 us -> 5.12 us  [gather_rows(): pl.pallas_call(functools.partial(gather_kernel, row), in_specs=[pl.BlockS...]
  transfers between devices with their start and end apart: 27 -> 30, of which waited for: 14 -> 17; matrix products, arithmetic and copies ran while one was open for 1% -> 1% of each run, Pallas kernels for 11% -> 32%
where the time goes in v4:
time: 113 us; the launch traced here: 112 us
  Pallas kernels  41.8 us (37%)
  starting transfers between devices  30.8 us (27%)
  waiting for transfers between devices  28 us (25%)
  local copies, waits for them, and re-layouts  8.77 us (8%)
  between operations  1.55 us (1%)
  other arithmetic  1.44 us (1%)
    ppermute x30, starting transfers between devices, swap(): return lax.ppermute(value, axis, [(i, i ^ bit) for i in range(size)])  30.8 us
    ppermute x30, waiting for transfers between devices, swap(): return lax.ppermute(value, axis, [(i, i ^ bit) for i in range(size)])  28 us
    pallas_call x1, Pallas kernels, bands_of(): pl.pallas_call(functools.partial(bands_kernel, small_places, large_places...  17.5 us
    pallas_call x1, Pallas kernels, blend(): pl.pallas_call(blend_kernel, in_specs=[pl.BlockSpec(memory_space=pltpu.SM...  12.6 us
    unnamed x32, local copies, waits for them, and re-layouts  8.77 us
    pallas_call x3, Pallas kernels, gather_rows(): pl.pallas_call(functools.partial(gather_kernel, row), in_specs=[pl.BlockS...  5.12 us
    pallas_call x1, Pallas kernels, routes_of(): pl.pallas_call(routes_kernel, in_specs=[smem], out_specs=[smem, smem], ou...  2.44 us
  transfers between devices with their start and end apart: 30, of which 17 were waited for; matrix products, arithmetic and copies ran while one was open for 1% of the time, Pallas kernels for 32%

profile of v4, /device:TPU:0, one launch (start us, length us, event | category | flops | bytes accessed | tf_op | source)
XLA Modules:
  0.0 112.4 jit_solution(8876488880357337892)
XLA Ops:
  2.9 1.9 %strips.1 = bf16[288,128]{1,0:T(8,128)(2,1)S(1)} custom-call(s32[1]{0:T(128)} %copy.12.cell, bf16[1,3,128,1024]{3,2,1,0:T(8,128)(2,1)S(1)} %copy-done, bf16[1,3,128,1024]{3,2,1,0:T(8,128)(2,1)S(1)} %copy-done, bf16[512,512]{1,0:T(8,128)(2,1)S(1)} %copy-done.2), custom_call_target="tpu_custom_call" | custom-call | flops 1000000 | bytes 10000 | tf_op jit(solution)/shard_map/strips/pallas_call | solution.py:250
  5.5 3.0 %collective-permute-start = (bf16[288,128]{1,0:T(8,128)(2,1)S(1)}, bf16[288,128]{1,0:T(8,128)(2,1)S(1)}, u32[]{:S(2)}, u32[]{:S(2)}) collective-permute-start(bf16[288,128]{1,0:T(8,128)(2,1)S(1)} %strips.1), channel_id=1, source_target_pairs={{0,4},{4,0},{8,12},{12,8},{16,20},{20,16},{24,28},{28,24},{1,5},{5... | collective-permute-start | bytes 221192 | tf_op jit(solution)/shard_map/ppermute | solution.py:635
  14.2 17.5 %bands.1 = (bf16[32,32,128]{2,1,0:T(8,128)(2,1)}, bf16[28,96,128]{2,1,0:T(8,128)(2,1)S(1)}, bf16[28,48,128]{2,1,0:T(8,128)(2,1)S(1)}, f32[816,1024]{1,0:T(8,128)S(1)}) custom-call(s32[1]{0:T(128)} %copy.12.cell, bf16[1,3,128,1024]{3,2,1,0:T(8,128)(2,1)S(1)} %copy-done.1, bf16[1,128,1024]{2,1,0:T(8,128)(2,1)S(1)} %copy-done.10, s32[1,64,128]{2,1,0:T(8,128)S(1)} %bitcast.22, ...), custom_call_target="tpu_custom_call" | custom-call | flops 1000000 | bytes 10000 | tf_op jit(solution)/shard_map/bands/pallas_call | solution.py:393
  33.3 1.5 %collective-permute-start.2 = (bf16[32,32,128]{2,1,0:T(8,128)(2,1)}, bf16[32,32,128]{2,1,0:T(8,128)(2,1)}, u32[]{:S(2)}, u32[]{:S(2)}) collective-permute-start(bf16[32,32,128]{2,1,0:T(8,128)(2,1)} %get-tuple-element.80.refs_0_), channel_id=1, source_target_pairs={{0,2},{1,3},{2,0},{3,1},{4,6},{5,7},{6,4},{7,5},{8,10},{9,11},{10,... | collective-permute-start | bytes 786440 | tf_op jit(solution)/shard_map/ppermute | solution.py:635
  34.8 1.6 %collective-permute-start.1 = (bf16[288,128]{1,0:T(8,128)(2,1)S(1)}, bf16[288,128]{1,0:T(8,128)(2,1)S(1)}, u32[]{:S(2)}, u32[]{:S(2)}) collective-permute-start(bf16[288,128]{1,0:T(8,128)(2,1)S(1)} %broadcast_select_fusion), channel_id=1, source_target_pairs={{0,8},{4,12},{8,0},{12,4},{16,24},{20,28},{24,16},{28,20},{1,9},{5... | collective-permute-start | bytes 221192 | tf_op jit(solution)/shard_map/ppermute | solution.py:635
  37.9 3.5 %collective-permute-done.6 = s32[32]{0:T(128)S(1)} collective-permute-done((s32[32]{0:T(128)S(1)}, s32[32]{0:T(128)S(1)}, u32[]{:S(2)}, u32[]{:S(2)}) %collective-permute-start.6) | collective-permute-done | bytes 160 | tf_op jit(solution)/shard_map/ppermute | solution.py:635
  41.4 1.6 %collective-permute-start.10 = (bf16[28,96,128]{2,1,0:T(8,128)(2,1)}, bf16[28,96,128]{2,1,0:T(8,128)(2,1)}, u32[]{:S(2)}, u32[]{:S(2)}) collective-permute-start(bf16[28,96,128]{2,1,0:T(8,128)(2,1)} %copy-done.4), channel_id=1, source_target_pairs={{0,2},{1,3},{2,0},{3,1},{4,6},{5,7},{6,4},{7,5},{8,10},{9,11},{10,... | collective-permute-start | bytes 2064392 | tf_op jit(solution)/shard_map/ppermute | solution.py:635
  43.2 2.7 %collective-permute-start.4 = (bf16[288,128]{1,0:T(8,128)(2,1)S(1)}, bf16[288,128]{1,0:T(8,128)(2,1)S(1)}, u32[]{:S(2)}, u32[]{:S(2)}) collective-permute-start(bf16[288,128]{1,0:T(8,128)(2,1)S(1)} %broadcast_select_fusion.1), channel_id=1, source_target_pairs={{0,16},{4,20},{8,24},{12,28},{16,0},{20,4},{24,8},{28,12},{1,17},{... | collective-permute-start | bytes 221192 | tf_op jit(solution)/shard_map/ppermute | solution.py:635
  46.5 2.4 %routes.1 = (s32[4,33]{1,0:T(4,128)}, s32[8]{0:T(128)}) custom-call(s32[4,32]{1,0:T(4,128)} %fusion.4.spot), custom_call_target="tpu_custom_call" | custom-call | tf_op jit(solution)/shard_map/routes/pallas_call | solution.py:476
  50.2 12.6 %blend.1.refs_4_ = bf16[4,144,128]{2,1,0:T(8,128)(2,1)S(1)} custom-call(s32[1]{0:T(128)} %copy.12.cell, bf16[288,128]{1,0:T(8,128)(2,1)S(1)} %broadcast_select_fusion.2.strips, f32[816,1024]{1,0:T(8,128)S(1)} %get-tuple-element.87.state), custom_call_target="tpu_custom_call" | custom-call | flops 1000000 | bytes 10000 | tf_op jit(solution)/shard_map/blend/pallas_call | solution.py:451
  63.6 1.8 %gather_rows.3 = (f32[16,32,128]{2,1,0:T(8,128)S(1)}, bf16[16,32,128]{2,1,0:T(8,128)(2,1)S(1)}) custom-call(s32[4,33]{1,0:T(4,128)S(1)} %copy-done.12, s32[8]{0:T(128)S(1)} %copy-done.13, bf16[32,32,128]{2,1,0:T(8,128)(2,1)} %get-tuple-element.80.refs_0_, bf16[32,32,128]{2,1,0:T(8,128)(2,1)} %collective-permute-done.3.refs_1_, ...), custom_call_target="tpu_custom_call" | custom-call | flops 1000000 | bytes 10000 | tf_op jit(solution)/shard_map/gather_rows/pallas_call | solution.py:518
  66.1 3.0 %collective-permute-done.12.refs_6_ = bf16[4,144,128]{2,1,0:T(8,128)(2,1)S(1)} collective-permute-done((bf16[4,144,128]{2,1,0:T(8,128)(2,1)S(1)}, bf16[4,144,128]{2,1,0:T(8,128)(2,1)S(1)}, u32[]{:S(2)}, u32[]{:S(2)}) %collective-permute-start.12) | collective-permute-done | bytes 147488 | tf_op jit(solution)/shard_map/ppermute | solution.py:635
  69.1 2.0 %collective-permute-done.14.got = bf16[16,32,128]{2,1,0:T(8,128)(2,1)S(1)} collective-permute-done((bf16[16,32,128]{2,1,0:T(8,128)(2,1)S(1)}, bf16[16,32,128]{2,1,0:T(8,128)(2,1)S(1)}, u32[]{:S(2)}, u32[]{:S(2)}) %collective-permute-start.14) | collective-permute-done | bytes 131104 | tf_op jit(solution)/shard_map/ppermute | solution.py:635
  73.9 2.1 %gather_rows.4 = (f32[16,96,128]{2,1,0:T(8,128)S(1)}, bf16[16,96,128]{2,1,0:T(8,128)(2,1)S(1)}) custom-call(s32[4,33]{1,0:T(4,128)S(1)} %copy-done.12, s32[8]{0:T(128)S(1)} %copy-done.13, bf16[28,96,128]{2,1,0:T(8,128)(2,1)S(1)} %copy-done.5, bf16[28,96,128]{2,1,0:T(8,128)(2,1)} %collective-permute-done.11.refs_1_, ...), custom_call_target="tpu_custom_call" | custom-call | flops 1000000 | bytes 10000 | tf_op jit(solution)/shard_map/gather_rows/pallas_call | solution.py:518
  77.3 3.6 %collective-permute-start.18 = (bf16[4,32,128]{2,1,0:T(8,128)(2,1)S(1)}, bf16[4,32,128]{2,1,0:T(8,128)(2,1)S(1)}, u32[]{:S(2)}, u32[]{:S(2)}) collective-permute-start(bf16[4,32,128]{2,1,0:T(8,128)(2,1)S(1)} %get-tuple-element.112), channel_id=1, source_target_pairs={{0,16},{4,20},{8,24},{12,28},{16,0},{20,4},{24,8},{28,12},{1,17},{... | collective-permute-start | bytes 98312 | tf_op jit(solution)/shard_map/ppermute | solution.py:635
  81.6 1.6 %collective-permute-done.18.refs_2_ = bf16[4,32,128]{2,1,0:T(8,128)(2,1)S(1)} collective-permute-done((bf16[4,32,128]{2,1,0:T(8,128)(2,1)S(1)}, bf16[4,32,128]{2,1,0:T(8,128)(2,1)S(1)}, u32[]{:S(2)}, u32[]{:S(2)}) %collective-permute-start.18) | collective-permute-done | bytes 32800 | tf_op jit(solution)/shard_map/ppermute | solution.py:635
  83.2 3.4 %collective-permute-done.19.refs_3_ = bf16[4,32,128]{2,1,0:T(8,128)(2,1)S(1)} collective-permute-done((bf16[4,32,128]{2,1,0:T(8,128)(2,1)S(1)}, bf16[4,32,128]{2,1,0:T(8,128)(2,1)S(1)}, u32[]{:S(2)}, u32[]{:S(2)}) %collective-permute-start.19) | collective-permute-done | bytes 32800 | tf_op jit(solution)/shard_map/ppermute | solution.py:635
  91.3 2.1 %collective-permute-start.25 = (bf16[4,96,128]{2,1,0:T(8,128)(2,1)S(1)}, bf16[4,96,128]{2,1,0:T(8,128)(2,1)S(1)}, u32[]{:S(2)}, u32[]{:S(2)}) collective-permute-start(bf16[4,96,128]{2,1,0:T(8,128)(2,1)S(1)} %get-tuple-element.129), channel_id=1, source_target_pairs={{0,16},{4,20},{8,24},{12,28},{16,0},{20,4},{24,8},{28,12},{1,17},{... | collective-permute-start | bytes 294920 | tf_op jit(solution)/shard_map/ppermute | solution.py:635
  93.4 2.3 %collective-permute-start.26 = (bf16[4,96,128]{2,1,0:T(8,128)(2,1)S(1)}, bf16[4,96,128]{2,1,0:T(8,128)(2,1)S(1)}, u32[]{:S(2)}, u32[]{:S(2)}) collective-permute-start(bf16[4,96,128]{2,1,0:T(8,128)(2,1)S(1)} %get-tuple-element.130), channel_id=1, source_target_pairs={{0,24},{4,28},{8,16},{12,20},{16,8},{20,12},{24,0},{28,4},{1,25},{... | collective-permute-start | bytes 294920 | tf_op jit(solution)/shard_map/ppermute | solution.py:635
  97.0 5.1 %collective-permute-done.25.refs_6_ = bf16[4,96,128]{2,1,0:T(8,128)(2,1)S(1)} collective-permute-done((bf16[4,96,128]{2,1,0:T(8,128)(2,1)S(1)}, bf16[4,96,128]{2,1,0:T(8,128)(2,1)S(1)}, u32[]{:S(2)}, u32[]{:S(2)}) %collective-permute-start.25) | collective-permute-done | bytes 98336 | tf_op jit(solution)/shard_map/ppermute | solution.py:635
  102.1 1.7 %collective-permute-start.27 = (bf16[4,48,128]{2,1,0:T(8,128)(2,1)S(1)}, bf16[4,48,128]{2,1,0:T(8,128)(2,1)S(1)}, u32[]{:S(2)}, u32[]{:S(2)}) collective-permute-start(bf16[4,48,128]{2,1,0:T(8,128)(2,1)S(1)} %get-tuple-element.138), channel_id=1, source_target_pairs={{0,8},{4,12},{8,0},{12,4},{16,24},{20,28},{24,16},{28,20},{1,9},{5... | collective-permute-start | bytes 147464 | tf_op jit(solution)/shard_map/ppermute | solution.py:635
  104.2 2.4 %collective-permute-start.29 = (bf16[4,48,128]{2,1,0:T(8,128)(2,1)S(1)}, bf16[4,48,128]{2,1,0:T(8,128)(2,1)S(1)}, u32[]{:S(2)}, u32[]{:S(2)}) collective-permute-start(bf16[4,48,128]{2,1,0:T(8,128)(2,1)S(1)} %get-tuple-element.140), channel_id=1, source_target_pairs={{0,24},{4,28},{8,16},{12,20},{16,8},{20,12},{24,0},{28,4},{1,25},{... | collective-permute-start | bytes 147464 | tf_op jit(solution)/shard_map/ppermute | solution.py:635
  106.8 2.4 %collective-permute-done.28.refs_10_ = bf16[4,48,128]{2,1,0:T(8,128)(2,1)S(1)} collective-permute-done((bf16[4,48,128]{2,1,0:T(8,128)(2,1)S(1)}, bf16[4,48,128]{2,1,0:T(8,128)(2,1)S(1)}, u32[]{:S(2)}, u32[]{:S(2)}) %collective-permute-start.28) | collective-permute-done | bytes 49184 | tf_op jit(solution)/shard_map/ppermute | solution.py:635
  110.2 2.2 %collapse.1 = f32[3,4,4096]{2,1,0:T(4,128)} custom-call(bf16[192,1280]{1,0:T(8,128)(2,1)S(1)} %copy-done.7, f32[4,32,128]{2,1,0:T(8,128)S(1)} %get-tuple-element.114.refs_0_, bf16[4,32,128]{2,1,0:T(8,128)(2,1)S(1)} %collective-permute-done.17.refs_1_, bf16[4,32,128]{2,1,0:T(8,128)(2,1)S(1)} %collective-permute-done.18.refs_2_, ...), custom_call_target="tpu_custom_call" | custom-call | flops 1000000 | bytes 10000 | tf_op jit(solution)/shard_map/collapse/pallas_call | solution.py:622
  (86 shorter events, 27.0 us)
Async XLA Ops:
  5.5 27.8 %collective-permute-start = (bf16[288,128]{1,0:T(8,128)(2,1)S(1)}, bf16[288,128]{1,0:T(8,128)(2,1)S(1)}, u32[]{:S(2)}, u32[]{:S(2)}) collective-permute-start(bf16[288,128]{1,0:T(8,128)(2,1)S(1)} %strips.1), channel_id=1, source_target_pairs={{0,4},{4,0},{8,12},{12,8},{16,20},{20,16},{24,28},{28,24},{1,5},{5... | collective-permute-start | bytes 221192 | tf_op jit(solution)/shard_map/ppermute | solution.py:635
  33.3 8.1 %collective-permute-start.2 = (bf16[32,32,128]{2,1,0:T(8,128)(2,1)}, bf16[32,32,128]{2,1,0:T(8,128)(2,1)}, u32[]{:S(2)}, u32[]{:S(2)}) collective-permute-start(bf16[32,32,128]{2,1,0:T(8,128)(2,1)} %get-tuple-element.80.refs_0_), channel_id=1, source_target_pairs={{0,2},{1,3},{2,0},{3,1},{4,6},{5,7},{6,4},{7,5},{8,10},{9,11},{10,... | collective-permute-start | bytes 786440 | tf_op jit(solution)/shard_map/ppermute | solution.py:635
  34.8 6.6 %collective-permute-start.3 = (bf16[32,32,128]{2,1,0:T(8,128)(2,1)}, bf16[32,32,128]{2,1,0:T(8,128)(2,1)}, u32[]{:S(2)}, u32[]{:S(2)}) collective-permute-start(bf16[32,32,128]{2,1,0:T(8,128)(2,1)} %get-tuple-element.80.refs_0_), channel_id=1, source_target_pairs={{0,1},{1,0},{2,3},{3,2},{4,5},{5,4},{6,7},{7,6},{8,9},{9,8},{10,11... | collective-permute-start | bytes 786440 | tf_op jit(solution)/shard_map/ppermute | solution.py:635
  34.8 6.6 %collective-permute-start.1 = (bf16[288,128]{1,0:T(8,128)(2,1)S(1)}, bf16[288,128]{1,0:T(8,128)(2,1)S(1)}, u32[]{:S(2)}, u32[]{:S(2)}) collective-permute-start(bf16[288,128]{1,0:T(8,128)(2,1)S(1)} %broadcast_select_fusion), channel_id=1, source_target_pairs={{0,8},{4,12},{8,0},{12,4},{16,24},{20,28},{24,16},{28,20},{1,9},{5... | collective-permute-start | bytes 221192 | tf_op jit(solution)/shard_map/ppermute | solution.py:635
  36.4 4.9 %collective-permute-start.6 = (s32[32]{0:T(128)S(1)}, s32[32]{0:T(128)S(1)}, u32[]{:S(2)}, u32[]{:S(2)}) collective-permute-start(s32[32]{0:T(128)S(1)} %select_reduce_fusion), channel_id=1, source_target_pairs={{0,2},{1,3},{2,0},{3,1},{4,6},{5,7},{6,4},{7,5},{8,10},{9,11},{10,... | collective-permute-start | bytes 392 | tf_op jit(solution)/shard_map/ppermute | solution.py:635
  37.1 8.8 %collective-permute-start.5 = (s32[32]{0:T(128)S(1)}, s32[32]{0:T(128)S(1)}, u32[]{:S(2)}, u32[]{:S(2)}) collective-permute-start(s32[32]{0:T(128)S(1)} %select_reduce_fusion), channel_id=1, source_target_pairs={{0,1},{1,0},{2,3},{3,2},{4,5},{5,4},{6,7},{7,6},{8,9},{9,8},{10,11... | collective-permute-start | bytes 392 | tf_op jit(solution)/shard_map/ppermute | solution.py:635
  41.4 29.7 %collective-permute-start.10 = (bf16[28,96,128]{2,1,0:T(8,128)(2,1)}, bf16[28,96,128]{2,1,0:T(8,128)(2,1)}, u32[]{:S(2)}, u32[]{:S(2)}) collective-permute-start(bf16[28,96,128]{2,1,0:T(8,128)(2,1)} %copy-done.4), channel_id=1, source_target_pairs={{0,2},{1,3},{2,0},{3,1},{4,6},{5,7},{6,4},{7,5},{8,10},{9,11},{10,... | collective-permute-start | bytes 2064392 | tf_op jit(solution)/shard_map/ppermute | solution.py:635
  43.0 28.1 %collective-permute-start.11 = (bf16[28,96,128]{2,1,0:T(8,128)(2,1)}, bf16[28,96,128]{2,1,0:T(8,128)(2,1)}, u32[]{:S(2)}, u32[]{:S(2)}) collective-permute-start(bf16[28,96,128]{2,1,0:T(8,128)(2,1)} %copy-done.4), channel_id=1, source_target_pairs={{0,1},{1,0},{2,3},{3,2},{4,5},{5,4},{6,7},{7,6},{8,9},{9,8},{10,11... | collective-permute-start | bytes 2064392 | tf_op jit(solution)/shard_map/ppermute | solution.py:635
  43.2 7.0 %collective-permute-start.4 = (bf16[288,128]{1,0:T(8,128)(2,1)S(1)}, bf16[288,128]{1,0:T(8,128)(2,1)S(1)}, u32[]{:S(2)}, u32[]{:S(2)}) collective-permute-start(bf16[288,128]{1,0:T(8,128)(2,1)S(1)} %broadcast_select_fusion.1), channel_id=1, source_target_pairs={{0,16},{4,20},{8,24},{12,28},{16,0},{20,4},{24,8},{28,12},{1,17},{... | collective-permute-start | bytes 221192 | tf_op jit(solution)/shard_map/ppermute | solution.py:635
  45.9 17.8 %collective-permute-start.13 = (bf16[32,32,128]{2,1,0:T(8,128)(2,1)}, bf16[32,32,128]{2,1,0:T(8,128)(2,1)}, u32[]{:S(2)}, u32[]{:S(2)}) collective-permute-start(bf16[32,32,128]{2,1,0:T(8,128)(2,1)} %collective-permute-done.2.refs_2_), channel_id=1, source_target_pairs={{0,1},{1,0},{2,3},{3,2},{4,5},{5,4},{6,7},{7,6},{8,9},{9,8},{10,11... | collective-permute-start | bytes 786440 | tf_op jit(solution)/shard_map/ppermute | solution.py:635
  62.8 6.3 %collective-permute-start.12 = (bf16[4,144,128]{2,1,0:T(8,128)(2,1)S(1)}, bf16[4,144,128]{2,1,0:T(8,128)(2,1)S(1)}, u32[]{:S(2)}, u32[]{:S(2)}) collective-permute-start(bf16[4,144,128]{2,1,0:T(8,128)(2,1)S(1)} %blend.1.refs_4_), channel_id=1, source_target_pairs={{0,2},{1,3},{2,0},{3,1},{4,6},{5,7},{6,4},{7,5},{8,10},{9,11},{10,... | collective-permute-start | bytes 442376 | tf_op jit(solution)/shard_map/ppermute | solution.py:635
  65.4 5.7 %collective-permute-start.14 = (bf16[16,32,128]{2,1,0:T(8,128)(2,1)S(1)}, bf16[16,32,128]{2,1,0:T(8,128)(2,1)S(1)}, u32[]{:S(2)}, u32[]{:S(2)}) collective-permute-start(bf16[16,32,128]{2,1,0:T(8,128)(2,1)S(1)} %get-tuple-element.97), channel_id=1, source_target_pairs={{0,4},{4,0},{8,12},{12,8},{16,20},{20,16},{24,28},{28,24},{1,5},{5... | collective-permute-start | bytes 393224 | tf_op jit(solution)/shard_map/ppermute | solution.py:635
  71.1 10.5 %collective-permute-start.9 = (bf16[28,48,128]{2,1,0:T(8,128)(2,1)S(1)}, bf16[28,48,128]{2,1,0:T(8,128)(2,1)S(1)}, u32[]{:S(2)}, u32[]{:S(2)}) collective-permute-start(bf16[28,48,128]{2,1,0:T(8,128)(2,1)S(1)} %copy-done.9), channel_id=1, source_target_pairs={{0,2},{1,3},{2,0},{3,1},{4,6},{5,7},{6,4},{7,5},{8,10},{9,11},{10,... | collective-permute-start | bytes 1032200 | tf_op jit(solution)/shard_map/ppermute | solution.py:635
  76.0 11.3 %collective-permute-start.22 = (bf16[16,96,128]{2,1,0:T(8,128)(2,1)S(1)}, bf16[16,96,128]{2,1,0:T(8,128)(2,1)S(1)}, u32[]{:S(2)}, u32[]{:S(2)}) collective-permute-start(bf16[16,96,128]{2,1,0:T(8,128)(2,1)S(1)} %get-tuple-element.120), channel_id=1, source_target_pairs={{0,4},{4,0},{8,12},{12,8},{16,20},{20,16},{24,28},{28,24},{1,5},{5... | collective-permute-start | bytes 1179656 | tf_op jit(solution)/shard_map/ppermute | solution.py:635
  76.7 4.9 %collective-permute-start.17 = (bf16[4,32,128]{2,1,0:T(8,128)(2,1)S(1)}, bf16[4,32,128]{2,1,0:T(8,128)(2,1)S(1)}, u32[]{:S(2)}, u32[]{:S(2)}) collective-permute-start(bf16[4,32,128]{2,1,0:T(8,128)(2,1)S(1)} %get-tuple-element.111), channel_id=1, source_target_pairs={{0,8},{4,12},{8,0},{12,4},{16,24},{20,28},{24,16},{28,20},{1,9},{5... | collective-permute-start | bytes 98312 | tf_op jit(solution)/shard_map/ppermute | solution.py:635
  77.3 5.9 %collective-permute-start.18 = (bf16[4,32,128]{2,1,0:T(8,128)(2,1)S(1)}, bf16[4,32,128]{2,1,0:T(8,128)(2,1)S(1)}, u32[]{:S(2)}, u32[]{:S(2)}) collective-permute-start(bf16[4,32,128]{2,1,0:T(8,128)(2,1)S(1)} %get-tuple-element.112), channel_id=1, source_target_pairs={{0,16},{4,20},{8,24},{12,28},{16,0},{20,4},{24,8},{28,12},{1,17},{... | collective-permute-start | bytes 98312 | tf_op jit(solution)/shard_map/ppermute | solution.py:635
  80.9 5.7 %collective-permute-start.19 = (bf16[4,32,128]{2,1,0:T(8,128)(2,1)S(1)}, bf16[4,32,128]{2,1,0:T(8,128)(2,1)S(1)}, u32[]{:S(2)}, u32[]{:S(2)}) collective-permute-start(bf16[4,32,128]{2,1,0:T(8,128)(2,1)S(1)} %get-tuple-element.113), channel_id=1, source_target_pairs={{0,24},{4,28},{8,16},{12,20},{16,8},{20,12},{24,0},{28,4},{1,25},{... | collective-permute-start | bytes 98312 | tf_op jit(solution)/shard_map/ppermute | solution.py:635
  90.0 12.1 %collective-permute-start.23 = (bf16[16,48,128]{2,1,0:T(8,128)(2,1)S(1)}, bf16[16,48,128]{2,1,0:T(8,128)(2,1)S(1)}, u32[]{:S(2)}, u32[]{:S(2)}) collective-permute-start(bf16[16,48,128]{2,1,0:T(8,128)(2,1)S(1)} %get-tuple-element.126), channel_id=1, source_target_pairs={{0,4},{4,0},{8,12},{12,8},{16,20},{20,16},{24,28},{28,24},{1,5},{5... | collective-permute-start | bytes 589832 | tf_op jit(solution)/shard_map/ppermute | solution.py:635
  91.3 5.7 %collective-permute-start.24 = (bf16[4,96,128]{2,1,0:T(8,128)(2,1)S(1)}, bf16[4,96,128]{2,1,0:T(8,128)(2,1)S(1)}, u32[]{:S(2)}, u32[]{:S(2)}) collective-permute-start(bf16[4,96,128]{2,1,0:T(8,128)(2,1)S(1)} %get-tuple-element.128), channel_id=1, source_target_pairs={{0,8},{4,12},{8,0},{12,4},{16,24},{20,28},{24,16},{28,20},{1,9},{5... | collective-permute-start | bytes 294920 | tf_op jit(solution)/shard_map/ppermute | solution.py:635
  91.3 10.8 %collective-permute-start.25 = (bf16[4,96,128]{2,1,0:T(8,128)(2,1)S(1)}, bf16[4,96,128]{2,1,0:T(8,128)(2,1)S(1)}, u32[]{:S(2)}, u32[]{:S(2)}) collective-permute-start(bf16[4,96,128]{2,1,0:T(8,128)(2,1)S(1)} %get-tuple-element.129), channel_id=1, source_target_pairs={{0,16},{4,20},{8,24},{12,28},{16,0},{20,4},{24,8},{28,12},{1,17},{... | collective-permute-start | bytes 294920 | tf_op jit(solution)/shard_map/ppermute | solution.py:635
  93.4 8.7 %collective-permute-start.26 = (bf16[4,96,128]{2,1,0:T(8,128)(2,1)S(1)}, bf16[4,96,128]{2,1,0:T(8,128)(2,1)S(1)}, u32[]{:S(2)}, u32[]{:S(2)}) collective-permute-start(bf16[4,96,128]{2,1,0:T(8,128)(2,1)S(1)} %get-tuple-element.130), channel_id=1, source_target_pairs={{0,24},{4,28},{8,16},{12,20},{16,8},{20,12},{24,0},{28,4},{1,25},{... | collective-permute-start | bytes 294920 | tf_op jit(solution)/shard_map/ppermute | solution.py:635
  102.1 4.7 %collective-permute-start.27 = (bf16[4,48,128]{2,1,0:T(8,128)(2,1)S(1)}, bf16[4,48,128]{2,1,0:T(8,128)(2,1)S(1)}, u32[]{:S(2)}, u32[]{:S(2)}) collective-permute-start(bf16[4,48,128]{2,1,0:T(8,128)(2,1)S(1)} %get-tuple-element.138), channel_id=1, source_target_pairs={{0,8},{4,12},{8,0},{12,4},{16,24},{20,28},{24,16},{28,20},{1,9},{5... | collective-permute-start | bytes 147464 | tf_op jit(solution)/shard_map/ppermute | solution.py:635
  103.8 5.4 %collective-permute-start.28 = (bf16[4,48,128]{2,1,0:T(8,128)(2,1)S(1)}, bf16[4,48,128]{2,1,0:T(8,128)(2,1)S(1)}, u32[]{:S(2)}, u32[]{:S(2)}) collective-permute-start(bf16[4,48,128]{2,1,0:T(8,128)(2,1)S(1)} %get-tuple-element.139), channel_id=1, source_target_pairs={{0,16},{4,20},{8,24},{12,28},{16,0},{20,4},{24,8},{28,12},{1,17},{... | collective-permute-start | bytes 147464 | tf_op jit(solution)/shard_map/ppermute | solution.py:635
  104.2 6.0 %collective-permute-start.29 = (bf16[4,48,128]{2,1,0:T(8,128)(2,1)S(1)}, bf16[4,48,128]{2,1,0:T(8,128)(2,1)S(1)}, u32[]{:S(2)}, u32[]{:S(2)}) collective-permute-start(bf16[4,48,128]{2,1,0:T(8,128)(2,1)S(1)} %get-tuple-element.140), channel_id=1, source_target_pairs={{0,24},{4,28},{8,16},{12,20},{16,8},{20,12},{24,0},{28,4},{1,25},{... | collective-permute-start | bytes 147464 | tf_op jit(solution)/shard_map/ppermute | solution.py:635
  (22 other events, 140.4 us)

commit v5 on v3

--- a/solution.py
+++ b/solution.py
@@ -412,7 +412,7 @@
         in_specs=[pl.BlockSpec(memory_space=pltpu.SMEM)] + [vmem] * 2,
         out_shape=[jax.ShapeDtypeStruct((QB, 80, 128), BF16), jax.ShapeDtypeStruct((QB, 64, 128), BF16)],
         compiler_params=pltpu.CompilerParams(vmem_limit_bytes=VMEM),
-        cost_estimate=pl.CostEstimate(flops=4 * 10**9, bytes_accessed=4 * 10**6, transcendentals=0),
+        cost_estimate=pl.CostEstimate(flops=10**6, bytes_accessed=10**4, transcendentals=0),
         name="blend",
     )(cell, strips, state)
 
@@ -465,7 +465,7 @@
         out_shape=[jax.ShapeDtypeStruct(shape, F32), jax.ShapeDtypeStruct(shape, BF16)],
         scratch_shapes=[pltpu.VMEM((tiles, height, 128), F32)],
         compiler_params=pltpu.CompilerParams(vmem_limit_bytes=VMEM),
-        cost_estimate=pl.CostEstimate(flops=10**9, bytes_accessed=4 * 10**6, transcendentals=0),
+        cost_estimate=pl.CostEstimate(flops=10**6, bytes_accessed=10**4, transcendentals=0),
         name="gather_rows",
     )(*routes, *rows)
 
@@ -487,7 +487,7 @@
         add_kernel,
         out_shape=[jax.ShapeDtypeStruct(shape, F32)] + [jax.ShapeDtypeStruct(shape, BF16)] * others,
         compiler_params=pltpu.CompilerParams(vmem_limit_bytes=VMEM),
-        cost_estimate=pl.CostEstimate(flops=10**8, bytes_accessed=2 * 10**6, transcendentals=0),
+        cost_estimate=pl.CostEstimate(flops=10**6, bytes_accessed=10**4, transcendentals=0),
         name="add_halves",
     )(home, got)
 
@@ -568,7 +568,7 @@
         out_shape=jax.ShapeDtypeStruct((COLOURS, TILE_DEV, 4096), F32),
         scratch_shapes=[pltpu.VMEM((COLOURS * 128, 128), F32)],
         compiler_params=pltpu.CompilerParams(vmem_limit_bytes=VMEM),
-        cost_estimate=pl.CostEstimate(flops=10**9, bytes_accessed=3 * 10**6, transcendentals=0),
+        cost_estimate=pl.CostEstimate(flops=10**6, bytes_accessed=10**4, transcendentals=0),
         name="collapse",
     )(packed, *a, *b, *c)
     return jnp.swapaxes(tiles, 0, 1)
@@ -585,7 +585,9 @@
     mine = lax.axis_index("tiles")
     mask = lax.bitwise_xor(partner[0] // parts, lax.axis_index("frames"))
 
+    strips = strips_of(frames, strip_cell)
     ids = tile_group.reshape(QB) * (parts * TILE_DEV) + tile_position_in_group.reshape(QB)
+    strips, frames, ids = lax.optimization_barrier((strips, frames, ids))
     ids_core = swap(ids, "tiles", 1)
     ids_far = swap(ids, "tiles", 2)
     ids_far_core = swap(ids_far, "tiles", 1)
@@ -597,47 +599,42 @@
     spot = jnp.where(owner == mine, relative * TILE_DEV + ids % TILE_DEV, -1)
 
     routes = routes_of(spot)
-    strips = strips_of(frames, strip_cell)
-    strips, frames = lax.optimization_barrier((strips, frames))
+    tie = lax.optimization_barrier
     weights, state = bands_of(frames, weight_map, seam_mask)
     bit = 1
     while bit < groups:
         got = swap(strips, "frames", bit)
         if bit == 1:
-            got, weights, state = lax.optimization_barrier((got, weights, state))
+            got, weights, state = tie((got, weights, state))
+            far, near = swap(weights, "tiles", 2), swap(weights, "tiles", 1)
+        if bit == groups // 2:
+            got, routes, near = tie((got, routes, near))
         strips = jnp.where((mask & bit) != 0, got, strips)
         bit *= 2
 
-    tie = lax.optimization_barrier
-
     def gather(rows, near, far, far_near):
         return gather_rows(routes, (rows, near, far, far_near), groups * TILE_DEV)
 
     def along(own, *away):
         return [own] + [swap(part, "frames", 2 * (j + 1)) for j, part in enumerate(away)]
 
-    far = swap(weights, "tiles", 2)
-    home, away = gather(weights, swap(weights, "tiles", 1), far, swap(far, "tiles", 1))
-    home, away, strips = tie((home, away, strips))
     first, second = blend(strip_cell, strips, state)
-    far = swap(first, "tiles", 2)
-    near = swap(first, "tiles", 1)
+    far_first, near_first = swap(first, "tiles", 2), swap(first, "tiles", 1)
+    near_first, far, second = tie((near_first, far, second))
+    far_second, near_second = swap(second, "tiles", 2), swap(second, "tiles", 1)
+    home, away = gather(weights, near, far, swap(far, "tiles", 1))
     sums = add_halves(home, swap(away, "frames", 1))
-    far, near, sums, second = tie((far, near, sums, second))
+    far_first, sums = tie((far_first, sums))
     got_weights = along(*sums)
-    far_second = swap(second, "tiles", 2)
-    near_second = swap(second, "tiles", 1)
-    home, away = gather(first, near, far, swap(far, "tiles", 1))
+    home, away = gather(first, near_first, far_first, swap(far_first, "tiles", 1))
     got = swap(away, "frames", 1)
-    far_second, got, got_weights = tie((far_second, got, got_weights))
+    far_second, got = tie((far_second, got))
     far_near = swap(far_second, "tiles", 1)
     sums = add_halves(home, got)
-    far_near, sums = tie((far_near, sums))
+    far_near, sums, got_weights = tie((far_near, sums, got_weights))
     got_first = along(*sums)
     home, away = gather(second, near_second, far_second, far_near)
-    got = swap(away, "frames", 1)
-    got, got_first = tie((got, got_first))
-    got_second = along(*add_halves(home, got))
+    got_second = along(*add_halves(home, swap(away, "frames", 1)))
     return collapse(got_weights, got_first, got_second)
 
 

time: 93 us -> 95.3 us (1.025)
  starting transfers between devices: 27.6 us -> 30.8 us
  local copies, waits for them, and re-layouts: 6.08 us -> 3.58 us
  Pallas kernels: 16 us -> 17.1 us
    ppermute x27, starting transfers between devices: 27.6 us -> 30.8 us  [swap(): return lax.ppermute(value, axis, [(i, i ^ bit) for i in range(size)])]
    unnamed x28 -> x22, local copies, waits for them, and re-layouts: 6.08 us -> 3.58 us
    pallas_call x3, Pallas kernels: 3.34 us -> 4.41 us  [gather_rows(): pl.pallas_call(gather_kernel, in_specs=[pl.BlockSpec(memory_space=pltpu.S...]
where the time goes in v5:
time: 95.3 us; the launch traced here: 95.2 us
  waiting for transfers between devices  40.9 us (43%)
  starting transfers between devices  30.8 us (32%)
  Pallas kernels  17.1 us (18%)
  local copies, waits for them, and re-layouts  3.58 us (4%)
  between operations  1.51 us (2%)
  other arithmetic  1.32 us (1%)
    ppermute x27, waiting for transfers between devices, swap(): return lax.ppermute(value, axis, [(i, i ^ bit) for i in range(size)])  40.9 us
    ppermute x27, starting transfers between devices, swap(): return lax.ppermute(value, axis, [(i, i ^ bit) for i in range(size)])  30.8 us
    pallas_call x1, Pallas kernels, bands_of(): pl.pallas_call(functools.partial(bands_kernel, small_places, large_places...  4.68 us
    pallas_call x3, Pallas kernels, gather_rows(): pl.pallas_call(gather_kernel, in_specs=[pl.BlockSpec(memory_space=pltpu.S...  4.41 us
    unnamed x22, local copies, waits for them, and re-layouts  3.58 us
    pallas_call x1, Pallas kernels, routes_of(): pl.pallas_call(routes_kernel, in_specs=[smem], out_specs=[smem, smem], ou...  2.45 us
    pallas_call x1, Pallas kernels, collapse(): pl.pallas_call(functools.partial(collapse_kernel, places, len(a)), out_sh...  2.18 us
  transfers between devices with their start and end apart: 27, of which 14 were waited for; matrix products, arithmetic and copies ran while one was open for 1% of the time, Pallas kernels for 11%

profile of v5, /device:TPU:0, one launch (start us, length us, event | category | flops | bytes accessed | tf_op | source)
XLA Modules:
  0.0 95.2 jit_solution(17875818789930687055)
XLA Ops:
  3.5 1.9 %strips.1 = bf16[288,128]{1,0:T(8,128)(2,1)S(1)} custom-call(s32[1]{0:T(128)S(6)} %copy.12.cell, bf16[1,3,128,1024]{3,2,1,0:T(8,128)(2,1)S(1)} %copy-done.5, bf16[1,3,128,1024]{3,2,1,0:T(8,128)(2,1)S(1)} %copy-done.5, bf16[512,512]{1,0:T(8,128)(2,1)S(1)} %copy-done.9), custom_call_target="tpu_custom_call" | custom-call | flops 2000000000 | bytes 1000000 | tf_op jit(solution)/shard_map/strips/pallas_call | solution.py:247
  5.4 3.0 %collective-permute-start = (bf16[288,128]{1,0:T(8,128)(2,1)S(1)}, bf16[288,128]{1,0:T(8,128)(2,1)S(1)}, u32[]{:S(2)}, u32[]{:S(2)}) collective-permute-start(bf16[288,128]{1,0:T(8,128)(2,1)S(1)} %strips.1), channel_id=1, source_target_pairs={{0,4},{4,0},{8,12},{12,8},{16,20},{20,16},{24,28},{28,24},{1,5},{5... | collective-permute-start | bytes 221192 | tf_op jit(solution)/shard_map/ppermute | solution.py:579
  8.4 4.7 %bands.1 = (bf16[32,32,128]{2,1,0:T(8,128)(2,1)S(1)}, f32[816,1024]{1,0:T(8,128)S(1)}) custom-call(bf16[1,3,128,1024]{3,2,1,0:T(8,128)(2,1)S(1)} %copy-done.5, bf16[1,128,1024]{2,1,0:T(8,128)(2,1)S(1)} %copy-done.6, s32[1,64,128]{2,1,0:T(8,128)S(1)} %bitcast.15, bf16[512,512]{1,0:T(8,128)(2,1)S(1)} %copy-done.9, bf16[512,640]{1,0:T(8,128)(2,1)S(1)} %copy-done.8), custom_call_target="tpu_custom_call" | custom-call | flops 8000000000 | bytes 6000000 | tf_op jit(solution)/shard_map/bands/pallas_call | solution.py:339
  15.2 1.7 %collective-permute-start.1 = (bf16[288,128]{1,0:T(8,128)(2,1)S(1)}, bf16[288,128]{1,0:T(8,128)(2,1)}, u32[]{:S(2)}, u32[]{:S(2)}) collective-permute-start(bf16[288,128]{1,0:T(8,128)(2,1)S(1)} %broadcast_select_fusion), channel_id=1, source_target_pairs={{0,8},{4,12},{8,0},{12,4},{16,24},{20,28},{24,16},{28,20},{1,9},{5... | collective-permute-start | bytes 221192 | tf_op jit(solution)/shard_map/ppermute | solution.py:579
  16.8 2.4 %collective-permute-start.4 = (s32[32]{0:T(128)S(1)}, s32[32]{0:T(128)S(1)}, u32[]{:S(2)}, u32[]{:S(2)}) collective-permute-start(s32[32]{0:T(128)S(1)} %bitcast_add_fusion), channel_id=1, source_target_pairs={{0,2},{1,3},{2,0},{3,1},{4,6},{5,7},{6,4},{7,5},{8,10},{9,11},{10,... | collective-permute-start | bytes 392 | tf_op jit(solution)/shard_map/ppermute | solution.py:579
  19.2 1.5 %collective-permute-done.4 = s32[32]{0:T(128)S(1)} collective-permute-done((s32[32]{0:T(128)S(1)}, s32[32]{0:T(128)S(1)}, u32[]{:S(2)}, u32[]{:S(2)}) %collective-permute-start.4) | collective-permute-done | bytes 160 | tf_op jit(solution)/shard_map/ppermute | solution.py:579
  21.3 2.7 %collective-permute-start.2 = (bf16[288,128]{1,0:T(8,128)(2,1)S(1)}, bf16[288,128]{1,0:T(8,128)(2,1)S(1)}, u32[]{:S(2)}, u32[]{:S(2)}) collective-permute-start(bf16[288,128]{1,0:T(8,128)(2,1)S(1)} %broadcast_select_fusion.1), channel_id=1, source_target_pairs={{0,16},{4,20},{8,24},{12,28},{16,0},{20,4},{24,8},{28,12},{1,17},{... | collective-permute-start | bytes 221192 | tf_op jit(solution)/shard_map/ppermute | solution.py:579
  24.5 2.4 %routes.1 = (s32[4,33]{1,0:T(4,128)}, s32[4]{0:T(128)}) custom-call(s32[4,32]{1,0:T(4,128)} %fusion.4.spot), custom_call_target="tpu_custom_call" | custom-call | tf_op jit(solution)/shard_map/routes/pallas_call | solution.py:433
  29.3 3.0 %collective-permute-start.8 = (bf16[32,32,128]{2,1,0:T(8,128)(2,1)S(1)}, bf16[32,32,128]{2,1,0:T(8,128)(2,1)S(1)}, u32[]{:S(2)}, u32[]{:S(2)}) collective-permute-start(bf16[32,32,128]{2,1,0:T(8,128)(2,1)S(1)} %copy-done.2), channel_id=1, source_target_pairs={{0,2},{1,3},{2,0},{3,1},{4,6},{5,7},{6,4},{7,5},{8,10},{9,11},{10,... | collective-permute-start | bytes 786440 | tf_op jit(solution)/shard_map/ppermute | solution.py:579
  32.4 7.1 %collective-permute-done.8.c = bf16[32,32,128]{2,1,0:T(8,128)(2,1)S(1)} collective-permute-done((bf16[32,32,128]{2,1,0:T(8,128)(2,1)S(1)}, bf16[32,32,128]{2,1,0:T(8,128)(2,1)S(1)}, u32[]{:S(2)}, u32[]{:S(2)}) %collective-permute-start.8) | collective-permute-done | bytes 262176 | tf_op jit(solution)/shard_map/ppermute | solution.py:579
  39.5 1.5 %collective-permute-done.11.d = bf16[32,32,128]{2,1,0:T(8,128)(2,1)S(1)} collective-permute-done((bf16[32,32,128]{2,1,0:T(8,128)(2,1)S(1)}, bf16[32,32,128]{2,1,0:T(8,128)(2,1)S(1)}, u32[]{:S(2)}, u32[]{:S(2)}) %collective-permute-start.11) | collective-permute-done | bytes 262176 | tf_op jit(solution)/shard_map/ppermute | solution.py:579
  41.0 1.6 %gather_rows.3 = (f32[16,32,128]{2,1,0:T(8,128)S(1)}, bf16[16,32,128]{2,1,0:T(8,128)(2,1)S(1)}) custom-call(s32[4,33]{1,0:T(4,128)S(1)} %copy-done.3, s32[4]{0:T(128)S(1)} %copy-done.4, bf16[32,32,128]{2,1,0:T(8,128)(2,1)S(1)} %copy-done.2, bf16[32,32,128]{2,1,0:T(8,128)(2,1)} %collective-permute-done.6.b, ...), custom_call_target="tpu_custom_call" | custom-call | flops 1000000 | bytes 10000 | tf_op jit(solution)/shard_map/gather_rows/pallas_call | solution.py:462
  43.3 4.8 %collective-permute-done.12.got = bf16[16,32,128]{2,1,0:T(8,128)(2,1)S(1)} collective-permute-done((bf16[16,32,128]{2,1,0:T(8,128)(2,1)S(1)}, bf16[16,32,128]{2,1,0:T(8,128)(2,1)S(1)}, u32[]{:S(2)}, u32[]{:S(2)}) %collective-permute-start.12) | collective-permute-done | bytes 131104 | tf_op jit(solution)/shard_map/ppermute | solution.py:579
  48.2 5.0 %collective-permute-done.10.c = bf16[32,80,128]{2,1,0:T(8,128)(2,1)S(1)} collective-permute-done((bf16[32,80,128]{2,1,0:T(8,128)(2,1)S(1)}, bf16[32,80,128]{2,1,0:T(8,128)(2,1)S(1)}, u32[]{:S(2)}, u32[]{:S(2)}) %collective-permute-start.10) | collective-permute-done | bytes 655392 | tf_op jit(solution)/shard_map/ppermute | solution.py:579
  53.3 1.8 %collective-permute-start.9 = (bf16[32,64,128]{2,1,0:T(8,128)(2,1)S(1)}, bf16[32,64,128]{2,1,0:T(8,128)(2,1)S(1)}, u32[]{:S(2)}, u32[]{:S(2)}) collective-permute-start(bf16[32,64,128]{2,1,0:T(8,128)(2,1)S(1)} %get-tuple-element.71.a), channel_id=1, source_target_pairs={{0,2},{1,3},{2,0},{3,1},{4,6},{5,7},{6,4},{7,5},{8,10},{9,11},{10,... | collective-permute-start | bytes 1572872 | tf_op jit(solution)/shard_map/ppermute | solution.py:579
  57.4 10.2 %collective-permute-done.9.c = bf16[32,64,128]{2,1,0:T(8,128)(2,1)S(1)} collective-permute-done((bf16[32,64,128]{2,1,0:T(8,128)(2,1)S(1)}, bf16[32,64,128]{2,1,0:T(8,128)(2,1)S(1)}, u32[]{:S(2)}, u32[]{:S(2)}) %collective-permute-start.9) | collective-permute-done | bytes 524320 | tf_op jit(solution)/shard_map/ppermute | solution.py:579
  68.1 3.1 %collective-permute-start.17 = (bf16[4,32,128]{2,1,0:T(8,128)(2,1)S(1)}, bf16[4,32,128]{2,1,0:T(8,128)(2,1)S(1)}, u32[]{:S(2)}, u32[]{:S(2)}) collective-permute-start(bf16[4,32,128]{2,1,0:T(8,128)(2,1)S(1)} %get-tuple-element.94), channel_id=1, source_target_pairs={{0,16},{4,20},{8,24},{12,28},{16,0},{20,4},{24,8},{28,12},{1,17},{... | collective-permute-start | bytes 98312 | tf_op jit(solution)/shard_map/ppermute | solution.py:579
  73.9 3.1 %collective-permute-done.18.refs_3_ = bf16[4,32,128]{2,1,0:T(8,128)(2,1)S(1)} collective-permute-done((bf16[4,32,128]{2,1,0:T(8,128)(2,1)S(1)}, bf16[4,32,128]{2,1,0:T(8,128)(2,1)S(1)}, u32[]{:S(2)}, u32[]{:S(2)}) %collective-permute-start.18) | collective-permute-done | bytes 32800 | tf_op jit(solution)/shard_map/ppermute | solution.py:579
  79.0 1.7 %collective-permute-start.20 = (bf16[4,80,128]{2,1,0:T(8,128)(2,1)S(1)}, bf16[4,80,128]{2,1,0:T(8,128)(2,1)S(1)}, u32[]{:S(2)}, u32[]{:S(2)}) collective-permute-start(bf16[4,80,128]{2,1,0:T(8,128)(2,1)S(1)} %get-tuple-element.102), channel_id=1, source_target_pairs={{0,16},{4,20},{8,24},{12,28},{16,0},{20,4},{24,8},{28,12},{1,17},{... | collective-permute-start | bytes 245768 | tf_op jit(solution)/shard_map/ppermute | solution.py:579
  80.7 2.7 %collective-permute-start.21 = (bf16[4,80,128]{2,1,0:T(8,128)(2,1)S(1)}, bf16[4,80,128]{2,1,0:T(8,128)(2,1)S(1)}, u32[]{:S(2)}, u32[]{:S(2)}) collective-permute-start(bf16[4,80,128]{2,1,0:T(8,128)(2,1)S(1)} %get-tuple-element.103), channel_id=1, source_target_pairs={{0,24},{4,28},{8,16},{12,20},{16,8},{20,12},{24,0},{28,4},{1,25},{... | collective-permute-start | bytes 245768 | tf_op jit(solution)/shard_map/ppermute | solution.py:579
  84.9 1.9 %collective-permute-start.25 = (bf16[4,64,128]{2,1,0:T(8,128)(2,1)S(1)}, bf16[4,64,128]{2,1,0:T(8,128)(2,1)S(1)}, u32[]{:S(2)}, u32[]{:S(2)}) collective-permute-start(bf16[4,64,128]{2,1,0:T(8,128)(2,1)S(1)} %get-tuple-element.109), channel_id=1, source_target_pairs={{0,16},{4,20},{8,24},{12,28},{16,0},{20,4},{24,8},{28,12},{1,17},{... | collective-permute-start | bytes 196616 | tf_op jit(solution)/shard_map/ppermute | solution.py:579
  86.8 2.5 %collective-permute-start.26 = (bf16[4,64,128]{2,1,0:T(8,128)(2,1)S(1)}, bf16[4,64,128]{2,1,0:T(8,128)(2,1)S(1)}, u32[]{:S(2)}, u32[]{:S(2)}) collective-permute-start(bf16[4,64,128]{2,1,0:T(8,128)(2,1)S(1)} %get-tuple-element.110), channel_id=1, source_target_pairs={{0,24},{4,28},{8,16},{12,20},{16,8},{20,12},{24,0},{28,4},{1,25},{... | collective-permute-start | bytes 196616 | tf_op jit(solution)/shard_map/ppermute | solution.py:579
  90.3 1.6 %collective-permute-done.25.refs_10_ = bf16[4,64,128]{2,1,0:T(8,128)(2,1)S(1)} collective-permute-done((bf16[4,64,128]{2,1,0:T(8,128)(2,1)S(1)}, bf16[4,64,128]{2,1,0:T(8,128)(2,1)S(1)}, u32[]{:S(2)}, u32[]{:S(2)}) %collective-permute-start.25) | collective-permute-done | bytes 65568 | tf_op jit(solution)/shard_map/ppermute | solution.py:579
  93.0 2.2 %collapse.1 = f32[3,4,4096]{2,1,0:T(4,128)} custom-call(bf16[192,1280]{1,0:T(8,128)(2,1)S(1)} %copy-done, f32[4,32,128]{2,1,0:T(8,128)S(1)} %get-tuple-element.96.refs_0_, bf16[4,32,128]{2,1,0:T(8,128)(2,1)S(1)} %collective-permute-done.16.refs_1_, bf16[4,32,128]{2,1,0:T(8,128)(2,1)S(1)} %collective-permute-done.17.refs_2_, ...), custom_call_target="tpu_custom_call" | custom-call | flops 1000000 | bytes 10000 | tf_op jit(solution)/shard_map/collapse/pallas_call | solution.py:566
  (68 shorter events, 19.5 us)
Async XLA Ops:
  5.4 9.2 %collective-permute-start = (bf16[288,128]{1,0:T(8,128)(2,1)S(1)}, bf16[288,128]{1,0:T(8,128)(2,1)S(1)}, u32[]{:S(2)}, u32[]{:S(2)}) collective-permute-start(bf16[288,128]{1,0:T(8,128)(2,1)S(1)} %strips.1), channel_id=1, source_target_pairs={{0,4},{4,0},{8,12},{12,8},{16,20},{20,16},{24,28},{28,24},{1,5},{5... | collective-permute-start | bytes 221192 | tf_op jit(solution)/shard_map/ppermute | solution.py:579
  15.2 6.1 %collective-permute-start.1 = (bf16[288,128]{1,0:T(8,128)(2,1)S(1)}, bf16[288,128]{1,0:T(8,128)(2,1)}, u32[]{:S(2)}, u32[]{:S(2)}) collective-permute-start(bf16[288,128]{1,0:T(8,128)(2,1)S(1)} %broadcast_select_fusion), channel_id=1, source_target_pairs={{0,8},{4,12},{8,0},{12,4},{16,24},{20,28},{24,16},{28,20},{1,9},{5... | collective-permute-start | bytes 221192 | tf_op jit(solution)/shard_map/ppermute | solution.py:579
  16.8 3.9 %collective-permute-start.4 = (s32[32]{0:T(128)S(1)}, s32[32]{0:T(128)S(1)}, u32[]{:S(2)}, u32[]{:S(2)}) collective-permute-start(s32[32]{0:T(128)S(1)} %bitcast_add_fusion), channel_id=1, source_target_pairs={{0,2},{1,3},{2,0},{3,1},{4,6},{5,7},{6,4},{7,5},{8,10},{9,11},{10,... | collective-permute-start | bytes 392 | tf_op jit(solution)/shard_map/ppermute | solution.py:579
  19.2 4.7 %collective-permute-start.3 = (s32[32]{0:T(128)S(1)}, s32[32]{0:T(128)S(1)}, u32[]{:S(2)}, u32[]{:S(2)}) collective-permute-start(s32[32]{0:T(128)S(1)} %bitcast_add_fusion), channel_id=1, source_target_pairs={{0,1},{1,0},{2,3},{3,2},{4,5},{5,4},{6,7},{7,6},{8,9},{9,8},{10,11... | collective-permute-start | bytes 392 | tf_op jit(solution)/shard_map/ppermute | solution.py:579
  20.7 7.1 %collective-permute-start.6 = (bf16[32,32,128]{2,1,0:T(8,128)(2,1)}, bf16[32,32,128]{2,1,0:T(8,128)(2,1)}, u32[]{:S(2)}, u32[]{:S(2)}) collective-permute-start(bf16[32,32,128]{2,1,0:T(8,128)(2,1)} %copy-done.1), channel_id=1, source_target_pairs={{0,1},{1,0},{2,3},{3,2},{4,5},{5,4},{6,7},{7,6},{8,9},{9,8},{10,11... | collective-permute-start | bytes 786440 | tf_op jit(solution)/shard_map/ppermute | solution.py:579
  21.3 6.6 %collective-permute-start.2 = (bf16[288,128]{1,0:T(8,128)(2,1)S(1)}, bf16[288,128]{1,0:T(8,128)(2,1)S(1)}, u32[]{:S(2)}, u32[]{:S(2)}) collective-permute-start(bf16[288,128]{1,0:T(8,128)(2,1)S(1)} %broadcast_select_fusion.1), channel_id=1, source_target_pairs={{0,16},{4,20},{8,24},{12,28},{16,0},{20,4},{24,8},{28,12},{1,17},{... | collective-permute-start | bytes 221192 | tf_op jit(solution)/shard_map/ppermute | solution.py:579
  29.3 10.2 %collective-permute-start.7 = (bf16[32,80,128]{2,1,0:T(8,128)(2,1)S(1)}, bf16[32,80,128]{2,1,0:T(8,128)(2,1)S(1)}, u32[]{:S(2)}, u32[]{:S(2)}) collective-permute-start(bf16[32,80,128]{2,1,0:T(8,128)(2,1)S(1)} %get-tuple-element.69.a), channel_id=1, source_target_pairs={{0,1},{1,0},{2,3},{3,2},{4,5},{5,4},{6,7},{7,6},{8,9},{9,8},{10,11... | collective-permute-start | bytes 1966088 | tf_op jit(solution)/shard_map/ppermute | solution.py:579
  29.3 10.1 %collective-permute-start.8 = (bf16[32,32,128]{2,1,0:T(8,128)(2,1)S(1)}, bf16[32,32,128]{2,1,0:T(8,128)(2,1)S(1)}, u32[]{:S(2)}, u32[]{:S(2)}) collective-permute-start(bf16[32,32,128]{2,1,0:T(8,128)(2,1)S(1)} %copy-done.2), channel_id=1, source_target_pairs={{0,2},{1,3},{2,0},{3,1},{4,6},{5,7},{6,4},{7,5},{8,10},{9,11},{10,... | collective-permute-start | bytes 786440 | tf_op jit(solution)/shard_map/ppermute | solution.py:579
  32.3 20.9 %collective-permute-start.10 = (bf16[32,80,128]{2,1,0:T(8,128)(2,1)S(1)}, bf16[32,80,128]{2,1,0:T(8,128)(2,1)S(1)}, u32[]{:S(2)}, u32[]{:S(2)}) collective-permute-start(bf16[32,80,128]{2,1,0:T(8,128)(2,1)S(1)} %get-tuple-element.69.a), channel_id=1, source_target_pairs={{0,2},{1,3},{2,0},{3,1},{4,6},{5,7},{6,4},{7,5},{8,10},{9,11},{10,... | collective-permute-start | bytes 1966088 | tf_op jit(solution)/shard_map/ppermute | solution.py:579
  42.7 5.5 %collective-permute-start.12 = (bf16[16,32,128]{2,1,0:T(8,128)(2,1)S(1)}, bf16[16,32,128]{2,1,0:T(8,128)(2,1)S(1)}, u32[]{:S(2)}, u32[]{:S(2)}) collective-permute-start(bf16[16,32,128]{2,1,0:T(8,128)(2,1)S(1)} %get-tuple-element.78), channel_id=1, source_target_pairs={{0,4},{4,0},{8,12},{12,8},{16,20},{20,16},{24,28},{28,24},{1,5},{5... | collective-permute-start | bytes 393224 | tf_op jit(solution)/shard_map/ppermute | solution.py:579
  53.3 14.4 %collective-permute-start.9 = (bf16[32,64,128]{2,1,0:T(8,128)(2,1)S(1)}, bf16[32,64,128]{2,1,0:T(8,128)(2,1)S(1)}, u32[]{:S(2)}, u32[]{:S(2)}) collective-permute-start(bf16[32,64,128]{2,1,0:T(8,128)(2,1)S(1)} %get-tuple-element.71.a), channel_id=1, source_target_pairs={{0,2},{1,3},{2,0},{3,1},{4,6},{5,7},{6,4},{7,5},{8,10},{9,11},{10,... | collective-permute-start | bytes 1572872 | tf_op jit(solution)/shard_map/ppermute | solution.py:579
  56.8 10.8 %collective-permute-start.14 = (bf16[16,80,128]{2,1,0:T(8,128)(2,1)S(1)}, bf16[16,80,128]{2,1,0:T(8,128)(2,1)S(1)}, u32[]{:S(2)}, u32[]{:S(2)}) collective-permute-start(bf16[16,80,128]{2,1,0:T(8,128)(2,1)S(1)} %get-tuple-element.84), channel_id=1, source_target_pairs={{0,4},{4,0},{8,12},{12,8},{16,20},{20,16},{24,28},{28,24},{1,5},{5... | collective-permute-start | bytes 983048 | tf_op jit(solution)/shard_map/ppermute | solution.py:579
  67.6 9.4 %collective-permute-start.15 = (bf16[32,64,128]{2,1,0:T(8,128)(2,1)S(1)}, bf16[32,64,128]{2,1,0:T(8,128)(2,1)S(1)}, u32[]{:S(2)}, u32[]{:S(2)}) collective-permute-start(bf16[32,64,128]{2,1,0:T(8,128)(2,1)S(1)} %collective-permute-done.9.c), channel_id=1, source_target_pairs={{0,1},{1,0},{2,3},{3,2},{4,5},{5,4},{6,7},{7,6},{8,9},{9,8},{10,11... | collective-permute-start | bytes 1572872 | tf_op jit(solution)/shard_map/ppermute | solution.py:579
  67.6 9.4 %collective-permute-start.22 = (bf16[32,64,128]{2,1,0:T(8,128)(2,1)S(1)}, bf16[32,64,128]{2,1,0:T(8,128)(2,1)S(1)}, u32[]{:S(2)}, u32[]{:S(2)}) collective-permute-start(bf16[32,64,128]{2,1,0:T(8,128)(2,1)S(1)} %get-tuple-element.71.a), channel_id=1, source_target_pairs={{0,1},{1,0},{2,3},{3,2},{4,5},{5,4},{6,7},{7,6},{8,9},{9,8},{10,11... | collective-permute-start | bytes 1572872 | tf_op jit(solution)/shard_map/ppermute | solution.py:579
  68.1 4.5 %collective-permute-start.16 = (bf16[4,32,128]{2,1,0:T(8,128)(2,1)S(1)}, bf16[4,32,128]{2,1,0:T(8,128)(2,1)S(1)}, u32[]{:S(2)}, u32[]{:S(2)}) collective-permute-start(bf16[4,32,128]{2,1,0:T(8,128)(2,1)S(1)} %get-tuple-element.93), channel_id=1, source_target_pairs={{0,8},{4,12},{8,0},{12,4},{16,24},{20,28},{24,16},{28,20},{1,9},{5... | collective-permute-start | bytes 98312 | tf_op jit(solution)/shard_map/ppermute | solution.py:579
  68.1 5.7 %collective-permute-start.17 = (bf16[4,32,128]{2,1,0:T(8,128)(2,1)S(1)}, bf16[4,32,128]{2,1,0:T(8,128)(2,1)S(1)}, u32[]{:S(2)}, u32[]{:S(2)}) collective-permute-start(bf16[4,32,128]{2,1,0:T(8,128)(2,1)S(1)} %get-tuple-element.94), channel_id=1, source_target_pairs={{0,16},{4,20},{8,24},{12,28},{16,0},{20,4},{24,8},{28,12},{1,17},{... | collective-permute-start | bytes 98312 | tf_op jit(solution)/shard_map/ppermute | solution.py:579
  71.3 5.7 %collective-permute-start.18 = (bf16[4,32,128]{2,1,0:T(8,128)(2,1)S(1)}, bf16[4,32,128]{2,1,0:T(8,128)(2,1)S(1)}, u32[]{:S(2)}, u32[]{:S(2)}) collective-permute-start(bf16[4,32,128]{2,1,0:T(8,128)(2,1)S(1)} %get-tuple-element.95), channel_id=1, source_target_pairs={{0,24},{4,28},{8,16},{12,20},{16,8},{20,12},{24,0},{28,4},{1,25},{... | collective-permute-start | bytes 98312 | tf_op jit(solution)/shard_map/ppermute | solution.py:579
  78.4 6.4 %collective-permute-start.23 = (bf16[16,64,128]{2,1,0:T(8,128)(2,1)S(1)}, bf16[16,64,128]{2,1,0:T(8,128)(2,1)S(1)}, u32[]{:S(2)}, u32[]{:S(2)}) collective-permute-start(bf16[16,64,128]{2,1,0:T(8,128)(2,1)S(1)} %get-tuple-element.106), channel_id=1, source_target_pairs={{0,4},{4,0},{8,12},{12,8},{16,20},{20,16},{24,28},{28,24},{1,5},{5... | collective-permute-start | bytes 786440 | tf_op jit(solution)/shard_map/ppermute | solution.py:579
  79.0 7.8 %collective-permute-start.19 = (bf16[4,80,128]{2,1,0:T(8,128)(2,1)S(1)}, bf16[4,80,128]{2,1,0:T(8,128)(2,1)S(1)}, u32[]{:S(2)}, u32[]{:S(2)}) collective-permute-start(bf16[4,80,128]{2,1,0:T(8,128)(2,1)S(1)} %get-tuple-element.101), channel_id=1, source_target_pairs={{0,8},{4,12},{8,0},{12,4},{16,24},{20,28},{24,16},{28,20},{1,9},{5... | collective-permute-start | bytes 245768 | tf_op jit(solution)/shard_map/ppermute | solution.py:579
  79.0 10.3 %collective-permute-start.20 = (bf16[4,80,128]{2,1,0:T(8,128)(2,1)S(1)}, bf16[4,80,128]{2,1,0:T(8,128)(2,1)S(1)}, u32[]{:S(2)}, u32[]{:S(2)}) collective-permute-start(bf16[4,80,128]{2,1,0:T(8,128)(2,1)S(1)} %get-tuple-element.102), channel_id=1, source_target_pairs={{0,16},{4,20},{8,24},{12,28},{16,0},{20,4},{24,8},{28,12},{1,17},{... | collective-permute-start | bytes 245768 | tf_op jit(solution)/shard_map/ppermute | solution.py:579
  80.7 8.6 %collective-permute-start.21 = (bf16[4,80,128]{2,1,0:T(8,128)(2,1)S(1)}, bf16[4,80,128]{2,1,0:T(8,128)(2,1)S(1)}, u32[]{:S(2)}, u32[]{:S(2)}) collective-permute-start(bf16[4,80,128]{2,1,0:T(8,128)(2,1)S(1)} %get-tuple-element.103), channel_id=1, source_target_pairs={{0,24},{4,28},{8,16},{12,20},{16,8},{20,12},{24,0},{28,4},{1,25},{... | collective-permute-start | bytes 245768 | tf_op jit(solution)/shard_map/ppermute | solution.py:579
  84.8 5.5 %collective-permute-start.24 = (bf16[4,64,128]{2,1,0:T(8,128)(2,1)S(1)}, bf16[4,64,128]{2,1,0:T(8,128)(2,1)S(1)}, u32[]{:S(2)}, u32[]{:S(2)}) collective-permute-start(bf16[4,64,128]{2,1,0:T(8,128)(2,1)S(1)} %get-tuple-element.108), channel_id=1, source_target_pairs={{0,8},{4,12},{8,0},{12,4},{16,24},{20,28},{24,16},{28,20},{1,9},{5... | collective-permute-start | bytes 196616 | tf_op jit(solution)/shard_map/ppermute | solution.py:579
  84.9 7.0 %collective-permute-start.25 = (bf16[4,64,128]{2,1,0:T(8,128)(2,1)S(1)}, bf16[4,64,128]{2,1,0:T(8,128)(2,1)S(1)}, u32[]{:S(2)}, u32[]{:S(2)}) collective-permute-start(bf16[4,64,128]{2,1,0:T(8,128)(2,1)S(1)} %get-tuple-element.109), channel_id=1, source_target_pairs={{0,16},{4,20},{8,24},{12,28},{16,0},{20,4},{24,8},{28,12},{1,17},{... | collective-permute-start | bytes 196616 | tf_op jit(solution)/shard_map/ppermute | solution.py:579
  86.8 6.2 %collective-permute-start.26 = (bf16[4,64,128]{2,1,0:T(8,128)(2,1)S(1)}, bf16[4,64,128]{2,1,0:T(8,128)(2,1)S(1)}, u32[]{:S(2)}, u32[]{:S(2)}) collective-permute-start(bf16[4,64,128]{2,1,0:T(8,128)(2,1)S(1)} %get-tuple-element.110), channel_id=1, source_target_pairs={{0,24},{4,28},{8,16},{12,20},{16,8},{20,12},{24,0},{28,4},{1,25},{... | collective-permute-start | bytes 196616 | tf_op jit(solution)/shard_map/ppermute | solution.py:579
  (14 other events, 100.3 us)

commit v6 on v5

--- a/solution.py
+++ b/solution.py
@@ -585,21 +585,26 @@
     mine = lax.axis_index("tiles")
     mask = lax.bitwise_xor(partner[0] // parts, lax.axis_index("frames"))
 
+    tie = lax.optimization_barrier
     strips = strips_of(frames, strip_cell)
     ids = tile_group.reshape(QB) * (parts * TILE_DEV) + tile_position_in_group.reshape(QB)
-    strips, frames, ids = lax.optimization_barrier((strips, frames, ids))
-    ids_core = swap(ids, "tiles", 1)
-    ids_far = swap(ids, "tiles", 2)
-    ids_far_core = swap(ids_far, "tiles", 1)
-    ids = jnp.stack([ids, ids_core, ids_far, ids_far_core])
-    group_size = parts * TILE_DEV
-    owner = ids % group_size // TILE_DEV
-    relative = lax.bitwise_xor(ids // group_size, lax.axis_index("frames"))
-    relative = (relative & 1) * (groups // 2) + (relative >> 1)
-    spot = jnp.where(owner == mine, relative * TILE_DEV + ids % TILE_DEV, -1)
-
-    routes = routes_of(spot)
-    tie = lax.optimization_barrier
+    strips, frames, ids = tie((strips, frames, ids))
+    ids = jnp.stack([ids, swap(ids, "tiles", 1)])
+    ids_x = jnp.concatenate([ids, swap(ids, "tiles", 2)])
+    ids_y = jnp.concatenate([ids, swap(ids, "frames", 1)])
+
+    def relative(ids):
+        group, tile = ids // (parts * TILE_DEV), ids % (parts * TILE_DEV)
+        group = lax.bitwise_xor(group, lax.axis_index("frames"))
+        return group, lax.bitwise_xor(tile // TILE_DEV, mine), tile % TILE_DEV
+
+    half = groups // 2
+    group, part, tile = relative(ids_x)
+    spot_x = jnp.where(part == 0, ((group & 1) * half + (group >> 1)) * TILE_DEV + tile, -1)
+    group, part, tile = relative(ids_y)
+    here = ((group & 1) == 0) & ((part & 1) == 0)
+    spot_y = jnp.where(here, ((part >> 1) * half + (group >> 1)) * TILE_DEV + tile, -1)
+
     weights, state = bands_of(frames, weight_map, seam_mask)
     bit = 1
     while bit < groups:
@@ -607,34 +612,40 @@
         if bit == 1:
             got, weights, state = tie((got, weights, state))
             far, near = swap(weights, "tiles", 2), swap(weights, "tiles", 1)
-        if bit == groups // 2:
-            got, routes, near = tie((got, routes, near))
+        if bit == 2:
+            got, far, near = tie((got, far, near))
+        if bit == half:
+            got, spot_x, spot_y = tie((got, spot_x, spot_y))
         strips = jnp.where((mask & bit) != 0, got, strips)
         bit *= 2
 
-    def gather(rows, near, far, far_near):
-        return gather_rows(routes, (rows, near, far, far_near), groups * TILE_DEV)
+    def gather(routes, *rows):
+        return gather_rows(routes, rows, groups * TILE_DEV)
 
     def along(own, *away):
         return [own] + [swap(part, "frames", 2 * (j + 1)) for j, part in enumerate(away)]
 
     first, second = blend(strip_cell, strips, state)
+    first, second, spot_x, spot_y, far = tie((first, second, spot_x, spot_y, far))
     far_first, near_first = swap(first, "tiles", 2), swap(first, "tiles", 1)
-    near_first, far, second = tie((near_first, far, second))
-    far_second, near_second = swap(second, "tiles", 2), swap(second, "tiles", 1)
-    home, away = gather(weights, near, far, swap(far, "tiles", 1))
-    sums = add_halves(home, swap(away, "frames", 1))
-    far_first, sums = tie((far_first, sums))
-    got_weights = along(*sums)
-    home, away = gather(first, near_first, far_first, swap(far_first, "tiles", 1))
-    got = swap(away, "frames", 1)
-    far_second, got = tie((far_second, got))
-    far_near = swap(far_second, "tiles", 1)
-    sums = add_halves(home, got)
-    far_near, sums, got_weights = tie((far_near, sums, got_weights))
-    got_first = along(*sums)
-    home, away = gather(second, near_second, far_second, far_near)
-    got_second = along(*add_halves(home, swap(away, "frames", 1)))
+    far_second, near_second = swap(second, "frames", 1), swap(second, "tiles", 1)
+    routes_x, routes_y = routes_of(spot_x), routes_of(spot_y)
+    home_w, away_w = gather(routes_x, weights, near, far, swap(far, "tiles", 1))
+    got_w = swap(away_w, "frames", 1)
+    far_second, home_w, routes_y = tie((far_second, home_w, routes_y))
+    home_s, away_s = gather(routes_y, second, near_second, far_second, swap(far_second, "tiles", 1))
+    got_s = swap(away_s, "tiles", 2)
+    far_first, home_s, got_w = tie((far_first, home_s, got_w))
+    far_near = swap(far_first, "tiles", 1)
+    sums_w = add_halves(home_w, got_w)
+    far_near, sums_w = tie((far_near, sums_w))
+    got_weights = along(*sums_w)
+    home_f, away_f = gather(routes_x, first, near_first, far_first, far_near)
+    got_f = swap(away_f, "frames", 1)
+    sums_s = add_halves(home_s, got_s)
+    got_f, sums_s, got_weights = tie((got_f, sums_s, got_weights))
+    got_second = along(*sums_s)
+    got_first = along(*add_halves(home_f, got_f))
     return collapse(got_weights, got_first, got_second)
 
 

time: 95.3 us -> 86.3 us (0.906)
  waiting for transfers between devices: 40.9 us -> 23.6 us
  local copies, waits for them, and re-layouts: 3.58 us -> 8.12 us
  Pallas kernels: 17.1 us -> 21.1 us
    ppermute x27, waiting for transfers between devices: 40.9 us -> 23.6 us  [swap(): return lax.ppermute(value, axis, [(i, i ^ bit) for i in range(size)])]
    unnamed x22 -> x32, local copies, waits for them, and re-layouts: 3.58 us -> 8.12 us
    pallas_call x1 -> x2, Pallas kernels: 2.45 us -> 4.9 us  [routes_of(): pl.pallas_call(routes_kernel, in_specs=[smem], out_specs=[smem, smem], ou...]
    pallas_call x1, Pallas kernels: 1.37 us -> 2.33 us  [blend(): pl.pallas_call(blend_kernel, in_specs=[pl.BlockSpec(memory_space=pltpu.SM...]
  transfers between devices with their start and end apart: 27 -> 27, of which waited for: 14 -> 10; matrix products, arithmetic and copies ran while one was open for 1% -> 1% of each run, Pallas kernels for 11% -> 15%
where the time goes in v6:
time: 86.3 us; the launch traced here: 85.9 us
  starting transfers between devices  30.3 us (35%)
  waiting for transfers between devices  23.6 us (27%)
  Pallas kernels  21.1 us (24%)
  local copies, waits for them, and re-layouts  8.12 us (9%)
  between operations  1.53 us (2%)
  other arithmetic  1.34 us (2%)
    ppermute x27, starting transfers between devices, swap(): return lax.ppermute(value, axis, [(i, i ^ bit) for i in range(size)])  30.3 us
    ppermute x27, waiting for transfers between devices, swap(): return lax.ppermute(value, axis, [(i, i ^ bit) for i in range(size)])  23.6 us
    unnamed x32, local copies, waits for them, and re-layouts  8.12 us
    pallas_call x3, Pallas kernels, gather_rows(): pl.pallas_call(gather_kernel, in_specs=[pl.BlockSpec(memory_space=pltpu.S...  5.02 us
    pallas_call x2, Pallas kernels, routes_of(): pl.pallas_call(routes_kernel, in_specs=[smem], out_specs=[smem, smem], ou...  4.9 us
    pallas_call x1, Pallas kernels, bands_of(): pl.pallas_call(functools.partial(bands_kernel, small_places, large_places...  4.68 us
    pallas_call x1, Pallas kernels, blend(): pl.pallas_call(blend_kernel, in_specs=[pl.BlockSpec(memory_space=pltpu.SM...  2.33 us
    pallas_call x1, Pallas kernels, collapse(): pl.pallas_call(functools.partial(collapse_kernel, places, len(a)), out_sh...  2.18 us
  transfers between devices with their start and end apart: 27, of which 10 were waited for; matrix products, arithmetic and copies ran while one was open for 1% of the time, Pallas kernels for 15%

profile of v6, /device:TPU:0, one launch (start us, length us, event | category | flops | bytes accessed | tf_op | source)
XLA Modules:
  0.0 85.9 jit_solution(6275483133980770676)
XLA Ops:
  3.5 1.8 %strips.1 = bf16[288,128]{1,0:T(8,128)(2,1)S(1)} custom-call(s32[1]{0:T(128)S(6)} %copy.12.cell, bf16[1,3,128,1024]{3,2,1,0:T(8,128)(2,1)S(1)} %copy-done.11, bf16[1,3,128,1024]{3,2,1,0:T(8,128)(2,1)S(1)} %copy-done.11, bf16[512,512]{1,0:T(8,128)(2,1)S(1)} %copy-done.15), custom_call_target="tpu_custom_call" | custom-call | flops 2000000000 | bytes 1000000 | tf_op jit(solution)/shard_map/strips/pallas_call | solution.py:247
  5.9 2.6 %collective-permute-start = (bf16[288,128]{1,0:T(8,128)(2,1)S(1)}, bf16[288,128]{1,0:T(8,128)(2,1)S(1)}, u32[]{:S(2)}, u32[]{:S(2)}) collective-permute-start(bf16[288,128]{1,0:T(8,128)(2,1)S(1)} %strips.1), channel_id=1, source_target_pairs={{0,4},{4,0},{8,12},{12,8},{16,20},{20,16},{24,28},{28,24},{1,5},{5... | collective-permute-start | bytes 221192 | tf_op jit(solution)/shard_map/ppermute | solution.py:579
  8.5 4.7 %bands.1 = (bf16[32,32,128]{2,1,0:T(8,128)(2,1)S(1)}, f32[816,1024]{1,0:T(8,128)S(1)}) custom-call(bf16[1,3,128,1024]{3,2,1,0:T(8,128)(2,1)S(1)} %copy-done.11, bf16[1,128,1024]{2,1,0:T(8,128)(2,1)S(1)} %copy-done.12, s32[1,64,128]{2,1,0:T(8,128)S(1)} %bitcast.13, bf16[512,512]{1,0:T(8,128)(2,1)S(1)} %copy-done.15, bf16[512,640]{1,0:T(8,128)(2,1)S(1)} %copy-done.14), custom_call_target="tpu_custom_call" | custom-call | flops 8000000000 | bytes 6000000 | tf_op jit(solution)/shard_map/bands/pallas_call | solution.py:339
  16.3 1.6 %collective-permute-start.1 = (bf16[288,128]{1,0:T(8,128)(2,1)S(1)}, bf16[288,128]{1,0:T(8,128)(2,1)S(1)}, u32[]{:S(2)}, u32[]{:S(2)}) collective-permute-start(bf16[288,128]{1,0:T(8,128)(2,1)S(1)} %broadcast_select_fusion), channel_id=1, source_target_pairs={{0,8},{4,12},{8,0},{12,4},{16,24},{20,28},{24,16},{28,20},{1,9},{5... | collective-permute-start | bytes 221192 | tf_op jit(solution)/shard_map/ppermute | solution.py:579
  19.1 1.7 %collective-permute-done.1 = bf16[288,128]{1,0:T(8,128)(2,1)S(1)} collective-permute-done((bf16[288,128]{1,0:T(8,128)(2,1)S(1)}, bf16[288,128]{1,0:T(8,128)(2,1)S(1)}, u32[]{:S(2)}, u32[]{:S(2)}) %collective-permute-start.1) | collective-permute-done | bytes 73760 | tf_op jit(solution)/shard_map/ppermute | solution.py:579
  21.4 2.3 %collective-permute-done.2.c = bf16[32,32,128]{2,1,0:T(8,128)(2,1)} collective-permute-done((bf16[32,32,128]{2,1,0:T(8,128)(2,1)}, bf16[32,32,128]{2,1,0:T(8,128)(2,1)}, u32[]{:S(2)}, u32[]{:S(2)}) %collective-permute-start.2) | collective-permute-done | bytes 262176 | tf_op jit(solution)/shard_map/ppermute | solution.py:579
  23.7 2.6 %collective-permute-start.4 = (bf16[288,128]{1,0:T(8,128)(2,1)S(1)}, bf16[288,128]{1,0:T(8,128)(2,1)S(1)}, u32[]{:S(2)}, u32[]{:S(2)}) collective-permute-start(bf16[288,128]{1,0:T(8,128)(2,1)S(1)} %broadcast_select_fusion.1), channel_id=1, source_target_pairs={{0,16},{4,20},{8,24},{12,28},{16,0},{20,4},{24,8},{28,12},{1,17},{... | collective-permute-start | bytes 221192 | tf_op jit(solution)/shard_map/ppermute | solution.py:579
  27.0 3.2 %collective-permute-done.4 = bf16[288,128]{1,0:T(8,128)(2,1)S(1)} collective-permute-done((bf16[288,128]{1,0:T(8,128)(2,1)S(1)}, bf16[288,128]{1,0:T(8,128)(2,1)S(1)}, u32[]{:S(2)}, u32[]{:S(2)}) %collective-permute-start.4) | collective-permute-done | bytes 73760 | tf_op jit(solution)/shard_map/ppermute | solution.py:579
  30.2 2.3 %blend.1 = (bf16[32,80,128]{2,1,0:T(8,128)(2,1)}, bf16[32,64,128]{2,1,0:T(8,128)(2,1)}) custom-call(s32[1]{0:T(128)S(6)} %copy.12.cell, bf16[288,128]{1,0:T(8,128)(2,1)S(1)} %broadcast_select_fusion.2.strips, f32[816,1024]{1,0:T(8,128)S(1)} %get-tuple-element.78.state), custom_call_target="tpu_custom_call" | custom-call | flops 1000000 | bytes 10000 | tf_op jit(solution)/shard_map/blend/pallas_call | solution.py:410
  34.8 2.4 %routes.2 = (s32[4,33]{1,0:T(4,128)}, s32[4]{0:T(128)}) custom-call(s32[4,32]{1,0:T(4,128)} %get-tuple-element.84.spot), custom_call_target="tpu_custom_call" | custom-call | tf_op jit(solution)/shard_map/routes/pallas_call | solution.py:433
  37.3 2.5 %routes.3 = (s32[4,33]{1,0:T(4,128)}, s32[4]{0:T(128)}) custom-call(s32[4,32]{1,0:T(4,128)} %get-tuple-element.92.spot), custom_call_target="tpu_custom_call" | custom-call | tf_op jit(solution)/shard_map/routes/pallas_call | solution.py:433
  44.8 1.6 %collective-permute-start.14 = (bf16[16,32,128]{2,1,0:T(8,128)(2,1)S(1)}, bf16[16,32,128]{2,1,0:T(8,128)(2,1)S(1)}, u32[]{:S(2)}, u32[]{:S(2)}) collective-permute-start(bf16[16,32,128]{2,1,0:T(8,128)(2,1)S(1)} %get-tuple-element.99), channel_id=1, source_target_pairs={{0,4},{4,0},{8,12},{12,8},{16,20},{20,16},{24,28},{28,24},{1,5},{5... | collective-permute-start | bytes 393224 | tf_op jit(solution)/shard_map/ppermute | solution.py:579
  47.7 1.8 %gather_rows.4 = (f32[16,64,128]{2,1,0:T(8,128)S(1)}, bf16[16,64,128]{2,1,0:T(8,128)(2,1)S(1)}) custom-call(s32[4,33]{1,0:T(4,128)S(1)} %copy-done.9, s32[4]{0:T(128)S(1)} %copy-done.10, bf16[32,64,128]{2,1,0:T(8,128)(2,1)} %get-tuple-element.88.a, bf16[32,64,128]{2,1,0:T(8,128)(2,1)S(1)} %collective-permute-done.12.b, ...), custom_call_target="tpu_custom_call" | custom-call | flops 1000000 | bytes 10000 | tf_op jit(solution)/shard_map/gather_rows/pallas_call | solution.py:462
  51.0 2.5 %collective-permute-done.15.d = bf16[32,80,128]{2,1,0:T(8,128)(2,1)S(1)} collective-permute-done((bf16[32,80,128]{2,1,0:T(8,128)(2,1)S(1)}, bf16[32,80,128]{2,1,0:T(8,128)(2,1)S(1)}, u32[]{:S(2)}, u32[]{:S(2)}) %collective-permute-start.15) | collective-permute-done | bytes 655392 | tf_op jit(solution)/shard_map/ppermute | solution.py:579
  53.7 1.8 %gather_rows.5 = (f32[16,80,128]{2,1,0:T(8,128)S(1)}, bf16[16,80,128]{2,1,0:T(8,128)(2,1)S(1)}) custom-call(s32[4,33]{1,0:T(4,128)S(1)} %copy-done.6, s32[4]{0:T(128)S(1)} %copy-done.8, bf16[32,80,128]{2,1,0:T(8,128)(2,1)} %get-tuple-element.87.a, bf16[32,80,128]{2,1,0:T(8,128)(2,1)S(1)} %collective-permute-done.8.b, ...), custom_call_target="tpu_custom_call" | custom-call | flops 1000000 | bytes 10000 | tf_op jit(solution)/shard_map/gather_rows/pallas_call | solution.py:462
  55.5 1.7 %collective-permute-start.16 = (bf16[16,80,128]{2,1,0:T(8,128)(2,1)S(1)}, bf16[16,80,128]{2,1,0:T(8,128)(2,1)S(1)}, u32[]{:S(2)}, u32[]{:S(2)}) collective-permute-start(bf16[16,80,128]{2,1,0:T(8,128)(2,1)S(1)} %get-tuple-element.108), channel_id=1, source_target_pairs={{0,4},{4,0},{8,12},{12,8},{16,20},{20,16},{24,28},{28,24},{1,5},{5... | collective-permute-start | bytes 983048 | tf_op jit(solution)/shard_map/ppermute | solution.py:579
  59.2 3.4 %collective-permute-start.19 = (bf16[4,32,128]{2,1,0:T(8,128)(2,1)S(1)}, bf16[4,32,128]{2,1,0:T(8,128)(2,1)S(1)}, u32[]{:S(2)}, u32[]{:S(2)}) collective-permute-start(bf16[4,32,128]{2,1,0:T(8,128)(2,1)S(1)} %get-tuple-element.117), channel_id=1, source_target_pairs={{0,16},{4,20},{8,24},{12,28},{16,0},{20,4},{24,8},{28,12},{1,17},{... | collective-permute-start | bytes 98312 | tf_op jit(solution)/shard_map/ppermute | solution.py:579
  63.0 2.3 %collective-permute-done.17.got = bf16[16,64,128]{2,1,0:T(8,128)(2,1)S(1)} collective-permute-done((bf16[16,64,128]{2,1,0:T(8,128)(2,1)S(1)}, bf16[16,64,128]{2,1,0:T(8,128)(2,1)S(1)}, u32[]{:S(2)}, u32[]{:S(2)}) %collective-permute-start.17) | collective-permute-done | bytes 262176 | tf_op jit(solution)/shard_map/ppermute | solution.py:579
  65.3 3.0 %collective-permute-done.20.refs_3_ = bf16[4,32,128]{2,1,0:T(8,128)(2,1)S(1)} collective-permute-done((bf16[4,32,128]{2,1,0:T(8,128)(2,1)S(1)}, bf16[4,32,128]{2,1,0:T(8,128)(2,1)S(1)}, u32[]{:S(2)}, u32[]{:S(2)}) %collective-permute-start.20) | collective-permute-done | bytes 32800 | tf_op jit(solution)/shard_map/ppermute | solution.py:579
  68.4 2.1 %collective-permute-start.21 = (bf16[4,80,128]{2,1,0:T(8,128)(2,1)S(1)}, bf16[4,80,128]{2,1,0:T(8,128)(2,1)S(1)}, u32[]{:S(2)}, u32[]{:S(2)}) collective-permute-start(bf16[4,80,128]{2,1,0:T(8,128)(2,1)S(1)} %get-tuple-element.126), channel_id=1, source_target_pairs={{0,8},{4,12},{8,0},{12,4},{16,24},{20,28},{24,16},{28,20},{1,9},{5... | collective-permute-start | bytes 245768 | tf_op jit(solution)/shard_map/ppermute | solution.py:579
  70.5 2.4 %collective-permute-start.23 = (bf16[4,80,128]{2,1,0:T(8,128)(2,1)S(1)}, bf16[4,80,128]{2,1,0:T(8,128)(2,1)S(1)}, u32[]{:S(2)}, u32[]{:S(2)}) collective-permute-start(bf16[4,80,128]{2,1,0:T(8,128)(2,1)S(1)} %get-tuple-element.128), channel_id=1, source_target_pairs={{0,24},{4,28},{8,16},{12,20},{16,8},{20,12},{24,0},{28,4},{1,25},{... | collective-permute-start | bytes 245768 | tf_op jit(solution)/shard_map/ppermute | solution.py:579
  73.8 2.5 %collective-permute-start.26 = (bf16[4,64,128]{2,1,0:T(8,128)(2,1)S(1)}, bf16[4,64,128]{2,1,0:T(8,128)(2,1)S(1)}, u32[]{:S(2)}, u32[]{:S(2)}) collective-permute-start(bf16[4,64,128]{2,1,0:T(8,128)(2,1)S(1)} %get-tuple-element.132), channel_id=1, source_target_pairs={{0,24},{4,28},{8,16},{12,20},{16,8},{20,12},{24,0},{28,4},{1,25},{... | collective-permute-start | bytes 196616 | tf_op jit(solution)/shard_map/ppermute | solution.py:579
  76.4 7.4 %collective-permute-done.25.refs_10_ = bf16[4,64,128]{2,1,0:T(8,128)(2,1)S(1)} collective-permute-done((bf16[4,64,128]{2,1,0:T(8,128)(2,1)S(1)}, bf16[4,64,128]{2,1,0:T(8,128)(2,1)S(1)}, u32[]{:S(2)}, u32[]{:S(2)}) %collective-permute-start.25) | collective-permute-done | bytes 65568 | tf_op jit(solution)/shard_map/ppermute | solution.py:579
  83.8 2.2 %collapse.1 = f32[3,4,4096]{2,1,0:T(4,128)} custom-call(bf16[192,1280]{1,0:T(8,128)(2,1)S(1)} %copy-done, f32[4,32,128]{2,1,0:T(8,128)S(1)} %get-tuple-element.119.refs_0_, bf16[4,32,128]{2,1,0:T(8,128)(2,1)S(1)} %collective-permute-done.18.refs_1_, bf16[4,32,128]{2,1,0:T(8,128)(2,1)S(1)} %collective-permute-done.19.refs_2_, ...), custom_call_target="tpu_custom_call" | custom-call | flops 1000000 | bytes 10000 | tf_op jit(solution)/shard_map/collapse/pallas_call | solution.py:566
  (80 shorter events, 22.1 us)
Async XLA Ops:
  5.4 12.6 %collective-permute-start.5 = (s32[32]{0:T(128)S(1)}, s32[32]{0:T(128)S(1)}, u32[]{:S(2)}, u32[]{:S(2)}) collective-permute-start(s32[32]{0:T(128)S(1)} %bitcast_add_fusion), channel_id=1, source_target_pairs={{0,1},{1,0},{2,3},{3,2},{4,5},{5,4},{6,7},{7,6},{8,9},{9,8},{10,11... | collective-permute-start | bytes 392 | tf_op jit(solution)/shard_map/ppermute | solution.py:579
  5.9 8.7 %collective-permute-start = (bf16[288,128]{1,0:T(8,128)(2,1)S(1)}, bf16[288,128]{1,0:T(8,128)(2,1)S(1)}, u32[]{:S(2)}, u32[]{:S(2)}) collective-permute-start(bf16[288,128]{1,0:T(8,128)(2,1)S(1)} %strips.1), channel_id=1, source_target_pairs={{0,4},{4,0},{8,12},{12,8},{16,20},{20,16},{24,28},{28,24},{1,5},{5... | collective-permute-start | bytes 221192 | tf_op jit(solution)/shard_map/ppermute | solution.py:579
  14.6 6.2 %collective-permute-start.3 = (bf16[32,32,128]{2,1,0:T(8,128)(2,1)}, bf16[32,32,128]{2,1,0:T(8,128)(2,1)S(1)}, u32[]{:S(2)}, u32[]{:S(2)}) collective-permute-start(bf16[32,32,128]{2,1,0:T(8,128)(2,1)} %copy-done.1), channel_id=1, source_target_pairs={{0,1},{1,0},{2,3},{3,2},{4,5},{5,4},{6,7},{7,6},{8,9},{9,8},{10,11... | collective-permute-start | bytes 786440 | tf_op jit(solution)/shard_map/ppermute | solution.py:579
  14.8 8.9 %collective-permute-start.2 = (bf16[32,32,128]{2,1,0:T(8,128)(2,1)}, bf16[32,32,128]{2,1,0:T(8,128)(2,1)}, u32[]{:S(2)}, u32[]{:S(2)}) collective-permute-start(bf16[32,32,128]{2,1,0:T(8,128)(2,1)} %copy-done.1), channel_id=1, source_target_pairs={{0,2},{1,3},{2,0},{3,1},{4,6},{5,7},{6,4},{7,5},{8,10},{9,11},{10,... | collective-permute-start | bytes 786440 | tf_op jit(solution)/shard_map/ppermute | solution.py:579
  16.3 4.4 %collective-permute-start.1 = (bf16[288,128]{1,0:T(8,128)(2,1)S(1)}, bf16[288,128]{1,0:T(8,128)(2,1)S(1)}, u32[]{:S(2)}, u32[]{:S(2)}) collective-permute-start(bf16[288,128]{1,0:T(8,128)(2,1)S(1)} %broadcast_select_fusion), channel_id=1, source_target_pairs={{0,8},{4,12},{8,0},{12,4},{16,24},{20,28},{24,16},{28,20},{1,9},{5... | collective-permute-start | bytes 221192 | tf_op jit(solution)/shard_map/ppermute | solution.py:579
  18.0 8.4 %collective-permute-start.7 = (s32[2,32]{1,0:T(2,128)S(1)}, s32[2,32]{1,0:T(2,128)S(1)}, u32[]{:S(2)}, u32[]{:S(2)}) collective-permute-start(s32[2,32]{1,0:T(2,128)S(1)} %pad_add_fusion.3), channel_id=1, source_target_pairs={{0,4},{4,0},{8,12},{12,8},{16,20},{20,16},{24,28},{28,24},{1,5},{5... | collective-permute-start | bytes 776 | tf_op jit(solution)/shard_map/ppermute | solution.py:579
  18.6 7.8 %collective-permute-start.6 = (s32[2,32]{1,0:T(2,128)S(1)}, s32[2,32]{1,0:T(2,128)S(1)}, u32[]{:S(2)}, u32[]{:S(2)}) collective-permute-start(s32[2,32]{1,0:T(2,128)S(1)} %pad_add_fusion.3), channel_id=1, source_target_pairs={{0,2},{1,3},{2,0},{3,1},{4,6},{5,7},{6,4},{7,5},{8,10},{9,11},{10,... | collective-permute-start | bytes 776 | tf_op jit(solution)/shard_map/ppermute | solution.py:579
  23.7 6.5 %collective-permute-start.4 = (bf16[288,128]{1,0:T(8,128)(2,1)S(1)}, bf16[288,128]{1,0:T(8,128)(2,1)S(1)}, u32[]{:S(2)}, u32[]{:S(2)}) collective-permute-start(bf16[288,128]{1,0:T(8,128)(2,1)S(1)} %broadcast_select_fusion.1), channel_id=1, source_target_pairs={{0,16},{4,20},{8,24},{12,28},{16,0},{20,4},{24,8},{28,12},{1,17},{... | collective-permute-start | bytes 221192 | tf_op jit(solution)/shard_map/ppermute | solution.py:579
  32.5 11.9 %collective-permute-start.10 = (bf16[32,64,128]{2,1,0:T(8,128)(2,1)}, bf16[32,64,128]{2,1,0:T(8,128)(2,1)S(1)}, u32[]{:S(2)}, u32[]{:S(2)}) collective-permute-start(bf16[32,64,128]{2,1,0:T(8,128)(2,1)} %get-tuple-element.88.a), channel_id=1, source_target_pairs={{0,4},{4,0},{8,12},{12,8},{16,20},{20,16},{24,28},{28,24},{1,5},{5... | collective-permute-start | bytes 1572872 | tf_op jit(solution)/shard_map/ppermute | solution.py:579
  33.0 6.7 %collective-permute-start.11 = (bf16[32,32,128]{2,1,0:T(8,128)(2,1)}, bf16[32,32,128]{2,1,0:T(8,128)(2,1)S(1)}, u32[]{:S(2)}, u32[]{:S(2)}) collective-permute-start(bf16[32,32,128]{2,1,0:T(8,128)(2,1)} %collective-permute-done.2.c), channel_id=1, source_target_pairs={{0,1},{1,0},{2,3},{3,2},{4,5},{5,4},{6,7},{7,6},{8,9},{9,8},{10,11... | collective-permute-start | bytes 786440 | tf_op jit(solution)/shard_map/ppermute | solution.py:579
  33.0 17.4 %collective-permute-start.9 = (bf16[32,80,128]{2,1,0:T(8,128)(2,1)}, bf16[32,80,128]{2,1,0:T(8,128)(2,1)S(1)}, u32[]{:S(2)}, u32[]{:S(2)}) collective-permute-start(bf16[32,80,128]{2,1,0:T(8,128)(2,1)} %get-tuple-element.87.a), channel_id=1, source_target_pairs={{0,2},{1,3},{2,0},{3,1},{4,6},{5,7},{6,4},{7,5},{8,10},{9,11},{10,... | collective-permute-start | bytes 1966088 | tf_op jit(solution)/shard_map/ppermute | solution.py:579
  34.6 11.8 %collective-permute-start.12 = (bf16[32,64,128]{2,1,0:T(8,128)(2,1)}, bf16[32,64,128]{2,1,0:T(8,128)(2,1)S(1)}, u32[]{:S(2)}, u32[]{:S(2)}) collective-permute-start(bf16[32,64,128]{2,1,0:T(8,128)(2,1)} %get-tuple-element.88.a), channel_id=1, source_target_pairs={{0,1},{1,0},{2,3},{3,2},{4,5},{5,4},{6,7},{7,6},{8,9},{9,8},{10,11... | collective-permute-start | bytes 1572872 | tf_op jit(solution)/shard_map/ppermute | solution.py:579
  44.8 5.6 %collective-permute-start.14 = (bf16[16,32,128]{2,1,0:T(8,128)(2,1)S(1)}, bf16[16,32,128]{2,1,0:T(8,128)(2,1)S(1)}, u32[]{:S(2)}, u32[]{:S(2)}) collective-permute-start(bf16[16,32,128]{2,1,0:T(8,128)(2,1)S(1)} %get-tuple-element.99), channel_id=1, source_target_pairs={{0,4},{4,0},{8,12},{12,8},{16,20},{20,16},{24,28},{28,24},{1,5},{5... | collective-permute-start | bytes 393224 | tf_op jit(solution)/shard_map/ppermute | solution.py:579
  55.5 12.9 %collective-permute-start.16 = (bf16[16,80,128]{2,1,0:T(8,128)(2,1)S(1)}, bf16[16,80,128]{2,1,0:T(8,128)(2,1)S(1)}, u32[]{:S(2)}, u32[]{:S(2)}) collective-permute-start(bf16[16,80,128]{2,1,0:T(8,128)(2,1)S(1)} %get-tuple-element.108), channel_id=1, source_target_pairs={{0,4},{4,0},{8,12},{12,8},{16,20},{20,16},{24,28},{28,24},{1,5},{5... | collective-permute-start | bytes 983048 | tf_op jit(solution)/shard_map/ppermute | solution.py:579
  57.2 8.1 %collective-permute-start.17 = (bf16[16,64,128]{2,1,0:T(8,128)(2,1)S(1)}, bf16[16,64,128]{2,1,0:T(8,128)(2,1)S(1)}, u32[]{:S(2)}, u32[]{:S(2)}) collective-permute-start(bf16[16,64,128]{2,1,0:T(8,128)(2,1)S(1)} %get-tuple-element.110), channel_id=1, source_target_pairs={{0,2},{1,3},{2,0},{3,1},{4,6},{5,7},{6,4},{7,5},{8,10},{9,11},{10,... | collective-permute-start | bytes 786440 | tf_op jit(solution)/shard_map/ppermute | solution.py:579
  58.6 6.7 %collective-permute-start.18 = (bf16[4,32,128]{2,1,0:T(8,128)(2,1)S(1)}, bf16[4,32,128]{2,1,0:T(8,128)(2,1)S(1)}, u32[]{:S(2)}, u32[]{:S(2)}) collective-permute-start(bf16[4,32,128]{2,1,0:T(8,128)(2,1)S(1)} %get-tuple-element.116), channel_id=1, source_target_pairs={{0,8},{4,12},{8,0},{12,4},{16,24},{20,28},{24,16},{28,20},{1,9},{5... | collective-permute-start | bytes 98312 | tf_op jit(solution)/shard_map/ppermute | solution.py:579
  59.2 6.1 %collective-permute-start.19 = (bf16[4,32,128]{2,1,0:T(8,128)(2,1)S(1)}, bf16[4,32,128]{2,1,0:T(8,128)(2,1)S(1)}, u32[]{:S(2)}, u32[]{:S(2)}) collective-permute-start(bf16[4,32,128]{2,1,0:T(8,128)(2,1)S(1)} %get-tuple-element.117), channel_id=1, source_target_pairs={{0,16},{4,20},{8,24},{12,28},{16,0},{20,4},{24,8},{28,12},{1,17},{... | collective-permute-start | bytes 98312 | tf_op jit(solution)/shard_map/ppermute | solution.py:579
  62.6 5.7 %collective-permute-start.20 = (bf16[4,32,128]{2,1,0:T(8,128)(2,1)S(1)}, bf16[4,32,128]{2,1,0:T(8,128)(2,1)S(1)}, u32[]{:S(2)}, u32[]{:S(2)}) collective-permute-start(bf16[4,32,128]{2,1,0:T(8,128)(2,1)S(1)} %get-tuple-element.118), channel_id=1, source_target_pairs={{0,24},{4,28},{8,16},{12,20},{16,8},{20,12},{24,0},{28,4},{1,25},{... | collective-permute-start | bytes 98312 | tf_op jit(solution)/shard_map/ppermute | solution.py:579
  68.4 5.5 %collective-permute-start.24 = (bf16[4,64,128]{2,1,0:T(8,128)(2,1)S(1)}, bf16[4,64,128]{2,1,0:T(8,128)(2,1)S(1)}, u32[]{:S(2)}, u32[]{:S(2)}) collective-permute-start(bf16[4,64,128]{2,1,0:T(8,128)(2,1)S(1)} %get-tuple-element.130), channel_id=1, source_target_pairs={{0,8},{4,12},{8,0},{12,4},{16,24},{20,28},{24,16},{28,20},{1,9},{5... | collective-permute-start | bytes 196616 | tf_op jit(solution)/shard_map/ppermute | solution.py:579
  68.4 15.3 %collective-permute-start.21 = (bf16[4,80,128]{2,1,0:T(8,128)(2,1)S(1)}, bf16[4,80,128]{2,1,0:T(8,128)(2,1)S(1)}, u32[]{:S(2)}, u32[]{:S(2)}) collective-permute-start(bf16[4,80,128]{2,1,0:T(8,128)(2,1)S(1)} %get-tuple-element.126), channel_id=1, source_target_pairs={{0,8},{4,12},{8,0},{12,4},{16,24},{20,28},{24,16},{28,20},{1,9},{5... | collective-permute-start | bytes 245768 | tf_op jit(solution)/shard_map/ppermute | solution.py:579
  70.5 13.2 %collective-permute-start.22 = (bf16[4,80,128]{2,1,0:T(8,128)(2,1)S(1)}, bf16[4,80,128]{2,1,0:T(8,128)(2,1)S(1)}, u32[]{:S(2)}, u32[]{:S(2)}) collective-permute-start(bf16[4,80,128]{2,1,0:T(8,128)(2,1)S(1)} %get-tuple-element.127), channel_id=1, source_target_pairs={{0,16},{4,20},{8,24},{12,28},{16,0},{20,4},{24,8},{28,12},{1,17},{... | collective-permute-start | bytes 245768 | tf_op jit(solution)/shard_map/ppermute | solution.py:579
  70.5 13.2 %collective-permute-start.23 = (bf16[4,80,128]{2,1,0:T(8,128)(2,1)S(1)}, bf16[4,80,128]{2,1,0:T(8,128)(2,1)S(1)}, u32[]{:S(2)}, u32[]{:S(2)}) collective-permute-start(bf16[4,80,128]{2,1,0:T(8,128)(2,1)S(1)} %get-tuple-element.128), channel_id=1, source_target_pairs={{0,24},{4,28},{8,16},{12,20},{16,8},{20,12},{24,0},{28,4},{1,25},{... | collective-permute-start | bytes 245768 | tf_op jit(solution)/shard_map/ppermute | solution.py:579
  73.0 10.8 %collective-permute-start.25 = (bf16[4,64,128]{2,1,0:T(8,128)(2,1)S(1)}, bf16[4,64,128]{2,1,0:T(8,128)(2,1)S(1)}, u32[]{:S(2)}, u32[]{:S(2)}) collective-permute-start(bf16[4,64,128]{2,1,0:T(8,128)(2,1)S(1)} %get-tuple-element.131), channel_id=1, source_target_pairs={{0,16},{4,20},{8,24},{12,28},{16,0},{20,4},{24,8},{28,12},{1,17},{... | collective-permute-start | bytes 196616 | tf_op jit(solution)/shard_map/ppermute | solution.py:579
  73.8 9.9 %collective-permute-start.26 = (bf16[4,64,128]{2,1,0:T(8,128)(2,1)S(1)}, bf16[4,64,128]{2,1,0:T(8,128)(2,1)S(1)}, u32[]{:S(2)}, u32[]{:S(2)}) collective-permute-start(bf16[4,64,128]{2,1,0:T(8,128)(2,1)S(1)} %get-tuple-element.132), channel_id=1, source_target_pairs={{0,24},{4,28},{8,16},{12,20},{16,8},{20,12},{24,0},{28,4},{1,25},{... | collective-permute-start | bytes 196616 | tf_op jit(solution)/shard_map/ppermute | solution.py:579
  (19 other events, 103.1 us)

commit v7 on v6

--- a/solution.py
+++ b/solution.py
@@ -425,7 +425,7 @@
             lists[source, count] = q * ROUTE + at
             return jnp.where(at >= 0, count + 1, count)
 
-        counts[source] = lax.fori_loop(0, QB, body, 0)
+        counts[source] = lax.fori_loop(0, QB, body, 0, unroll=True)
 
 
 def routes_of(spot):
@@ -612,10 +612,9 @@
         if bit == 1:
             got, weights, state = tie((got, weights, state))
             far, near = swap(weights, "tiles", 2), swap(weights, "tiles", 1)
-        if bit == 2:
-            got, far, near = tie((got, far, near))
         if bit == half:
-            got, spot_x, spot_y = tie((got, spot_x, spot_y))
+            far_near = swap(far, "tiles", 1)
+            got, far, near, far_near, routes_x, spot_y = tie((got, far, near, far_near, routes_of(spot_x), spot_y))
         strips = jnp.where((mask & bit) != 0, got, strips)
         bit *= 2
 
@@ -626,25 +625,23 @@
         return [own] + [swap(part, "frames", 2 * (j + 1)) for j, part in enumerate(away)]
 
     first, second = blend(strip_cell, strips, state)
-    first, second, spot_x, spot_y, far = tie((first, second, spot_x, spot_y, far))
+    first, second, near, spot_y = tie((first, second, near, spot_y))
     far_first, near_first = swap(first, "tiles", 2), swap(first, "tiles", 1)
     far_second, near_second = swap(second, "frames", 1), swap(second, "tiles", 1)
-    routes_x, routes_y = routes_of(spot_x), routes_of(spot_y)
-    home_w, away_w = gather(routes_x, weights, near, far, swap(far, "tiles", 1))
+    home_w, away_w = gather(routes_x, weights, near, far, far_near)
     got_w = swap(away_w, "frames", 1)
-    far_second, home_w, routes_y = tie((far_second, home_w, routes_y))
+    near_first, near_second, got_w, routes_y = tie((near_first, near_second, got_w, routes_of(spot_y)))
+    sums_w = add_halves(home_w, got_w)
+    far_second, sums_w = tie((far_second, sums_w))
+    got_weights = along(*sums_w)
     home_s, away_s = gather(routes_y, second, near_second, far_second, swap(far_second, "tiles", 1))
     got_s = swap(away_s, "tiles", 2)
-    far_first, home_s, got_w = tie((far_first, home_s, got_w))
-    far_near = swap(far_first, "tiles", 1)
-    sums_w = add_halves(home_w, got_w)
-    far_near, sums_w = tie((far_near, sums_w))
-    got_weights = along(*sums_w)
+    far_first, home_s, got_weights = tie((far_first, home_s, got_weights))
+    far_near, got_s = tie((swap(far_first, "tiles", 1), got_s))
     home_f, away_f = gather(routes_x, first, near_first, far_first, far_near)
     got_f = swap(away_f, "frames", 1)
-    sums_s = add_halves(home_s, got_s)
-    got_f, sums_s, got_weights = tie((got_f, sums_s, got_weights))
-    got_second = along(*sums_s)
+    got_second = along(*add_halves(home_s, got_s))
+    got_f, got_second = tie((got_f, got_second))
     got_first = along(*add_halves(home_f, got_f))
     return collapse(got_weights, got_first, got_second)
 

time: 86.3 us -> 91.7 us (1.063)
  waiting for transfers between devices: 23.6 us -> 34.7 us
  local copies, waits for them, and re-layouts: 8.12 us -> 4.28 us
  starting transfers between devices: 30.3 us -> 29.2 us
  Pallas kernels: 21.1 us -> 20.1 us
    ppermute x27, waiting for transfers between devices: 23.6 us -> 34.7 us  [swap(): return lax.ppermute(value, axis, [(i, i ^ bit) for i in range(size)])]
    unnamed x32 -> x24, local copies, waits for them, and re-layouts: 8.12 us -> 4.28 us
    pallas_call x2, Pallas kernels: 4.9 us -> 3.29 us  [routes_of(): pl.pallas_call(routes_kernel, in_specs=[smem], out_specs=[smem, smem], ou...]
    ppermute x27, starting transfers between devices: 30.3 us -> 29.2 us  [swap(): return lax.ppermute(value, axis, [(i, i ^ bit) for i in range(size)])]
  transfers between devices with their start and end apart: 27 -> 27, of which waited for: 10 -> 11; matrix products, arithmetic and copies ran while one was open for 1% -> 1% of each run, Pallas kernels for 15% -> 13%
where the time goes in v7:
time: 91.7 us; the launch traced here: 91.2 us
  waiting for transfers between devices  34.7 us (38%)
  starting transfers between devices  29.2 us (32%)
  Pallas kernels  20.1 us (22%)
  local copies, waits for them, and re-layouts  4.28 us (5%)
  between operations  1.53 us (2%)
  other arithmetic  1.33 us (1%)
    ppermute x27, waiting for transfers between devices, swap(): return lax.ppermute(value, axis, [(i, i ^ bit) for i in range(size)])  34.7 us
    ppermute x27, starting transfers between devices, swap(): return lax.ppermute(value, axis, [(i, i ^ bit) for i in range(size)])  29.2 us
    pallas_call x3, Pallas kernels, gather_rows(): pl.pallas_call(gather_kernel, in_specs=[pl.BlockSpec(memory_space=pltpu.S...  5.7 us
    pallas_call x1, Pallas kernels, bands_of(): pl.pallas_call(functools.partial(bands_kernel, small_places, large_places...  4.68 us
    unnamed x24, local copies, waits for them, and re-layouts  4.28 us
    pallas_call x2, Pallas kernels, routes_of(): pl.pallas_call(routes_kernel, in_specs=[smem], out_specs=[smem, smem], ou...  3.29 us
    pallas_call x1, Pallas kernels, blend(): pl.pallas_call(blend_kernel, in_specs=[pl.BlockSpec(memory_space=pltpu.SM...  2.3 us
    pallas_call x1, Pallas kernels, collapse(): pl.pallas_call(functools.partial(collapse_kernel, places, len(a)), out_sh...  2.17 us
  transfers between devices with their start and end apart: 27, of which 11 were waited for; matrix products, arithmetic and copies ran while one was open for 1% of the time, Pallas kernels for 13%

profile of v7, /device:TPU:0, one launch (start us, length us, event | category | flops | bytes accessed | tf_op | source)
XLA Modules:
  0.0 91.2 jit_solution(6816580144874197699)
XLA Ops:
  3.5 1.8 %strips.1 = bf16[288,128]{1,0:T(8,128)(2,1)S(1)} custom-call(s32[1]{0:T(128)S(6)} %copy.12.cell, bf16[1,3,128,1024]{3,2,1,0:T(8,128)(2,1)S(1)} %copy-done.7, bf16[1,3,128,1024]{3,2,1,0:T(8,128)(2,1)S(1)} %copy-done.7, bf16[512,512]{1,0:T(8,128)(2,1)S(1)} %copy-done.11), custom_call_target="tpu_custom_call" | custom-call | flops 2000000000 | bytes 1000000 | tf_op jit(solution)/shard_map/strips/pallas_call | solution.py:247
  5.9 2.6 %collective-permute-start = (bf16[288,128]{1,0:T(8,128)(2,1)S(1)}, bf16[288,128]{1,0:T(8,128)(2,1)S(1)}, u32[]{:S(2)}, u32[]{:S(2)}) collective-permute-start(bf16[288,128]{1,0:T(8,128)(2,1)S(1)} %strips.1), channel_id=1, source_target_pairs={{0,4},{4,0},{8,12},{12,8},{16,20},{20,16},{24,28},{28,24},{1,5},{5... | collective-permute-start | bytes 221192 | tf_op jit(solution)/shard_map/ppermute | solution.py:579
  8.5 4.7 %bands.1 = (bf16[32,32,128]{2,1,0:T(8,128)(2,1)S(1)}, f32[816,1024]{1,0:T(8,128)S(1)}) custom-call(bf16[1,3,128,1024]{3,2,1,0:T(8,128)(2,1)S(1)} %copy-done.7, bf16[1,128,1024]{2,1,0:T(8,128)(2,1)S(1)} %copy-done.8, s32[1,64,128]{2,1,0:T(8,128)S(1)} %bitcast.13, bf16[512,512]{1,0:T(8,128)(2,1)S(1)} %copy-done.11, bf16[512,640]{1,0:T(8,128)(2,1)S(1)} %copy-done.10), custom_call_target="tpu_custom_call" | custom-call | flops 8000000000 | bytes 6000000 | tf_op jit(solution)/shard_map/bands/pallas_call | solution.py:339
  16.2 1.6 %collective-permute-start.1 = (bf16[288,128]{1,0:T(8,128)(2,1)S(1)}, bf16[288,128]{1,0:T(8,128)(2,1)S(1)}, u32[]{:S(2)}, u32[]{:S(2)}) collective-permute-start(bf16[288,128]{1,0:T(8,128)(2,1)S(1)} %broadcast_select_fusion), channel_id=1, source_target_pairs={{0,8},{4,12},{8,0},{12,4},{16,24},{20,28},{24,16},{28,20},{1,9},{5... | collective-permute-start | bytes 221192 | tf_op jit(solution)/shard_map/ppermute | solution.py:579
  18.9 4.4 %collective-permute-done.3.c = bf16[32,32,128]{2,1,0:T(8,128)(2,1)} collective-permute-done((bf16[32,32,128]{2,1,0:T(8,128)(2,1)}, bf16[32,32,128]{2,1,0:T(8,128)(2,1)}, u32[]{:S(2)}, u32[]{:S(2)}) %collective-permute-start.3) | collective-permute-done | bytes 262176 | tf_op jit(solution)/shard_map/ppermute | solution.py:579
  23.4 2.7 %collective-permute-start.2 = (bf16[288,128]{1,0:T(8,128)(2,1)S(1)}, bf16[288,128]{1,0:T(8,128)(2,1)S(1)}, u32[]{:S(2)}, u32[]{:S(2)}) collective-permute-start(bf16[288,128]{1,0:T(8,128)(2,1)S(1)} %broadcast_select_fusion.1), channel_id=1, source_target_pairs={{0,16},{4,20},{8,24},{12,28},{16,0},{20,4},{24,8},{28,12},{1,17},{... | collective-permute-start | bytes 221192 | tf_op jit(solution)/shard_map/ppermute | solution.py:579
  26.7 1.6 %routes.2 = (s32[4,33]{1,0:T(4,128)}, s32[4]{0:T(128)}) custom-call(s32[4,32]{1,0:T(4,128)} %get-tuple-element.138.spot), custom_call_target="tpu_custom_call" | custom-call | tf_op jit(solution)/shard_map/routes/pallas_call | solution.py:433
  28.4 2.3 %collective-permute-done.2 = bf16[288,128]{1,0:T(8,128)(2,1)S(1)} collective-permute-done((bf16[288,128]{1,0:T(8,128)(2,1)S(1)}, bf16[288,128]{1,0:T(8,128)(2,1)S(1)}, u32[]{:S(2)}, u32[]{:S(2)}) %collective-permute-start.2) | collective-permute-done | bytes 73760 | tf_op jit(solution)/shard_map/ppermute | solution.py:579
  30.6 2.3 %blend.1 = (bf16[32,80,128]{2,1,0:T(8,128)(2,1)}, bf16[32,64,128]{2,1,0:T(8,128)(2,1)}) custom-call(s32[1]{0:T(128)S(6)} %copy.12.cell, bf16[288,128]{1,0:T(8,128)(2,1)S(1)} %broadcast_select_fusion.2.strips, f32[816,1024]{1,0:T(8,128)S(1)} %get-tuple-element.81.state), custom_call_target="tpu_custom_call" | custom-call | flops 1000000 | bytes 10000 | tf_op jit(solution)/shard_map/blend/pallas_call | solution.py:410
  33.9 1.9 %gather_rows.3 = (f32[16,32,128]{2,1,0:T(8,128)S(1)}, bf16[16,32,128]{2,1,0:T(8,128)(2,1)S(1)}) custom-call(s32[4,33]{1,0:T(4,128)S(1)} %copy-done.3, s32[4]{0:T(128)S(1)} %copy-done.4, bf16[32,32,128]{2,1,0:T(8,128)(2,1)S(1)} %copy-done.2, bf16[32,32,128]{2,1,0:T(8,128)(2,1)} %collective-permute-done.4.b, bf16[32,32,128]{2,1,0:T(8,128)(2,1)} %collective-permute-done.3.c, ...), custom_call_target="tpu_custom_call" | custom-call | flops 1000000 | bytes 10000 | tf_op jit(solution)/shard_map/gather_rows/pallas_call | solution.py:462
  37.1 1.7 %collective-permute-start.9 = (bf16[32,80,128]{2,1,0:T(8,128)(2,1)}, bf16[32,80,128]{2,1,0:T(8,128)(2,1)S(1)}, u32[]{:S(2)}, u32[]{:S(2)}) collective-permute-start(bf16[32,80,128]{2,1,0:T(8,128)(2,1)} %get-tuple-element.86.a), channel_id=1, source_target_pairs={{0,2},{1,3},{2,0},{3,1},{4,6},{5,7},{6,4},{7,5},{8,10},{9,11},{10,... | collective-permute-start | bytes 1966088 | tf_op jit(solution)/shard_map/ppermute | solution.py:579
  40.5 9.8 %collective-permute-done.12.got = bf16[16,32,128]{2,1,0:T(8,128)(2,1)S(1)} collective-permute-done((bf16[16,32,128]{2,1,0:T(8,128)(2,1)S(1)}, bf16[16,32,128]{2,1,0:T(8,128)(2,1)S(1)}, u32[]{:S(2)}, u32[]{:S(2)}) %collective-permute-start.12) | collective-permute-done | bytes 131104 | tf_op jit(solution)/shard_map/ppermute | solution.py:579
  51.2 3.4 %collective-permute-start.16 = (bf16[4,32,128]{2,1,0:T(8,128)(2,1)S(1)}, bf16[4,32,128]{2,1,0:T(8,128)(2,1)S(1)}, u32[]{:S(2)}, u32[]{:S(2)}) collective-permute-start(bf16[4,32,128]{2,1,0:T(8,128)(2,1)S(1)} %get-tuple-element.110), channel_id=1, source_target_pairs={{0,16},{4,20},{8,24},{12,28},{16,0},{20,4},{24,8},{28,12},{1,17},{... | collective-permute-start | bytes 98312 | tf_op jit(solution)/shard_map/ppermute | solution.py:579
  56.2 1.8 %gather_rows.4 = (f32[16,64,128]{2,1,0:T(8,128)S(1)}, bf16[16,64,128]{2,1,0:T(8,128)(2,1)S(1)}) custom-call(s32[4,33]{1,0:T(4,128)S(1)} %copy-done.5, s32[4]{0:T(128)S(1)} %copy-done.6, bf16[32,64,128]{2,1,0:T(8,128)(2,1)} %get-tuple-element.87.a, bf16[32,64,128]{2,1,0:T(8,128)(2,1)S(1)} %collective-permute-done.11.b, ...), custom_call_target="tpu_custom_call" | custom-call | flops 1000000 | bytes 10000 | tf_op jit(solution)/shard_map/gather_rows/pallas_call | solution.py:462
  58.1 2.3 %collective-permute-done.17.refs_3_ = bf16[4,32,128]{2,1,0:T(8,128)(2,1)S(1)} collective-permute-done((bf16[4,32,128]{2,1,0:T(8,128)(2,1)S(1)}, bf16[4,32,128]{2,1,0:T(8,128)(2,1)S(1)}, u32[]{:S(2)}, u32[]{:S(2)}) %collective-permute-start.17) | collective-permute-done | bytes 32800 | tf_op jit(solution)/shard_map/ppermute | solution.py:579
  61.8 7.2 %collective-permute-done.19.got = bf16[16,64,128]{2,1,0:T(8,128)(2,1)S(1)} collective-permute-done((bf16[16,64,128]{2,1,0:T(8,128)(2,1)S(1)}, bf16[16,64,128]{2,1,0:T(8,128)(2,1)S(1)}, u32[]{:S(2)}, u32[]{:S(2)}) %collective-permute-start.19) | collective-permute-done | bytes 262176 | tf_op jit(solution)/shard_map/ppermute | solution.py:579
  69.1 2.0 %gather_rows.5 = (f32[16,80,128]{2,1,0:T(8,128)S(1)}, bf16[16,80,128]{2,1,0:T(8,128)(2,1)S(1)}) custom-call(s32[4,33]{1,0:T(4,128)S(1)} %copy-done.3, s32[4]{0:T(128)S(1)} %copy-done.4, bf16[32,80,128]{2,1,0:T(8,128)(2,1)} %get-tuple-element.86.a, bf16[32,80,128]{2,1,0:T(8,128)(2,1)S(1)} %collective-permute-done.10.b, ...), custom_call_target="tpu_custom_call" | custom-call | flops 1000000 | bytes 10000 | tf_op jit(solution)/shard_map/gather_rows/pallas_call | solution.py:462
  71.4 1.9 %collective-permute-start.22 = (bf16[4,64,128]{2,1,0:T(8,128)(2,1)S(1)}, bf16[4,64,128]{2,1,0:T(8,128)(2,1)S(1)}, u32[]{:S(2)}, u32[]{:S(2)}) collective-permute-start(bf16[4,64,128]{2,1,0:T(8,128)(2,1)S(1)} %get-tuple-element.126), channel_id=1, source_target_pairs={{0,16},{4,20},{8,24},{12,28},{16,0},{20,4},{24,8},{28,12},{1,17},{... | collective-permute-start | bytes 196616 | tf_op jit(solution)/shard_map/ppermute | solution.py:579
  73.3 2.5 %collective-permute-start.23 = (bf16[4,64,128]{2,1,0:T(8,128)(2,1)S(1)}, bf16[4,64,128]{2,1,0:T(8,128)(2,1)S(1)}, u32[]{:S(2)}, u32[]{:S(2)}) collective-permute-start(bf16[4,64,128]{2,1,0:T(8,128)(2,1)S(1)} %get-tuple-element.127), channel_id=1, source_target_pairs={{0,24},{4,28},{8,16},{12,20},{16,8},{20,12},{24,0},{28,4},{1,25},{... | collective-permute-start | bytes 196616 | tf_op jit(solution)/shard_map/ppermute | solution.py:579
  76.1 3.5 %collective-permute-done.22.refs_10_ = bf16[4,64,128]{2,1,0:T(8,128)(2,1)S(1)} collective-permute-done((bf16[4,64,128]{2,1,0:T(8,128)(2,1)S(1)}, bf16[4,64,128]{2,1,0:T(8,128)(2,1)S(1)}, u32[]{:S(2)}, u32[]{:S(2)}) %collective-permute-start.22) | collective-permute-done | bytes 65568 | tf_op jit(solution)/shard_map/ppermute | solution.py:579
  81.0 1.7 %collective-permute-start.25 = (bf16[4,80,128]{2,1,0:T(8,128)(2,1)S(1)}, bf16[4,80,128]{2,1,0:T(8,128)(2,1)S(1)}, u32[]{:S(2)}, u32[]{:S(2)}) collective-permute-start(bf16[4,80,128]{2,1,0:T(8,128)(2,1)S(1)} %get-tuple-element.131), channel_id=1, source_target_pairs={{0,16},{4,20},{8,24},{12,28},{16,0},{20,4},{24,8},{28,12},{1,17},{... | collective-permute-start | bytes 245768 | tf_op jit(solution)/shard_map/ppermute | solution.py:579
  82.7 2.1 %collective-permute-start.26 = (bf16[4,80,128]{2,1,0:T(8,128)(2,1)S(1)}, bf16[4,80,128]{2,1,0:T(8,128)(2,1)S(1)}, u32[]{:S(2)}, u32[]{:S(2)}) collective-permute-start(bf16[4,80,128]{2,1,0:T(8,128)(2,1)S(1)} %get-tuple-element.132), channel_id=1, source_target_pairs={{0,24},{4,28},{8,16},{12,20},{16,8},{20,12},{24,0},{28,4},{1,25},{... | collective-permute-start | bytes 245768 | tf_op jit(solution)/shard_map/ppermute | solution.py:579
  84.8 3.0 %collective-permute-done.25.refs_6_ = bf16[4,80,128]{2,1,0:T(8,128)(2,1)S(1)} collective-permute-done((bf16[4,80,128]{2,1,0:T(8,128)(2,1)S(1)}, bf16[4,80,128]{2,1,0:T(8,128)(2,1)S(1)}, u32[]{:S(2)}, u32[]{:S(2)}) %collective-permute-start.25) | collective-permute-done | bytes 81952 | tf_op jit(solution)/shard_map/ppermute | solution.py:579
  89.0 2.2 %collapse.1 = f32[3,4,4096]{2,1,0:T(4,128)} custom-call(bf16[192,1280]{1,0:T(8,128)(2,1)S(1)} %copy-done, f32[4,32,128]{2,1,0:T(8,128)S(1)} %get-tuple-element.112.refs_0_, bf16[4,32,128]{2,1,0:T(8,128)(2,1)S(1)} %collective-permute-done.15.refs_1_, bf16[4,32,128]{2,1,0:T(8,128)(2,1)S(1)} %collective-permute-done.16.refs_2_, ...), custom_call_target="tpu_custom_call" | custom-call | flops 1000000 | bytes 10000 | tf_op jit(solution)/shard_map/collapse/pallas_call | solution.py:566
  (72 shorter events, 18.6 us)
Async XLA Ops:
  5.4 12.5 %collective-permute-start.6 = (s32[32]{0:T(128)S(1)}, s32[32]{0:T(128)S(1)}, u32[]{:S(2)}, u32[]{:S(2)}) collective-permute-start(s32[32]{0:T(128)S(1)} %bitcast_add_fusion), channel_id=1, source_target_pairs={{0,1},{1,0},{2,3},{3,2},{4,5},{5,4},{6,7},{7,6},{8,9},{9,8},{10,11... | collective-permute-start | bytes 392 | tf_op jit(solution)/shard_map/ppermute | solution.py:579
  5.9 8.7 %collective-permute-start = (bf16[288,128]{1,0:T(8,128)(2,1)S(1)}, bf16[288,128]{1,0:T(8,128)(2,1)S(1)}, u32[]{:S(2)}, u32[]{:S(2)}) collective-permute-start(bf16[288,128]{1,0:T(8,128)(2,1)S(1)} %strips.1), channel_id=1, source_target_pairs={{0,4},{4,0},{8,12},{12,8},{16,20},{20,16},{24,28},{28,24},{1,5},{5... | collective-permute-start | bytes 221192 | tf_op jit(solution)/shard_map/ppermute | solution.py:579
  14.6 8.8 %collective-permute-start.3 = (bf16[32,32,128]{2,1,0:T(8,128)(2,1)}, bf16[32,32,128]{2,1,0:T(8,128)(2,1)}, u32[]{:S(2)}, u32[]{:S(2)}) collective-permute-start(bf16[32,32,128]{2,1,0:T(8,128)(2,1)} %copy-done.1), channel_id=1, source_target_pairs={{0,2},{1,3},{2,0},{3,1},{4,6},{5,7},{6,4},{7,5},{8,10},{9,11},{10,... | collective-permute-start | bytes 786440 | tf_op jit(solution)/shard_map/ppermute | solution.py:579
  16.2 7.2 %collective-permute-start.1 = (bf16[288,128]{1,0:T(8,128)(2,1)S(1)}, bf16[288,128]{1,0:T(8,128)(2,1)S(1)}, u32[]{:S(2)}, u32[]{:S(2)}) collective-permute-start(bf16[288,128]{1,0:T(8,128)(2,1)S(1)} %broadcast_select_fusion), channel_id=1, source_target_pairs={{0,8},{4,12},{8,0},{12,4},{16,24},{20,28},{24,16},{28,20},{1,9},{5... | collective-permute-start | bytes 221192 | tf_op jit(solution)/shard_map/ppermute | solution.py:579
  17.8 8.2 %collective-permute-start.8 = (s32[2,32]{1,0:T(2,128)S(1)}, s32[2,32]{1,0:T(2,128)S(1)}, u32[]{:S(2)}, u32[]{:S(2)}) collective-permute-start(s32[2,32]{1,0:T(2,128)S(1)} %pad_add_fusion.3), channel_id=1, source_target_pairs={{0,4},{4,0},{8,12},{12,8},{16,20},{20,16},{24,28},{28,24},{1,5},{5... | collective-permute-start | bytes 776 | tf_op jit(solution)/shard_map/ppermute | solution.py:579
  18.4 7.7 %collective-permute-start.7 = (s32[2,32]{1,0:T(2,128)S(1)}, s32[2,32]{1,0:T(2,128)S(1)}, u32[]{:S(2)}, u32[]{:S(2)}) collective-permute-start(s32[2,32]{1,0:T(2,128)S(1)} %pad_add_fusion.3), channel_id=1, source_target_pairs={{0,2},{1,3},{2,0},{3,1},{4,6},{5,7},{6,4},{7,5},{8,10},{9,11},{10,... | collective-permute-start | bytes 776 | tf_op jit(solution)/shard_map/ppermute | solution.py:579
  18.9 11.7 %collective-permute-start.4 = (bf16[32,32,128]{2,1,0:T(8,128)(2,1)}, bf16[32,32,128]{2,1,0:T(8,128)(2,1)}, u32[]{:S(2)}, u32[]{:S(2)}) collective-permute-start(bf16[32,32,128]{2,1,0:T(8,128)(2,1)} %copy-done.1), channel_id=1, source_target_pairs={{0,1},{1,0},{2,3},{3,2},{4,5},{5,4},{6,7},{7,6},{8,9},{9,8},{10,11... | collective-permute-start | bytes 786440 | tf_op jit(solution)/shard_map/ppermute | solution.py:579
  23.4 7.3 %collective-permute-start.5 = (bf16[32,32,128]{2,1,0:T(8,128)(2,1)}, bf16[32,32,128]{2,1,0:T(8,128)(2,1)}, u32[]{:S(2)}, u32[]{:S(2)}) collective-permute-start(bf16[32,32,128]{2,1,0:T(8,128)(2,1)} %collective-permute-done.3.c), channel_id=1, source_target_pairs={{0,1},{1,0},{2,3},{3,2},{4,5},{5,4},{6,7},{7,6},{8,9},{9,8},{10,11... | collective-permute-start | bytes 786440 | tf_op jit(solution)/shard_map/ppermute | solution.py:579
  23.4 7.2 %collective-permute-start.2 = (bf16[288,128]{1,0:T(8,128)(2,1)S(1)}, bf16[288,128]{1,0:T(8,128)(2,1)S(1)}, u32[]{:S(2)}, u32[]{:S(2)}) collective-permute-start(bf16[288,128]{1,0:T(8,128)(2,1)S(1)} %broadcast_select_fusion.1), channel_id=1, source_target_pairs={{0,16},{4,20},{8,24},{12,28},{16,0},{20,4},{24,8},{28,12},{1,17},{... | collective-permute-start | bytes 221192 | tf_op jit(solution)/shard_map/ppermute | solution.py:579
  32.9 17.4 %collective-permute-start.10 = (bf16[32,80,128]{2,1,0:T(8,128)(2,1)}, bf16[32,80,128]{2,1,0:T(8,128)(2,1)S(1)}, u32[]{:S(2)}, u32[]{:S(2)}) collective-permute-start(bf16[32,80,128]{2,1,0:T(8,128)(2,1)} %get-tuple-element.86.a), channel_id=1, source_target_pairs={{0,1},{1,0},{2,3},{3,2},{4,5},{5,4},{6,7},{7,6},{8,9},{9,8},{10,11... | collective-permute-start | bytes 1966088 | tf_op jit(solution)/shard_map/ppermute | solution.py:579
  32.9 17.4 %collective-permute-start.11 = (bf16[32,64,128]{2,1,0:T(8,128)(2,1)}, bf16[32,64,128]{2,1,0:T(8,128)(2,1)S(1)}, u32[]{:S(2)}, u32[]{:S(2)}) collective-permute-start(bf16[32,64,128]{2,1,0:T(8,128)(2,1)} %get-tuple-element.87.a), channel_id=1, source_target_pairs={{0,1},{1,0},{2,3},{3,2},{4,5},{5,4},{6,7},{7,6},{8,9},{9,8},{10,11... | collective-permute-start | bytes 1572872 | tf_op jit(solution)/shard_map/ppermute | solution.py:579
  33.4 16.9 %collective-permute-start.13 = (bf16[32,64,128]{2,1,0:T(8,128)(2,1)}, bf16[32,64,128]{2,1,0:T(8,128)(2,1)S(1)}, u32[]{:S(2)}, u32[]{:S(2)}) collective-permute-start(bf16[32,64,128]{2,1,0:T(8,128)(2,1)} %get-tuple-element.87.a), channel_id=1, source_target_pairs={{0,4},{4,0},{8,12},{12,8},{16,20},{20,16},{24,28},{28,24},{1,5},{5... | collective-permute-start | bytes 1572872 | tf_op jit(solution)/shard_map/ppermute | solution.py:579
  35.8 14.5 %collective-permute-start.12 = (bf16[16,32,128]{2,1,0:T(8,128)(2,1)S(1)}, bf16[16,32,128]{2,1,0:T(8,128)(2,1)S(1)}, u32[]{:S(2)}, u32[]{:S(2)}) collective-permute-start(bf16[16,32,128]{2,1,0:T(8,128)(2,1)S(1)} %get-tuple-element.93), channel_id=1, source_target_pairs={{0,4},{4,0},{8,12},{12,8},{16,20},{20,16},{24,28},{28,24},{1,5},{5... | collective-permute-start | bytes 393224 | tf_op jit(solution)/shard_map/ppermute | solution.py:579
  37.1 20.9 %collective-permute-start.9 = (bf16[32,80,128]{2,1,0:T(8,128)(2,1)}, bf16[32,80,128]{2,1,0:T(8,128)(2,1)S(1)}, u32[]{:S(2)}, u32[]{:S(2)}) collective-permute-start(bf16[32,80,128]{2,1,0:T(8,128)(2,1)} %get-tuple-element.86.a), channel_id=1, source_target_pairs={{0,2},{1,3},{2,0},{3,1},{4,6},{5,7},{6,4},{7,5},{8,10},{9,11},{10,... | collective-permute-start | bytes 1966088 | tf_op jit(solution)/shard_map/ppermute | solution.py:579
  50.4 7.6 %collective-permute-start.15 = (bf16[4,32,128]{2,1,0:T(8,128)(2,1)S(1)}, bf16[4,32,128]{2,1,0:T(8,128)(2,1)S(1)}, u32[]{:S(2)}, u32[]{:S(2)}) collective-permute-start(bf16[4,32,128]{2,1,0:T(8,128)(2,1)S(1)} %get-tuple-element.109), channel_id=1, source_target_pairs={{0,8},{4,12},{8,0},{12,4},{16,24},{20,28},{24,16},{28,20},{1,9},{5... | collective-permute-start | bytes 98312 | tf_op jit(solution)/shard_map/ppermute | solution.py:579
  51.2 6.8 %collective-permute-start.16 = (bf16[4,32,128]{2,1,0:T(8,128)(2,1)S(1)}, bf16[4,32,128]{2,1,0:T(8,128)(2,1)S(1)}, u32[]{:S(2)}, u32[]{:S(2)}) collective-permute-start(bf16[4,32,128]{2,1,0:T(8,128)(2,1)S(1)} %get-tuple-element.110), channel_id=1, source_target_pairs={{0,16},{4,20},{8,24},{12,28},{16,0},{20,4},{24,8},{28,12},{1,17},{... | collective-permute-start | bytes 98312 | tf_op jit(solution)/shard_map/ppermute | solution.py:579
  54.6 5.7 %collective-permute-start.17 = (bf16[4,32,128]{2,1,0:T(8,128)(2,1)S(1)}, bf16[4,32,128]{2,1,0:T(8,128)(2,1)S(1)}, u32[]{:S(2)}, u32[]{:S(2)}) collective-permute-start(bf16[4,32,128]{2,1,0:T(8,128)(2,1)S(1)} %get-tuple-element.111), channel_id=1, source_target_pairs={{0,24},{4,28},{8,16},{12,20},{16,8},{20,12},{24,0},{28,4},{1,25},{... | collective-permute-start | bytes 98312 | tf_op jit(solution)/shard_map/ppermute | solution.py:579
  60.3 8.7 %collective-permute-start.18 = (bf16[32,80,128]{2,1,0:T(8,128)(2,1)S(1)}, bf16[32,80,128]{2,1,0:T(8,128)(2,1)S(1)}, u32[]{:S(2)}, u32[]{:S(2)}) collective-permute-start(bf16[32,80,128]{2,1,0:T(8,128)(2,1)S(1)} %collective-permute-done.9.c), channel_id=1, source_target_pairs={{0,1},{1,0},{2,3},{3,2},{4,5},{5,4},{6,7},{7,6},{8,9},{9,8},{10,11... | collective-permute-start | bytes 1966088 | tf_op jit(solution)/shard_map/ppermute | solution.py:579
  60.3 8.7 %collective-permute-start.19 = (bf16[16,64,128]{2,1,0:T(8,128)(2,1)S(1)}, bf16[16,64,128]{2,1,0:T(8,128)(2,1)S(1)}, u32[]{:S(2)}, u32[]{:S(2)}) collective-permute-start(bf16[16,64,128]{2,1,0:T(8,128)(2,1)S(1)} %get-tuple-element.118), channel_id=1, source_target_pairs={{0,2},{1,3},{2,0},{3,1},{4,6},{5,7},{6,4},{7,5},{8,10},{9,11},{10,... | collective-permute-start | bytes 786440 | tf_op jit(solution)/shard_map/ppermute | solution.py:579
  71.1 9.2 %collective-permute-start.20 = (bf16[16,80,128]{2,1,0:T(8,128)(2,1)S(1)}, bf16[16,80,128]{2,1,0:T(8,128)(2,1)S(1)}, u32[]{:S(2)}, u32[]{:S(2)}) collective-permute-start(bf16[16,80,128]{2,1,0:T(8,128)(2,1)S(1)} %get-tuple-element.121), channel_id=1, source_target_pairs={{0,4},{4,0},{8,12},{12,8},{16,20},{20,16},{24,28},{28,24},{1,5},{5... | collective-permute-start | bytes 983048 | tf_op jit(solution)/shard_map/ppermute | solution.py:579
  71.4 8.2 %collective-permute-start.22 = (bf16[4,64,128]{2,1,0:T(8,128)(2,1)S(1)}, bf16[4,64,128]{2,1,0:T(8,128)(2,1)S(1)}, u32[]{:S(2)}, u32[]{:S(2)}) collective-permute-start(bf16[4,64,128]{2,1,0:T(8,128)(2,1)S(1)} %get-tuple-element.126), channel_id=1, source_target_pairs={{0,16},{4,20},{8,24},{12,28},{16,0},{20,4},{24,8},{28,12},{1,17},{... | collective-permute-start | bytes 196616 | tf_op jit(solution)/shard_map/ppermute | solution.py:579
  73.3 6.3 %collective-permute-start.23 = (bf16[4,64,128]{2,1,0:T(8,128)(2,1)S(1)}, bf16[4,64,128]{2,1,0:T(8,128)(2,1)S(1)}, u32[]{:S(2)}, u32[]{:S(2)}) collective-permute-start(bf16[4,64,128]{2,1,0:T(8,128)(2,1)S(1)} %get-tuple-element.127), channel_id=1, source_target_pairs={{0,24},{4,28},{8,16},{12,20},{16,8},{20,12},{24,0},{28,4},{1,25},{... | collective-permute-start | bytes 196616 | tf_op jit(solution)/shard_map/ppermute | solution.py:579
  81.0 6.9 %collective-permute-start.25 = (bf16[4,80,128]{2,1,0:T(8,128)(2,1)S(1)}, bf16[4,80,128]{2,1,0:T(8,128)(2,1)S(1)}, u32[]{:S(2)}, u32[]{:S(2)}) collective-permute-start(bf16[4,80,128]{2,1,0:T(8,128)(2,1)S(1)} %get-tuple-element.131), channel_id=1, source_target_pairs={{0,16},{4,20},{8,24},{12,28},{16,0},{20,4},{24,8},{28,12},{1,17},{... | collective-permute-start | bytes 245768 | tf_op jit(solution)/shard_map/ppermute | solution.py:579
  82.7 6.3 %collective-permute-start.26 = (bf16[4,80,128]{2,1,0:T(8,128)(2,1)S(1)}, bf16[4,80,128]{2,1,0:T(8,128)(2,1)S(1)}, u32[]{:S(2)}, u32[]{:S(2)}) collective-permute-start(bf16[4,80,128]{2,1,0:T(8,128)(2,1)S(1)} %get-tuple-element.132), channel_id=1, source_target_pairs={{0,24},{4,28},{8,16},{12,20},{16,8},{20,12},{24,0},{28,4},{1,25},{... | collective-permute-start | bytes 245768 | tf_op jit(solution)/shard_map/ppermute | solution.py:579
  (15 other events, 88.4 us)

commit v8 on v7

--- a/solution.py
+++ b/solution.py
@@ -439,14 +439,19 @@
     )(spot)
 
 
-def gather_kernel(lists, counts, a, b, c, d, home, away, acc):
+def gather_kernel(lists, counts, *refs):
+    home, away, acc = refs[-3:]
     acc[...] = jnp.zeros_like(acc)
-    for source, ref in enumerate((a, b, c, d)):
-
-        def body(i, carry, source=source, ref=ref):
+    for source in range(4):
+
+        def body(i, carry, source=source):
             entry = lists[source, i]
             q, at = entry // ROUTE, entry % ROUTE
-            acc[at] = acc[at] + ref[q].astype(F32)
+            lo = 0
+            for ref in refs[source:-3:4]:
+                hi = lo + ref.shape[1]
+                acc[at, lo:hi, :] = acc[at, lo:hi, :] + ref[q].astype(F32)
+                lo = hi
             return carry
 
         lax.fori_loop(0, counts[source], body, 0)
@@ -456,12 +461,12 @@
 
 
 def gather_rows(routes, rows, tiles):
-    height = rows[0].shape[1]
+    height = sum(each.shape[1] for each in rows[::4])
     vmem = pl.BlockSpec(memory_space=pltpu.VMEM)
     shape = (tiles // 2, height, 128)
     return pl.pallas_call(
         gather_kernel,
-        in_specs=[pl.BlockSpec(memory_space=pltpu.SMEM)] * 2 + [vmem] * 4,
+        in_specs=[pl.BlockSpec(memory_space=pltpu.SMEM)] * 2 + [vmem] * len(rows),
         out_shape=[jax.ShapeDtypeStruct(shape, F32), jax.ShapeDtypeStruct(shape, BF16)],
         scratch_shapes=[pltpu.VMEM((tiles, height, 128), F32)],
         compiler_params=pltpu.CompilerParams(vmem_limit_bytes=VMEM),
@@ -522,8 +527,8 @@
 
 def collapse_kernel(places, each, packed, *refs):
     mats = unpack(packed, places)
-    a, b, c = (refs[i * each : (i + 1) * each] for i in range(3))
-    out, level0 = refs[3 * each :]
+    b, c = (refs[i * each : (i + 1) * each] for i in range(2))
+    out, level0 = refs[2 * each :]
 
     def total(sources, lo, hi):
         acc = sources[0][:, lo:hi, :]
@@ -551,7 +556,7 @@
     hi, lo = split(wide)
     up = mm(mats["even"], hi) + mm(mats["even"], lo)
     down = mm(mats["odd"], hi) + mm(mats["odd"], lo)
-    bottom = jnp.maximum(total(a, 0, 32), 1.0)
+    bottom = jnp.maximum(total(c, 64, 96), 1.0)
     for ch in range(COLOURS):
         own = total(b, 0, 32) if ch == 0 else total(c, 32 * (ch - 1), 32 * ch)
         back = jnp.where(lane < 64, up[:, ch * 128 : ch * 128 + 128], down[:, ch * 128 : ch * 128 + 128])
@@ -561,16 +566,16 @@
             out[ch, :, row * 128 : row * 128 + 128] = level0[pl.ds(ch * 128 + row, TILE_DEV, stride=32), :]
 
 
-def collapse(a, b, c):
+def collapse(b, c):
     packed, places = collapse_matrices()
     tiles = pl.pallas_call(
-        functools.partial(collapse_kernel, places, len(a)),
+        functools.partial(collapse_kernel, places, len(b)),
         out_shape=jax.ShapeDtypeStruct((COLOURS, TILE_DEV, 4096), F32),
         scratch_shapes=[pltpu.VMEM((COLOURS * 128, 128), F32)],
         compiler_params=pltpu.CompilerParams(vmem_limit_bytes=VMEM),
         cost_estimate=pl.CostEstimate(flops=10**6, bytes_accessed=10**4, transcendentals=0),
         name="collapse",
-    )(packed, *a, *b, *c)
+    )(packed, *b, *c)
     return jnp.swapaxes(tiles, 0, 1)
 
 
@@ -611,10 +616,10 @@
         got = swap(strips, "frames", bit)
         if bit == 1:
             got, weights, state = tie((got, weights, state))
-            far, near = swap(weights, "tiles", 2), swap(weights, "tiles", 1)
+            far, near = swap(weights, "frames", 1), swap(weights, "tiles", 1)
         if bit == half:
             far_near = swap(far, "tiles", 1)
-            got, far, near, far_near, routes_x, spot_y = tie((got, far, near, far_near, routes_of(spot_x), spot_y))
+            got, far, near, far_near, spot_x, spot_y = tie((got, far, near, far_near, spot_x, spot_y))
         strips = jnp.where((mask & bit) != 0, got, strips)
         bit *= 2
 
@@ -625,25 +630,22 @@
         return [own] + [swap(part, "frames", 2 * (j + 1)) for j, part in enumerate(away)]
 
     first, second = blend(strip_cell, strips, state)
-    first, second, near, spot_y = tie((first, second, near, spot_y))
+    first, second, spot_x, spot_y = tie((first, second, spot_x, spot_y))
     far_first, near_first = swap(first, "tiles", 2), swap(first, "tiles", 1)
     far_second, near_second = swap(second, "frames", 1), swap(second, "tiles", 1)
-    home_w, away_w = gather(routes_x, weights, near, far, far_near)
-    got_w = swap(away_w, "frames", 1)
-    near_first, near_second, got_w, routes_y = tie((near_first, near_second, got_w, routes_of(spot_y)))
-    sums_w = add_halves(home_w, got_w)
-    far_second, sums_w = tie((far_second, sums_w))
-    got_weights = along(*sums_w)
-    home_s, away_s = gather(routes_y, second, near_second, far_second, swap(far_second, "tiles", 1))
+    routes_x, routes_y = routes_of(spot_x), routes_of(spot_y)
+    far_second, routes_x, routes_y, near_first = tie((far_second, routes_x, routes_y, near_first))
+    rows = (second, near_second, far_second, swap(far_second, "tiles", 1))
+    home_s, away_s = gather(routes_y, *rows, weights, near, far, far_near)
     got_s = swap(away_s, "tiles", 2)
-    far_first, home_s, got_weights = tie((far_first, home_s, got_weights))
+    far_first, home_s = tie((far_first, home_s))
     far_near, got_s = tie((swap(far_first, "tiles", 1), got_s))
     home_f, away_f = gather(routes_x, first, near_first, far_first, far_near)
     got_f = swap(away_f, "frames", 1)
     got_second = along(*add_halves(home_s, got_s))
     got_f, got_second = tie((got_f, got_second))
     got_first = along(*add_halves(home_f, got_f))
-    return collapse(got_weights, got_first, got_second)
+    return collapse(got_first, got_second)
 
 
 def solution(mesh):

time: 91.7 us -> 98.2 us (1.071)
  local copies, waits for them, and re-layouts: 4.28 us -> 11.5 us
  waiting for transfers between devices: 34.7 us -> 40.9 us
  starting transfers between devices: 29.2 us -> 24.2 us
  Pallas kernels: 20.1 us -> 18.2 us
    unnamed x24 -> x36, local copies, waits for them, and re-layouts: 4.28 us -> 11.5 us
    ppermute x27 -> x23, waiting for transfers between devices: 34.7 us -> 40.9 us  [swap(): return lax.ppermute(value, axis, [(i, i ^ bit) for i in range(size)])]
    ppermute x27 -> x23, starting transfers between devices: 29.2 us -> 24.2 us  [swap(): return lax.ppermute(value, axis, [(i, i ^ bit) for i in range(size)])]
    pallas_call x3 -> x2, Pallas kernels: 5.7 us -> 3.8 us  [gather_rows(): pl.pallas_call(gather_kernel, in_specs=[pl.BlockSpec(memory_space=pltpu.S...]
  transfers between devices with their start and end apart: 27 -> 23, of which waited for: 11 -> 9; matrix products, arithmetic and copies ran while one was open for 1% -> 1% of each run, Pallas kernels for 13% -> 10%
where the time goes in v8:
time: 98.2 us; the launch traced here: 97.6 us
  waiting for transfers between devices  40.9 us (42%)
  starting transfers between devices  24.2 us (25%)
  Pallas kernels  18.2 us (19%)
  local copies, waits for them, and re-layouts  11.5 us (12%)
  between operations  1.47 us (1%)
  other arithmetic  1.34 us (1%)
    ppermute x23, waiting for transfers between devices, swap(): return lax.ppermute(value, axis, [(i, i ^ bit) for i in range(size)])  40.9 us
    ppermute x23, starting transfers between devices, swap(): return lax.ppermute(value, axis, [(i, i ^ bit) for i in range(size)])  24.2 us
    unnamed x36, local copies, waits for them, and re-layouts  11.5 us
    pallas_call x1, Pallas kernels, bands_of(): pl.pallas_call(functools.partial(bands_kernel, small_places, large_places...  4.68 us
    pallas_call x2, Pallas kernels, gather_rows(): pl.pallas_call(gather_kernel, in_specs=[pl.BlockSpec(memory_space=pltpu.S...  3.8 us
    pallas_call x2, Pallas kernels, routes_of(): pl.pallas_call(routes_kernel, in_specs=[smem], out_specs=[smem, smem], ou...  3.29 us
    pallas_call x1, Pallas kernels, blend(): pl.pallas_call(blend_kernel, in_specs=[pl.BlockSpec(memory_space=pltpu.SM...  2.29 us
    pallas_call x1, Pallas kernels, collapse(): pl.pallas_call(functools.partial(collapse_kernel, places, len(b)), out_sh...  2.17 us
  transfers between devices with their start and end apart: 23, of which 9 were waited for; matrix products, arithmetic and copies ran while one was open for 1% of the time, Pallas kernels for 10%

profile of v8, /device:TPU:0, one launch (start us, length us, event | category | flops | bytes accessed | tf_op | source)
XLA Modules:
  0.0 97.6 jit_solution(1495249630953946414)
XLA Ops:
  3.5 1.8 %strips.1 = bf16[288,128]{1,0:T(8,128)(2,1)S(1)} custom-call(s32[1]{0:T(128)S(6)} %copy.12.cell, bf16[1,3,128,1024]{3,2,1,0:T(8,128)(2,1)S(1)} %copy-done.13, bf16[1,3,128,1024]{3,2,1,0:T(8,128)(2,1)S(1)} %copy-done.13, bf16[512,512]{1,0:T(8,128)(2,1)S(1)} %copy-done.17), custom_call_target="tpu_custom_call" | custom-call | flops 2000000000 | bytes 1000000 | tf_op jit(solution)/shard_map/strips/pallas_call | solution.py:247
  5.4 3.0 %collective-permute-start = (bf16[288,128]{1,0:T(8,128)(2,1)S(1)}, bf16[288,128]{1,0:T(8,128)(2,1)S(1)}, u32[]{:S(2)}, u32[]{:S(2)}) collective-permute-start(bf16[288,128]{1,0:T(8,128)(2,1)S(1)} %strips.1), channel_id=1, source_target_pairs={{0,4},{4,0},{8,12},{12,8},{16,20},{20,16},{24,28},{28,24},{1,5},{5... | collective-permute-start | bytes 221192 | tf_op jit(solution)/shard_map/ppermute | solution.py:584
  8.4 4.7 %bands.1 = (bf16[32,32,128]{2,1,0:T(8,128)(2,1)S(1)}, f32[816,1024]{1,0:T(8,128)S(1)}) custom-call(bf16[1,3,128,1024]{3,2,1,0:T(8,128)(2,1)S(1)} %copy-done.13, bf16[1,128,1024]{2,1,0:T(8,128)(2,1)S(1)} %copy-done.14, s32[1,64,128]{2,1,0:T(8,128)S(1)} %bitcast.13, bf16[512,512]{1,0:T(8,128)(2,1)S(1)} %copy-done.17, bf16[512,640]{1,0:T(8,128)(2,1)S(1)} %copy-done.16), custom_call_target="tpu_custom_call" | custom-call | flops 8000000000 | bytes 6000000 | tf_op jit(solution)/shard_map/bands/pallas_call | solution.py:339
  14.7 2.0 %collective-permute-start.1 = (bf16[288,128]{1,0:T(8,128)(2,1)S(1)}, bf16[288,128]{1,0:T(8,128)(2,1)S(1)}, u32[]{:S(2)}, u32[]{:S(2)}) collective-permute-start(bf16[288,128]{1,0:T(8,128)(2,1)S(1)} %broadcast_select_fusion), channel_id=1, source_target_pairs={{0,8},{4,12},{8,0},{12,4},{16,24},{20,28},{24,16},{28,20},{1,9},{5... | collective-permute-start | bytes 221192 | tf_op jit(solution)/shard_map/ppermute | solution.py:584
  16.8 1.6 %collective-permute-start.7 = (s32[2,32]{1,0:T(2,128)S(1)}, s32[2,32]{1,0:T(2,128)S(1)}, u32[]{:S(2)}, u32[]{:S(2)}) collective-permute-start(s32[2,32]{1,0:T(2,128)S(1)} %pad_add_fusion.3), channel_id=1, source_target_pairs={{0,2},{1,3},{2,0},{3,1},{4,6},{5,7},{6,4},{7,5},{8,10},{9,11},{10,... | collective-permute-start | bytes 776 | tf_op jit(solution)/shard_map/ppermute | solution.py:584
  18.3 1.5 %collective-permute-start.8 = (s32[2,32]{1,0:T(2,128)S(1)}, s32[2,32]{1,0:T(2,128)S(1)}, u32[]{:S(2)}, u32[]{:S(2)}) collective-permute-start(s32[2,32]{1,0:T(2,128)S(1)} %pad_add_fusion.3), channel_id=1, source_target_pairs={{0,4},{4,0},{8,12},{12,8},{16,20},{20,16},{24,28},{28,24},{1,5},{5... | collective-permute-start | bytes 776 | tf_op jit(solution)/shard_map/ppermute | solution.py:584
  19.9 3.7 %collective-permute-done.3.refs_6_ = bf16[32,32,128]{2,1,0:T(8,128)(2,1)S(1)} collective-permute-done((bf16[32,32,128]{2,1,0:T(8,128)(2,1)}, bf16[32,32,128]{2,1,0:T(8,128)(2,1)S(1)}, u32[]{:S(2)}, u32[]{:S(2)}) %collective-permute-start.3) | collective-permute-done | bytes 262176 | tf_op jit(solution)/shard_map/ppermute | solution.py:584
  24.3 2.7 %collective-permute-start.2 = (bf16[288,128]{1,0:T(8,128)(2,1)S(1)}, bf16[288,128]{1,0:T(8,128)(2,1)S(1)}, u32[]{:S(2)}, u32[]{:S(2)}) collective-permute-start(bf16[288,128]{1,0:T(8,128)(2,1)S(1)} %broadcast_select_fusion.1), channel_id=1, source_target_pairs={{0,16},{4,20},{8,24},{12,28},{16,0},{20,4},{24,8},{28,12},{1,17},{... | collective-permute-start | bytes 221192 | tf_op jit(solution)/shard_map/ppermute | solution.py:584
  27.5 3.9 %collective-permute-done.2 = bf16[288,128]{1,0:T(8,128)(2,1)S(1)} collective-permute-done((bf16[288,128]{1,0:T(8,128)(2,1)S(1)}, bf16[288,128]{1,0:T(8,128)(2,1)S(1)}, u32[]{:S(2)}, u32[]{:S(2)}) %collective-permute-start.2) | collective-permute-done | bytes 73760 | tf_op jit(solution)/shard_map/ppermute | solution.py:584
  32.9 2.3 %blend.1 = (bf16[32,80,128]{2,1,0:T(8,128)(2,1)}, bf16[32,64,128]{2,1,0:T(8,128)(2,1)}) custom-call(s32[1]{0:T(128)S(6)} %copy.12.cell, bf16[288,128]{1,0:T(8,128)(2,1)S(1)} %broadcast_select_fusion.2.strips, f32[816,1024]{1,0:T(8,128)S(1)} %get-tuple-element.64.state), custom_call_target="tpu_custom_call" | custom-call | flops 1000000 | bytes 10000 | tf_op jit(solution)/shard_map/blend/pallas_call | solution.py:410
  35.7 1.5 %collective-permute-start.11 = (bf16[32,80,128]{2,1,0:T(8,128)(2,1)}, bf16[32,80,128]{2,1,0:T(8,128)(2,1)S(1)}, u32[]{:S(2)}, u32[]{:S(2)}) collective-permute-start(bf16[32,80,128]{2,1,0:T(8,128)(2,1)} %get-tuple-element.76.refs_0_), channel_id=1, source_target_pairs={{0,2},{1,3},{2,0},{3,1},{4,6},{5,7},{6,4},{7,5},{8,10},{9,11},{10,... | collective-permute-start | bytes 1966088 | tf_op jit(solution)/shard_map/ppermute | solution.py:584
  37.2 1.6 %routes.2 = (s32[4,33]{1,0:T(4,128)}, s32[4]{0:T(128)}) custom-call(s32[4,32]{1,0:T(4,128)} %get-tuple-element.70.spot), custom_call_target="tpu_custom_call" | custom-call | tf_op jit(solution)/shard_map/routes/pallas_call | solution.py:433
  38.9 1.6 %routes.3 = (s32[4,33]{1,0:T(4,128)}, s32[4]{0:T(128)}) custom-call(s32[4,32]{1,0:T(4,128)} %get-tuple-element.73.spot), custom_call_target="tpu_custom_call" | custom-call | tf_op jit(solution)/shard_map/routes/pallas_call | solution.py:433
  40.5 9.2 %collective-permute-done.9.refs_2_ = bf16[32,64,128]{2,1,0:T(8,128)(2,1)S(1)} collective-permute-done((bf16[32,64,128]{2,1,0:T(8,128)(2,1)}, bf16[32,64,128]{2,1,0:T(8,128)(2,1)S(1)}, u32[]{:S(2)}, u32[]{:S(2)}) %collective-permute-start.9) | collective-permute-done | bytes 524320 | tf_op jit(solution)/shard_map/ppermute | solution.py:584
  49.8 1.9 %collective-permute-done.13.refs_3_ = bf16[32,64,128]{2,1,0:T(8,128)(2,1)S(1)} collective-permute-done((bf16[32,64,128]{2,1,0:T(8,128)(2,1)S(1)}, bf16[32,64,128]{2,1,0:T(8,128)(2,1)S(1)}, u32[]{:S(2)}, u32[]{:S(2)}) %collective-permute-start.13) | collective-permute-done | bytes 524320 | tf_op jit(solution)/shard_map/ppermute | solution.py:584
  56.8 2.0 %gather_rows.2 = (f32[16,96,128]{2,1,0:T(8,128)S(1)}, bf16[16,96,128]{2,1,0:T(8,128)(2,1)S(1)}) custom-call(s32[4,33]{1,0:T(4,128)S(1)} %copy-done.10, s32[4]{0:T(128)S(1)} %copy-done.12, bf16[32,64,128]{2,1,0:T(8,128)(2,1)} %get-tuple-element.69.refs_0_, bf16[32,64,128]{2,1,0:T(8,128)(2,1)S(1)} %collective-permute-done.12.refs_1_, ...), custom_call_target="tpu_custom_call" | custom-call | flops 1000000 | bytes 10000 | tf_op jit(solution)/shard_map/gather_rows/pallas_call | solution.py:467
  59.0 1.6 %collective-permute-start.15 = (bf16[16,96,128]{2,1,0:T(8,128)(2,1)S(1)}, bf16[16,96,128]{2,1,0:T(8,128)(2,1)S(1)}, u32[]{:S(2)}, u32[]{:S(2)}) collective-permute-start(bf16[16,96,128]{2,1,0:T(8,128)(2,1)S(1)} %get-tuple-element.88), channel_id=1, source_target_pairs={{0,2},{1,3},{2,0},{3,1},{4,6},{5,7},{6,4},{7,5},{8,10},{9,11},{10,... | collective-permute-start | bytes 1179656 | tf_op jit(solution)/shard_map/ppermute | solution.py:584
  60.5 9.9 %collective-permute-done.15.got = bf16[16,96,128]{2,1,0:T(8,128)(2,1)S(1)} collective-permute-done((bf16[16,96,128]{2,1,0:T(8,128)(2,1)S(1)}, bf16[16,96,128]{2,1,0:T(8,128)(2,1)S(1)}, u32[]{:S(2)}, u32[]{:S(2)}) %collective-permute-start.15) | collective-permute-done | bytes 393248 | tf_op jit(solution)/shard_map/ppermute | solution.py:584
  71.7 1.8 %gather_rows.3 = (f32[16,80,128]{2,1,0:T(8,128)S(1)}, bf16[16,80,128]{2,1,0:T(8,128)(2,1)S(1)}) custom-call(s32[4,33]{1,0:T(4,128)S(1)} %copy-done.9, s32[4]{0:T(128)S(1)} %copy-done.11, bf16[32,80,128]{2,1,0:T(8,128)(2,1)} %get-tuple-element.76.refs_0_, bf16[32,80,128]{2,1,0:T(8,128)(2,1)S(1)} %collective-permute-done.10.refs_1_, ...), custom_call_target="tpu_custom_call" | custom-call | flops 1000000 | bytes 10000 | tf_op jit(solution)/shard_map/gather_rows/pallas_call | solution.py:467
  74.6 3.6 %collective-permute-start.18 = (bf16[4,96,128]{2,1,0:T(8,128)(2,1)S(1)}, bf16[4,96,128]{2,1,0:T(8,128)(2,1)S(1)}, u32[]{:S(2)}, u32[]{:S(2)}) collective-permute-start(bf16[4,96,128]{2,1,0:T(8,128)(2,1)S(1)} %get-tuple-element.96), channel_id=1, source_target_pairs={{0,16},{4,20},{8,24},{12,28},{16,0},{20,4},{24,8},{28,12},{1,17},{... | collective-permute-start | bytes 294920 | tf_op jit(solution)/shard_map/ppermute | solution.py:584
  79.9 5.7 %collective-permute-done.18.refs_6_ = bf16[4,96,128]{2,1,0:T(8,128)(2,1)S(1)} collective-permute-done((bf16[4,96,128]{2,1,0:T(8,128)(2,1)S(1)}, bf16[4,96,128]{2,1,0:T(8,128)(2,1)S(1)}, u32[]{:S(2)}, u32[]{:S(2)}) %collective-permute-start.18) | collective-permute-done | bytes 98336 | tf_op jit(solution)/shard_map/ppermute | solution.py:584
  85.6 1.7 %collective-permute-start.20 = (bf16[4,80,128]{2,1,0:T(8,128)(2,1)S(1)}, bf16[4,80,128]{2,1,0:T(8,128)(2,1)S(1)}, u32[]{:S(2)}, u32[]{:S(2)}) collective-permute-start(bf16[4,80,128]{2,1,0:T(8,128)(2,1)S(1)} %get-tuple-element.100), channel_id=1, source_target_pairs={{0,8},{4,12},{8,0},{12,4},{16,24},{20,28},{24,16},{28,20},{1,9},{5... | collective-permute-start | bytes 245768 | tf_op jit(solution)/shard_map/ppermute | solution.py:584
  90.8 4.6 %collective-permute-done.21.refs_2_ = bf16[4,80,128]{2,1,0:T(8,128)(2,1)S(1)} collective-permute-done((bf16[4,80,128]{2,1,0:T(8,128)(2,1)S(1)}, bf16[4,80,128]{2,1,0:T(8,128)(2,1)S(1)}, u32[]{:S(2)}, u32[]{:S(2)}) %collective-permute-start.21) | collective-permute-done | bytes 81952 | tf_op jit(solution)/shard_map/ppermute | solution.py:584
  95.4 2.2 %collapse.1 = f32[3,4,4096]{2,1,0:T(4,128)} custom-call(bf16[192,1280]{1,0:T(8,128)(2,1)S(1)} %copy-done, f32[4,80,128]{2,1,0:T(8,128)S(1)} %get-tuple-element.99.refs_0_, bf16[4,80,128]{2,1,0:T(8,128)(2,1)S(1)} %collective-permute-done.20.refs_1_, bf16[4,80,128]{2,1,0:T(8,128)(2,1)S(1)} %collective-permute-done.21.refs_2_, ...), custom_call_target="tpu_custom_call" | custom-call | flops 1000000 | bytes 10000 | tf_op jit(solution)/shard_map/collapse/pallas_call | solution.py:571
  (74 shorter events, 19.8 us)
Async XLA Ops:
  5.4 9.2 %collective-permute-start = (bf16[288,128]{1,0:T(8,128)(2,1)S(1)}, bf16[288,128]{1,0:T(8,128)(2,1)S(1)}, u32[]{:S(2)}, u32[]{:S(2)}) collective-permute-start(bf16[288,128]{1,0:T(8,128)(2,1)S(1)} %strips.1), channel_id=1, source_target_pairs={{0,4},{4,0},{8,12},{12,8},{16,20},{20,16},{24,28},{28,24},{1,5},{5... | collective-permute-start | bytes 221192 | tf_op jit(solution)/shard_map/ppermute | solution.py:584
  8.4 8.4 %collective-permute-start.6 = (s32[32]{0:T(128)S(1)}, s32[32]{0:T(128)S(1)}, u32[]{:S(2)}, u32[]{:S(2)}) collective-permute-start(s32[32]{0:T(128)S(1)} %bitcast_add_fusion), channel_id=1, source_target_pairs={{0,1},{1,0},{2,3},{3,2},{4,5},{5,4},{6,7},{7,6},{8,9},{9,8},{10,11... | collective-permute-start | bytes 392 | tf_op jit(solution)/shard_map/ppermute | solution.py:584
  14.5 9.0 %collective-permute-start.3 = (bf16[32,32,128]{2,1,0:T(8,128)(2,1)}, bf16[32,32,128]{2,1,0:T(8,128)(2,1)S(1)}, u32[]{:S(2)}, u32[]{:S(2)}) collective-permute-start(bf16[32,32,128]{2,1,0:T(8,128)(2,1)} %copy-done.1), channel_id=1, source_target_pairs={{0,4},{4,0},{8,12},{12,8},{16,20},{20,16},{24,28},{28,24},{1,5},{5... | collective-permute-start | bytes 786440 | tf_op jit(solution)/shard_map/ppermute | solution.py:584
  14.7 9.5 %collective-permute-start.1 = (bf16[288,128]{1,0:T(8,128)(2,1)S(1)}, bf16[288,128]{1,0:T(8,128)(2,1)S(1)}, u32[]{:S(2)}, u32[]{:S(2)}) collective-permute-start(bf16[288,128]{1,0:T(8,128)(2,1)S(1)} %broadcast_select_fusion), channel_id=1, source_target_pairs={{0,8},{4,12},{8,0},{12,4},{16,24},{20,28},{24,16},{28,20},{1,9},{5... | collective-permute-start | bytes 221192 | tf_op jit(solution)/shard_map/ppermute | solution.py:584
  16.8 10.1 %collective-permute-start.7 = (s32[2,32]{1,0:T(2,128)S(1)}, s32[2,32]{1,0:T(2,128)S(1)}, u32[]{:S(2)}, u32[]{:S(2)}) collective-permute-start(s32[2,32]{1,0:T(2,128)S(1)} %pad_add_fusion.3), channel_id=1, source_target_pairs={{0,2},{1,3},{2,0},{3,1},{4,6},{5,7},{6,4},{7,5},{8,10},{9,11},{10,... | collective-permute-start | bytes 776 | tf_op jit(solution)/shard_map/ppermute | solution.py:584
  18.3 8.6 %collective-permute-start.8 = (s32[2,32]{1,0:T(2,128)S(1)}, s32[2,32]{1,0:T(2,128)S(1)}, u32[]{:S(2)}, u32[]{:S(2)}) collective-permute-start(s32[2,32]{1,0:T(2,128)S(1)} %pad_add_fusion.3), channel_id=1, source_target_pairs={{0,4},{4,0},{8,12},{12,8},{16,20},{20,16},{24,28},{28,24},{1,5},{5... | collective-permute-start | bytes 776 | tf_op jit(solution)/shard_map/ppermute | solution.py:584
  19.9 11.6 %collective-permute-start.4 = (bf16[32,32,128]{2,1,0:T(8,128)(2,1)}, bf16[32,32,128]{2,1,0:T(8,128)(2,1)S(1)}, u32[]{:S(2)}, u32[]{:S(2)}) collective-permute-start(bf16[32,32,128]{2,1,0:T(8,128)(2,1)} %copy-done.1), channel_id=1, source_target_pairs={{0,1},{1,0},{2,3},{3,2},{4,5},{5,4},{6,7},{7,6},{8,9},{9,8},{10,11... | collective-permute-start | bytes 786440 | tf_op jit(solution)/shard_map/ppermute | solution.py:584
  23.5 8.6 %collective-permute-start.5 = (bf16[32,32,128]{2,1,0:T(8,128)(2,1)S(1)}, bf16[32,32,128]{2,1,0:T(8,128)(2,1)S(1)}, u32[]{:S(2)}, u32[]{:S(2)}) collective-permute-start(bf16[32,32,128]{2,1,0:T(8,128)(2,1)S(1)} %collective-permute-done.3.refs_6_), channel_id=1, source_target_pairs={{0,1},{1,0},{2,3},{3,2},{4,5},{5,4},{6,7},{7,6},{8,9},{9,8},{10,11... | collective-permute-start | bytes 786440 | tf_op jit(solution)/shard_map/ppermute | solution.py:584
  24.3 7.2 %collective-permute-start.2 = (bf16[288,128]{1,0:T(8,128)(2,1)S(1)}, bf16[288,128]{1,0:T(8,128)(2,1)S(1)}, u32[]{:S(2)}, u32[]{:S(2)}) collective-permute-start(bf16[288,128]{1,0:T(8,128)(2,1)S(1)} %broadcast_select_fusion.1), channel_id=1, source_target_pairs={{0,16},{4,20},{8,24},{12,28},{16,0},{20,4},{24,8},{28,12},{1,17},{... | collective-permute-start | bytes 221192 | tf_op jit(solution)/shard_map/ppermute | solution.py:584
  35.2 14.6 %collective-permute-start.10 = (bf16[32,80,128]{2,1,0:T(8,128)(2,1)}, bf16[32,80,128]{2,1,0:T(8,128)(2,1)S(1)}, u32[]{:S(2)}, u32[]{:S(2)}) collective-permute-start(bf16[32,80,128]{2,1,0:T(8,128)(2,1)} %get-tuple-element.76.refs_0_), channel_id=1, source_target_pairs={{0,1},{1,0},{2,3},{3,2},{4,5},{5,4},{6,7},{7,6},{8,9},{9,8},{10,11... | collective-permute-start | bytes 1966088 | tf_op jit(solution)/shard_map/ppermute | solution.py:584
  35.2 14.5 %collective-permute-start.9 = (bf16[32,64,128]{2,1,0:T(8,128)(2,1)}, bf16[32,64,128]{2,1,0:T(8,128)(2,1)S(1)}, u32[]{:S(2)}, u32[]{:S(2)}) collective-permute-start(bf16[32,64,128]{2,1,0:T(8,128)(2,1)} %get-tuple-element.69.refs_0_), channel_id=1, source_target_pairs={{0,4},{4,0},{8,12},{12,8},{16,20},{20,16},{24,28},{28,24},{1,5},{5... | collective-permute-start | bytes 1572872 | tf_op jit(solution)/shard_map/ppermute | solution.py:584
  35.7 23.1 %collective-permute-start.11 = (bf16[32,80,128]{2,1,0:T(8,128)(2,1)}, bf16[32,80,128]{2,1,0:T(8,128)(2,1)S(1)}, u32[]{:S(2)}, u32[]{:S(2)}) collective-permute-start(bf16[32,80,128]{2,1,0:T(8,128)(2,1)} %get-tuple-element.76.refs_0_), channel_id=1, source_target_pairs={{0,2},{1,3},{2,0},{3,1},{4,6},{5,7},{6,4},{7,5},{8,10},{9,11},{10,... | collective-permute-start | bytes 1966088 | tf_op jit(solution)/shard_map/ppermute | solution.py:584
  37.2 12.6 %collective-permute-start.12 = (bf16[32,64,128]{2,1,0:T(8,128)(2,1)}, bf16[32,64,128]{2,1,0:T(8,128)(2,1)S(1)}, u32[]{:S(2)}, u32[]{:S(2)}) collective-permute-start(bf16[32,64,128]{2,1,0:T(8,128)(2,1)} %get-tuple-element.69.refs_0_), channel_id=1, source_target_pairs={{0,1},{1,0},{2,3},{3,2},{4,5},{5,4},{6,7},{7,6},{8,9},{9,8},{10,11... | collective-permute-start | bytes 1572872 | tf_op jit(solution)/shard_map/ppermute | solution.py:584
  49.7 45.7 %copy-start = (bf16[192,1280]{1,0:T(8,128)(2,1)S(1)}, bf16[192,1280]{1,0:T(8,128)(2,1)}, u32[]{:S(2)}) copy-start(bf16[192,1280]{1,0:T(8,128)(2,1)} %constant.105.clone.packed) | copy-start | bytes 1474564
  49.8 1.9 %collective-permute-start.13 = (bf16[32,64,128]{2,1,0:T(8,128)(2,1)S(1)}, bf16[32,64,128]{2,1,0:T(8,128)(2,1)S(1)}, u32[]{:S(2)}, u32[]{:S(2)}) collective-permute-start(bf16[32,64,128]{2,1,0:T(8,128)(2,1)S(1)} %collective-permute-done.9.refs_2_), channel_id=1, source_target_pairs={{0,1},{1,0},{2,3},{3,2},{4,5},{5,4},{6,7},{7,6},{8,9},{9,8},{10,11... | collective-permute-start | bytes 1572872 | tf_op jit(solution)/shard_map/ppermute | solution.py:584
  58.8 11.6 %collective-permute-start.14 = (bf16[32,80,128]{2,1,0:T(8,128)(2,1)S(1)}, bf16[32,80,128]{2,1,0:T(8,128)(2,1)S(1)}, u32[]{:S(2)}, u32[]{:S(2)}) collective-permute-start(bf16[32,80,128]{2,1,0:T(8,128)(2,1)S(1)} %collective-permute-done.11.refs_2_), channel_id=1, source_target_pairs={{0,1},{1,0},{2,3},{3,2},{4,5},{5,4},{6,7},{7,6},{8,9},{9,8},{10,11... | collective-permute-start | bytes 1966088 | tf_op jit(solution)/shard_map/ppermute | solution.py:584
  59.0 11.4 %collective-permute-start.15 = (bf16[16,96,128]{2,1,0:T(8,128)(2,1)S(1)}, bf16[16,96,128]{2,1,0:T(8,128)(2,1)S(1)}, u32[]{:S(2)}, u32[]{:S(2)}) collective-permute-start(bf16[16,96,128]{2,1,0:T(8,128)(2,1)S(1)} %get-tuple-element.88), channel_id=1, source_target_pairs={{0,2},{1,3},{2,0},{3,1},{4,6},{5,7},{6,4},{7,5},{8,10},{9,11},{10,... | collective-permute-start | bytes 1179656 | tf_op jit(solution)/shard_map/ppermute | solution.py:584
  73.5 12.0 %collective-permute-start.16 = (bf16[16,80,128]{2,1,0:T(8,128)(2,1)S(1)}, bf16[16,80,128]{2,1,0:T(8,128)(2,1)S(1)}, u32[]{:S(2)}, u32[]{:S(2)}) collective-permute-start(bf16[16,80,128]{2,1,0:T(8,128)(2,1)S(1)} %get-tuple-element.91), channel_id=1, source_target_pairs={{0,4},{4,0},{8,12},{12,8},{16,20},{20,16},{24,28},{28,24},{1,5},{5... | collective-permute-start | bytes 983048 | tf_op jit(solution)/shard_map/ppermute | solution.py:584
  74.1 5.7 %collective-permute-start.17 = (bf16[4,96,128]{2,1,0:T(8,128)(2,1)S(1)}, bf16[4,96,128]{2,1,0:T(8,128)(2,1)S(1)}, u32[]{:S(2)}, u32[]{:S(2)}) collective-permute-start(bf16[4,96,128]{2,1,0:T(8,128)(2,1)S(1)} %get-tuple-element.95), channel_id=1, source_target_pairs={{0,8},{4,12},{8,0},{12,4},{16,24},{20,28},{24,16},{28,20},{1,9},{5... | collective-permute-start | bytes 294920 | tf_op jit(solution)/shard_map/ppermute | solution.py:584
  74.6 11.0 %collective-permute-start.18 = (bf16[4,96,128]{2,1,0:T(8,128)(2,1)S(1)}, bf16[4,96,128]{2,1,0:T(8,128)(2,1)S(1)}, u32[]{:S(2)}, u32[]{:S(2)}) collective-permute-start(bf16[4,96,128]{2,1,0:T(8,128)(2,1)S(1)} %get-tuple-element.96), channel_id=1, source_target_pairs={{0,16},{4,20},{8,24},{12,28},{16,0},{20,4},{24,8},{28,12},{1,17},{... | collective-permute-start | bytes 294920 | tf_op jit(solution)/shard_map/ppermute | solution.py:584
  78.2 7.3 %collective-permute-start.19 = (bf16[4,96,128]{2,1,0:T(8,128)(2,1)S(1)}, bf16[4,96,128]{2,1,0:T(8,128)(2,1)S(1)}, u32[]{:S(2)}, u32[]{:S(2)}) collective-permute-start(bf16[4,96,128]{2,1,0:T(8,128)(2,1)S(1)} %get-tuple-element.97), channel_id=1, source_target_pairs={{0,24},{4,28},{8,16},{12,20},{16,8},{20,12},{24,0},{28,4},{1,25},{... | collective-permute-start | bytes 294920 | tf_op jit(solution)/shard_map/ppermute | solution.py:584
  85.6 5.1 %collective-permute-start.20 = (bf16[4,80,128]{2,1,0:T(8,128)(2,1)S(1)}, bf16[4,80,128]{2,1,0:T(8,128)(2,1)S(1)}, u32[]{:S(2)}, u32[]{:S(2)}) collective-permute-start(bf16[4,80,128]{2,1,0:T(8,128)(2,1)S(1)} %get-tuple-element.100), channel_id=1, source_target_pairs={{0,8},{4,12},{8,0},{12,4},{16,24},{20,28},{24,16},{28,20},{1,9},{5... | collective-permute-start | bytes 245768 | tf_op jit(solution)/shard_map/ppermute | solution.py:584
  87.3 8.1 %collective-permute-start.21 = (bf16[4,80,128]{2,1,0:T(8,128)(2,1)S(1)}, bf16[4,80,128]{2,1,0:T(8,128)(2,1)S(1)}, u32[]{:S(2)}, u32[]{:S(2)}) collective-permute-start(bf16[4,80,128]{2,1,0:T(8,128)(2,1)S(1)} %get-tuple-element.101), channel_id=1, source_target_pairs={{0,16},{4,20},{8,24},{12,28},{16,0},{20,4},{24,8},{28,12},{1,17},{... | collective-permute-start | bytes 245768 | tf_op jit(solution)/shard_map/ppermute | solution.py:584
  88.7 6.7 %collective-permute-start.22 = (bf16[4,80,128]{2,1,0:T(8,128)(2,1)S(1)}, bf16[4,80,128]{2,1,0:T(8,128)(2,1)S(1)}, u32[]{:S(2)}, u32[]{:S(2)}) collective-permute-start(bf16[4,80,128]{2,1,0:T(8,128)(2,1)S(1)} %get-tuple-element.102), channel_id=1, source_target_pairs={{0,24},{4,28},{8,16},{12,20},{16,8},{20,12},{24,0},{28,4},{1,25},{... | collective-permute-start | bytes 245768 | tf_op jit(solution)/shard_map/ppermute | solution.py:584
  (17 other events, 26.2 us)

commit v9 on v8

--- a/solution.py
+++ b/solution.py
@@ -475,26 +475,27 @@
     )(*routes, *rows)
 
 
-def add_kernel(home, got, own, *away):
-    for j in range(len(away) + 1):
-        lo = j * TILE_DEV
-        total = home[lo : lo + TILE_DEV] + got[lo : lo + TILE_DEV].astype(F32)
-        if j == 0:
-            own[...] = total
-        else:
-            away[j - 1][...] = total.astype(BF16)
-
-
-def add_halves(home, got):
-    shape = (TILE_DEV,) + home.shape[1:]
-    others = home.shape[0] // TILE_DEV - 1
+def add_kernel(pairs, *refs):
+    out = refs[2 * pairs :]
+    lo = 0
+    for home, got in zip(refs[:pairs], refs[pairs : 2 * pairs]):
+        hi = lo + home.shape[1]
+        for j, ref in enumerate(out):
+            tiles = slice(j * TILE_DEV, (j + 1) * TILE_DEV)
+            ref[:, lo:hi, :] = (home[tiles] + got[tiles].astype(F32)).astype(ref.dtype)
+        lo = hi
+
+
+def add_halves(homes, gots):
+    shape = (TILE_DEV, sum(home.shape[1] for home in homes), 128)
+    others = homes[0].shape[0] // TILE_DEV - 1
     return pl.pallas_call(
-        add_kernel,
+        functools.partial(add_kernel, len(homes)),
         out_shape=[jax.ShapeDtypeStruct(shape, F32)] + [jax.ShapeDtypeStruct(shape, BF16)] * others,
         compiler_params=pltpu.CompilerParams(vmem_limit_bytes=VMEM),
         cost_estimate=pl.CostEstimate(flops=10**6, bytes_accessed=10**4, transcendentals=0),
         name="add_halves",
-    )(home, got)
+    )(*homes, *gots)
 
 
 def collapse_matrices():
@@ -616,10 +617,11 @@
         got = swap(strips, "frames", bit)
         if bit == 1:
             got, weights, state = tie((got, weights, state))
-            far, near = swap(weights, "frames", 1), swap(weights, "tiles", 1)
+            far, near = swap(weights, "tiles", 2), swap(weights, "tiles", 1)
+        if bit == 2:
+            got, far, near = tie((got, far, near))
         if bit == half:
-            far_near = swap(far, "tiles", 1)
-            got, far, near, far_near, spot_x, spot_y = tie((got, far, near, far_near, spot_x, spot_y))
+            got, spot_x, spot_y = tie((got, spot_x, spot_y))
         strips = jnp.where((mask & bit) != 0, got, strips)
         bit *= 2
 
@@ -630,21 +632,22 @@
         return [own] + [swap(part, "frames", 2 * (j + 1)) for j, part in enumerate(away)]
 
     first, second = blend(strip_cell, strips, state)
-    first, second, spot_x, spot_y = tie((first, second, spot_x, spot_y))
+    first, second, spot_x, spot_y, far = tie((first, second, spot_x, spot_y, far))
     far_first, near_first = swap(first, "tiles", 2), swap(first, "tiles", 1)
     far_second, near_second = swap(second, "frames", 1), swap(second, "tiles", 1)
     routes_x, routes_y = routes_of(spot_x), routes_of(spot_y)
-    far_second, routes_x, routes_y, near_first = tie((far_second, routes_x, routes_y, near_first))
-    rows = (second, near_second, far_second, swap(far_second, "tiles", 1))
-    home_s, away_s = gather(routes_y, *rows, weights, near, far, far_near)
+    home_w, away_w = gather(routes_x, weights, near, far, swap(far, "tiles", 1))
+    got_w = swap(away_w, "frames", 1)
+    far_second, home_w, routes_y = tie((far_second, home_w, routes_y))
+    home_s, away_s = gather(routes_y, second, near_second, far_second, swap(far_second, "tiles", 1))
     got_s = swap(away_s, "tiles", 2)
-    far_first, home_s = tie((far_first, home_s))
+    far_first, home_s, got_w = tie((far_first, home_s, got_w))
     far_near, got_s = tie((swap(far_first, "tiles", 1), got_s))
     home_f, away_f = gather(routes_x, first, near_first, far_first, far_near)
     got_f = swap(away_f, "frames", 1)
-    got_second = along(*add_halves(home_s, got_s))
+    got_second = along(*add_halves((home_s, home_w), (got_s, got_w)))
     got_f, got_second = tie((got_f, got_second))
-    got_first = along(*add_halves(home_f, got_f))
+    got_first = along(*add_halves((home_f,), (got_f,)))
     return collapse(got_first, got_second)
 
 

time: 98.2 us -> 87.3 us (0.89)
  waiting for transfers between devices: 40.9 us -> 29.4 us
  local copies, waits for them, and re-layouts: 11.5 us -> 9.41 us
  starting transfers between devices: 24.2 us -> 26 us
  Pallas kernels: 18.2 us -> 19.2 us
    ppermute x23 -> x24, waiting for transfers between devices: 40.9 us -> 29.4 us  [swap(): return lax.ppermute(value, axis, [(i, i ^ bit) for i in range(size)])]
    unnamed x36 -> x32, local copies, waits for them, and re-layouts: 11.5 us -> 9.41 us
    ppermute x23 -> x24, starting transfers between devices: 24.2 us -> 26 us  [swap(): return lax.ppermute(value, axis, [(i, i ^ bit) for i in range(size)])]
    pallas_call x2 -> x3, Pallas kernels: 3.8 us -> 4.75 us  [gather_rows(): pl.pallas_call(gather_kernel, in_specs=[pl.BlockSpec(memory_space=pltpu.S...]
  transfers between devices with their start and end apart: 23 -> 24, of which waited for: 9 -> 12; matrix products, arithmetic and copies ran while one was open for 1% -> 1% of each run, Pallas kernels for 10% -> 13%
where the time goes in v9:
time: 87.3 us; the launch traced here: 86.9 us
  waiting for transfers between devices  29.4 us (34%)
  starting transfers between devices  26 us (30%)
  Pallas kernels  19.2 us (22%)
  local copies, waits for them, and re-layouts  9.41 us (11%)
  between operations  1.46 us (2%)
  other arithmetic  1.33 us (2%)
    ppermute x24, waiting for transfers between devices, swap(): return lax.ppermute(value, axis, [(i, i ^ bit) for i in range(size)])  29.4 us
    ppermute x24, starting transfers between devices, swap(): return lax.ppermute(value, axis, [(i, i ^ bit) for i in range(size)])  26 us
    unnamed x32, local copies, waits for them, and re-layouts  9.41 us
    pallas_call x3, Pallas kernels, gather_rows(): pl.pallas_call(gather_kernel, in_specs=[pl.BlockSpec(memory_space=pltpu.S...  4.75 us
    pallas_call x1, Pallas kernels, bands_of(): pl.pallas_call(functools.partial(bands_kernel, small_places, large_places...  4.69 us
    pallas_call x2, Pallas kernels, routes_of(): pl.pallas_call(routes_kernel, in_specs=[smem], out_specs=[smem, smem], ou...  3.29 us
    pallas_call x1, Pallas kernels, blend(): pl.pallas_call(blend_kernel, in_specs=[pl.BlockSpec(memory_space=pltpu.SM...  2.3 us
    pallas_call x1, Pallas kernels, collapse(): pl.pallas_call(functools.partial(collapse_kernel, places, len(b)), out_sh...  2.18 us
  transfers between devices with their start and end apart: 24, of which 12 were waited for; matrix products, arithmetic and copies ran while one was open for 1% of the time, Pallas kernels for 13%

profile of v9, /device:TPU:0, one launch (start us, length us, event | category | flops | bytes accessed | tf_op | source)
XLA Modules:
  0.0 86.9 jit_solution(5403638953165633618)
XLA Ops:
  3.5 1.9 %strips.1 = bf16[288,128]{1,0:T(8,128)(2,1)S(1)} custom-call(s32[1]{0:T(128)S(6)} %copy.12.cell, bf16[1,3,128,1024]{3,2,1,0:T(8,128)(2,1)S(1)} %copy-done.11, bf16[1,3,128,1024]{3,2,1,0:T(8,128)(2,1)S(1)} %copy-done.11, bf16[512,512]{1,0:T(8,128)(2,1)S(1)} %copy-done.15), custom_call_target="tpu_custom_call" | custom-call | flops 2000000000 | bytes 1000000 | tf_op jit(solution)/shard_map/strips/pallas_call | solution.py:247
  5.9 2.6 %collective-permute-start = (bf16[288,128]{1,0:T(8,128)(2,1)S(1)}, bf16[288,128]{1,0:T(8,128)(2,1)S(1)}, u32[]{:S(2)}, u32[]{:S(2)}) collective-permute-start(bf16[288,128]{1,0:T(8,128)(2,1)S(1)} %strips.1), channel_id=1, source_target_pairs={{0,4},{4,0},{8,12},{12,8},{16,20},{20,16},{24,28},{28,24},{1,5},{5... | collective-permute-start | bytes 221192 | tf_op jit(solution)/shard_map/ppermute | solution.py:585
  8.5 4.7 %bands.1 = (bf16[32,32,128]{2,1,0:T(8,128)(2,1)S(1)}, f32[816,1024]{1,0:T(8,128)S(1)}) custom-call(bf16[1,3,128,1024]{3,2,1,0:T(8,128)(2,1)S(1)} %copy-done.11, bf16[1,128,1024]{2,1,0:T(8,128)(2,1)S(1)} %copy-done.12, s32[1,64,128]{2,1,0:T(8,128)S(1)} %bitcast.13, bf16[512,512]{1,0:T(8,128)(2,1)S(1)} %copy-done.15, bf16[512,640]{1,0:T(8,128)(2,1)S(1)} %copy-done.14), custom_call_target="tpu_custom_call" | custom-call | flops 8000000000 | bytes 6000000 | tf_op jit(solution)/shard_map/bands/pallas_call | solution.py:339
  14.8 1.5 %collective-permute-start.2 = (bf16[32,32,128]{2,1,0:T(8,128)(2,1)}, bf16[32,32,128]{2,1,0:T(8,128)(2,1)}, u32[]{:S(2)}, u32[]{:S(2)}) collective-permute-start(bf16[32,32,128]{2,1,0:T(8,128)(2,1)} %copy-done.1), channel_id=1, source_target_pairs={{0,2},{1,3},{2,0},{3,1},{4,6},{5,7},{6,4},{7,5},{8,10},{9,11},{10,... | collective-permute-start | bytes 786440 | tf_op jit(solution)/shard_map/ppermute | solution.py:585
  16.3 1.6 %collective-permute-start.1 = (bf16[288,128]{1,0:T(8,128)(2,1)S(1)}, bf16[288,128]{1,0:T(8,128)(2,1)S(1)}, u32[]{:S(2)}, u32[]{:S(2)}) collective-permute-start(bf16[288,128]{1,0:T(8,128)(2,1)S(1)} %broadcast_select_fusion), channel_id=1, source_target_pairs={{0,8},{4,12},{8,0},{12,4},{16,24},{20,28},{24,16},{28,20},{1,9},{5... | collective-permute-start | bytes 221192 | tf_op jit(solution)/shard_map/ppermute | solution.py:585
  19.1 1.7 %collective-permute-done.1 = bf16[288,128]{1,0:T(8,128)(2,1)S(1)} collective-permute-done((bf16[288,128]{1,0:T(8,128)(2,1)S(1)}, bf16[288,128]{1,0:T(8,128)(2,1)S(1)}, u32[]{:S(2)}, u32[]{:S(2)}) %collective-permute-start.1) | collective-permute-done | bytes 73760 | tf_op jit(solution)/shard_map/ppermute | solution.py:585
  21.5 2.3 %collective-permute-done.2.refs_2_ = bf16[32,32,128]{2,1,0:T(8,128)(2,1)} collective-permute-done((bf16[32,32,128]{2,1,0:T(8,128)(2,1)}, bf16[32,32,128]{2,1,0:T(8,128)(2,1)}, u32[]{:S(2)}, u32[]{:S(2)}) %collective-permute-start.2) | collective-permute-done | bytes 262176 | tf_op jit(solution)/shard_map/ppermute | solution.py:585
  23.7 2.6 %collective-permute-start.4 = (bf16[288,128]{1,0:T(8,128)(2,1)S(1)}, bf16[288,128]{1,0:T(8,128)(2,1)S(1)}, u32[]{:S(2)}, u32[]{:S(2)}) collective-permute-start(bf16[288,128]{1,0:T(8,128)(2,1)S(1)} %broadcast_select_fusion.1), channel_id=1, source_target_pairs={{0,16},{4,20},{8,24},{12,28},{16,0},{20,4},{24,8},{28,12},{1,17},{... | collective-permute-start | bytes 221192 | tf_op jit(solution)/shard_map/ppermute | solution.py:585
  27.0 3.2 %collective-permute-done.4 = bf16[288,128]{1,0:T(8,128)(2,1)S(1)} collective-permute-done((bf16[288,128]{1,0:T(8,128)(2,1)S(1)}, bf16[288,128]{1,0:T(8,128)(2,1)S(1)}, u32[]{:S(2)}, u32[]{:S(2)}) %collective-permute-start.4) | collective-permute-done | bytes 73760 | tf_op jit(solution)/shard_map/ppermute | solution.py:585
  30.2 2.3 %blend.1 = (bf16[32,80,128]{2,1,0:T(8,128)(2,1)}, bf16[32,64,128]{2,1,0:T(8,128)(2,1)}) custom-call(s32[1]{0:T(128)S(6)} %copy.12.cell, bf16[288,128]{1,0:T(8,128)(2,1)S(1)} %broadcast_select_fusion.2.strips, f32[816,1024]{1,0:T(8,128)S(1)} %get-tuple-element.67.state), custom_call_target="tpu_custom_call" | custom-call | flops 1000000 | bytes 10000 | tf_op jit(solution)/shard_map/blend/pallas_call | solution.py:410
  33.0 1.5 %collective-permute-start.9 = (bf16[32,80,128]{2,1,0:T(8,128)(2,1)}, bf16[32,80,128]{2,1,0:T(8,128)(2,1)S(1)}, u32[]{:S(2)}, u32[]{:S(2)}) collective-permute-start(bf16[32,80,128]{2,1,0:T(8,128)(2,1)} %get-tuple-element.76.refs_0_), channel_id=1, source_target_pairs={{0,2},{1,3},{2,0},{3,1},{4,6},{5,7},{6,4},{7,5},{8,10},{9,11},{10,... | collective-permute-start | bytes 1966088 | tf_op jit(solution)/shard_map/ppermute | solution.py:585
  34.7 1.6 %routes.2 = (s32[4,33]{1,0:T(4,128)}, s32[4]{0:T(128)}) custom-call(s32[4,32]{1,0:T(4,128)} %get-tuple-element.73.spot), custom_call_target="tpu_custom_call" | custom-call | tf_op jit(solution)/shard_map/routes/pallas_call | solution.py:433
  36.4 1.6 %routes.3 = (s32[4,33]{1,0:T(4,128)}, s32[4]{0:T(128)}) custom-call(s32[4,32]{1,0:T(4,128)} %get-tuple-element.81.spot), custom_call_target="tpu_custom_call" | custom-call | tf_op jit(solution)/shard_map/routes/pallas_call | solution.py:433
  41.3 1.5 %gather_rows.3 = (f32[16,32,128]{2,1,0:T(8,128)S(1)}, bf16[16,32,128]{2,1,0:T(8,128)(2,1)S(1)}) custom-call(s32[4,33]{1,0:T(4,128)S(1)} %copy-done.5, s32[4]{0:T(128)S(1)} %copy-done.7, bf16[32,32,128]{2,1,0:T(8,128)(2,1)S(1)} %copy-done.2, bf16[32,32,128]{2,1,0:T(8,128)(2,1)S(1)} %copy-done.4, bf16[32,32,128]{2,1,0:T(8,128)(2,1)} %collective-permute-done.2.refs_2_, ...), custom_call_target="tpu_custom_call" | custom-call | flops 1000000 | bytes 10000 | tf_op jit(solution)/shard_map/gather_rows/pallas_call | solution.py:467
  47.0 1.5 %gather_rows.4 = (f32[16,64,128]{2,1,0:T(8,128)S(1)}, bf16[16,64,128]{2,1,0:T(8,128)(2,1)S(1)}) custom-call(s32[4,33]{1,0:T(4,128)S(1)} %copy-done.9, s32[4]{0:T(128)S(1)} %copy-done.10, bf16[32,64,128]{2,1,0:T(8,128)(2,1)} %get-tuple-element.77.refs_0_, bf16[32,64,128]{2,1,0:T(8,128)(2,1)S(1)} %collective-permute-done.12.refs_1_, ...), custom_call_target="tpu_custom_call" | custom-call | flops 1000000 | bytes 10000 | tf_op jit(solution)/shard_map/gather_rows/pallas_call | solution.py:467
  50.9 1.5 %collective-permute-start.16 = (bf16[16,64,128]{2,1,0:T(8,128)(2,1)S(1)}, bf16[16,64,128]{2,1,0:T(8,128)(2,1)S(1)}, u32[]{:S(2)}, u32[]{:S(2)}) collective-permute-start(bf16[16,64,128]{2,1,0:T(8,128)(2,1)S(1)} %get-tuple-element.90), channel_id=1, source_target_pairs={{0,2},{1,3},{2,0},{3,1},{4,6},{5,7},{6,4},{7,5},{8,10},{9,11},{10,... | collective-permute-start | bytes 786440 | tf_op jit(solution)/shard_map/ppermute | solution.py:585
  52.4 6.7 %collective-permute-done.16.refs_2_ = bf16[16,64,128]{2,1,0:T(8,128)(2,1)S(1)} collective-permute-done((bf16[16,64,128]{2,1,0:T(8,128)(2,1)S(1)}, bf16[16,64,128]{2,1,0:T(8,128)(2,1)S(1)}, u32[]{:S(2)}, u32[]{:S(2)}) %collective-permute-start.16) | collective-permute-done | bytes 262176 | tf_op jit(solution)/shard_map/ppermute | solution.py:585
  60.4 1.8 %gather_rows.5 = (f32[16,80,128]{2,1,0:T(8,128)S(1)}, bf16[16,80,128]{2,1,0:T(8,128)(2,1)S(1)}) custom-call(s32[4,33]{1,0:T(4,128)S(1)} %copy-done.6, s32[4]{0:T(128)S(1)} %copy-done.8, bf16[32,80,128]{2,1,0:T(8,128)(2,1)} %get-tuple-element.76.refs_0_, bf16[32,80,128]{2,1,0:T(8,128)(2,1)S(1)} %collective-permute-done.8.refs_1_, ...), custom_call_target="tpu_custom_call" | custom-call | flops 1000000 | bytes 10000 | tf_op jit(solution)/shard_map/gather_rows/pallas_call | solution.py:467
  62.2 1.8 %collective-permute-start.17 = (bf16[16,80,128]{2,1,0:T(8,128)(2,1)S(1)}, bf16[16,80,128]{2,1,0:T(8,128)(2,1)S(1)}, u32[]{:S(2)}, u32[]{:S(2)}) collective-permute-start(bf16[16,80,128]{2,1,0:T(8,128)(2,1)S(1)} %get-tuple-element.93), channel_id=1, source_target_pairs={{0,4},{4,0},{8,12},{12,8},{16,20},{20,16},{24,28},{28,24},{1,5},{5... | collective-permute-start | bytes 983048 | tf_op jit(solution)/shard_map/ppermute | solution.py:585
  64.3 3.5 %collective-permute-start.19 = (bf16[4,96,128]{2,1,0:T(8,128)(2,1)S(1)}, bf16[4,96,128]{2,1,0:T(8,128)(2,1)S(1)}, u32[]{:S(2)}, u32[]{:S(2)}) collective-permute-start(bf16[4,96,128]{2,1,0:T(8,128)(2,1)S(1)} %get-tuple-element.100), channel_id=1, source_target_pairs={{0,16},{4,20},{8,24},{12,28},{16,0},{20,4},{24,8},{28,12},{1,17},{... | collective-permute-start | bytes 294920 | tf_op jit(solution)/shard_map/ppermute | solution.py:585
  69.6 5.2 %collective-permute-done.19.refs_6_ = bf16[4,96,128]{2,1,0:T(8,128)(2,1)S(1)} collective-permute-done((bf16[4,96,128]{2,1,0:T(8,128)(2,1)S(1)}, bf16[4,96,128]{2,1,0:T(8,128)(2,1)S(1)}, u32[]{:S(2)}, u32[]{:S(2)}) %collective-permute-start.19) | collective-permute-done | bytes 98336 | tf_op jit(solution)/shard_map/ppermute | solution.py:585
  74.9 1.7 %collective-permute-start.21 = (bf16[4,80,128]{2,1,0:T(8,128)(2,1)S(1)}, bf16[4,80,128]{2,1,0:T(8,128)(2,1)S(1)}, u32[]{:S(2)}, u32[]{:S(2)}) collective-permute-start(bf16[4,80,128]{2,1,0:T(8,128)(2,1)S(1)} %get-tuple-element.104), channel_id=1, source_target_pairs={{0,8},{4,12},{8,0},{12,4},{16,24},{20,28},{24,16},{28,20},{1,9},{5... | collective-permute-start | bytes 245768 | tf_op jit(solution)/shard_map/ppermute | solution.py:585
  80.0 4.6 %collective-permute-done.22.refs_2_ = bf16[4,80,128]{2,1,0:T(8,128)(2,1)S(1)} collective-permute-done((bf16[4,80,128]{2,1,0:T(8,128)(2,1)S(1)}, bf16[4,80,128]{2,1,0:T(8,128)(2,1)S(1)}, u32[]{:S(2)}, u32[]{:S(2)}) %collective-permute-start.22) | collective-permute-done | bytes 81952 | tf_op jit(solution)/shard_map/ppermute | solution.py:585
  84.7 2.2 %collapse.1 = f32[3,4,4096]{2,1,0:T(4,128)} custom-call(bf16[192,1280]{1,0:T(8,128)(2,1)S(1)} %copy-done, f32[4,80,128]{2,1,0:T(8,128)S(1)} %get-tuple-element.103.refs_0_, bf16[4,80,128]{2,1,0:T(8,128)(2,1)S(1)} %collective-permute-done.21.refs_1_, bf16[4,80,128]{2,1,0:T(8,128)(2,1)S(1)} %collective-permute-done.22.refs_2_, ...), custom_call_target="tpu_custom_call" | custom-call | flops 1000000 | bytes 10000 | tf_op jit(solution)/shard_map/collapse/pallas_call | solution.py:572
  (73 shorter events, 24.3 us)
Async XLA Ops:
  5.4 12.6 %collective-permute-start.5 = (s32[32]{0:T(128)S(1)}, s32[32]{0:T(128)S(1)}, u32[]{:S(2)}, u32[]{:S(2)}) collective-permute-start(s32[32]{0:T(128)S(1)} %bitcast_add_fusion), channel_id=1, source_target_pairs={{0,1},{1,0},{2,3},{3,2},{4,5},{5,4},{6,7},{7,6},{8,9},{9,8},{10,11... | collective-permute-start | bytes 392 | tf_op jit(solution)/shard_map/ppermute | solution.py:585
  5.9 8.7 %collective-permute-start = (bf16[288,128]{1,0:T(8,128)(2,1)S(1)}, bf16[288,128]{1,0:T(8,128)(2,1)S(1)}, u32[]{:S(2)}, u32[]{:S(2)}) collective-permute-start(bf16[288,128]{1,0:T(8,128)(2,1)S(1)} %strips.1), channel_id=1, source_target_pairs={{0,4},{4,0},{8,12},{12,8},{16,20},{20,16},{24,28},{28,24},{1,5},{5... | collective-permute-start | bytes 221192 | tf_op jit(solution)/shard_map/ppermute | solution.py:585
  14.6 6.2 %collective-permute-start.3 = (bf16[32,32,128]{2,1,0:T(8,128)(2,1)}, bf16[32,32,128]{2,1,0:T(8,128)(2,1)S(1)}, u32[]{:S(2)}, u32[]{:S(2)}) collective-permute-start(bf16[32,32,128]{2,1,0:T(8,128)(2,1)} %copy-done.1), channel_id=1, source_target_pairs={{0,1},{1,0},{2,3},{3,2},{4,5},{5,4},{6,7},{7,6},{8,9},{9,8},{10,11... | collective-permute-start | bytes 786440 | tf_op jit(solution)/shard_map/ppermute | solution.py:585
  14.8 8.9 %collective-permute-start.2 = (bf16[32,32,128]{2,1,0:T(8,128)(2,1)}, bf16[32,32,128]{2,1,0:T(8,128)(2,1)}, u32[]{:S(2)}, u32[]{:S(2)}) collective-permute-start(bf16[32,32,128]{2,1,0:T(8,128)(2,1)} %copy-done.1), channel_id=1, source_target_pairs={{0,2},{1,3},{2,0},{3,1},{4,6},{5,7},{6,4},{7,5},{8,10},{9,11},{10,... | collective-permute-start | bytes 786440 | tf_op jit(solution)/shard_map/ppermute | solution.py:585
  16.3 4.4 %collective-permute-start.1 = (bf16[288,128]{1,0:T(8,128)(2,1)S(1)}, bf16[288,128]{1,0:T(8,128)(2,1)S(1)}, u32[]{:S(2)}, u32[]{:S(2)}) collective-permute-start(bf16[288,128]{1,0:T(8,128)(2,1)S(1)} %broadcast_select_fusion), channel_id=1, source_target_pairs={{0,8},{4,12},{8,0},{12,4},{16,24},{20,28},{24,16},{28,20},{1,9},{5... | collective-permute-start | bytes 221192 | tf_op jit(solution)/shard_map/ppermute | solution.py:585
  18.0 8.4 %collective-permute-start.7 = (s32[2,32]{1,0:T(2,128)S(1)}, s32[2,32]{1,0:T(2,128)S(1)}, u32[]{:S(2)}, u32[]{:S(2)}) collective-permute-start(s32[2,32]{1,0:T(2,128)S(1)} %pad_add_fusion.3), channel_id=1, source_target_pairs={{0,4},{4,0},{8,12},{12,8},{16,20},{20,16},{24,28},{28,24},{1,5},{5... | collective-permute-start | bytes 776 | tf_op jit(solution)/shard_map/ppermute | solution.py:585
  18.6 7.8 %collective-permute-start.6 = (s32[2,32]{1,0:T(2,128)S(1)}, s32[2,32]{1,0:T(2,128)S(1)}, u32[]{:S(2)}, u32[]{:S(2)}) collective-permute-start(s32[2,32]{1,0:T(2,128)S(1)} %pad_add_fusion.3), channel_id=1, source_target_pairs={{0,2},{1,3},{2,0},{3,1},{4,6},{5,7},{6,4},{7,5},{8,10},{9,11},{10,... | collective-permute-start | bytes 776 | tf_op jit(solution)/shard_map/ppermute | solution.py:585
  23.7 6.4 %collective-permute-start.4 = (bf16[288,128]{1,0:T(8,128)(2,1)S(1)}, bf16[288,128]{1,0:T(8,128)(2,1)S(1)}, u32[]{:S(2)}, u32[]{:S(2)}) collective-permute-start(bf16[288,128]{1,0:T(8,128)(2,1)S(1)} %broadcast_select_fusion.1), channel_id=1, source_target_pairs={{0,16},{4,20},{8,24},{12,28},{16,0},{20,4},{24,8},{28,12},{1,17},{... | collective-permute-start | bytes 221192 | tf_op jit(solution)/shard_map/ppermute | solution.py:585
  32.5 11.3 %collective-permute-start.10 = (bf16[32,64,128]{2,1,0:T(8,128)(2,1)}, bf16[32,64,128]{2,1,0:T(8,128)(2,1)S(1)}, u32[]{:S(2)}, u32[]{:S(2)}) collective-permute-start(bf16[32,64,128]{2,1,0:T(8,128)(2,1)} %get-tuple-element.77.refs_0_), channel_id=1, source_target_pairs={{0,4},{4,0},{8,12},{12,8},{16,20},{20,16},{24,28},{28,24},{1,5},{5... | collective-permute-start | bytes 1572872 | tf_op jit(solution)/shard_map/ppermute | solution.py:585
  33.0 5.0 %collective-permute-start.11 = (bf16[32,32,128]{2,1,0:T(8,128)(2,1)}, bf16[32,32,128]{2,1,0:T(8,128)(2,1)S(1)}, u32[]{:S(2)}, u32[]{:S(2)}) collective-permute-start(bf16[32,32,128]{2,1,0:T(8,128)(2,1)} %collective-permute-done.2.refs_2_), channel_id=1, source_target_pairs={{0,1},{1,0},{2,3},{3,2},{4,5},{5,4},{6,7},{7,6},{8,9},{9,8},{10,11... | collective-permute-start | bytes 786440 | tf_op jit(solution)/shard_map/ppermute | solution.py:585
  33.0 17.4 %collective-permute-start.9 = (bf16[32,80,128]{2,1,0:T(8,128)(2,1)}, bf16[32,80,128]{2,1,0:T(8,128)(2,1)S(1)}, u32[]{:S(2)}, u32[]{:S(2)}) collective-permute-start(bf16[32,80,128]{2,1,0:T(8,128)(2,1)} %get-tuple-element.76.refs_0_), channel_id=1, source_target_pairs={{0,2},{1,3},{2,0},{3,1},{4,6},{5,7},{6,4},{7,5},{8,10},{9,11},{10,... | collective-permute-start | bytes 1966088 | tf_op jit(solution)/shard_map/ppermute | solution.py:585
  34.5 10.2 %collective-permute-start.12 = (bf16[32,64,128]{2,1,0:T(8,128)(2,1)}, bf16[32,64,128]{2,1,0:T(8,128)(2,1)S(1)}, u32[]{:S(2)}, u32[]{:S(2)}) collective-permute-start(bf16[32,64,128]{2,1,0:T(8,128)(2,1)} %get-tuple-element.77.refs_0_), channel_id=1, source_target_pairs={{0,1},{1,0},{2,3},{3,2},{4,5},{5,4},{6,7},{7,6},{8,9},{9,8},{10,11... | collective-permute-start | bytes 1572872 | tf_op jit(solution)/shard_map/ppermute | solution.py:585
  43.8 1.9 %collective-permute-start.13 = (bf16[32,64,128]{2,1,0:T(8,128)(2,1)S(1)}, bf16[32,64,128]{2,1,0:T(8,128)(2,1)S(1)}, u32[]{:S(2)}, u32[]{:S(2)}) collective-permute-start(bf16[32,64,128]{2,1,0:T(8,128)(2,1)S(1)} %collective-permute-done.10.refs_2_), channel_id=1, source_target_pairs={{0,1},{1,0},{2,3},{3,2},{4,5},{5,4},{6,7},{7,6},{8,9},{9,8},{10,11... | collective-permute-start | bytes 1572872 | tf_op jit(solution)/shard_map/ppermute | solution.py:585
  43.8 5.9 %collective-permute-start.14 = (bf16[16,32,128]{2,1,0:T(8,128)(2,1)S(1)}, bf16[16,32,128]{2,1,0:T(8,128)(2,1)S(1)}, u32[]{:S(2)}, u32[]{:S(2)}) collective-permute-start(bf16[16,32,128]{2,1,0:T(8,128)(2,1)S(1)} %get-tuple-element.88), channel_id=1, source_target_pairs={{0,4},{4,0},{8,12},{12,8},{16,20},{20,16},{24,28},{28,24},{1,5},{5... | collective-permute-start | bytes 393224 | tf_op jit(solution)/shard_map/ppermute | solution.py:585
  50.4 8.7 %collective-permute-start.15 = (bf16[32,80,128]{2,1,0:T(8,128)(2,1)S(1)}, bf16[32,80,128]{2,1,0:T(8,128)(2,1)S(1)}, u32[]{:S(2)}, u32[]{:S(2)}) collective-permute-start(bf16[32,80,128]{2,1,0:T(8,128)(2,1)S(1)} %collective-permute-done.9.refs_2_), channel_id=1, source_target_pairs={{0,1},{1,0},{2,3},{3,2},{4,5},{5,4},{6,7},{7,6},{8,9},{9,8},{10,11... | collective-permute-start | bytes 1966088 | tf_op jit(solution)/shard_map/ppermute | solution.py:585
  50.4 8.7 %collective-permute-start.8 = (bf16[32,80,128]{2,1,0:T(8,128)(2,1)}, bf16[32,80,128]{2,1,0:T(8,128)(2,1)S(1)}, u32[]{:S(2)}, u32[]{:S(2)}) collective-permute-start(bf16[32,80,128]{2,1,0:T(8,128)(2,1)} %get-tuple-element.76.refs_0_), channel_id=1, source_target_pairs={{0,1},{1,0},{2,3},{3,2},{4,5},{5,4},{6,7},{7,6},{8,9},{9,8},{10,11... | collective-permute-start | bytes 1966088 | tf_op jit(solution)/shard_map/ppermute | solution.py:585
  50.9 8.2 %collective-permute-start.16 = (bf16[16,64,128]{2,1,0:T(8,128)(2,1)S(1)}, bf16[16,64,128]{2,1,0:T(8,128)(2,1)S(1)}, u32[]{:S(2)}, u32[]{:S(2)}) collective-permute-start(bf16[16,64,128]{2,1,0:T(8,128)(2,1)S(1)} %get-tuple-element.90), channel_id=1, source_target_pairs={{0,2},{1,3},{2,0},{3,1},{4,6},{5,7},{6,4},{7,5},{8,10},{9,11},{10,... | collective-permute-start | bytes 786440 | tf_op jit(solution)/shard_map/ppermute | solution.py:585
  62.2 12.6 %collective-permute-start.17 = (bf16[16,80,128]{2,1,0:T(8,128)(2,1)S(1)}, bf16[16,80,128]{2,1,0:T(8,128)(2,1)S(1)}, u32[]{:S(2)}, u32[]{:S(2)}) collective-permute-start(bf16[16,80,128]{2,1,0:T(8,128)(2,1)S(1)} %get-tuple-element.93), channel_id=1, source_target_pairs={{0,4},{4,0},{8,12},{12,8},{16,20},{20,16},{24,28},{28,24},{1,5},{5... | collective-permute-start | bytes 983048 | tf_op jit(solution)/shard_map/ppermute | solution.py:585
  64.1 5.5 %collective-permute-start.18 = (bf16[4,96,128]{2,1,0:T(8,128)(2,1)S(1)}, bf16[4,96,128]{2,1,0:T(8,128)(2,1)S(1)}, u32[]{:S(2)}, u32[]{:S(2)}) collective-permute-start(bf16[4,96,128]{2,1,0:T(8,128)(2,1)S(1)} %get-tuple-element.99), channel_id=1, source_target_pairs={{0,8},{4,12},{8,0},{12,4},{16,24},{20,28},{24,16},{28,20},{1,9},{5... | collective-permute-start | bytes 294920 | tf_op jit(solution)/shard_map/ppermute | solution.py:585
  64.3 10.5 %collective-permute-start.19 = (bf16[4,96,128]{2,1,0:T(8,128)(2,1)S(1)}, bf16[4,96,128]{2,1,0:T(8,128)(2,1)S(1)}, u32[]{:S(2)}, u32[]{:S(2)}) collective-permute-start(bf16[4,96,128]{2,1,0:T(8,128)(2,1)S(1)} %get-tuple-element.100), channel_id=1, source_target_pairs={{0,16},{4,20},{8,24},{12,28},{16,0},{20,4},{24,8},{28,12},{1,17},{... | collective-permute-start | bytes 294920 | tf_op jit(solution)/shard_map/ppermute | solution.py:585
  67.8 7.0 %collective-permute-start.20 = (bf16[4,96,128]{2,1,0:T(8,128)(2,1)S(1)}, bf16[4,96,128]{2,1,0:T(8,128)(2,1)S(1)}, u32[]{:S(2)}, u32[]{:S(2)}) collective-permute-start(bf16[4,96,128]{2,1,0:T(8,128)(2,1)S(1)} %get-tuple-element.101), channel_id=1, source_target_pairs={{0,24},{4,28},{8,16},{12,20},{16,8},{20,12},{24,0},{28,4},{1,25},{... | collective-permute-start | bytes 294920 | tf_op jit(solution)/shard_map/ppermute | solution.py:585
  74.9 5.1 %collective-permute-start.21 = (bf16[4,80,128]{2,1,0:T(8,128)(2,1)S(1)}, bf16[4,80,128]{2,1,0:T(8,128)(2,1)S(1)}, u32[]{:S(2)}, u32[]{:S(2)}) collective-permute-start(bf16[4,80,128]{2,1,0:T(8,128)(2,1)S(1)} %get-tuple-element.104), channel_id=1, source_target_pairs={{0,8},{4,12},{8,0},{12,4},{16,24},{20,28},{24,16},{28,20},{1,9},{5... | collective-permute-start | bytes 245768 | tf_op jit(solution)/shard_map/ppermute | solution.py:585
  76.6 8.1 %collective-permute-start.22 = (bf16[4,80,128]{2,1,0:T(8,128)(2,1)S(1)}, bf16[4,80,128]{2,1,0:T(8,128)(2,1)S(1)}, u32[]{:S(2)}, u32[]{:S(2)}) collective-permute-start(bf16[4,80,128]{2,1,0:T(8,128)(2,1)S(1)} %get-tuple-element.105), channel_id=1, source_target_pairs={{0,16},{4,20},{8,24},{12,28},{16,0},{20,4},{24,8},{28,12},{1,17},{... | collective-permute-start | bytes 245768 | tf_op jit(solution)/shard_map/ppermute | solution.py:585
  78.0 6.7 %collective-permute-start.23 = (bf16[4,80,128]{2,1,0:T(8,128)(2,1)S(1)}, bf16[4,80,128]{2,1,0:T(8,128)(2,1)S(1)}, u32[]{:S(2)}, u32[]{:S(2)}) collective-permute-start(bf16[4,80,128]{2,1,0:T(8,128)(2,1)S(1)} %get-tuple-element.106), channel_id=1, source_target_pairs={{0,24},{4,28},{8,16},{12,20},{16,8},{20,12},{24,0},{28,4},{1,25},{... | collective-permute-start | bytes 245768 | tf_op jit(solution)/shard_map/ppermute | solution.py:585
  (16 other events, 65.2 us)

commit v10 on v9

--- a/solution.py
+++ b/solution.py
@@ -14,7 +14,7 @@
 QB = 32
 WIN = 256
 TILE_DEV = 4
-VMEM = 30 << 20
+VMEM = 20 << 20
 ROUTE = 4096
 F32 = jnp.float32
 BF16 = jnp.bfloat16
@@ -618,10 +618,8 @@
         if bit == 1:
             got, weights, state = tie((got, weights, state))
             far, near = swap(weights, "tiles", 2), swap(weights, "tiles", 1)
-        if bit == 2:
-            got, far, near = tie((got, far, near))
         if bit == half:
-            got, spot_x, spot_y = tie((got, spot_x, spot_y))
+            got, far, near, spot_x, spot_y = tie((got, far, near, spot_x, spot_y))
         strips = jnp.where((mask & bit) != 0, got, strips)
         bit *= 2
 
@@ -642,7 +640,7 @@
     home_s, away_s = gather(routes_y, second, near_second, far_second, swap(far_second, "tiles", 1))
     got_s = swap(away_s, "tiles", 2)
     far_first, home_s, got_w = tie((far_first, home_s, got_w))
-    far_near, got_s = tie((swap(far_first, "tiles", 1), got_s))
+    far_near = swap(far_first, "tiles", 1)
     home_f, away_f = gather(routes_x, first, near_first, far_first, far_near)
     got_f = swap(away_f, "frames", 1)
     got_second = along(*add_halves((home_s, home_w), (got_s, got_w)))

time: 87.3 us -> 83.4 us (0.955)
  waiting for transfers between devices: 29.4 us -> 25 us
    ppermute x24, waiting for transfers between devices: 29.4 us -> 25 us  [swap(): return lax.ppermute(value, axis, [(i, i ^ bit) for i in range(size)])]
  transfers between devices with their start and end apart: 24 -> 24, of which waited for: 12 -> 11; matrix products, arithmetic and copies ran while one was open for 1% -> 1% of each run, Pallas kernels for 13% -> 16%
where the time goes in v10:
time: 83.4 us; the launch traced here: 82.9 us
  starting transfers between devices  26.1 us (31%)
  waiting for transfers between devices  25 us (30%)
  Pallas kernels  19.5 us (23%)
  local copies, waits for them, and re-layouts  9.41 us (11%)
  between operations  1.47 us (2%)
  other arithmetic  1.34 us (2%)
    ppermute x24, starting transfers between devices, swap(): return lax.ppermute(value, axis, [(i, i ^ bit) for i in range(size)])  26.1 us
    ppermute x24, waiting for transfers between devices, swap(): return lax.ppermute(value, axis, [(i, i ^ bit) for i in range(size)])  25 us
    unnamed x32, local copies, waits for them, and re-layouts  9.41 us
    pallas_call x3, Pallas kernels, gather_rows(): pl.pallas_call(gather_kernel, in_specs=[pl.BlockSpec(memory_space=pltpu.S...  5.05 us
    pallas_call x1, Pallas kernels, bands_of(): pl.pallas_call(functools.partial(bands_kernel, small_places, large_places...  4.69 us
    pallas_call x2, Pallas kernels, routes_of(): pl.pallas_call(routes_kernel, in_specs=[smem], out_specs=[smem, smem], ou...  3.29 us
    pallas_call x1, Pallas kernels, blend(): pl.pallas_call(blend_kernel, in_specs=[pl.BlockSpec(memory_space=pltpu.SM...  2.3 us
    pallas_call x1, Pallas kernels, collapse(): pl.pallas_call(functools.partial(collapse_kernel, places, len(b)), out_sh...  2.17 us
  transfers between devices with their start and end apart: 24, of which 11 were waited for; matrix products, arithmetic and copies ran while one was open for 1% of the time, Pallas kernels for 16%

profile of v10, /device:TPU:0, one launch (start us, length us, event | category | flops | bytes accessed | tf_op | source)
XLA Modules:
  0.0 82.9 jit_solution(1865643033414668845)
XLA Ops:
  3.5 1.9 %strips.1 = bf16[288,128]{1,0:T(8,128)(2,1)S(1)} custom-call(s32[1]{0:T(128)S(6)} %copy.12.cell, bf16[1,3,128,1024]{3,2,1,0:T(8,128)(2,1)S(1)} %copy-done.11, bf16[1,3,128,1024]{3,2,1,0:T(8,128)(2,1)S(1)} %copy-done.11, bf16[512,512]{1,0:T(8,128)(2,1)S(1)} %copy-done.15), custom_call_target="tpu_custom_call" | custom-call | flops 2000000000 | bytes 1000000 | tf_op jit(solution)/shard_map/strips/pallas_call | solution.py:247
  5.9 2.6 %collective-permute-start = (bf16[288,128]{1,0:T(8,128)(2,1)S(1)}, bf16[288,128]{1,0:T(8,128)(2,1)S(1)}, u32[]{:S(2)}, u32[]{:S(2)}) collective-permute-start(bf16[288,128]{1,0:T(8,128)(2,1)S(1)} %strips.1), channel_id=1, source_target_pairs={{0,4},{4,0},{8,12},{12,8},{16,20},{20,16},{24,28},{28,24},{1,5},{5... | collective-permute-start | bytes 221192 | tf_op jit(solution)/shard_map/ppermute | solution.py:585
  8.5 4.7 %bands.1 = (bf16[32,32,128]{2,1,0:T(8,128)(2,1)S(1)}, f32[816,1024]{1,0:T(8,128)S(1)}) custom-call(bf16[1,3,128,1024]{3,2,1,0:T(8,128)(2,1)S(1)} %copy-done.11, bf16[1,128,1024]{2,1,0:T(8,128)(2,1)S(1)} %copy-done.12, s32[1,64,128]{2,1,0:T(8,128)S(1)} %bitcast.13, bf16[512,512]{1,0:T(8,128)(2,1)S(1)} %copy-done.15, bf16[512,640]{1,0:T(8,128)(2,1)S(1)} %copy-done.14), custom_call_target="tpu_custom_call" | custom-call | flops 8000000000 | bytes 6000000 | tf_op jit(solution)/shard_map/bands/pallas_call | solution.py:339
  14.6 1.6 %collective-permute-start.1 = (bf16[288,128]{1,0:T(8,128)(2,1)S(1)}, bf16[288,128]{1,0:T(8,128)(2,1)S(1)}, u32[]{:S(2)}, u32[]{:S(2)}) collective-permute-start(bf16[288,128]{1,0:T(8,128)(2,1)S(1)} %broadcast_select_fusion), channel_id=1, source_target_pairs={{0,8},{4,12},{8,0},{12,4},{16,24},{20,28},{24,16},{28,20},{1,9},{5... | collective-permute-start | bytes 221192 | tf_op jit(solution)/shard_map/ppermute | solution.py:585
  16.8 1.5 %collective-permute-start.6 = (s32[2,32]{1,0:T(2,128)S(1)}, s32[2,32]{1,0:T(2,128)S(1)}, u32[]{:S(2)}, u32[]{:S(2)}) collective-permute-start(s32[2,32]{1,0:T(2,128)S(1)} %pad_add_fusion.3), channel_id=1, source_target_pairs={{0,2},{1,3},{2,0},{3,1},{4,6},{5,7},{6,4},{7,5},{8,10},{9,11},{10,... | collective-permute-start | bytes 776 | tf_op jit(solution)/shard_map/ppermute | solution.py:585
  19.1 2.6 %collective-permute-start.2 = (bf16[288,128]{1,0:T(8,128)(2,1)S(1)}, bf16[288,128]{1,0:T(8,128)(2,1)S(1)}, u32[]{:S(2)}, u32[]{:S(2)}) collective-permute-start(bf16[288,128]{1,0:T(8,128)(2,1)S(1)} %broadcast_select_fusion.1), channel_id=1, source_target_pairs={{0,16},{4,20},{8,24},{12,28},{16,0},{20,4},{24,8},{28,12},{1,17},{... | collective-permute-start | bytes 221192 | tf_op jit(solution)/shard_map/ppermute | solution.py:585
  22.3 3.5 %collective-permute-done.2 = bf16[288,128]{1,0:T(8,128)(2,1)S(1)} collective-permute-done((bf16[288,128]{1,0:T(8,128)(2,1)S(1)}, bf16[288,128]{1,0:T(8,128)(2,1)S(1)}, u32[]{:S(2)}, u32[]{:S(2)}) %collective-permute-start.2) | collective-permute-done | bytes 73760 | tf_op jit(solution)/shard_map/ppermute | solution.py:585
  27.4 2.3 %blend.1 = (bf16[32,80,128]{2,1,0:T(8,128)(2,1)}, bf16[32,64,128]{2,1,0:T(8,128)(2,1)}) custom-call(s32[1]{0:T(128)S(6)} %copy.12.cell, bf16[288,128]{1,0:T(8,128)(2,1)S(1)} %broadcast_select_fusion.2.strips, f32[816,1024]{1,0:T(8,128)S(1)} %get-tuple-element.63.state), custom_call_target="tpu_custom_call" | custom-call | flops 1000000 | bytes 10000 | tf_op jit(solution)/shard_map/blend/pallas_call | solution.py:410
  29.7 1.5 %collective-permute-start.10 = (bf16[32,64,128]{2,1,0:T(8,128)(2,1)}, bf16[32,64,128]{2,1,0:T(8,128)(2,1)S(1)}, u32[]{:S(2)}, u32[]{:S(2)}) collective-permute-start(bf16[32,64,128]{2,1,0:T(8,128)(2,1)} %get-tuple-element.73.refs_0_), channel_id=1, source_target_pairs={{0,4},{4,0},{8,12},{12,8},{16,20},{20,16},{24,28},{28,24},{1,5},{5... | collective-permute-start | bytes 1572872 | tf_op jit(solution)/shard_map/ppermute | solution.py:585
  32.0 1.6 %routes.2 = (s32[4,33]{1,0:T(4,128)}, s32[4]{0:T(128)}) custom-call(s32[4,32]{1,0:T(4,128)} %get-tuple-element.69.spot), custom_call_target="tpu_custom_call" | custom-call | tf_op jit(solution)/shard_map/routes/pallas_call | solution.py:433
  33.6 1.6 %routes.3 = (s32[4,33]{1,0:T(4,128)}, s32[4]{0:T(128)}) custom-call(s32[4,32]{1,0:T(4,128)} %get-tuple-element.77.spot), custom_call_target="tpu_custom_call" | custom-call | tf_op jit(solution)/shard_map/routes/pallas_call | solution.py:433
  40.0 3.4 %collective-permute-done.10.refs_2_ = bf16[32,64,128]{2,1,0:T(8,128)(2,1)S(1)} collective-permute-done((bf16[32,64,128]{2,1,0:T(8,128)(2,1)}, bf16[32,64,128]{2,1,0:T(8,128)(2,1)S(1)}, u32[]{:S(2)}, u32[]{:S(2)}) %collective-permute-start.10) | collective-permute-done | bytes 524320 | tf_op jit(solution)/shard_map/ppermute | solution.py:585
  43.5 1.5 %collective-permute-start.14 = (bf16[16,32,128]{2,1,0:T(8,128)(2,1)S(1)}, bf16[16,32,128]{2,1,0:T(8,128)(2,1)S(1)}, u32[]{:S(2)}, u32[]{:S(2)}) collective-permute-start(bf16[16,32,128]{2,1,0:T(8,128)(2,1)S(1)} %get-tuple-element.84), channel_id=1, source_target_pairs={{0,4},{4,0},{8,12},{12,8},{16,20},{20,16},{24,28},{28,24},{1,5},{5... | collective-permute-start | bytes 393224 | tf_op jit(solution)/shard_map/ppermute | solution.py:585
  46.6 1.8 %gather_rows.4 = (f32[16,64,128]{2,1,0:T(8,128)S(1)}, bf16[16,64,128]{2,1,0:T(8,128)(2,1)S(1)}) custom-call(s32[4,33]{1,0:T(4,128)S(1)} %copy-done.9, s32[4]{0:T(128)S(1)} %copy-done.10, bf16[32,64,128]{2,1,0:T(8,128)(2,1)} %get-tuple-element.73.refs_0_, bf16[32,64,128]{2,1,0:T(8,128)(2,1)S(1)} %collective-permute-done.12.refs_1_, ...), custom_call_target="tpu_custom_call" | custom-call | flops 1000000 | bytes 10000 | tf_op jit(solution)/shard_map/gather_rows/pallas_call | solution.py:467
  52.8 1.8 %gather_rows.5 = (f32[16,80,128]{2,1,0:T(8,128)S(1)}, bf16[16,80,128]{2,1,0:T(8,128)(2,1)S(1)}) custom-call(s32[4,33]{1,0:T(4,128)S(1)} %copy-done.6, s32[4]{0:T(128)S(1)} %copy-done.8, bf16[32,80,128]{2,1,0:T(8,128)(2,1)} %get-tuple-element.72.refs_0_, bf16[32,80,128]{2,1,0:T(8,128)(2,1)S(1)} %collective-permute-done.8.refs_1_, ...), custom_call_target="tpu_custom_call" | custom-call | flops 1000000 | bytes 10000 | tf_op jit(solution)/shard_map/gather_rows/pallas_call | solution.py:467
  54.6 1.5 %collective-permute-start.16 = (bf16[16,80,128]{2,1,0:T(8,128)(2,1)S(1)}, bf16[16,80,128]{2,1,0:T(8,128)(2,1)S(1)}, u32[]{:S(2)}, u32[]{:S(2)}) collective-permute-start(bf16[16,80,128]{2,1,0:T(8,128)(2,1)S(1)} %get-tuple-element.87), channel_id=1, source_target_pairs={{0,4},{4,0},{8,12},{12,8},{16,20},{20,16},{24,28},{28,24},{1,5},{5... | collective-permute-start | bytes 983048 | tf_op jit(solution)/shard_map/ppermute | solution.py:585
  56.1 2.0 %collective-permute-done.17.refs_2_ = bf16[16,64,128]{2,1,0:T(8,128)(2,1)S(1)} collective-permute-done((bf16[16,64,128]{2,1,0:T(8,128)(2,1)S(1)}, bf16[16,64,128]{2,1,0:T(8,128)(2,1)S(1)}, u32[]{:S(2)}, u32[]{:S(2)}) %collective-permute-start.17) | collective-permute-done | bytes 262176 | tf_op jit(solution)/shard_map/ppermute | solution.py:585
  58.7 2.6 %collective-permute-start.19 = (bf16[4,96,128]{2,1,0:T(8,128)(2,1)S(1)}, bf16[4,96,128]{2,1,0:T(8,128)(2,1)S(1)}, u32[]{:S(2)}, u32[]{:S(2)}) collective-permute-start(bf16[4,96,128]{2,1,0:T(8,128)(2,1)S(1)} %get-tuple-element.94), channel_id=1, source_target_pairs={{0,16},{4,20},{8,24},{12,28},{16,0},{20,4},{24,8},{28,12},{1,17},{... | collective-permute-start | bytes 294920 | tf_op jit(solution)/shard_map/ppermute | solution.py:585
  62.6 1.7 %collective-permute-done.18.refs_5_ = bf16[4,96,128]{2,1,0:T(8,128)(2,1)S(1)} collective-permute-done((bf16[4,96,128]{2,1,0:T(8,128)(2,1)S(1)}, bf16[4,96,128]{2,1,0:T(8,128)(2,1)S(1)}, u32[]{:S(2)}, u32[]{:S(2)}) %collective-permute-start.18) | collective-permute-done | bytes 98336 | tf_op jit(solution)/shard_map/ppermute | solution.py:585
  64.4 4.5 %collective-permute-done.19.refs_6_ = bf16[4,96,128]{2,1,0:T(8,128)(2,1)S(1)} collective-permute-done((bf16[4,96,128]{2,1,0:T(8,128)(2,1)S(1)}, bf16[4,96,128]{2,1,0:T(8,128)(2,1)S(1)}, u32[]{:S(2)}, u32[]{:S(2)}) %collective-permute-start.19) | collective-permute-done | bytes 98336 | tf_op jit(solution)/shard_map/ppermute | solution.py:585
  69.0 2.2 %collective-permute-start.21 = (bf16[4,80,128]{2,1,0:T(8,128)(2,1)S(1)}, bf16[4,80,128]{2,1,0:T(8,128)(2,1)S(1)}, u32[]{:S(2)}, u32[]{:S(2)}) collective-permute-start(bf16[4,80,128]{2,1,0:T(8,128)(2,1)S(1)} %get-tuple-element.98), channel_id=1, source_target_pairs={{0,8},{4,12},{8,0},{12,4},{16,24},{20,28},{24,16},{28,20},{1,9},{5... | collective-permute-start | bytes 245768 | tf_op jit(solution)/shard_map/ppermute | solution.py:585
  71.2 1.6 %collective-permute-start.22 = (bf16[4,80,128]{2,1,0:T(8,128)(2,1)S(1)}, bf16[4,80,128]{2,1,0:T(8,128)(2,1)S(1)}, u32[]{:S(2)}, u32[]{:S(2)}) collective-permute-start(bf16[4,80,128]{2,1,0:T(8,128)(2,1)S(1)} %get-tuple-element.99), channel_id=1, source_target_pairs={{0,16},{4,20},{8,24},{12,28},{16,0},{20,4},{24,8},{28,12},{1,17},{... | collective-permute-start | bytes 245768 | tf_op jit(solution)/shard_map/ppermute | solution.py:585
  74.3 6.4 %collective-permute-done.22.refs_2_ = bf16[4,80,128]{2,1,0:T(8,128)(2,1)S(1)} collective-permute-done((bf16[4,80,128]{2,1,0:T(8,128)(2,1)S(1)}, bf16[4,80,128]{2,1,0:T(8,128)(2,1)S(1)}, u32[]{:S(2)}, u32[]{:S(2)}) %collective-permute-start.22) | collective-permute-done | bytes 81952 | tf_op jit(solution)/shard_map/ppermute | solution.py:585
  80.7 2.2 %collapse.1 = f32[3,4,4096]{2,1,0:T(4,128)} custom-call(bf16[192,1280]{1,0:T(8,128)(2,1)S(1)} %copy-done, f32[4,80,128]{2,1,0:T(8,128)S(1)} %get-tuple-element.97.refs_0_, bf16[4,80,128]{2,1,0:T(8,128)(2,1)S(1)} %collective-permute-done.21.refs_1_, bf16[4,80,128]{2,1,0:T(8,128)(2,1)S(1)} %collective-permute-done.22.refs_2_, ...), custom_call_target="tpu_custom_call" | custom-call | flops 1000000 | bytes 10000 | tf_op jit(solution)/shard_map/collapse/pallas_call | solution.py:572
  (73 shorter events, 22.5 us)
Async XLA Ops:
  5.4 10.9 %collective-permute-start.5 = (s32[32]{0:T(128)S(1)}, s32[32]{0:T(128)S(1)}, u32[]{:S(2)}, u32[]{:S(2)}) collective-permute-start(s32[32]{0:T(128)S(1)} %bitcast_add_fusion), channel_id=1, source_target_pairs={{0,1},{1,0},{2,3},{3,2},{4,5},{5,4},{6,7},{7,6},{8,9},{9,8},{10,11... | collective-permute-start | bytes 392 | tf_op jit(solution)/shard_map/ppermute | solution.py:585
  5.9 8.7 %collective-permute-start = (bf16[288,128]{1,0:T(8,128)(2,1)S(1)}, bf16[288,128]{1,0:T(8,128)(2,1)S(1)}, u32[]{:S(2)}, u32[]{:S(2)}) collective-permute-start(bf16[288,128]{1,0:T(8,128)(2,1)S(1)} %strips.1), channel_id=1, source_target_pairs={{0,4},{4,0},{8,12},{12,8},{16,20},{20,16},{24,28},{28,24},{1,5},{5... | collective-permute-start | bytes 221192 | tf_op jit(solution)/shard_map/ppermute | solution.py:585
  14.6 4.4 %collective-permute-start.1 = (bf16[288,128]{1,0:T(8,128)(2,1)S(1)}, bf16[288,128]{1,0:T(8,128)(2,1)S(1)}, u32[]{:S(2)}, u32[]{:S(2)}) collective-permute-start(bf16[288,128]{1,0:T(8,128)(2,1)S(1)} %broadcast_select_fusion), channel_id=1, source_target_pairs={{0,8},{4,12},{8,0},{12,4},{16,24},{20,28},{24,16},{28,20},{1,9},{5... | collective-permute-start | bytes 221192 | tf_op jit(solution)/shard_map/ppermute | solution.py:585
  16.3 5.4 %collective-permute-start.7 = (s32[2,32]{1,0:T(2,128)S(1)}, s32[2,32]{1,0:T(2,128)S(1)}, u32[]{:S(2)}, u32[]{:S(2)}) collective-permute-start(s32[2,32]{1,0:T(2,128)S(1)} %pad_add_fusion.3), channel_id=1, source_target_pairs={{0,4},{4,0},{8,12},{12,8},{16,20},{20,16},{24,28},{28,24},{1,5},{5... | collective-permute-start | bytes 776 | tf_op jit(solution)/shard_map/ppermute | solution.py:585
  16.8 4.9 %collective-permute-start.6 = (s32[2,32]{1,0:T(2,128)S(1)}, s32[2,32]{1,0:T(2,128)S(1)}, u32[]{:S(2)}, u32[]{:S(2)}) collective-permute-start(s32[2,32]{1,0:T(2,128)S(1)} %pad_add_fusion.3), channel_id=1, source_target_pairs={{0,2},{1,3},{2,0},{3,1},{4,6},{5,7},{6,4},{7,5},{8,10},{9,11},{10,... | collective-permute-start | bytes 776 | tf_op jit(solution)/shard_map/ppermute | solution.py:585
  18.3 7.5 %collective-permute-start.4 = (bf16[32,32,128]{2,1,0:T(8,128)(2,1)}, bf16[32,32,128]{2,1,0:T(8,128)(2,1)S(1)}, u32[]{:S(2)}, u32[]{:S(2)}) collective-permute-start(bf16[32,32,128]{2,1,0:T(8,128)(2,1)} %copy-done.1), channel_id=1, source_target_pairs={{0,1},{1,0},{2,3},{3,2},{4,5},{5,4},{6,7},{7,6},{8,9},{9,8},{10,11... | collective-permute-start | bytes 786440 | tf_op jit(solution)/shard_map/ppermute | solution.py:585
  18.3 9.0 %collective-permute-start.3 = (bf16[32,32,128]{2,1,0:T(8,128)(2,1)}, bf16[32,32,128]{2,1,0:T(8,128)(2,1)}, u32[]{:S(2)}, u32[]{:S(2)}) collective-permute-start(bf16[32,32,128]{2,1,0:T(8,128)(2,1)} %copy-done.1), channel_id=1, source_target_pairs={{0,2},{1,3},{2,0},{3,1},{4,6},{5,7},{6,4},{7,5},{8,10},{9,11},{10,... | collective-permute-start | bytes 786440 | tf_op jit(solution)/shard_map/ppermute | solution.py:585
  19.1 6.7 %collective-permute-start.2 = (bf16[288,128]{1,0:T(8,128)(2,1)S(1)}, bf16[288,128]{1,0:T(8,128)(2,1)S(1)}, u32[]{:S(2)}, u32[]{:S(2)}) collective-permute-start(bf16[288,128]{1,0:T(8,128)(2,1)S(1)} %broadcast_select_fusion.1), channel_id=1, source_target_pairs={{0,16},{4,20},{8,24},{12,28},{16,0},{20,4},{24,8},{28,12},{1,17},{... | collective-permute-start | bytes 221192 | tf_op jit(solution)/shard_map/ppermute | solution.py:585
  29.7 13.8 %collective-permute-start.10 = (bf16[32,64,128]{2,1,0:T(8,128)(2,1)}, bf16[32,64,128]{2,1,0:T(8,128)(2,1)S(1)}, u32[]{:S(2)}, u32[]{:S(2)}) collective-permute-start(bf16[32,64,128]{2,1,0:T(8,128)(2,1)} %get-tuple-element.73.refs_0_), channel_id=1, source_target_pairs={{0,4},{4,0},{8,12},{12,8},{16,20},{20,16},{24,28},{28,24},{1,5},{5... | collective-permute-start | bytes 1572872 | tf_op jit(solution)/shard_map/ppermute | solution.py:585
  31.2 4.1 %collective-permute-start.11 = (bf16[32,32,128]{2,1,0:T(8,128)(2,1)}, bf16[32,32,128]{2,1,0:T(8,128)(2,1)S(1)}, u32[]{:S(2)}, u32[]{:S(2)}) collective-permute-start(bf16[32,32,128]{2,1,0:T(8,128)(2,1)} %collective-permute-done.3.refs_2_), channel_id=1, source_target_pairs={{0,1},{1,0},{2,3},{3,2},{4,5},{5,4},{6,7},{7,6},{8,9},{9,8},{10,11... | collective-permute-start | bytes 786440 | tf_op jit(solution)/shard_map/ppermute | solution.py:585
  31.2 18.2 %collective-permute-start.9 = (bf16[32,80,128]{2,1,0:T(8,128)(2,1)}, bf16[32,80,128]{2,1,0:T(8,128)(2,1)S(1)}, u32[]{:S(2)}, u32[]{:S(2)}) collective-permute-start(bf16[32,80,128]{2,1,0:T(8,128)(2,1)} %get-tuple-element.72.refs_0_), channel_id=1, source_target_pairs={{0,2},{1,3},{2,0},{3,1},{4,6},{5,7},{6,4},{7,5},{8,10},{9,11},{10,... | collective-permute-start | bytes 1966088 | tf_op jit(solution)/shard_map/ppermute | solution.py:585
  31.8 13.5 %collective-permute-start.12 = (bf16[32,64,128]{2,1,0:T(8,128)(2,1)}, bf16[32,64,128]{2,1,0:T(8,128)(2,1)S(1)}, u32[]{:S(2)}, u32[]{:S(2)}) collective-permute-start(bf16[32,64,128]{2,1,0:T(8,128)(2,1)} %get-tuple-element.73.refs_0_), channel_id=1, source_target_pairs={{0,1},{1,0},{2,3},{3,2},{4,5},{5,4},{6,7},{7,6},{8,9},{9,8},{10,11... | collective-permute-start | bytes 1572872 | tf_op jit(solution)/shard_map/ppermute | solution.py:585
  43.5 1.9 %collective-permute-start.13 = (bf16[32,64,128]{2,1,0:T(8,128)(2,1)S(1)}, bf16[32,64,128]{2,1,0:T(8,128)(2,1)S(1)}, u32[]{:S(2)}, u32[]{:S(2)}) collective-permute-start(bf16[32,64,128]{2,1,0:T(8,128)(2,1)S(1)} %collective-permute-done.10.refs_2_), channel_id=1, source_target_pairs={{0,1},{1,0},{2,3},{3,2},{4,5},{5,4},{6,7},{7,6},{8,9},{9,8},{10,11... | collective-permute-start | bytes 1572872 | tf_op jit(solution)/shard_map/ppermute | solution.py:585
  43.5 5.9 %collective-permute-start.14 = (bf16[16,32,128]{2,1,0:T(8,128)(2,1)S(1)}, bf16[16,32,128]{2,1,0:T(8,128)(2,1)S(1)}, u32[]{:S(2)}, u32[]{:S(2)}) collective-permute-start(bf16[16,32,128]{2,1,0:T(8,128)(2,1)S(1)} %get-tuple-element.84), channel_id=1, source_target_pairs={{0,4},{4,0},{8,12},{12,8},{16,20},{20,16},{24,28},{28,24},{1,5},{5... | collective-permute-start | bytes 393224 | tf_op jit(solution)/shard_map/ppermute | solution.py:585
  45.0 5.2 %collective-permute-start.8 = (bf16[32,80,128]{2,1,0:T(8,128)(2,1)}, bf16[32,80,128]{2,1,0:T(8,128)(2,1)S(1)}, u32[]{:S(2)}, u32[]{:S(2)}) collective-permute-start(bf16[32,80,128]{2,1,0:T(8,128)(2,1)} %get-tuple-element.72.refs_0_), channel_id=1, source_target_pairs={{0,1},{1,0},{2,3},{3,2},{4,5},{5,4},{6,7},{7,6},{8,9},{9,8},{10,11... | collective-permute-start | bytes 1966088 | tf_op jit(solution)/shard_map/ppermute | solution.py:585
  49.4 2.1 %collective-permute-start.15 = (bf16[32,80,128]{2,1,0:T(8,128)(2,1)S(1)}, bf16[32,80,128]{2,1,0:T(8,128)(2,1)S(1)}, u32[]{:S(2)}, u32[]{:S(2)}) collective-permute-start(bf16[32,80,128]{2,1,0:T(8,128)(2,1)S(1)} %collective-permute-done.9.refs_2_), channel_id=1, source_target_pairs={{0,1},{1,0},{2,3},{3,2},{4,5},{5,4},{6,7},{7,6},{8,9},{9,8},{10,11... | collective-permute-start | bytes 1966088 | tf_op jit(solution)/shard_map/ppermute | solution.py:585
  49.4 8.7 %collective-permute-start.17 = (bf16[16,64,128]{2,1,0:T(8,128)(2,1)S(1)}, bf16[16,64,128]{2,1,0:T(8,128)(2,1)S(1)}, u32[]{:S(2)}, u32[]{:S(2)}) collective-permute-start(bf16[16,64,128]{2,1,0:T(8,128)(2,1)S(1)} %get-tuple-element.90), channel_id=1, source_target_pairs={{0,2},{1,3},{2,0},{3,1},{4,6},{5,7},{6,4},{7,5},{8,10},{9,11},{10,... | collective-permute-start | bytes 786440 | tf_op jit(solution)/shard_map/ppermute | solution.py:585
  54.6 14.3 %collective-permute-start.16 = (bf16[16,80,128]{2,1,0:T(8,128)(2,1)S(1)}, bf16[16,80,128]{2,1,0:T(8,128)(2,1)S(1)}, u32[]{:S(2)}, u32[]{:S(2)}) collective-permute-start(bf16[16,80,128]{2,1,0:T(8,128)(2,1)S(1)} %get-tuple-element.87), channel_id=1, source_target_pairs={{0,4},{4,0},{8,12},{12,8},{16,20},{20,16},{24,28},{28,24},{1,5},{5... | collective-permute-start | bytes 983048 | tf_op jit(solution)/shard_map/ppermute | solution.py:585
  58.2 6.2 %collective-permute-start.18 = (bf16[4,96,128]{2,1,0:T(8,128)(2,1)S(1)}, bf16[4,96,128]{2,1,0:T(8,128)(2,1)S(1)}, u32[]{:S(2)}, u32[]{:S(2)}) collective-permute-start(bf16[4,96,128]{2,1,0:T(8,128)(2,1)S(1)} %get-tuple-element.93), channel_id=1, source_target_pairs={{0,8},{4,12},{8,0},{12,4},{16,24},{20,28},{24,16},{28,20},{1,9},{5... | collective-permute-start | bytes 294920 | tf_op jit(solution)/shard_map/ppermute | solution.py:585
  58.7 10.2 %collective-permute-start.19 = (bf16[4,96,128]{2,1,0:T(8,128)(2,1)S(1)}, bf16[4,96,128]{2,1,0:T(8,128)(2,1)S(1)}, u32[]{:S(2)}, u32[]{:S(2)}) collective-permute-start(bf16[4,96,128]{2,1,0:T(8,128)(2,1)S(1)} %get-tuple-element.94), channel_id=1, source_target_pairs={{0,16},{4,20},{8,24},{12,28},{16,0},{20,4},{24,8},{28,12},{1,17},{... | collective-permute-start | bytes 294920 | tf_op jit(solution)/shard_map/ppermute | solution.py:585
  61.3 7.6 %collective-permute-start.20 = (bf16[4,96,128]{2,1,0:T(8,128)(2,1)S(1)}, bf16[4,96,128]{2,1,0:T(8,128)(2,1)S(1)}, u32[]{:S(2)}, u32[]{:S(2)}) collective-permute-start(bf16[4,96,128]{2,1,0:T(8,128)(2,1)S(1)} %get-tuple-element.95), channel_id=1, source_target_pairs={{0,24},{4,28},{8,16},{12,20},{16,8},{20,12},{24,0},{28,4},{1,25},{... | collective-permute-start | bytes 294920 | tf_op jit(solution)/shard_map/ppermute | solution.py:585
  69.0 5.3 %collective-permute-start.21 = (bf16[4,80,128]{2,1,0:T(8,128)(2,1)S(1)}, bf16[4,80,128]{2,1,0:T(8,128)(2,1)S(1)}, u32[]{:S(2)}, u32[]{:S(2)}) collective-permute-start(bf16[4,80,128]{2,1,0:T(8,128)(2,1)S(1)} %get-tuple-element.98), channel_id=1, source_target_pairs={{0,8},{4,12},{8,0},{12,4},{16,24},{20,28},{24,16},{28,20},{1,9},{5... | collective-permute-start | bytes 245768 | tf_op jit(solution)/shard_map/ppermute | solution.py:585
  71.2 9.4 %collective-permute-start.22 = (bf16[4,80,128]{2,1,0:T(8,128)(2,1)S(1)}, bf16[4,80,128]{2,1,0:T(8,128)(2,1)S(1)}, u32[]{:S(2)}, u32[]{:S(2)}) collective-permute-start(bf16[4,80,128]{2,1,0:T(8,128)(2,1)S(1)} %get-tuple-element.99), channel_id=1, source_target_pairs={{0,16},{4,20},{8,24},{12,28},{16,0},{20,4},{24,8},{28,12},{1,17},{... | collective-permute-start | bytes 245768 | tf_op jit(solution)/shard_map/ppermute | solution.py:585
  72.9 7.8 %collective-permute-start.23 = (bf16[4,80,128]{2,1,0:T(8,128)(2,1)S(1)}, bf16[4,80,128]{2,1,0:T(8,128)(2,1)S(1)}, u32[]{:S(2)}, u32[]{:S(2)}) collective-permute-start(bf16[4,80,128]{2,1,0:T(8,128)(2,1)S(1)} %get-tuple-element.100), channel_id=1, source_target_pairs={{0,24},{4,28},{8,16},{12,20},{16,8},{20,12},{24,0},{28,4},{1,25},{... | collective-permute-start | bytes 245768 | tf_op jit(solution)/shard_map/ppermute | solution.py:585
  (16 other events, 61.6 us)

commit v11 on v10

--- a/solution.py
+++ b/solution.py
@@ -644,7 +644,7 @@
     home_f, away_f = gather(routes_x, first, near_first, far_first, far_near)
     got_f = swap(away_f, "frames", 1)
     got_second = along(*add_halves((home_s, home_w), (got_s, got_w)))
-    got_f, got_second = tie((got_f, got_second))
+    got_f, got_second[1] = tie((got_f, got_second[1]))
     got_first = along(*add_halves((home_f,), (got_f,)))
     return collapse(got_first, got_second)
 

time: 83.4 us -> 79 us (0.947)
  waiting for transfers between devices: 25 us -> 21.5 us
    ppermute x24, waiting for transfers between devices: 25 us -> 21.5 us  [swap(): return lax.ppermute(value, axis, [(i, i ^ bit) for i in range(size)])]
  transfers between devices with their start and end apart: 24 -> 24, of which waited for: 11 -> 13; matrix products, arithmetic and copies ran while one was open for 1% -> 1% of each run, Pallas kernels for 16% -> 17%
where the time goes in v11:
time: 79 us; the launch traced here: 78.5 us
  starting transfers between devices  25.4 us (32%)
  waiting for transfers between devices  21.5 us (27%)
  Pallas kernels  19.3 us (24%)
  local copies, waits for them, and re-layouts  9.41 us (12%)
  between operations  1.47 us (2%)
  other arithmetic  1.34 us (2%)
    ppermute x24, starting transfers between devices, swap(): return lax.ppermute(value, axis, [(i, i ^ bit) for i in range(size)])  25.4 us
    ppermute x24, waiting for transfers between devices, swap(): return lax.ppermute(value, axis, [(i, i ^ bit) for i in range(size)])  21.5 us
    unnamed x32, local copies, waits for them, and re-layouts  9.41 us
    pallas_call x3, Pallas kernels, gather_rows(): pl.pallas_call(gather_kernel, in_specs=[pl.BlockSpec(memory_space=pltpu.S...  4.88 us
    pallas_call x1, Pallas kernels, bands_of(): pl.pallas_call(functools.partial(bands_kernel, small_places, large_places...  4.68 us
    pallas_call x2, Pallas kernels, routes_of(): pl.pallas_call(routes_kernel, in_specs=[smem], out_specs=[smem, smem], ou...  3.29 us
    pallas_call x1, Pallas kernels, blend(): pl.pallas_call(blend_kernel, in_specs=[pl.BlockSpec(memory_space=pltpu.SM...  2.3 us
    pallas_call x1, Pallas kernels, collapse(): pl.pallas_call(functools.partial(collapse_kernel, places, len(b)), out_sh...  2.18 us
  transfers between devices with their start and end apart: 24, of which 13 were waited for; matrix products, arithmetic and copies ran while one was open for 1% of the time, Pallas kernels for 17%

profile of v11, /device:TPU:0, one launch (start us, length us, event | category | flops | bytes accessed | tf_op | source)
XLA Modules:
  0.0 78.5 jit_solution(15430899703184848367)
XLA Ops:
  3.5 1.9 %strips.1 = bf16[288,128]{1,0:T(8,128)(2,1)S(1)} custom-call(s32[1]{0:T(128)S(6)} %copy.12.cell, bf16[1,3,128,1024]{3,2,1,0:T(8,128)(2,1)S(1)} %copy-done.11, bf16[1,3,128,1024]{3,2,1,0:T(8,128)(2,1)S(1)} %copy-done.11, bf16[512,512]{1,0:T(8,128)(2,1)S(1)} %copy-done.15), custom_call_target="tpu_custom_call" | custom-call | flops 2000000000 | bytes 1000000 | tf_op jit(solution)/shard_map/strips/pallas_call | solution.py:247
  5.9 2.6 %collective-permute-start = (bf16[288,128]{1,0:T(8,128)(2,1)S(1)}, bf16[288,128]{1,0:T(8,128)(2,1)S(1)}, u32[]{:S(2)}, u32[]{:S(2)}) collective-permute-start(bf16[288,128]{1,0:T(8,128)(2,1)S(1)} %strips.1), channel_id=1, source_target_pairs={{0,4},{4,0},{8,12},{12,8},{16,20},{20,16},{24,28},{28,24},{1,5},{5... | collective-permute-start | bytes 221192 | tf_op jit(solution)/shard_map/ppermute | solution.py:585
  8.5 4.7 %bands.1 = (bf16[32,32,128]{2,1,0:T(8,128)(2,1)S(1)}, f32[816,1024]{1,0:T(8,128)S(1)}) custom-call(bf16[1,3,128,1024]{3,2,1,0:T(8,128)(2,1)S(1)} %copy-done.11, bf16[1,128,1024]{2,1,0:T(8,128)(2,1)S(1)} %copy-done.12, s32[1,64,128]{2,1,0:T(8,128)S(1)} %bitcast.13, bf16[512,512]{1,0:T(8,128)(2,1)S(1)} %copy-done.15, bf16[512,640]{1,0:T(8,128)(2,1)S(1)} %copy-done.14), custom_call_target="tpu_custom_call" | custom-call | flops 8000000000 | bytes 6000000 | tf_op jit(solution)/shard_map/bands/pallas_call | solution.py:339
  14.6 1.6 %collective-permute-start.1 = (bf16[288,128]{1,0:T(8,128)(2,1)S(1)}, bf16[288,128]{1,0:T(8,128)(2,1)S(1)}, u32[]{:S(2)}, u32[]{:S(2)}) collective-permute-start(bf16[288,128]{1,0:T(8,128)(2,1)S(1)} %broadcast_select_fusion), channel_id=1, source_target_pairs={{0,8},{4,12},{8,0},{12,4},{16,24},{20,28},{24,16},{28,20},{1,9},{5... | collective-permute-start | bytes 221192 | tf_op jit(solution)/shard_map/ppermute | solution.py:585
  16.8 1.5 %collective-permute-start.6 = (s32[2,32]{1,0:T(2,128)S(1)}, s32[2,32]{1,0:T(2,128)S(1)}, u32[]{:S(2)}, u32[]{:S(2)}) collective-permute-start(s32[2,32]{1,0:T(2,128)S(1)} %pad_add_fusion.3), channel_id=1, source_target_pairs={{0,2},{1,3},{2,0},{3,1},{4,6},{5,7},{6,4},{7,5},{8,10},{9,11},{10,... | collective-permute-start | bytes 776 | tf_op jit(solution)/shard_map/ppermute | solution.py:585
  19.0 2.7 %collective-permute-start.2 = (bf16[288,128]{1,0:T(8,128)(2,1)S(1)}, bf16[288,128]{1,0:T(8,128)(2,1)S(1)}, u32[]{:S(2)}, u32[]{:S(2)}) collective-permute-start(bf16[288,128]{1,0:T(8,128)(2,1)S(1)} %broadcast_select_fusion.1), channel_id=1, source_target_pairs={{0,16},{4,20},{8,24},{12,28},{16,0},{20,4},{24,8},{28,12},{1,17},{... | collective-permute-start | bytes 221192 | tf_op jit(solution)/shard_map/ppermute | solution.py:585
  22.3 3.5 %collective-permute-done.2 = bf16[288,128]{1,0:T(8,128)(2,1)S(1)} collective-permute-done((bf16[288,128]{1,0:T(8,128)(2,1)S(1)}, bf16[288,128]{1,0:T(8,128)(2,1)S(1)}, u32[]{:S(2)}, u32[]{:S(2)}) %collective-permute-start.2) | collective-permute-done | bytes 73760 | tf_op jit(solution)/shard_map/ppermute | solution.py:585
  27.4 2.3 %blend.1 = (bf16[32,80,128]{2,1,0:T(8,128)(2,1)}, bf16[32,64,128]{2,1,0:T(8,128)(2,1)}) custom-call(s32[1]{0:T(128)S(6)} %copy.12.cell, bf16[288,128]{1,0:T(8,128)(2,1)S(1)} %broadcast_select_fusion.2.strips, f32[816,1024]{1,0:T(8,128)S(1)} %get-tuple-element.60.state), custom_call_target="tpu_custom_call" | custom-call | flops 1000000 | bytes 10000 | tf_op jit(solution)/shard_map/blend/pallas_call | solution.py:410
  29.7 1.5 %collective-permute-start.10 = (bf16[32,64,128]{2,1,0:T(8,128)(2,1)}, bf16[32,64,128]{2,1,0:T(8,128)(2,1)S(1)}, u32[]{:S(2)}, u32[]{:S(2)}) collective-permute-start(bf16[32,64,128]{2,1,0:T(8,128)(2,1)} %get-tuple-element.70.refs_0_), channel_id=1, source_target_pairs={{0,4},{4,0},{8,12},{12,8},{16,20},{20,16},{24,28},{28,24},{1,5},{5... | collective-permute-start | bytes 1572872 | tf_op jit(solution)/shard_map/ppermute | solution.py:585
  32.0 1.6 %routes.2 = (s32[4,33]{1,0:T(4,128)}, s32[4]{0:T(128)}) custom-call(s32[4,32]{1,0:T(4,128)} %get-tuple-element.66.spot), custom_call_target="tpu_custom_call" | custom-call | tf_op jit(solution)/shard_map/routes/pallas_call | solution.py:433
  33.6 1.6 %routes.3 = (s32[4,33]{1,0:T(4,128)}, s32[4]{0:T(128)}) custom-call(s32[4,32]{1,0:T(4,128)} %get-tuple-element.74.spot), custom_call_target="tpu_custom_call" | custom-call | tf_op jit(solution)/shard_map/routes/pallas_call | solution.py:433
  38.5 1.4 %gather_rows.3 = (f32[16,32,128]{2,1,0:T(8,128)S(1)}, bf16[16,32,128]{2,1,0:T(8,128)(2,1)S(1)}) custom-call(s32[4,33]{1,0:T(4,128)S(1)} %copy-done.5, s32[4]{0:T(128)S(1)} %copy-done.7, bf16[32,32,128]{2,1,0:T(8,128)(2,1)S(1)} %copy-done.2, bf16[32,32,128]{2,1,0:T(8,128)(2,1)S(1)} %copy-done.4, bf16[32,32,128]{2,1,0:T(8,128)(2,1)} %collective-permute-done.3.refs_2_, ...), custom_call_target="tpu_custom_call" | custom-call | flops 1000000 | bytes 10000 | tf_op jit(solution)/shard_map/gather_rows/pallas_call | solution.py:467
  40.0 3.5 %collective-permute-done.10.refs_2_ = bf16[32,64,128]{2,1,0:T(8,128)(2,1)S(1)} collective-permute-done((bf16[32,64,128]{2,1,0:T(8,128)(2,1)}, bf16[32,64,128]{2,1,0:T(8,128)(2,1)S(1)}, u32[]{:S(2)}, u32[]{:S(2)}) %collective-permute-start.10) | collective-permute-done | bytes 524320 | tf_op jit(solution)/shard_map/ppermute | solution.py:585
  43.5 1.5 %collective-permute-start.14 = (bf16[16,32,128]{2,1,0:T(8,128)(2,1)S(1)}, bf16[16,32,128]{2,1,0:T(8,128)(2,1)S(1)}, u32[]{:S(2)}, u32[]{:S(2)}) collective-permute-start(bf16[16,32,128]{2,1,0:T(8,128)(2,1)S(1)} %get-tuple-element.81), channel_id=1, source_target_pairs={{0,4},{4,0},{8,12},{12,8},{16,20},{20,16},{24,28},{28,24},{1,5},{5... | collective-permute-start | bytes 393224 | tf_op jit(solution)/shard_map/ppermute | solution.py:585
  46.6 1.7 %gather_rows.4 = (f32[16,64,128]{2,1,0:T(8,128)S(1)}, bf16[16,64,128]{2,1,0:T(8,128)(2,1)S(1)}) custom-call(s32[4,33]{1,0:T(4,128)S(1)} %copy-done.9, s32[4]{0:T(128)S(1)} %copy-done.10, bf16[32,64,128]{2,1,0:T(8,128)(2,1)} %get-tuple-element.70.refs_0_, bf16[32,64,128]{2,1,0:T(8,128)(2,1)S(1)} %collective-permute-done.12.refs_1_, ...), custom_call_target="tpu_custom_call" | custom-call | flops 1000000 | bytes 10000 | tf_op jit(solution)/shard_map/gather_rows/pallas_call | solution.py:467
  52.8 1.7 %gather_rows.5 = (f32[16,80,128]{2,1,0:T(8,128)S(1)}, bf16[16,80,128]{2,1,0:T(8,128)(2,1)S(1)}) custom-call(s32[4,33]{1,0:T(4,128)S(1)} %copy-done.6, s32[4]{0:T(128)S(1)} %copy-done.8, bf16[32,80,128]{2,1,0:T(8,128)(2,1)} %get-tuple-element.69.refs_0_, bf16[32,80,128]{2,1,0:T(8,128)(2,1)S(1)} %collective-permute-done.8.refs_1_, ...), custom_call_target="tpu_custom_call" | custom-call | flops 1000000 | bytes 10000 | tf_op jit(solution)/shard_map/gather_rows/pallas_call | solution.py:467
  54.5 1.6 %collective-permute-start.16 = (bf16[16,80,128]{2,1,0:T(8,128)(2,1)S(1)}, bf16[16,80,128]{2,1,0:T(8,128)(2,1)S(1)}, u32[]{:S(2)}, u32[]{:S(2)}) collective-permute-start(bf16[16,80,128]{2,1,0:T(8,128)(2,1)S(1)} %get-tuple-element.84), channel_id=1, source_target_pairs={{0,4},{4,0},{8,12},{12,8},{16,20},{20,16},{24,28},{28,24},{1,5},{5... | collective-permute-start | bytes 983048 | tf_op jit(solution)/shard_map/ppermute | solution.py:585
  56.2 1.9 %collective-permute-done.17.refs_2_ = bf16[16,64,128]{2,1,0:T(8,128)(2,1)S(1)} collective-permute-done((bf16[16,64,128]{2,1,0:T(8,128)(2,1)S(1)}, bf16[16,64,128]{2,1,0:T(8,128)(2,1)S(1)}, u32[]{:S(2)}, u32[]{:S(2)}) %collective-permute-start.17) | collective-permute-done | bytes 262176 | tf_op jit(solution)/shard_map/ppermute | solution.py:585
  58.7 2.6 %collective-permute-start.22 = (bf16[4,96,128]{2,1,0:T(8,128)(2,1)S(1)}, bf16[4,96,128]{2,1,0:T(8,128)(2,1)S(1)}, u32[]{:S(2)}, u32[]{:S(2)}) collective-permute-start(bf16[4,96,128]{2,1,0:T(8,128)(2,1)S(1)} %get-tuple-element.97), channel_id=1, source_target_pairs={{0,16},{4,20},{8,24},{12,28},{16,0},{20,4},{24,8},{28,12},{1,17},{... | collective-permute-start | bytes 294920 | tf_op jit(solution)/shard_map/ppermute | solution.py:585
  61.3 1.4 %collective-permute-start.23 = (bf16[4,96,128]{2,1,0:T(8,128)(2,1)S(1)}, bf16[4,96,128]{2,1,0:T(8,128)(2,1)S(1)}, u32[]{:S(2)}, u32[]{:S(2)}) collective-permute-start(bf16[4,96,128]{2,1,0:T(8,128)(2,1)S(1)} %get-tuple-element.98), channel_id=1, source_target_pairs={{0,24},{4,28},{8,16},{12,20},{16,8},{20,12},{24,0},{28,4},{1,25},{... | collective-permute-start | bytes 294920 | tf_op jit(solution)/shard_map/ppermute | solution.py:585
  62.6 1.8 %collective-permute-done.18.refs_5_ = bf16[4,96,128]{2,1,0:T(8,128)(2,1)S(1)} collective-permute-done((bf16[4,96,128]{2,1,0:T(8,128)(2,1)S(1)}, bf16[4,96,128]{2,1,0:T(8,128)(2,1)S(1)}, u32[]{:S(2)}, u32[]{:S(2)}) %collective-permute-start.18) | collective-permute-done | bytes 98336 | tf_op jit(solution)/shard_map/ppermute | solution.py:585
  65.1 2.7 %collective-permute-start.20 = (bf16[4,80,128]{2,1,0:T(8,128)(2,1)S(1)}, bf16[4,80,128]{2,1,0:T(8,128)(2,1)S(1)}, u32[]{:S(2)}, u32[]{:S(2)}) collective-permute-start(bf16[4,80,128]{2,1,0:T(8,128)(2,1)S(1)} %get-tuple-element.93), channel_id=1, source_target_pairs={{0,16},{4,20},{8,24},{12,28},{16,0},{20,4},{24,8},{28,12},{1,17},{... | collective-permute-start | bytes 245768 | tf_op jit(solution)/shard_map/ppermute | solution.py:585
  70.0 6.3 %collective-permute-done.20.refs_2_ = bf16[4,80,128]{2,1,0:T(8,128)(2,1)S(1)} collective-permute-done((bf16[4,80,128]{2,1,0:T(8,128)(2,1)S(1)}, bf16[4,80,128]{2,1,0:T(8,128)(2,1)S(1)}, u32[]{:S(2)}, u32[]{:S(2)}) %collective-permute-start.20) | collective-permute-done | bytes 81952 | tf_op jit(solution)/shard_map/ppermute | solution.py:585
  76.3 2.2 %collapse.1 = f32[3,4,4096]{2,1,0:T(4,128)} custom-call(bf16[192,1280]{1,0:T(8,128)(2,1)S(1)} %copy-done, f32[4,80,128]{2,1,0:T(8,128)S(1)} %get-tuple-element.91.refs_0_, bf16[4,80,128]{2,1,0:T(8,128)(2,1)S(1)} %collective-permute-done.19.refs_1_, bf16[4,80,128]{2,1,0:T(8,128)(2,1)S(1)} %collective-permute-done.20.refs_2_, ...), custom_call_target="tpu_custom_call" | custom-call | flops 1000000 | bytes 10000 | tf_op jit(solution)/shard_map/collapse/pallas_call | solution.py:572
  (73 shorter events, 21.3 us)
Async XLA Ops:
  5.4 10.9 %collective-permute-start.5 = (s32[32]{0:T(128)S(1)}, s32[32]{0:T(128)S(1)}, u32[]{:S(2)}, u32[]{:S(2)}) collective-permute-start(s32[32]{0:T(128)S(1)} %bitcast_add_fusion), channel_id=1, source_target_pairs={{0,1},{1,0},{2,3},{3,2},{4,5},{5,4},{6,7},{7,6},{8,9},{9,8},{10,11... | collective-permute-start | bytes 392 | tf_op jit(solution)/shard_map/ppermute | solution.py:585
  5.9 8.7 %collective-permute-start = (bf16[288,128]{1,0:T(8,128)(2,1)S(1)}, bf16[288,128]{1,0:T(8,128)(2,1)S(1)}, u32[]{:S(2)}, u32[]{:S(2)}) collective-permute-start(bf16[288,128]{1,0:T(8,128)(2,1)S(1)} %strips.1), channel_id=1, source_target_pairs={{0,4},{4,0},{8,12},{12,8},{16,20},{20,16},{24,28},{28,24},{1,5},{5... | collective-permute-start | bytes 221192 | tf_op jit(solution)/shard_map/ppermute | solution.py:585
  14.6 4.4 %collective-permute-start.1 = (bf16[288,128]{1,0:T(8,128)(2,1)S(1)}, bf16[288,128]{1,0:T(8,128)(2,1)S(1)}, u32[]{:S(2)}, u32[]{:S(2)}) collective-permute-start(bf16[288,128]{1,0:T(8,128)(2,1)S(1)} %broadcast_select_fusion), channel_id=1, source_target_pairs={{0,8},{4,12},{8,0},{12,4},{16,24},{20,28},{24,16},{28,20},{1,9},{5... | collective-permute-start | bytes 221192 | tf_op jit(solution)/shard_map/ppermute | solution.py:585
  16.3 5.4 %collective-permute-start.7 = (s32[2,32]{1,0:T(2,128)S(1)}, s32[2,32]{1,0:T(2,128)S(1)}, u32[]{:S(2)}, u32[]{:S(2)}) collective-permute-start(s32[2,32]{1,0:T(2,128)S(1)} %pad_add_fusion.3), channel_id=1, source_target_pairs={{0,4},{4,0},{8,12},{12,8},{16,20},{20,16},{24,28},{28,24},{1,5},{5... | collective-permute-start | bytes 776 | tf_op jit(solution)/shard_map/ppermute | solution.py:585
  16.8 4.9 %collective-permute-start.6 = (s32[2,32]{1,0:T(2,128)S(1)}, s32[2,32]{1,0:T(2,128)S(1)}, u32[]{:S(2)}, u32[]{:S(2)}) collective-permute-start(s32[2,32]{1,0:T(2,128)S(1)} %pad_add_fusion.3), channel_id=1, source_target_pairs={{0,2},{1,3},{2,0},{3,1},{4,6},{5,7},{6,4},{7,5},{8,10},{9,11},{10,... | collective-permute-start | bytes 776 | tf_op jit(solution)/shard_map/ppermute | solution.py:585
  18.3 7.5 %collective-permute-start.4 = (bf16[32,32,128]{2,1,0:T(8,128)(2,1)}, bf16[32,32,128]{2,1,0:T(8,128)(2,1)S(1)}, u32[]{:S(2)}, u32[]{:S(2)}) collective-permute-start(bf16[32,32,128]{2,1,0:T(8,128)(2,1)} %copy-done.1), channel_id=1, source_target_pairs={{0,1},{1,0},{2,3},{3,2},{4,5},{5,4},{6,7},{7,6},{8,9},{9,8},{10,11... | collective-permute-start | bytes 786440 | tf_op jit(solution)/shard_map/ppermute | solution.py:585
  18.3 9.0 %collective-permute-start.3 = (bf16[32,32,128]{2,1,0:T(8,128)(2,1)}, bf16[32,32,128]{2,1,0:T(8,128)(2,1)}, u32[]{:S(2)}, u32[]{:S(2)}) collective-permute-start(bf16[32,32,128]{2,1,0:T(8,128)(2,1)} %copy-done.1), channel_id=1, source_target_pairs={{0,2},{1,3},{2,0},{3,1},{4,6},{5,7},{6,4},{7,5},{8,10},{9,11},{10,... | collective-permute-start | bytes 786440 | tf_op jit(solution)/shard_map/ppermute | solution.py:585
  19.0 6.8 %collective-permute-start.2 = (bf16[288,128]{1,0:T(8,128)(2,1)S(1)}, bf16[288,128]{1,0:T(8,128)(2,1)S(1)}, u32[]{:S(2)}, u32[]{:S(2)}) collective-permute-start(bf16[288,128]{1,0:T(8,128)(2,1)S(1)} %broadcast_select_fusion.1), channel_id=1, source_target_pairs={{0,16},{4,20},{8,24},{12,28},{16,0},{20,4},{24,8},{28,12},{1,17},{... | collective-permute-start | bytes 221192 | tf_op jit(solution)/shard_map/ppermute | solution.py:585
  29.7 13.8 %collective-permute-start.10 = (bf16[32,64,128]{2,1,0:T(8,128)(2,1)}, bf16[32,64,128]{2,1,0:T(8,128)(2,1)S(1)}, u32[]{:S(2)}, u32[]{:S(2)}) collective-permute-start(bf16[32,64,128]{2,1,0:T(8,128)(2,1)} %get-tuple-element.70.refs_0_), channel_id=1, source_target_pairs={{0,4},{4,0},{8,12},{12,8},{16,20},{20,16},{24,28},{28,24},{1,5},{5... | collective-permute-start | bytes 1572872 | tf_op jit(solution)/shard_map/ppermute | solution.py:585
  31.2 4.1 %collective-permute-start.11 = (bf16[32,32,128]{2,1,0:T(8,128)(2,1)}, bf16[32,32,128]{2,1,0:T(8,128)(2,1)S(1)}, u32[]{:S(2)}, u32[]{:S(2)}) collective-permute-start(bf16[32,32,128]{2,1,0:T(8,128)(2,1)} %collective-permute-done.3.refs_2_), channel_id=1, source_target_pairs={{0,1},{1,0},{2,3},{3,2},{4,5},{5,4},{6,7},{7,6},{8,9},{9,8},{10,11... | collective-permute-start | bytes 786440 | tf_op jit(solution)/shard_map/ppermute | solution.py:585
  31.2 18.2 %collective-permute-start.9 = (bf16[32,80,128]{2,1,0:T(8,128)(2,1)}, bf16[32,80,128]{2,1,0:T(8,128)(2,1)S(1)}, u32[]{:S(2)}, u32[]{:S(2)}) collective-permute-start(bf16[32,80,128]{2,1,0:T(8,128)(2,1)} %get-tuple-element.69.refs_0_), channel_id=1, source_target_pairs={{0,2},{1,3},{2,0},{3,1},{4,6},{5,7},{6,4},{7,5},{8,10},{9,11},{10,... | collective-permute-start | bytes 1966088 | tf_op jit(solution)/shard_map/ppermute | solution.py:585
  31.7 13.5 %collective-permute-start.12 = (bf16[32,64,128]{2,1,0:T(8,128)(2,1)}, bf16[32,64,128]{2,1,0:T(8,128)(2,1)S(1)}, u32[]{:S(2)}, u32[]{:S(2)}) collective-permute-start(bf16[32,64,128]{2,1,0:T(8,128)(2,1)} %get-tuple-element.70.refs_0_), channel_id=1, source_target_pairs={{0,1},{1,0},{2,3},{3,2},{4,5},{5,4},{6,7},{7,6},{8,9},{9,8},{10,11... | collective-permute-start | bytes 1572872 | tf_op jit(solution)/shard_map/ppermute | solution.py:585
  43.5 1.9 %collective-permute-start.13 = (bf16[32,64,128]{2,1,0:T(8,128)(2,1)S(1)}, bf16[32,64,128]{2,1,0:T(8,128)(2,1)S(1)}, u32[]{:S(2)}, u32[]{:S(2)}) collective-permute-start(bf16[32,64,128]{2,1,0:T(8,128)(2,1)S(1)} %collective-permute-done.10.refs_2_), channel_id=1, source_target_pairs={{0,1},{1,0},{2,3},{3,2},{4,5},{5,4},{6,7},{7,6},{8,9},{9,8},{10,11... | collective-permute-start | bytes 1572872 | tf_op jit(solution)/shard_map/ppermute | solution.py:585
  43.5 5.9 %collective-permute-start.14 = (bf16[16,32,128]{2,1,0:T(8,128)(2,1)S(1)}, bf16[16,32,128]{2,1,0:T(8,128)(2,1)S(1)}, u32[]{:S(2)}, u32[]{:S(2)}) collective-permute-start(bf16[16,32,128]{2,1,0:T(8,128)(2,1)S(1)} %get-tuple-element.81), channel_id=1, source_target_pairs={{0,4},{4,0},{8,12},{12,8},{16,20},{20,16},{24,28},{28,24},{1,5},{5... | collective-permute-start | bytes 393224 | tf_op jit(solution)/shard_map/ppermute | solution.py:585
  45.0 5.3 %collective-permute-start.8 = (bf16[32,80,128]{2,1,0:T(8,128)(2,1)}, bf16[32,80,128]{2,1,0:T(8,128)(2,1)S(1)}, u32[]{:S(2)}, u32[]{:S(2)}) collective-permute-start(bf16[32,80,128]{2,1,0:T(8,128)(2,1)} %get-tuple-element.69.refs_0_), channel_id=1, source_target_pairs={{0,1},{1,0},{2,3},{3,2},{4,5},{5,4},{6,7},{7,6},{8,9},{9,8},{10,11... | collective-permute-start | bytes 1966088 | tf_op jit(solution)/shard_map/ppermute | solution.py:585
  49.4 2.1 %collective-permute-start.15 = (bf16[32,80,128]{2,1,0:T(8,128)(2,1)S(1)}, bf16[32,80,128]{2,1,0:T(8,128)(2,1)S(1)}, u32[]{:S(2)}, u32[]{:S(2)}) collective-permute-start(bf16[32,80,128]{2,1,0:T(8,128)(2,1)S(1)} %collective-permute-done.9.refs_2_), channel_id=1, source_target_pairs={{0,1},{1,0},{2,3},{3,2},{4,5},{5,4},{6,7},{7,6},{8,9},{9,8},{10,11... | collective-permute-start | bytes 1966088 | tf_op jit(solution)/shard_map/ppermute | solution.py:585
  49.4 8.7 %collective-permute-start.17 = (bf16[16,64,128]{2,1,0:T(8,128)(2,1)S(1)}, bf16[16,64,128]{2,1,0:T(8,128)(2,1)S(1)}, u32[]{:S(2)}, u32[]{:S(2)}) collective-permute-start(bf16[16,64,128]{2,1,0:T(8,128)(2,1)S(1)} %get-tuple-element.87), channel_id=1, source_target_pairs={{0,2},{1,3},{2,0},{3,1},{4,6},{5,7},{6,4},{7,5},{8,10},{9,11},{10,... | collective-permute-start | bytes 786440 | tf_op jit(solution)/shard_map/ppermute | solution.py:585
  54.5 10.0 %collective-permute-start.16 = (bf16[16,80,128]{2,1,0:T(8,128)(2,1)S(1)}, bf16[16,80,128]{2,1,0:T(8,128)(2,1)S(1)}, u32[]{:S(2)}, u32[]{:S(2)}) collective-permute-start(bf16[16,80,128]{2,1,0:T(8,128)(2,1)S(1)} %get-tuple-element.84), channel_id=1, source_target_pairs={{0,4},{4,0},{8,12},{12,8},{16,20},{20,16},{24,28},{28,24},{1,5},{5... | collective-permute-start | bytes 983048 | tf_op jit(solution)/shard_map/ppermute | solution.py:585
  58.2 6.2 %collective-permute-start.18 = (bf16[4,96,128]{2,1,0:T(8,128)(2,1)S(1)}, bf16[4,96,128]{2,1,0:T(8,128)(2,1)S(1)}, u32[]{:S(2)}, u32[]{:S(2)}) collective-permute-start(bf16[4,96,128]{2,1,0:T(8,128)(2,1)S(1)} %get-tuple-element.89), channel_id=1, source_target_pairs={{0,8},{4,12},{8,0},{12,4},{16,24},{20,28},{24,16},{28,20},{1,9},{5... | collective-permute-start | bytes 294920 | tf_op jit(solution)/shard_map/ppermute | solution.py:585
  58.7 10.4 %collective-permute-start.22 = (bf16[4,96,128]{2,1,0:T(8,128)(2,1)S(1)}, bf16[4,96,128]{2,1,0:T(8,128)(2,1)S(1)}, u32[]{:S(2)}, u32[]{:S(2)}) collective-permute-start(bf16[4,96,128]{2,1,0:T(8,128)(2,1)S(1)} %get-tuple-element.97), channel_id=1, source_target_pairs={{0,16},{4,20},{8,24},{12,28},{16,0},{20,4},{24,8},{28,12},{1,17},{... | collective-permute-start | bytes 294920 | tf_op jit(solution)/shard_map/ppermute | solution.py:585
  61.3 7.9 %collective-permute-start.23 = (bf16[4,96,128]{2,1,0:T(8,128)(2,1)S(1)}, bf16[4,96,128]{2,1,0:T(8,128)(2,1)S(1)}, u32[]{:S(2)}, u32[]{:S(2)}) collective-permute-start(bf16[4,96,128]{2,1,0:T(8,128)(2,1)S(1)} %get-tuple-element.98), channel_id=1, source_target_pairs={{0,24},{4,28},{8,16},{12,20},{16,8},{20,12},{24,0},{28,4},{1,25},{... | collective-permute-start | bytes 294920 | tf_op jit(solution)/shard_map/ppermute | solution.py:585
  64.6 5.4 %collective-permute-start.19 = (bf16[4,80,128]{2,1,0:T(8,128)(2,1)S(1)}, bf16[4,80,128]{2,1,0:T(8,128)(2,1)S(1)}, u32[]{:S(2)}, u32[]{:S(2)}) collective-permute-start(bf16[4,80,128]{2,1,0:T(8,128)(2,1)S(1)} %get-tuple-element.92), channel_id=1, source_target_pairs={{0,8},{4,12},{8,0},{12,4},{16,24},{20,28},{24,16},{28,20},{1,9},{5... | collective-permute-start | bytes 245768 | tf_op jit(solution)/shard_map/ppermute | solution.py:585
  65.1 11.2 %collective-permute-start.20 = (bf16[4,80,128]{2,1,0:T(8,128)(2,1)S(1)}, bf16[4,80,128]{2,1,0:T(8,128)(2,1)S(1)}, u32[]{:S(2)}, u32[]{:S(2)}) collective-permute-start(bf16[4,80,128]{2,1,0:T(8,128)(2,1)S(1)} %get-tuple-element.93), channel_id=1, source_target_pairs={{0,16},{4,20},{8,24},{12,28},{16,0},{20,4},{24,8},{28,12},{1,17},{... | collective-permute-start | bytes 245768 | tf_op jit(solution)/shard_map/ppermute | solution.py:585
  67.7 8.6 %collective-permute-start.21 = (bf16[4,80,128]{2,1,0:T(8,128)(2,1)S(1)}, bf16[4,80,128]{2,1,0:T(8,128)(2,1)S(1)}, u32[]{:S(2)}, u32[]{:S(2)}) collective-permute-start(bf16[4,80,128]{2,1,0:T(8,128)(2,1)S(1)} %get-tuple-element.94), channel_id=1, source_target_pairs={{0,24},{4,28},{8,16},{12,20},{16,8},{20,12},{24,0},{28,4},{1,25},{... | collective-permute-start | bytes 245768 | tf_op jit(solution)/shard_map/ppermute | solution.py:585
  (16 other events, 57.2 us)

commit v12 on v11

--- a/solution.py
+++ b/solution.py
@@ -277,22 +277,30 @@
     return pltpu.roll(out, (base - cc * width) % 128, 1)
 
 
-STATE_ROWS = 816
-
-
-def state_views(state):
-    at = lambda r, h, c, w: (slice(r, r + h), slice(c, c + w))
-    b0 = [at(128 * c, 128, 0, 1024) for c in range(3)]
-    l1 = [at(384, 64, 0, 512), at(384, 64, 512, 512), at(448, 64, 0, 512), at(448, 64, 512, 512)]
-    l2 = [at(512, 32, 256 * c, 256) for c in range(4)]
-    l3 = [at(544, 16, 128 * c, 128) for c in range(4)]
-    l4 = [at(544, 16, 512 + 128 * c, 128) for c in range(4)]
-    levels = [b0 + [at(560, 128, 0, 1024)], l1, l2, l3, l4]
-    masks = [at(688, 128 >> k, 128 * k, 64 >> k) for k in range(4)] + [at(688, 16, 512, 4)]
+COLOUR_ROWS = 560
+WEIGHT_ROWS = 320
+
+
+def at(r, h, c, w):
+    return slice(r, r + h), slice(c, c + w)
+
+
+def colour_views():
+    levels = [[at(128 * c, 128, 0, 1024) for c in range(3)]]
+    levels.append([at(384, 64, 0, 512), at(384, 64, 512, 512), at(448, 64, 0, 512)])
+    levels.append([at(512, 32, 256 * c, 256) for c in range(3)])
+    levels.append([at(544, 16, 128 * c, 128) for c in range(3)])
+    levels.append([at(544, 16, 512 + 128 * c, 128) for c in range(3)])
+    return levels
+
+
+def weight_views():
+    levels = [at(0, 128, 0, 1024), at(128, 64, 0, 512), at(128, 32, 512, 256), at(128, 16, 768, 128), at(128, 16, 896, 128)]
+    masks = [at(192, 128 >> k, 128 * k, 64 >> k) for k in range(4)] + [at(192, 16, 512, 4)]
     return levels, masks
 
 
-def bands_kernel(small_places, large_places, x, w, m, small, large, wblocks, state):
+def filters(small_places, large_places, small, large):
     mats = unpack(small, small_places)
     v, gv, sm = (levels_of(mats, letter) for letter in "vgm")
     order = mats["order"]
@@ -302,30 +310,22 @@
     twice = lambda each: windows(each, mats["grow"], 128)
     s = {1: half, 2: half, 3: half, 4: right_of(mats["last"])}
     gh = {0: twice, 1: twice, 2: twice, 3: right_of(mats["least"])}
-    views, mask_views = state_views(state)
-    planes = [x[0, c] for c in range(COLOURS)] + [w[0]]
-    weights = mm(order, planes[3])
-    state[views[0][3]] = weights
+    return v, gv, sm, s, gh, order
+
+
+def weights_kernel(small_places, large_places, w, m, small, large, wblocks, state):
+    v, _, sm, s, _, order = filters(small_places, large_places, small, large)
+    views, mask_views = weight_views()
+    weights = mm(order, w[0])
+    state[views[0]] = weights
 
     def store(q, piece):
         wblocks[q] = piece.astype(BF16)
 
     fold_level0(weights, store)
-    levels = pyramid(planes, v, s)
+    levels = pyramid([w[0]], v, s)
     for k in range(1, 5):
-        rows = levels[k].shape[0] // 4
-        state[views[k][3]] = levels[k][3 * rows :]
-    back = grown(levels[1][: 3 * 64], COLOURS, gv[0], gh[0])
-    for c in range(COLOURS):
-        state[views[0][c]] = mm(order, planes[c]) - back[c]
-    for k in range(1, 4):
-        rows = levels[k].shape[0] // 4
-        below = levels[k + 1].shape[0] // 4
-        back = grown(levels[k + 1][: 3 * below], COLOURS, gv[k], gh[k])
-        for c in range(COLOURS):
-            state[views[k][c]] = levels[k][c * rows : (c + 1) * rows] - back[c]
-    for c in range(COLOURS):
-        state[views[4][c]] = levels[4][c * 16 : (c + 1) * 16]
+        state[views[k]] = levels[k]
     other = (1.0 - m[0].astype(F32)).astype(BF16)
     state[mask_views[0]] = mmt(order, other)
     masks = pyramid([other], v, sm, mmt)
@@ -333,23 +333,52 @@
         state[mask_views[k]] = masks[k]
 
 
-def bands_of(frames, weight_map, seam_mask):
+def colours_kernel(small_places, large_places, x, small, large, state):
+    v, gv, _, s, gh, order = filters(small_places, large_places, small, large)
+    views = colour_views()
+    planes = [x[0, c] for c in range(COLOURS)]
+    levels = pyramid(planes, v, s)
+    back = grown(levels[1], COLOURS, gv[0], gh[0])
+    for c in range(COLOURS):
+        state[views[0][c]] = mm(order, planes[c]) - back[c]
+    for k in range(1, 4):
+        rows = levels[k].shape[0] // COLOURS
+        back = grown(levels[k + 1], COLOURS, gv[k], gh[k])
+        for c in range(COLOURS):
+            state[views[k][c]] = levels[k][c * rows : (c + 1) * rows] - back[c]
+    for c in range(COLOURS):
+        state[views[4][c]] = levels[4][c * 16 : (c + 1) * 16]
+
+
+def weights_of(weight_map, seam_mask):
     small, small_places = small_matrices()
     large, large_places = large_matrices()
     return pl.pallas_call(
-        functools.partial(bands_kernel, small_places, large_places),
-        out_shape=[jax.ShapeDtypeStruct((QB, 32, 128), BF16), jax.ShapeDtypeStruct((STATE_ROWS, FW), F32)],
+        functools.partial(weights_kernel, small_places, large_places),
+        out_shape=[jax.ShapeDtypeStruct((QB, 32, 128), BF16), jax.ShapeDtypeStruct((WEIGHT_ROWS, FW), F32)],
         compiler_params=pltpu.CompilerParams(vmem_limit_bytes=VMEM),
-        cost_estimate=pl.CostEstimate(flops=8 * 10**9, bytes_accessed=6 * 10**6, transcendentals=0),
-        name="bands",
-    )(frames, weight_map, jnp.swapaxes(seam_mask, 1, 2), small, large)
-
-
-def blend_kernel(cell, strips, state, first, second):
-    views, mask_views = state_views(state)
-    (b0, b1, b2, b3, b4) = [[state[view] for view in views[k][:3]] for k in range(5)]
-    (wp, w1, w2, w3, w4) = [state[views[k][3]] for k in range(5)]
-    (n0, n1, n2, n3, n4) = [state[view] for view in mask_views]
+        cost_estimate=pl.CostEstimate(flops=4 * 10**9, bytes_accessed=2 * 10**6, transcendentals=0),
+        name="weights",
+    )(weight_map, jnp.swapaxes(seam_mask, 1, 2), small, large)
+
+
+def colours_of(frames):
+    small, small_places = small_matrices()
+    large, large_places = large_matrices()
+    return pl.pallas_call(
+        functools.partial(colours_kernel, small_places, large_places),
+        out_shape=jax.ShapeDtypeStruct((COLOUR_ROWS, FW), F32),
+        compiler_params=pltpu.CompilerParams(vmem_limit_bytes=VMEM),
+        cost_estimate=pl.CostEstimate(flops=6 * 10**9, bytes_accessed=4 * 10**6, transcendentals=0),
+        name="colours",
+    )(frames, small, large)
+
+
+def blend_kernel(cell, strips, colours, masked, first, second):
+    views, mask_views = weight_views()
+    (b0, b1, b2, b3, b4) = [[colours[view] for view in level] for level in colour_views()]
+    (wp, w1, w2, w3, w4) = [masked[view] for view in views]
+    (n0, n1, n2, n3, n4) = [masked[view] for view in mask_views]
     start = cell[0] * 16
     low = strips[192:288]
 
@@ -405,16 +434,16 @@
                 first[r * 16 + c, 64:80, :] = jnp.concatenate([head, tail], axis=0).astype(BF16)
 
 
-def blend(cell, strips, state):
+def blend(cell, strips, colours, masked):
     vmem = pl.BlockSpec(memory_space=pltpu.VMEM)
     return pl.pallas_call(
         blend_kernel,
-        in_specs=[pl.BlockSpec(memory_space=pltpu.SMEM)] + [vmem] * 2,
+        in_specs=[pl.BlockSpec(memory_space=pltpu.SMEM)] + [vmem] * 3,
         out_shape=[jax.ShapeDtypeStruct((QB, 80, 128), BF16), jax.ShapeDtypeStruct((QB, 64, 128), BF16)],
         compiler_params=pltpu.CompilerParams(vmem_limit_bytes=VMEM),
         cost_estimate=pl.CostEstimate(flops=10**6, bytes_accessed=10**4, transcendentals=0),
         name="blend",
-    )(cell, strips, state)
+    )(cell, strips, colours, masked)
 
 
 def routes_kernel(spot, lists, counts):
@@ -594,7 +623,7 @@
     tie = lax.optimization_barrier
     strips = strips_of(frames, strip_cell)
     ids = tile_group.reshape(QB) * (parts * TILE_DEV) + tile_position_in_group.reshape(QB)
-    strips, frames, ids = tie((strips, frames, ids))
+    strips, weight_map, ids = tie((strips, weight_map, ids))
     ids = jnp.stack([ids, swap(ids, "tiles", 1)])
     ids_x = jnp.concatenate([ids, swap(ids, "tiles", 2)])
     ids_y = jnp.concatenate([ids, swap(ids, "frames", 1)])
@@ -611,15 +640,18 @@
     here = ((group & 1) == 0) & ((part & 1) == 0)
     spot_y = jnp.where(here, ((part >> 1) * half + (group >> 1)) * TILE_DEV + tile, -1)
 
-    weights, state = bands_of(frames, weight_map, seam_mask)
+    weights, masked = weights_of(weight_map, seam_mask)
     bit = 1
     while bit < groups:
         got = swap(strips, "frames", bit)
         if bit == 1:
-            got, weights, state = tie((got, weights, state))
+            got, weights, masked = tie((got, weights, masked))
             far, near = swap(weights, "tiles", 2), swap(weights, "tiles", 1)
+        if bit == half // 2:
+            got, frames = tie((got, frames))
         if bit == half:
-            got, far, near, spot_x, spot_y = tie((got, far, near, spot_x, spot_y))
+            colours = colours_of(frames)
+            got, far, near, spot_x, spot_y, colours = tie((got, far, near, spot_x, spot_y, colours))
         strips = jnp.where((mask & bit) != 0, got, strips)
         bit *= 2
 
@@ -629,7 +661,7 @@
     def along(own, *away):
         return [own] + [swap(part, "frames", 2 * (j + 1)) for j, part in enumerate(away)]
 
-    first, second = blend(strip_cell, strips, state)
+    first, second = blend(strip_cell, strips, colours, masked)
     first, second, spot_x, spot_y, far = tie((first, second, spot_x, spot_y, far))
     far_first, near_first = swap(first, "tiles", 2), swap(first, "tiles", 1)
     far_second, near_second = swap(second, "frames", 1), swap(second, "tiles", 1)

time: 79 us -> 77.9 us (0.986)
  starting transfers between devices: 25.4 us -> 28 us
  waiting for transfers between devices: 21.5 us -> 19.2 us
  Pallas kernels: 19.3 us -> 18.5 us
    ppermute x24, starting transfers between devices: 25.4 us -> 28 us  [swap(): return lax.ppermute(value, axis, [(i, i ^ bit) for i in range(size)])]
    ppermute x24, waiting for transfers between devices: 21.5 us -> 19.2 us  [swap(): return lax.ppermute(value, axis, [(i, i ^ bit) for i in range(size)])]
    pallas_call x1 -> x2, Pallas kernels: 4.68 us -> 5.77 us  [the longest x1 3.55 us: colours_of(): pl.pallas_call(functools.partial(colours_kernel, small_places, large_plac...]
    pallas_call x3, Pallas kernels: 4.88 us -> 3.8 us  [gather_rows(): pl.pallas_call(gather_kernel, in_specs=[pl.BlockSpec(memory_space=pltpu.S...]
    pallas_call x1, Pallas kernels: 2.3 us -> 1.45 us  [blend(): pl.pallas_call(blend_kernel, in_specs=[pl.BlockSpec(memory_space=pltpu.SM...]
    unnamed x32 -> x38, local copies, waits for them, and re-layouts: 9.41 us -> 8.84 us
  transfers between devices with their start and end apart: 24 -> 24, of which waited for: 13 -> 9; matrix products, arithmetic and copies ran while one was open for 1% -> 1% of each run, Pallas kernels for 17% -> 17%
where the time goes in v12:
time: 77.9 us; the launch traced here: 77.4 us
  starting transfers between devices  28 us (36%)
  waiting for transfers between devices  19.2 us (25%)
  Pallas kernels  18.5 us (24%)
  local copies, waits for them, and re-layouts  8.84 us (11%)
  between operations  1.55 us (2%)
  other arithmetic  1.37 us (2%)
    ppermute x24, starting transfers between devices, swap(): return lax.ppermute(value, axis, [(i, i ^ bit) for i in range(size)])  28 us
    ppermute x24, waiting for transfers between devices, swap(): return lax.ppermute(value, axis, [(i, i ^ bit) for i in range(size)])  19.2 us
    unnamed x38, local copies, waits for them, and re-layouts  8.84 us
    pallas_call x3, Pallas kernels, gather_rows(): pl.pallas_call(gather_kernel, in_specs=[pl.BlockSpec(memory_space=pltpu.S...  3.8 us
    pallas_call x1, Pallas kernels, colours_of(): pl.pallas_call(functools.partial(colours_kernel, small_places, large_plac...  3.55 us
    pallas_call x2, Pallas kernels, routes_of(): pl.pallas_call(routes_kernel, in_specs=[smem], out_specs=[smem, smem], ou...  3.29 us
    pallas_call x1, Pallas kernels, weights_of(): pl.pallas_call(functools.partial(weights_kernel, small_places, large_plac...  2.22 us
    pallas_call x1, Pallas kernels, collapse(): pl.pallas_call(functools.partial(collapse_kernel, places, len(b)), out_sh...  2.18 us
  transfers between devices with their start and end apart: 24, of which 9 were waited for; matrix products, arithmetic and copies ran while one was open for 1% of the time, Pallas kernels for 17%

profile of v12, /device:TPU:0, one launch (start us, length us, event | category | flops | bytes accessed | tf_op | source)
XLA Modules:
  0.0 77.4 jit_solution(422972252752990693)
XLA Ops:
  3.5 1.8 %strips.1 = bf16[288,128]{1,0:T(8,128)(2,1)S(1)} custom-call(s32[1]{0:T(128)S(6)} %copy.14.cell, bf16[1,3,128,1024]{3,2,1,0:T(8,128)(2,1)S(1)} %copy-done.11, bf16[1,3,128,1024]{3,2,1,0:T(8,128)(2,1)S(1)} %copy-done.11, bf16[512,512]{1,0:T(8,128)(2,1)S(1)} %copy-done.16), custom_call_target="tpu_custom_call" | custom-call | flops 2000000000 | bytes 1000000 | tf_op jit(solution)/shard_map/strips/pallas_call | solution.py:247
  5.9 2.6 %collective-permute-start = (bf16[288,128]{1,0:T(8,128)(2,1)S(1)}, bf16[288,128]{1,0:T(8,128)(2,1)S(1)}, u32[]{:S(2)}, u32[]{:S(2)}) collective-permute-start(bf16[288,128]{1,0:T(8,128)(2,1)S(1)} %strips.1), channel_id=1, source_target_pairs={{0,4},{4,0},{8,12},{12,8},{16,20},{20,16},{24,28},{28,24},{1,5},{5... | collective-permute-start | bytes 221192 | tf_op jit(solution)/shard_map/ppermute | solution.py:614
  10.2 2.2 %weights.1 = (bf16[32,32,128]{2,1,0:T(8,128)(2,1)S(1)}, f32[320,1024]{1,0:T(8,128)S(1)}) custom-call(bf16[1,128,1024]{2,1,0:T(8,128)(2,1)S(1)} %copy-done.13, s32[1,64,128]{2,1,0:T(8,128)S(1)} %bitcast.13, bf16[512,512]{1,0:T(8,128)(2,1)S(1)} %copy-done.17, bf16[512,640]{1,0:T(8,128)(2,1)S(1)} %copy-done.15), custom_call_target="tpu_custom_call" | custom-call | flops 4000000000 | bytes 2000000 | tf_op jit(solution)/shard_map/weights/pallas_call | solution.py:356
  12.6 2.0 %collective-permute-start.6 = (s32[2,32]{1,0:T(2,128)S(1)}, s32[2,32]{1,0:T(2,128)S(1)}, u32[]{:S(2)}, u32[]{:S(2)}) collective-permute-start(s32[2,32]{1,0:T(2,128)S(1)} %pad_add_fusion.3), channel_id=1, source_target_pairs={{0,2},{1,3},{2,0},{3,1},{4,6},{5,7},{6,4},{7,5},{8,10},{9,11},{10,... | collective-permute-start | bytes 776 | tf_op jit(solution)/shard_map/ppermute | solution.py:614
  14.6 1.6 %collective-permute-start.1 = (bf16[288,128]{1,0:T(8,128)(2,1)S(1)}, bf16[288,128]{1,0:T(8,128)(2,1)S(1)}, u32[]{:S(2)}, u32[]{:S(2)}) collective-permute-start(bf16[288,128]{1,0:T(8,128)(2,1)S(1)} %broadcast_select_fusion), channel_id=1, source_target_pairs={{0,8},{4,12},{8,0},{12,4},{16,24},{20,28},{24,16},{28,20},{1,9},{5... | collective-permute-start | bytes 221192 | tf_op jit(solution)/shard_map/ppermute | solution.py:614
  16.9 1.9 %collective-permute-start.3 = (bf16[32,32,128]{2,1,0:T(8,128)(2,1)S(1)}, bf16[32,32,128]{2,1,0:T(8,128)(2,1)}, u32[]{:S(2)}, u32[]{:S(2)}) collective-permute-start(bf16[32,32,128]{2,1,0:T(8,128)(2,1)S(1)} %get-tuple-element.61.refs_0_), channel_id=1, source_target_pairs={{0,2},{1,3},{2,0},{3,1},{4,6},{5,7},{6,4},{7,5},{8,10},{9,11},{10,... | collective-permute-start | bytes 786440 | tf_op jit(solution)/shard_map/ppermute | solution.py:614
  19.0 2.7 %collective-permute-start.2 = (bf16[288,128]{1,0:T(8,128)(2,1)S(1)}, bf16[288,128]{1,0:T(8,128)(2,1)S(1)}, u32[]{:S(2)}, u32[]{:S(2)}) collective-permute-start(bf16[288,128]{1,0:T(8,128)(2,1)S(1)} %broadcast_select_fusion.1), channel_id=1, source_target_pairs={{0,16},{4,20},{8,24},{12,28},{16,0},{20,4},{24,8},{28,12},{1,17},{... | collective-permute-start | bytes 221192 | tf_op jit(solution)/shard_map/ppermute | solution.py:614
  22.7 3.6 %colours.1 = f32[560,1024]{1,0:T(8,128)S(1)} custom-call(bf16[1,3,128,1024]{3,2,1,0:T(8,128)(2,1)S(1)} %copy-done.12, bf16[512,512]{1,0:T(8,128)(2,1)S(1)} %copy-done.18, bf16[512,640]{1,0:T(8,128)(2,1)S(1)} %copy-done.15), custom_call_target="tpu_custom_call" | custom-call | flops 6000000000 | bytes 4000000 | tf_op jit(solution)/shard_map/colours/pallas_call | solution.py:368
  26.4 1.5 %blend.1 = (bf16[32,80,128]{2,1,0:T(8,128)(2,1)S(1)}, bf16[32,64,128]{2,1,0:T(8,128)(2,1)S(1)}) custom-call(s32[1]{0:T(128)S(6)} %copy.14.cell, bf16[288,128]{1,0:T(8,128)(2,1)S(1)} %broadcast_select_fusion.2.strips, f32[560,1024]{1,0:T(8,128)S(1)} %colours.1, f32[320,1024]{1,0:T(8,128)S(1)} %get-tuple-element.66.masked), custom_call_target="tpu_custom_call" | custom-call | flops 1000000 | bytes 10000 | tf_op jit(solution)/shard_map/blend/pallas_call | solution.py:439
  27.8 1.6 %collective-permute-start.10 = (bf16[32,64,128]{2,1,0:T(8,128)(2,1)S(1)}, bf16[32,64,128]{2,1,0:T(8,128)(2,1)S(1)}, u32[]{:S(2)}, u32[]{:S(2)}) collective-permute-start(bf16[32,64,128]{2,1,0:T(8,128)(2,1)S(1)} %get-tuple-element.76.refs_0_), channel_id=1, source_target_pairs={{0,4},{4,0},{8,12},{12,8},{16,20},{20,16},{24,28},{28,24},{1,5},{5... | collective-permute-start | bytes 1572872 | tf_op jit(solution)/shard_map/ppermute | solution.py:614
  30.9 1.6 %routes.2 = (s32[4,33]{1,0:T(4,128)}, s32[4]{0:T(128)}) custom-call(s32[4,32]{1,0:T(4,128)} %get-tuple-element.72.spot), custom_call_target="tpu_custom_call" | custom-call | tf_op jit(solution)/shard_map/routes/pallas_call | solution.py:462
  32.6 1.6 %routes.3 = (s32[4,33]{1,0:T(4,128)}, s32[4]{0:T(128)}) custom-call(s32[4,32]{1,0:T(4,128)} %get-tuple-element.80.spot), custom_call_target="tpu_custom_call" | custom-call | tf_op jit(solution)/shard_map/routes/pallas_call | solution.py:462
  37.5 1.4 %gather_rows.3 = (f32[16,32,128]{2,1,0:T(8,128)S(1)}, bf16[16,32,128]{2,1,0:T(8,128)(2,1)S(1)}) custom-call(s32[4,33]{1,0:T(4,128)S(1)} %copy-done.5, s32[4]{0:T(128)S(1)} %copy-done.7, bf16[32,32,128]{2,1,0:T(8,128)(2,1)S(1)} %copy-done.2, bf16[32,32,128]{2,1,0:T(8,128)(2,1)S(1)} %copy-done.4, bf16[32,32,128]{2,1,0:T(8,128)(2,1)} %collective-permute-done.3.refs_2_, ...), custom_call_target="tpu_custom_call" | custom-call | flops 1000000 | bytes 10000 | tf_op jit(solution)/shard_map/gather_rows/pallas_call | solution.py:496
  38.9 2.5 %collective-permute-done.10.refs_2_ = bf16[32,64,128]{2,1,0:T(8,128)(2,1)S(1)} collective-permute-done((bf16[32,64,128]{2,1,0:T(8,128)(2,1)S(1)}, bf16[32,64,128]{2,1,0:T(8,128)(2,1)S(1)}, u32[]{:S(2)}, u32[]{:S(2)}) %collective-permute-start.10) | collective-permute-done | bytes 524320 | tf_op jit(solution)/shard_map/ppermute | solution.py:614
  41.4 1.5 %collective-permute-start.14 = (bf16[16,32,128]{2,1,0:T(8,128)(2,1)S(1)}, bf16[16,32,128]{2,1,0:T(8,128)(2,1)S(1)}, u32[]{:S(2)}, u32[]{:S(2)}) collective-permute-start(bf16[16,32,128]{2,1,0:T(8,128)(2,1)S(1)} %get-tuple-element.87), channel_id=1, source_target_pairs={{0,4},{4,0},{8,12},{12,8},{16,20},{20,16},{24,28},{28,24},{1,5},{5... | collective-permute-start | bytes 393224 | tf_op jit(solution)/shard_map/ppermute | solution.py:614
  45.8 1.5 %collective-permute-done.14.refs_3_ = bf16[16,32,128]{2,1,0:T(8,128)(2,1)S(1)} collective-permute-done((bf16[16,32,128]{2,1,0:T(8,128)(2,1)S(1)}, bf16[16,32,128]{2,1,0:T(8,128)(2,1)S(1)}, u32[]{:S(2)}, u32[]{:S(2)}) %collective-permute-start.14) | collective-permute-done | bytes 131104 | tf_op jit(solution)/shard_map/ppermute | solution.py:614
  50.6 1.6 %collective-permute-start.16 = (bf16[16,80,128]{2,1,0:T(8,128)(2,1)S(1)}, bf16[16,80,128]{2,1,0:T(8,128)(2,1)S(1)}, u32[]{:S(2)}, u32[]{:S(2)}) collective-permute-start(bf16[16,80,128]{2,1,0:T(8,128)(2,1)S(1)} %get-tuple-element.90), channel_id=1, source_target_pairs={{0,4},{4,0},{8,12},{12,8},{16,20},{20,16},{24,28},{28,24},{1,5},{5... | collective-permute-start | bytes 983048 | tf_op jit(solution)/shard_map/ppermute | solution.py:614
  52.2 3.8 %collective-permute-done.17.refs_2_ = bf16[16,64,128]{2,1,0:T(8,128)(2,1)S(1)} collective-permute-done((bf16[16,64,128]{2,1,0:T(8,128)(2,1)S(1)}, bf16[16,64,128]{2,1,0:T(8,128)(2,1)S(1)}, u32[]{:S(2)}, u32[]{:S(2)}) %collective-permute-start.17) | collective-permute-done | bytes 262176 | tf_op jit(solution)/shard_map/ppermute | solution.py:614
  56.1 1.6 %collective-permute-start.18 = (bf16[4,96,128]{2,1,0:T(8,128)(2,1)S(1)}, bf16[4,96,128]{2,1,0:T(8,128)(2,1)S(1)}, u32[]{:S(2)}, u32[]{:S(2)}) collective-permute-start(bf16[4,96,128]{2,1,0:T(8,128)(2,1)S(1)} %get-tuple-element.95), channel_id=1, source_target_pairs={{0,8},{4,12},{8,0},{12,4},{16,24},{20,28},{24,16},{28,20},{1,9},{5... | collective-permute-start | bytes 294920 | tf_op jit(solution)/shard_map/ppermute | solution.py:614
  57.8 2.4 %collective-permute-start.22 = (bf16[4,96,128]{2,1,0:T(8,128)(2,1)S(1)}, bf16[4,96,128]{2,1,0:T(8,128)(2,1)S(1)}, u32[]{:S(2)}, u32[]{:S(2)}) collective-permute-start(bf16[4,96,128]{2,1,0:T(8,128)(2,1)S(1)} %get-tuple-element.103), channel_id=1, source_target_pairs={{0,16},{4,20},{8,24},{12,28},{16,0},{20,4},{24,8},{28,12},{1,17},{... | collective-permute-start | bytes 294920 | tf_op jit(solution)/shard_map/ppermute | solution.py:614
  62.8 2.8 %collective-permute-start.20 = (bf16[4,80,128]{2,1,0:T(8,128)(2,1)S(1)}, bf16[4,80,128]{2,1,0:T(8,128)(2,1)S(1)}, u32[]{:S(2)}, u32[]{:S(2)}) collective-permute-start(bf16[4,80,128]{2,1,0:T(8,128)(2,1)S(1)} %get-tuple-element.99), channel_id=1, source_target_pairs={{0,16},{4,20},{8,24},{12,28},{16,0},{20,4},{24,8},{28,12},{1,17},{... | collective-permute-start | bytes 245768 | tf_op jit(solution)/shard_map/ppermute | solution.py:614
  66.1 2.7 %collective-permute-done.22.refs_6_ = bf16[4,96,128]{2,1,0:T(8,128)(2,1)S(1)} collective-permute-done((bf16[4,96,128]{2,1,0:T(8,128)(2,1)S(1)}, bf16[4,96,128]{2,1,0:T(8,128)(2,1)S(1)}, u32[]{:S(2)}, u32[]{:S(2)}) %collective-permute-start.22) | collective-permute-done | bytes 98336 | tf_op jit(solution)/shard_map/ppermute | solution.py:614
  68.8 6.4 %collective-permute-done.20.refs_2_ = bf16[4,80,128]{2,1,0:T(8,128)(2,1)S(1)} collective-permute-done((bf16[4,80,128]{2,1,0:T(8,128)(2,1)S(1)}, bf16[4,80,128]{2,1,0:T(8,128)(2,1)S(1)}, u32[]{:S(2)}, u32[]{:S(2)}) %collective-permute-start.20) | collective-permute-done | bytes 81952 | tf_op jit(solution)/shard_map/ppermute | solution.py:614
  75.2 2.2 %collapse.1 = f32[3,4,4096]{2,1,0:T(4,128)} custom-call(bf16[192,1280]{1,0:T(8,128)(2,1)S(1)} %copy-done, f32[4,80,128]{2,1,0:T(8,128)S(1)} %get-tuple-element.97.refs_0_, bf16[4,80,128]{2,1,0:T(8,128)(2,1)S(1)} %collective-permute-done.19.refs_1_, bf16[4,80,128]{2,1,0:T(8,128)(2,1)S(1)} %collective-permute-done.20.refs_2_, ...), custom_call_target="tpu_custom_call" | custom-call | flops 1000000 | bytes 10000 | tf_op jit(solution)/shard_map/collapse/pallas_call | solution.py:601
  (80 shorter events, 20.6 us)
Async XLA Ops:
  5.4 7.1 %collective-permute-start.5 = (s32[32]{0:T(128)S(1)}, s32[32]{0:T(128)S(1)}, u32[]{:S(2)}, u32[]{:S(2)}) collective-permute-start(s32[32]{0:T(128)S(1)} %bitcast_add_fusion), channel_id=1, source_target_pairs={{0,1},{1,0},{2,3},{3,2},{4,5},{5,4},{6,7},{7,6},{8,9},{9,8},{10,11... | collective-permute-start | bytes 392 | tf_op jit(solution)/shard_map/ppermute | solution.py:614
  5.9 8.7 %collective-permute-start = (bf16[288,128]{1,0:T(8,128)(2,1)S(1)}, bf16[288,128]{1,0:T(8,128)(2,1)S(1)}, u32[]{:S(2)}, u32[]{:S(2)}) collective-permute-start(bf16[288,128]{1,0:T(8,128)(2,1)S(1)} %strips.1), channel_id=1, source_target_pairs={{0,4},{4,0},{8,12},{12,8},{16,20},{20,16},{24,28},{28,24},{1,5},{5... | collective-permute-start | bytes 221192 | tf_op jit(solution)/shard_map/ppermute | solution.py:614
  12.5 3.7 %collective-permute-start.7 = (s32[2,32]{1,0:T(2,128)S(1)}, s32[2,32]{1,0:T(2,128)S(1)}, u32[]{:S(2)}, u32[]{:S(2)}) collective-permute-start(s32[2,32]{1,0:T(2,128)S(1)} %pad_add_fusion.3), channel_id=1, source_target_pairs={{0,4},{4,0},{8,12},{12,8},{16,20},{20,16},{24,28},{28,24},{1,5},{5... | collective-permute-start | bytes 776 | tf_op jit(solution)/shard_map/ppermute | solution.py:614
  12.6 3.6 %collective-permute-start.6 = (s32[2,32]{1,0:T(2,128)S(1)}, s32[2,32]{1,0:T(2,128)S(1)}, u32[]{:S(2)}, u32[]{:S(2)}) collective-permute-start(s32[2,32]{1,0:T(2,128)S(1)} %pad_add_fusion.3), channel_id=1, source_target_pairs={{0,2},{1,3},{2,0},{3,1},{4,6},{5,7},{6,4},{7,5},{8,10},{9,11},{10,... | collective-permute-start | bytes 776 | tf_op jit(solution)/shard_map/ppermute | solution.py:614
  14.6 4.4 %collective-permute-start.1 = (bf16[288,128]{1,0:T(8,128)(2,1)S(1)}, bf16[288,128]{1,0:T(8,128)(2,1)S(1)}, u32[]{:S(2)}, u32[]{:S(2)}) collective-permute-start(bf16[288,128]{1,0:T(8,128)(2,1)S(1)} %broadcast_select_fusion), channel_id=1, source_target_pairs={{0,8},{4,12},{8,0},{12,4},{16,24},{20,28},{24,16},{28,20},{1,9},{5... | collective-permute-start | bytes 221192 | tf_op jit(solution)/shard_map/ppermute | solution.py:614
  16.9 9.4 %collective-permute-start.4 = (bf16[32,32,128]{2,1,0:T(8,128)(2,1)S(1)}, bf16[32,32,128]{2,1,0:T(8,128)(2,1)S(1)}, u32[]{:S(2)}, u32[]{:S(2)}) collective-permute-start(bf16[32,32,128]{2,1,0:T(8,128)(2,1)S(1)} %get-tuple-element.61.refs_0_), channel_id=1, source_target_pairs={{0,1},{1,0},{2,3},{3,2},{4,5},{5,4},{6,7},{7,6},{8,9},{9,8},{10,11... | collective-permute-start | bytes 786440 | tf_op jit(solution)/shard_map/ppermute | solution.py:614
  16.9 9.5 %collective-permute-start.3 = (bf16[32,32,128]{2,1,0:T(8,128)(2,1)S(1)}, bf16[32,32,128]{2,1,0:T(8,128)(2,1)}, u32[]{:S(2)}, u32[]{:S(2)}) collective-permute-start(bf16[32,32,128]{2,1,0:T(8,128)(2,1)S(1)} %get-tuple-element.61.refs_0_), channel_id=1, source_target_pairs={{0,2},{1,3},{2,0},{3,1},{4,6},{5,7},{6,4},{7,5},{8,10},{9,11},{10,... | collective-permute-start | bytes 786440 | tf_op jit(solution)/shard_map/ppermute | solution.py:614
  19.0 7.3 %collective-permute-start.2 = (bf16[288,128]{1,0:T(8,128)(2,1)S(1)}, bf16[288,128]{1,0:T(8,128)(2,1)S(1)}, u32[]{:S(2)}, u32[]{:S(2)}) collective-permute-start(bf16[288,128]{1,0:T(8,128)(2,1)S(1)} %broadcast_select_fusion.1), channel_id=1, source_target_pairs={{0,16},{4,20},{8,24},{12,28},{16,0},{20,4},{24,8},{28,12},{1,17},{... | collective-permute-start | bytes 221192 | tf_op jit(solution)/shard_map/ppermute | solution.py:614
  27.8 13.6 %collective-permute-start.10 = (bf16[32,64,128]{2,1,0:T(8,128)(2,1)S(1)}, bf16[32,64,128]{2,1,0:T(8,128)(2,1)S(1)}, u32[]{:S(2)}, u32[]{:S(2)}) collective-permute-start(bf16[32,64,128]{2,1,0:T(8,128)(2,1)S(1)} %get-tuple-element.76.refs_0_), channel_id=1, source_target_pairs={{0,4},{4,0},{8,12},{12,8},{16,20},{20,16},{24,28},{28,24},{1,5},{5... | collective-permute-start | bytes 1572872 | tf_op jit(solution)/shard_map/ppermute | solution.py:614
  29.4 4.8 %collective-permute-start.11 = (bf16[32,32,128]{2,1,0:T(8,128)(2,1)}, bf16[32,32,128]{2,1,0:T(8,128)(2,1)S(1)}, u32[]{:S(2)}, u32[]{:S(2)}) collective-permute-start(bf16[32,32,128]{2,1,0:T(8,128)(2,1)} %collective-permute-done.3.refs_2_), channel_id=1, source_target_pairs={{0,1},{1,0},{2,3},{3,2},{4,5},{5,4},{6,7},{7,6},{8,9},{9,8},{10,11... | collective-permute-start | bytes 786440 | tf_op jit(solution)/shard_map/ppermute | solution.py:614
  29.4 17.9 %collective-permute-start.9 = (bf16[32,80,128]{2,1,0:T(8,128)(2,1)S(1)}, bf16[32,80,128]{2,1,0:T(8,128)(2,1)S(1)}, u32[]{:S(2)}, u32[]{:S(2)}) collective-permute-start(bf16[32,80,128]{2,1,0:T(8,128)(2,1)S(1)} %get-tuple-element.75.refs_0_), channel_id=1, source_target_pairs={{0,2},{1,3},{2,0},{3,1},{4,6},{5,7},{6,4},{7,5},{8,10},{9,11},{10,... | collective-permute-start | bytes 1966088 | tf_op jit(solution)/shard_map/ppermute | solution.py:614
  30.7 12.5 %collective-permute-start.12 = (bf16[32,64,128]{2,1,0:T(8,128)(2,1)S(1)}, bf16[32,64,128]{2,1,0:T(8,128)(2,1)S(1)}, u32[]{:S(2)}, u32[]{:S(2)}) collective-permute-start(bf16[32,64,128]{2,1,0:T(8,128)(2,1)S(1)} %get-tuple-element.76.refs_0_), channel_id=1, source_target_pairs={{0,1},{1,0},{2,3},{3,2},{4,5},{5,4},{6,7},{7,6},{8,9},{9,8},{10,11... | collective-permute-start | bytes 1572872 | tf_op jit(solution)/shard_map/ppermute | solution.py:614
  41.4 1.9 %collective-permute-start.13 = (bf16[32,64,128]{2,1,0:T(8,128)(2,1)S(1)}, bf16[32,64,128]{2,1,0:T(8,128)(2,1)S(1)}, u32[]{:S(2)}, u32[]{:S(2)}) collective-permute-start(bf16[32,64,128]{2,1,0:T(8,128)(2,1)S(1)} %collective-permute-done.10.refs_2_), channel_id=1, source_target_pairs={{0,1},{1,0},{2,3},{3,2},{4,5},{5,4},{6,7},{7,6},{8,9},{9,8},{10,11... | collective-permute-start | bytes 1572872 | tf_op jit(solution)/shard_map/ppermute | solution.py:614
  41.4 5.9 %collective-permute-start.14 = (bf16[16,32,128]{2,1,0:T(8,128)(2,1)S(1)}, bf16[16,32,128]{2,1,0:T(8,128)(2,1)S(1)}, u32[]{:S(2)}, u32[]{:S(2)}) collective-permute-start(bf16[16,32,128]{2,1,0:T(8,128)(2,1)S(1)} %get-tuple-element.87), channel_id=1, source_target_pairs={{0,4},{4,0},{8,12},{12,8},{16,20},{20,16},{24,28},{28,24},{1,5},{5... | collective-permute-start | bytes 393224 | tf_op jit(solution)/shard_map/ppermute | solution.py:614
  42.9 5.7 %collective-permute-start.8 = (bf16[32,80,128]{2,1,0:T(8,128)(2,1)S(1)}, bf16[32,80,128]{2,1,0:T(8,128)(2,1)S(1)}, u32[]{:S(2)}, u32[]{:S(2)}) collective-permute-start(bf16[32,80,128]{2,1,0:T(8,128)(2,1)S(1)} %get-tuple-element.75.refs_0_), channel_id=1, source_target_pairs={{0,1},{1,0},{2,3},{3,2},{4,5},{5,4},{6,7},{7,6},{8,9},{9,8},{10,11... | collective-permute-start | bytes 1966088 | tf_op jit(solution)/shard_map/ppermute | solution.py:614
  47.3 2.1 %collective-permute-start.15 = (bf16[32,80,128]{2,1,0:T(8,128)(2,1)S(1)}, bf16[32,80,128]{2,1,0:T(8,128)(2,1)S(1)}, u32[]{:S(2)}, u32[]{:S(2)}) collective-permute-start(bf16[32,80,128]{2,1,0:T(8,128)(2,1)S(1)} %collective-permute-done.9.refs_2_), channel_id=1, source_target_pairs={{0,1},{1,0},{2,3},{3,2},{4,5},{5,4},{6,7},{7,6},{8,9},{9,8},{10,11... | collective-permute-start | bytes 1966088 | tf_op jit(solution)/shard_map/ppermute | solution.py:614
  47.3 8.7 %collective-permute-start.17 = (bf16[16,64,128]{2,1,0:T(8,128)(2,1)S(1)}, bf16[16,64,128]{2,1,0:T(8,128)(2,1)S(1)}, u32[]{:S(2)}, u32[]{:S(2)}) collective-permute-start(bf16[16,64,128]{2,1,0:T(8,128)(2,1)S(1)} %get-tuple-element.93), channel_id=1, source_target_pairs={{0,2},{1,3},{2,0},{3,1},{4,6},{5,7},{6,4},{7,5},{8,10},{9,11},{10,... | collective-permute-start | bytes 786440 | tf_op jit(solution)/shard_map/ppermute | solution.py:614
  50.6 10.9 %collective-permute-start.16 = (bf16[16,80,128]{2,1,0:T(8,128)(2,1)S(1)}, bf16[16,80,128]{2,1,0:T(8,128)(2,1)S(1)}, u32[]{:S(2)}, u32[]{:S(2)}) collective-permute-start(bf16[16,80,128]{2,1,0:T(8,128)(2,1)S(1)} %get-tuple-element.90), channel_id=1, source_target_pairs={{0,4},{4,0},{8,12},{12,8},{16,20},{20,16},{24,28},{28,24},{1,5},{5... | collective-permute-start | bytes 983048 | tf_op jit(solution)/shard_map/ppermute | solution.py:614
  56.1 5.4 %collective-permute-start.18 = (bf16[4,96,128]{2,1,0:T(8,128)(2,1)S(1)}, bf16[4,96,128]{2,1,0:T(8,128)(2,1)S(1)}, u32[]{:S(2)}, u32[]{:S(2)}) collective-permute-start(bf16[4,96,128]{2,1,0:T(8,128)(2,1)S(1)} %get-tuple-element.95), channel_id=1, source_target_pairs={{0,8},{4,12},{8,0},{12,4},{16,24},{20,28},{24,16},{28,20},{1,9},{5... | collective-permute-start | bytes 294920 | tf_op jit(solution)/shard_map/ppermute | solution.py:614
  57.8 11.0 %collective-permute-start.22 = (bf16[4,96,128]{2,1,0:T(8,128)(2,1)S(1)}, bf16[4,96,128]{2,1,0:T(8,128)(2,1)S(1)}, u32[]{:S(2)}, u32[]{:S(2)}) collective-permute-start(bf16[4,96,128]{2,1,0:T(8,128)(2,1)S(1)} %get-tuple-element.103), channel_id=1, source_target_pairs={{0,16},{4,20},{8,24},{12,28},{16,0},{20,4},{24,8},{28,12},{1,17},{... | collective-permute-start | bytes 294920 | tf_op jit(solution)/shard_map/ppermute | solution.py:614
  60.1 8.6 %collective-permute-start.23 = (bf16[4,96,128]{2,1,0:T(8,128)(2,1)S(1)}, bf16[4,96,128]{2,1,0:T(8,128)(2,1)S(1)}, u32[]{:S(2)}, u32[]{:S(2)}) collective-permute-start(bf16[4,96,128]{2,1,0:T(8,128)(2,1)S(1)} %get-tuple-element.104), channel_id=1, source_target_pairs={{0,24},{4,28},{8,16},{12,20},{16,8},{20,12},{24,0},{28,4},{1,25},{... | collective-permute-start | bytes 294920 | tf_op jit(solution)/shard_map/ppermute | solution.py:614
  61.6 7.1 %collective-permute-start.19 = (bf16[4,80,128]{2,1,0:T(8,128)(2,1)S(1)}, bf16[4,80,128]{2,1,0:T(8,128)(2,1)S(1)}, u32[]{:S(2)}, u32[]{:S(2)}) collective-permute-start(bf16[4,80,128]{2,1,0:T(8,128)(2,1)S(1)} %get-tuple-element.98), channel_id=1, source_target_pairs={{0,8},{4,12},{8,0},{12,4},{16,24},{20,28},{24,16},{28,20},{1,9},{5... | collective-permute-start | bytes 245768 | tf_op jit(solution)/shard_map/ppermute | solution.py:614
  62.8 12.4 %collective-permute-start.20 = (bf16[4,80,128]{2,1,0:T(8,128)(2,1)S(1)}, bf16[4,80,128]{2,1,0:T(8,128)(2,1)S(1)}, u32[]{:S(2)}, u32[]{:S(2)}) collective-permute-start(bf16[4,80,128]{2,1,0:T(8,128)(2,1)S(1)} %get-tuple-element.99), channel_id=1, source_target_pairs={{0,16},{4,20},{8,24},{12,28},{16,0},{20,4},{24,8},{28,12},{1,17},{... | collective-permute-start | bytes 245768 | tf_op jit(solution)/shard_map/ppermute | solution.py:614
  65.7 9.5 %collective-permute-start.21 = (bf16[4,80,128]{2,1,0:T(8,128)(2,1)S(1)}, bf16[4,80,128]{2,1,0:T(8,128)(2,1)S(1)}, u32[]{:S(2)}, u32[]{:S(2)}) collective-permute-start(bf16[4,80,128]{2,1,0:T(8,128)(2,1)S(1)} %get-tuple-element.100), channel_id=1, source_target_pairs={{0,24},{4,28},{8,16},{12,20},{16,8},{20,12},{24,0},{28,4},{1,25},{... | collective-permute-start | bytes 245768 | tf_op jit(solution)/shard_map/ppermute | solution.py:614
  (19 other events, 115.8 us)

commit v13 on v12

--- a/solution.py
+++ b/solution.py
@@ -557,8 +557,8 @@
 
 def collapse_kernel(places, each, packed, *refs):
     mats = unpack(packed, places)
-    b, c = (refs[i * each : (i + 1) * each] for i in range(2))
-    out, level0 = refs[2 * each :]
+    a, b, c = (refs[i * each : (i + 1) * each] for i in range(3))
+    out, level0 = refs[3 * each :]
 
     def total(sources, lo, hi):
         acc = sources[0][:, lo:hi, :]
@@ -586,7 +586,7 @@
     hi, lo = split(wide)
     up = mm(mats["even"], hi) + mm(mats["even"], lo)
     down = mm(mats["odd"], hi) + mm(mats["odd"], lo)
-    bottom = jnp.maximum(total(c, 64, 96), 1.0)
+    bottom = jnp.maximum(total(a, 0, 32), 1.0)
     for ch in range(COLOURS):
         own = total(b, 0, 32) if ch == 0 else total(c, 32 * (ch - 1), 32 * ch)
         back = jnp.where(lane < 64, up[:, ch * 128 : ch * 128 + 128], down[:, ch * 128 : ch * 128 + 128])
@@ -596,16 +596,16 @@
             out[ch, :, row * 128 : row * 128 + 128] = level0[pl.ds(ch * 128 + row, TILE_DEV, stride=32), :]
 
 
-def collapse(b, c):
+def collapse(a, b, c):
     packed, places = collapse_matrices()
     tiles = pl.pallas_call(
-        functools.partial(collapse_kernel, places, len(b)),
+        functools.partial(collapse_kernel, places, len(a)),
         out_shape=jax.ShapeDtypeStruct((COLOURS, TILE_DEV, 4096), F32),
         scratch_shapes=[pltpu.VMEM((COLOURS * 128, 128), F32)],
         compiler_params=pltpu.CompilerParams(vmem_limit_bytes=VMEM),
         cost_estimate=pl.CostEstimate(flops=10**6, bytes_accessed=10**4, transcendentals=0),
         name="collapse",
-    )(packed, *b, *c)
+    )(packed, *a, *b, *c)
     return jnp.swapaxes(tiles, 0, 1)
 
 
@@ -675,10 +675,13 @@
     far_near = swap(far_first, "tiles", 1)
     home_f, away_f = gather(routes_x, first, near_first, far_first, far_near)
     got_f = swap(away_f, "frames", 1)
-    got_second = along(*add_halves((home_s, home_w), (got_s, got_w)))
-    got_f, got_second[1] = tie((got_f, got_second[1]))
+    home_w, home_f = tie((home_w, home_f))
+    got_weights = along(*add_halves((home_w,), (got_w,)))
+    got_s, got_weights = tie((got_s, got_weights))
+    got_second = along(*add_halves((home_s,), (got_s,)))
+    got_f, got_second[1], got_second[2] = tie((got_f, got_second[1], got_second[2]))
     got_first = along(*add_halves((home_f,), (got_f,)))
-    return collapse(got_first, got_second)
+    return collapse(got_weights, got_first, got_second)
 
 
 def solution(mesh):

time: 77.9 us -> 81.4 us (1.045)
  starting transfers between devices: 28 us -> 31.2 us
    ppermute x24 -> x27, starting transfers between devices: 28 us -> 31.2 us  [swap(): return lax.ppermute(value, axis, [(i, i ^ bit) for i in range(size)])]
    ppermute x24 -> x27, waiting for transfers between devices: 19.2 us -> 19.1 us  [swap(): return lax.ppermute(value, axis, [(i, i ^ bit) for i in range(size)])]
  transfers between devices with their start and end apart: 24 -> 27, of which waited for: 9 -> 10; matrix products, arithmetic and copies ran while one was open for 1% -> 1% of each run, Pallas kernels for 17% -> 16%
where the time goes in v13:
time: 81.4 us; the launch traced here: 80.8 us
  starting transfers between devices  31.2 us (38%)
  waiting for transfers between devices  19.1 us (23%)
  Pallas kernels  18.8 us (23%)
  local copies, waits for them, and re-layouts  8.73 us (11%)
  between operations  1.58 us (2%)
  other arithmetic  1.37 us (2%)
    ppermute x27, starting transfers between devices, swap(): return lax.ppermute(value, axis, [(i, i ^ bit) for i in range(size)])  31.2 us
    ppermute x27, waiting for transfers between devices, swap(): return lax.ppermute(value, axis, [(i, i ^ bit) for i in range(size)])  19.1 us
    unnamed x38, local copies, waits for them, and re-layouts  8.73 us
    pallas_call x3, Pallas kernels, gather_rows(): pl.pallas_call(gather_kernel, in_specs=[pl.BlockSpec(memory_space=pltpu.S...  4.12 us
    pallas_call x1, Pallas kernels, colours_of(): pl.pallas_call(functools.partial(colours_kernel, small_places, large_plac...  3.55 us
    pallas_call x2, Pallas kernels, routes_of(): pl.pallas_call(routes_kernel, in_specs=[smem], out_specs=[smem, smem], ou...  3.29 us
    pallas_call x1, Pallas kernels, weights_of(): pl.pallas_call(functools.partial(weights_kernel, small_places, large_plac...  2.22 us
    pallas_call x1, Pallas kernels, collapse(): pl.pallas_call(functools.partial(collapse_kernel, places, len(a)), out_sh...  2.18 us
  transfers between devices with their start and end apart: 27, of which 10 were waited for; matrix products, arithmetic and copies ran while one was open for 1% of the time, Pallas kernels for 16%

profile of v13, /device:TPU:0, one launch (start us, length us, event | category | flops | bytes accessed | tf_op | source)
XLA Modules:
  0.0 80.8 jit_solution(10624753044542753688)
XLA Ops:
  3.5 1.9 %strips.1 = bf16[288,128]{1,0:T(8,128)(2,1)S(1)} custom-call(s32[1]{0:T(128)S(6)} %copy.14.cell, bf16[1,3,128,1024]{3,2,1,0:T(8,128)(2,1)S(1)} %copy-done.11, bf16[1,3,128,1024]{3,2,1,0:T(8,128)(2,1)S(1)} %copy-done.11, bf16[512,512]{1,0:T(8,128)(2,1)S(1)} %copy-done.16), custom_call_target="tpu_custom_call" | custom-call | flops 2000000000 | bytes 1000000 | tf_op jit(solution)/shard_map/strips/pallas_call | solution.py:247
  5.9 2.6 %collective-permute-start = (bf16[288,128]{1,0:T(8,128)(2,1)S(1)}, bf16[288,128]{1,0:T(8,128)(2,1)S(1)}, u32[]{:S(2)}, u32[]{:S(2)}) collective-permute-start(bf16[288,128]{1,0:T(8,128)(2,1)S(1)} %strips.1), channel_id=1, source_target_pairs={{0,4},{4,0},{8,12},{12,8},{16,20},{20,16},{24,28},{28,24},{1,5},{5... | collective-permute-start | bytes 221192 | tf_op jit(solution)/shard_map/ppermute | solution.py:614
  10.2 2.2 %weights.1 = (bf16[32,32,128]{2,1,0:T(8,128)(2,1)S(1)}, f32[320,1024]{1,0:T(8,128)S(1)}) custom-call(bf16[1,128,1024]{2,1,0:T(8,128)(2,1)S(1)} %copy-done.13, s32[1,64,128]{2,1,0:T(8,128)S(1)} %bitcast.13, bf16[512,512]{1,0:T(8,128)(2,1)S(1)} %copy-done.17, bf16[512,640]{1,0:T(8,128)(2,1)S(1)} %copy-done.15), custom_call_target="tpu_custom_call" | custom-call | flops 4000000000 | bytes 2000000 | tf_op jit(solution)/shard_map/weights/pallas_call | solution.py:356
  12.6 2.0 %collective-permute-start.6 = (s32[2,32]{1,0:T(2,128)S(1)}, s32[2,32]{1,0:T(2,128)S(1)}, u32[]{:S(2)}, u32[]{:S(2)}) collective-permute-start(s32[2,32]{1,0:T(2,128)S(1)} %pad_add_fusion.3), channel_id=1, source_target_pairs={{0,2},{1,3},{2,0},{3,1},{4,6},{5,7},{6,4},{7,5},{8,10},{9,11},{10,... | collective-permute-start | bytes 776 | tf_op jit(solution)/shard_map/ppermute | solution.py:614
  14.6 1.6 %collective-permute-start.1 = (bf16[288,128]{1,0:T(8,128)(2,1)S(1)}, bf16[288,128]{1,0:T(8,128)(2,1)S(1)}, u32[]{:S(2)}, u32[]{:S(2)}) collective-permute-start(bf16[288,128]{1,0:T(8,128)(2,1)S(1)} %broadcast_select_fusion), channel_id=1, source_target_pairs={{0,8},{4,12},{8,0},{12,4},{16,24},{20,28},{24,16},{28,20},{1,9},{5... | collective-permute-start | bytes 221192 | tf_op jit(solution)/shard_map/ppermute | solution.py:614
  16.9 1.9 %collective-permute-start.3 = (bf16[32,32,128]{2,1,0:T(8,128)(2,1)S(1)}, bf16[32,32,128]{2,1,0:T(8,128)(2,1)}, u32[]{:S(2)}, u32[]{:S(2)}) collective-permute-start(bf16[32,32,128]{2,1,0:T(8,128)(2,1)S(1)} %get-tuple-element.73.refs_0_), channel_id=1, source_target_pairs={{0,2},{1,3},{2,0},{3,1},{4,6},{5,7},{6,4},{7,5},{8,10},{9,11},{10,... | collective-permute-start | bytes 786440 | tf_op jit(solution)/shard_map/ppermute | solution.py:614
  19.0 2.7 %collective-permute-start.2 = (bf16[288,128]{1,0:T(8,128)(2,1)S(1)}, bf16[288,128]{1,0:T(8,128)(2,1)S(1)}, u32[]{:S(2)}, u32[]{:S(2)}) collective-permute-start(bf16[288,128]{1,0:T(8,128)(2,1)S(1)} %broadcast_select_fusion.1), channel_id=1, source_target_pairs={{0,16},{4,20},{8,24},{12,28},{16,0},{20,4},{24,8},{28,12},{1,17},{... | collective-permute-start | bytes 221192 | tf_op jit(solution)/shard_map/ppermute | solution.py:614
  22.7 3.5 %colours.1 = f32[560,1024]{1,0:T(8,128)S(1)} custom-call(bf16[1,3,128,1024]{3,2,1,0:T(8,128)(2,1)S(1)} %copy-done.12, bf16[512,512]{1,0:T(8,128)(2,1)S(1)} %copy-done.18, bf16[512,640]{1,0:T(8,128)(2,1)S(1)} %copy-done.15), custom_call_target="tpu_custom_call" | custom-call | flops 6000000000 | bytes 4000000 | tf_op jit(solution)/shard_map/colours/pallas_call | solution.py:368
  27.8 1.6 %collective-permute-start.8 = (bf16[32,64,128]{2,1,0:T(8,128)(2,1)S(1)}, bf16[32,64,128]{2,1,0:T(8,128)(2,1)S(1)}, u32[]{:S(2)}, u32[]{:S(2)}) collective-permute-start(bf16[32,64,128]{2,1,0:T(8,128)(2,1)S(1)} %get-tuple-element.84.refs_0_), channel_id=1, source_target_pairs={{0,4},{4,0},{8,12},{12,8},{16,20},{20,16},{24,28},{28,24},{1,5},{5... | collective-permute-start | bytes 1572872 | tf_op jit(solution)/shard_map/ppermute | solution.py:614
  30.9 1.6 %routes.2 = (s32[4,33]{1,0:T(4,128)}, s32[4]{0:T(128)}) custom-call(s32[4,32]{1,0:T(4,128)} %get-tuple-element.85.spot), custom_call_target="tpu_custom_call" | custom-call | tf_op jit(solution)/shard_map/routes/pallas_call | solution.py:462
  32.6 1.6 %routes.3 = (s32[4,33]{1,0:T(4,128)}, s32[4]{0:T(128)}) custom-call(s32[4,32]{1,0:T(4,128)} %get-tuple-element.91.spot), custom_call_target="tpu_custom_call" | custom-call | tf_op jit(solution)/shard_map/routes/pallas_call | solution.py:462
  38.9 2.5 %collective-permute-done.8.refs_2_ = bf16[32,64,128]{2,1,0:T(8,128)(2,1)S(1)} collective-permute-done((bf16[32,64,128]{2,1,0:T(8,128)(2,1)S(1)}, bf16[32,64,128]{2,1,0:T(8,128)(2,1)S(1)}, u32[]{:S(2)}, u32[]{:S(2)}) %collective-permute-start.8) | collective-permute-done | bytes 524320 | tf_op jit(solution)/shard_map/ppermute | solution.py:614
  41.4 1.5 %collective-permute-start.15 = (bf16[16,32,128]{2,1,0:T(8,128)(2,1)S(1)}, bf16[16,32,128]{2,1,0:T(8,128)(2,1)S(1)}, u32[]{:S(2)}, u32[]{:S(2)}) collective-permute-start(bf16[16,32,128]{2,1,0:T(8,128)(2,1)S(1)} %get-tuple-element.101), channel_id=1, source_target_pairs={{0,4},{4,0},{8,12},{12,8},{16,20},{20,16},{24,28},{28,24},{1,5},{5... | collective-permute-start | bytes 393224 | tf_op jit(solution)/shard_map/ppermute | solution.py:614
  50.7 1.6 %collective-permute-start.20 = (bf16[16,80,128]{2,1,0:T(8,128)(2,1)S(1)}, bf16[16,80,128]{2,1,0:T(8,128)(2,1)S(1)}, u32[]{:S(2)}, u32[]{:S(2)}) collective-permute-start(bf16[16,80,128]{2,1,0:T(8,128)(2,1)S(1)} %get-tuple-element.115), channel_id=1, source_target_pairs={{0,4},{4,0},{8,12},{12,8},{16,20},{20,16},{24,28},{28,24},{1,5},{5... | collective-permute-start | bytes 983048 | tf_op jit(solution)/shard_map/ppermute | solution.py:614
  52.3 1.9 %collective-permute-start.17 = (bf16[4,32,128]{2,1,0:T(8,128)(2,1)S(1)}, bf16[4,32,128]{2,1,0:T(8,128)(2,1)S(1)}, u32[]{:S(2)}, u32[]{:S(2)}) collective-permute-start(bf16[4,32,128]{2,1,0:T(8,128)(2,1)S(1)} %get-tuple-element.107), channel_id=1, source_target_pairs={{0,8},{4,12},{8,0},{12,4},{16,24},{20,28},{24,16},{28,20},{1,9},{5... | collective-permute-start | bytes 98312 | tf_op jit(solution)/shard_map/ppermute | solution.py:614
  54.2 2.2 %collective-permute-start.18 = (bf16[4,32,128]{2,1,0:T(8,128)(2,1)S(1)}, bf16[4,32,128]{2,1,0:T(8,128)(2,1)S(1)}, u32[]{:S(2)}, u32[]{:S(2)}) collective-permute-start(bf16[4,32,128]{2,1,0:T(8,128)(2,1)S(1)} %get-tuple-element.108), channel_id=1, source_target_pairs={{0,16},{4,20},{8,24},{12,28},{16,0},{20,4},{24,8},{28,12},{1,17},{... | collective-permute-start | bytes 98312 | tf_op jit(solution)/shard_map/ppermute | solution.py:614
  56.8 2.4 %collective-permute-done.18.refs_2_ = bf16[4,32,128]{2,1,0:T(8,128)(2,1)S(1)} collective-permute-done((bf16[4,32,128]{2,1,0:T(8,128)(2,1)S(1)}, bf16[4,32,128]{2,1,0:T(8,128)(2,1)S(1)}, u32[]{:S(2)}, u32[]{:S(2)}) %collective-permute-start.18) | collective-permute-done | bytes 32800 | tf_op jit(solution)/shard_map/ppermute | solution.py:614
  59.2 2.9 %collective-permute-done.19.refs_3_ = bf16[4,32,128]{2,1,0:T(8,128)(2,1)S(1)} collective-permute-done((bf16[4,32,128]{2,1,0:T(8,128)(2,1)S(1)}, bf16[4,32,128]{2,1,0:T(8,128)(2,1)S(1)}, u32[]{:S(2)}, u32[]{:S(2)}) %collective-permute-start.19) | collective-permute-done | bytes 32800 | tf_op jit(solution)/shard_map/ppermute | solution.py:614
  63.2 3.2 %collective-permute-done.21.refs_9_ = bf16[4,64,128]{2,1,0:T(8,128)(2,1)S(1)} collective-permute-done((bf16[4,64,128]{2,1,0:T(8,128)(2,1)S(1)}, bf16[4,64,128]{2,1,0:T(8,128)(2,1)S(1)}, u32[]{:S(2)}, u32[]{:S(2)}) %collective-permute-start.21) | collective-permute-done | bytes 65568 | tf_op jit(solution)/shard_map/ppermute | solution.py:614
  67.5 2.5 %collective-permute-start.23 = (bf16[4,80,128]{2,1,0:T(8,128)(2,1)S(1)}, bf16[4,80,128]{2,1,0:T(8,128)(2,1)S(1)}, u32[]{:S(2)}, u32[]{:S(2)}) collective-permute-start(bf16[4,80,128]{2,1,0:T(8,128)(2,1)S(1)} %get-tuple-element.122), channel_id=1, source_target_pairs={{0,8},{4,12},{8,0},{12,4},{16,24},{20,28},{24,16},{28,20},{1,9},{5... | collective-permute-start | bytes 245768 | tf_op jit(solution)/shard_map/ppermute | solution.py:614
  70.2 2.2 %collective-permute-start.25 = (bf16[4,80,128]{2,1,0:T(8,128)(2,1)S(1)}, bf16[4,80,128]{2,1,0:T(8,128)(2,1)S(1)}, u32[]{:S(2)}, u32[]{:S(2)}) collective-permute-start(bf16[4,80,128]{2,1,0:T(8,128)(2,1)S(1)} %get-tuple-element.124), channel_id=1, source_target_pairs={{0,24},{4,28},{8,16},{12,20},{16,8},{20,12},{24,0},{28,4},{1,25},{... | collective-permute-start | bytes 245768 | tf_op jit(solution)/shard_map/ppermute | solution.py:614
  72.5 1.6 %collective-permute-start.26 = (bf16[4,64,128]{2,1,0:T(8,128)(2,1)S(1)}, bf16[4,64,128]{2,1,0:T(8,128)(2,1)S(1)}, u32[]{:S(2)}, u32[]{:S(2)}) collective-permute-start(bf16[4,64,128]{2,1,0:T(8,128)(2,1)S(1)} %get-tuple-element.128), channel_id=1, source_target_pairs={{0,24},{4,28},{8,16},{12,20},{16,8},{20,12},{24,0},{28,4},{1,25},{... | collective-permute-start | bytes 196616 | tf_op jit(solution)/shard_map/ppermute | solution.py:614
  74.1 4.6 %collective-permute-done.26.refs_11_ = bf16[4,64,128]{2,1,0:T(8,128)(2,1)S(1)} collective-permute-done((bf16[4,64,128]{2,1,0:T(8,128)(2,1)S(1)}, bf16[4,64,128]{2,1,0:T(8,128)(2,1)S(1)}, u32[]{:S(2)}, u32[]{:S(2)}) %collective-permute-start.26) | collective-permute-done | bytes 65568 | tf_op jit(solution)/shard_map/ppermute | solution.py:614
  78.6 2.2 %collapse.1 = f32[3,4,4096]{2,1,0:T(4,128)} custom-call(bf16[192,1280]{1,0:T(8,128)(2,1)S(1)} %copy-done, f32[4,32,128]{2,1,0:T(8,128)S(1)} %get-tuple-element.110.refs_0_, bf16[4,32,128]{2,1,0:T(8,128)(2,1)S(1)} %collective-permute-done.17.refs_1_, bf16[4,32,128]{2,1,0:T(8,128)(2,1)S(1)} %collective-permute-done.18.refs_2_, ...), custom_call_target="tpu_custom_call" | custom-call | flops 1000000 | bytes 10000 | tf_op jit(solution)/shard_map/collapse/pallas_call | solution.py:601
  (87 shorter events, 24.7 us)
Async XLA Ops:
  5.4 7.1 %collective-permute-start.5 = (s32[32]{0:T(128)S(1)}, s32[32]{0:T(128)S(1)}, u32[]{:S(2)}, u32[]{:S(2)}) collective-permute-start(s32[32]{0:T(128)S(1)} %bitcast_add_fusion), channel_id=1, source_target_pairs={{0,1},{1,0},{2,3},{3,2},{4,5},{5,4},{6,7},{7,6},{8,9},{9,8},{10,11... | collective-permute-start | bytes 392 | tf_op jit(solution)/shard_map/ppermute | solution.py:614
  5.9 8.7 %collective-permute-start = (bf16[288,128]{1,0:T(8,128)(2,1)S(1)}, bf16[288,128]{1,0:T(8,128)(2,1)S(1)}, u32[]{:S(2)}, u32[]{:S(2)}) collective-permute-start(bf16[288,128]{1,0:T(8,128)(2,1)S(1)} %strips.1), channel_id=1, source_target_pairs={{0,4},{4,0},{8,12},{12,8},{16,20},{20,16},{24,28},{28,24},{1,5},{5... | collective-permute-start | bytes 221192 | tf_op jit(solution)/shard_map/ppermute | solution.py:614
  12.5 3.7 %collective-permute-start.7 = (s32[2,32]{1,0:T(2,128)S(1)}, s32[2,32]{1,0:T(2,128)S(1)}, u32[]{:S(2)}, u32[]{:S(2)}) collective-permute-start(s32[2,32]{1,0:T(2,128)S(1)} %pad_add_fusion.3), channel_id=1, source_target_pairs={{0,4},{4,0},{8,12},{12,8},{16,20},{20,16},{24,28},{28,24},{1,5},{5... | collective-permute-start | bytes 776 | tf_op jit(solution)/shard_map/ppermute | solution.py:614
  14.6 4.4 %collective-permute-start.1 = (bf16[288,128]{1,0:T(8,128)(2,1)S(1)}, bf16[288,128]{1,0:T(8,128)(2,1)S(1)}, u32[]{:S(2)}, u32[]{:S(2)}) collective-permute-start(bf16[288,128]{1,0:T(8,128)(2,1)S(1)} %broadcast_select_fusion), channel_id=1, source_target_pairs={{0,8},{4,12},{8,0},{12,4},{16,24},{20,28},{24,16},{28,20},{1,9},{5... | collective-permute-start | bytes 221192 | tf_op jit(solution)/shard_map/ppermute | solution.py:614
  16.9 9.4 %collective-permute-start.4 = (bf16[32,32,128]{2,1,0:T(8,128)(2,1)S(1)}, bf16[32,32,128]{2,1,0:T(8,128)(2,1)S(1)}, u32[]{:S(2)}, u32[]{:S(2)}) collective-permute-start(bf16[32,32,128]{2,1,0:T(8,128)(2,1)S(1)} %get-tuple-element.73.refs_0_), channel_id=1, source_target_pairs={{0,1},{1,0},{2,3},{3,2},{4,5},{5,4},{6,7},{7,6},{8,9},{9,8},{10,11... | collective-permute-start | bytes 786440 | tf_op jit(solution)/shard_map/ppermute | solution.py:614
  16.9 9.5 %collective-permute-start.3 = (bf16[32,32,128]{2,1,0:T(8,128)(2,1)S(1)}, bf16[32,32,128]{2,1,0:T(8,128)(2,1)}, u32[]{:S(2)}, u32[]{:S(2)}) collective-permute-start(bf16[32,32,128]{2,1,0:T(8,128)(2,1)S(1)} %get-tuple-element.73.refs_0_), channel_id=1, source_target_pairs={{0,2},{1,3},{2,0},{3,1},{4,6},{5,7},{6,4},{7,5},{8,10},{9,11},{10,... | collective-permute-start | bytes 786440 | tf_op jit(solution)/shard_map/ppermute | solution.py:614
  19.0 7.3 %collective-permute-start.2 = (bf16[288,128]{1,0:T(8,128)(2,1)S(1)}, bf16[288,128]{1,0:T(8,128)(2,1)S(1)}, u32[]{:S(2)}, u32[]{:S(2)}) collective-permute-start(bf16[288,128]{1,0:T(8,128)(2,1)S(1)} %broadcast_select_fusion.1), channel_id=1, source_target_pairs={{0,16},{4,20},{8,24},{12,28},{16,0},{20,4},{24,8},{28,12},{1,17},{... | collective-permute-start | bytes 221192 | tf_op jit(solution)/shard_map/ppermute | solution.py:614
  27.8 13.6 %collective-permute-start.8 = (bf16[32,64,128]{2,1,0:T(8,128)(2,1)S(1)}, bf16[32,64,128]{2,1,0:T(8,128)(2,1)S(1)}, u32[]{:S(2)}, u32[]{:S(2)}) collective-permute-start(bf16[32,64,128]{2,1,0:T(8,128)(2,1)S(1)} %get-tuple-element.84.refs_0_), channel_id=1, source_target_pairs={{0,4},{4,0},{8,12},{12,8},{16,20},{20,16},{24,28},{28,24},{1,5},{5... | collective-permute-start | bytes 1572872 | tf_op jit(solution)/shard_map/ppermute | solution.py:614
  29.4 4.8 %collective-permute-start.9 = (bf16[32,32,128]{2,1,0:T(8,128)(2,1)}, bf16[32,32,128]{2,1,0:T(8,128)(2,1)S(1)}, u32[]{:S(2)}, u32[]{:S(2)}) collective-permute-start(bf16[32,32,128]{2,1,0:T(8,128)(2,1)} %collective-permute-done.3.refs_2_), channel_id=1, source_target_pairs={{0,1},{1,0},{2,3},{3,2},{4,5},{5,4},{6,7},{7,6},{8,9},{9,8},{10,11... | collective-permute-start | bytes 786440 | tf_op jit(solution)/shard_map/ppermute | solution.py:614
  29.4 17.9 %collective-permute-start.14 = (bf16[32,80,128]{2,1,0:T(8,128)(2,1)S(1)}, bf16[32,80,128]{2,1,0:T(8,128)(2,1)S(1)}, u32[]{:S(2)}, u32[]{:S(2)}) collective-permute-start(bf16[32,80,128]{2,1,0:T(8,128)(2,1)S(1)} %get-tuple-element.99.refs_0_), channel_id=1, source_target_pairs={{0,2},{1,3},{2,0},{3,1},{4,6},{5,7},{6,4},{7,5},{8,10},{9,11},{10,... | collective-permute-start | bytes 1966088 | tf_op jit(solution)/shard_map/ppermute | solution.py:614
  30.7 12.5 %collective-permute-start.10 = (bf16[32,64,128]{2,1,0:T(8,128)(2,1)S(1)}, bf16[32,64,128]{2,1,0:T(8,128)(2,1)S(1)}, u32[]{:S(2)}, u32[]{:S(2)}) collective-permute-start(bf16[32,64,128]{2,1,0:T(8,128)(2,1)S(1)} %get-tuple-element.84.refs_0_), channel_id=1, source_target_pairs={{0,1},{1,0},{2,3},{3,2},{4,5},{5,4},{6,7},{7,6},{8,9},{9,8},{10,11... | collective-permute-start | bytes 1572872 | tf_op jit(solution)/shard_map/ppermute | solution.py:614
  41.4 5.9 %collective-permute-start.15 = (bf16[16,32,128]{2,1,0:T(8,128)(2,1)S(1)}, bf16[16,32,128]{2,1,0:T(8,128)(2,1)S(1)}, u32[]{:S(2)}, u32[]{:S(2)}) collective-permute-start(bf16[16,32,128]{2,1,0:T(8,128)(2,1)S(1)} %get-tuple-element.101), channel_id=1, source_target_pairs={{0,4},{4,0},{8,12},{12,8},{16,20},{20,16},{24,28},{28,24},{1,5},{5... | collective-permute-start | bytes 393224 | tf_op jit(solution)/shard_map/ppermute | solution.py:614
  42.9 5.7 %collective-permute-start.13 = (bf16[32,80,128]{2,1,0:T(8,128)(2,1)S(1)}, bf16[32,80,128]{2,1,0:T(8,128)(2,1)S(1)}, u32[]{:S(2)}, u32[]{:S(2)}) collective-permute-start(bf16[32,80,128]{2,1,0:T(8,128)(2,1)S(1)} %get-tuple-element.99.refs_0_), channel_id=1, source_target_pairs={{0,1},{1,0},{2,3},{3,2},{4,5},{5,4},{6,7},{7,6},{8,9},{9,8},{10,11... | collective-permute-start | bytes 1966088 | tf_op jit(solution)/shard_map/ppermute | solution.py:614
  47.3 9.4 %collective-permute-start.12 = (bf16[16,64,128]{2,1,0:T(8,128)(2,1)S(1)}, bf16[16,64,128]{2,1,0:T(8,128)(2,1)S(1)}, u32[]{:S(2)}, u32[]{:S(2)}) collective-permute-start(bf16[16,64,128]{2,1,0:T(8,128)(2,1)S(1)} %get-tuple-element.97), channel_id=1, source_target_pairs={{0,2},{1,3},{2,0},{3,1},{4,6},{5,7},{6,4},{7,5},{8,10},{9,11},{10,... | collective-permute-start | bytes 786440 | tf_op jit(solution)/shard_map/ppermute | solution.py:614
  50.7 16.8 %collective-permute-start.20 = (bf16[16,80,128]{2,1,0:T(8,128)(2,1)S(1)}, bf16[16,80,128]{2,1,0:T(8,128)(2,1)S(1)}, u32[]{:S(2)}, u32[]{:S(2)}) collective-permute-start(bf16[16,80,128]{2,1,0:T(8,128)(2,1)S(1)} %get-tuple-element.115), channel_id=1, source_target_pairs={{0,4},{4,0},{8,12},{12,8},{16,20},{20,16},{24,28},{28,24},{1,5},{5... | collective-permute-start | bytes 983048 | tf_op jit(solution)/shard_map/ppermute | solution.py:614
  52.3 4.5 %collective-permute-start.17 = (bf16[4,32,128]{2,1,0:T(8,128)(2,1)S(1)}, bf16[4,32,128]{2,1,0:T(8,128)(2,1)S(1)}, u32[]{:S(2)}, u32[]{:S(2)}) collective-permute-start(bf16[4,32,128]{2,1,0:T(8,128)(2,1)S(1)} %get-tuple-element.107), channel_id=1, source_target_pairs={{0,8},{4,12},{8,0},{12,4},{16,24},{20,28},{24,16},{28,20},{1,9},{5... | collective-permute-start | bytes 98312 | tf_op jit(solution)/shard_map/ppermute | solution.py:614
  54.2 5.0 %collective-permute-start.18 = (bf16[4,32,128]{2,1,0:T(8,128)(2,1)S(1)}, bf16[4,32,128]{2,1,0:T(8,128)(2,1)S(1)}, u32[]{:S(2)}, u32[]{:S(2)}) collective-permute-start(bf16[4,32,128]{2,1,0:T(8,128)(2,1)S(1)} %get-tuple-element.108), channel_id=1, source_target_pairs={{0,16},{4,20},{8,24},{12,28},{16,0},{20,4},{24,8},{28,12},{1,17},{... | collective-permute-start | bytes 98312 | tf_op jit(solution)/shard_map/ppermute | solution.py:614
  56.3 5.7 %collective-permute-start.19 = (bf16[4,32,128]{2,1,0:T(8,128)(2,1)S(1)}, bf16[4,32,128]{2,1,0:T(8,128)(2,1)S(1)}, u32[]{:S(2)}, u32[]{:S(2)}) collective-permute-start(bf16[4,32,128]{2,1,0:T(8,128)(2,1)S(1)} %get-tuple-element.109), channel_id=1, source_target_pairs={{0,24},{4,28},{8,16},{12,20},{16,8},{20,12},{24,0},{28,4},{1,25},{... | collective-permute-start | bytes 98312 | tf_op jit(solution)/shard_map/ppermute | solution.py:614
  62.1 4.3 %collective-permute-start.21 = (bf16[4,64,128]{2,1,0:T(8,128)(2,1)S(1)}, bf16[4,64,128]{2,1,0:T(8,128)(2,1)S(1)}, u32[]{:S(2)}, u32[]{:S(2)}) collective-permute-start(bf16[4,64,128]{2,1,0:T(8,128)(2,1)S(1)} %get-tuple-element.118), channel_id=1, source_target_pairs={{0,8},{4,12},{8,0},{12,4},{16,24},{20,28},{24,16},{28,20},{1,9},{5... | collective-permute-start | bytes 196616 | tf_op jit(solution)/shard_map/ppermute | solution.py:614
  62.2 5.2 %collective-permute-start.22 = (bf16[4,64,128]{2,1,0:T(8,128)(2,1)S(1)}, bf16[4,64,128]{2,1,0:T(8,128)(2,1)S(1)}, u32[]{:S(2)}, u32[]{:S(2)}) collective-permute-start(bf16[4,64,128]{2,1,0:T(8,128)(2,1)S(1)} %get-tuple-element.119), channel_id=1, source_target_pairs={{0,16},{4,20},{8,24},{12,28},{16,0},{20,4},{24,8},{28,12},{1,17},{... | collective-permute-start | bytes 196616 | tf_op jit(solution)/shard_map/ppermute | solution.py:614
  67.5 11.1 %collective-permute-start.23 = (bf16[4,80,128]{2,1,0:T(8,128)(2,1)S(1)}, bf16[4,80,128]{2,1,0:T(8,128)(2,1)S(1)}, u32[]{:S(2)}, u32[]{:S(2)}) collective-permute-start(bf16[4,80,128]{2,1,0:T(8,128)(2,1)S(1)} %get-tuple-element.122), channel_id=1, source_target_pairs={{0,8},{4,12},{8,0},{12,4},{16,24},{20,28},{24,16},{28,20},{1,9},{5... | collective-permute-start | bytes 245768 | tf_op jit(solution)/shard_map/ppermute | solution.py:614
  70.0 8.6 %collective-permute-start.24 = (bf16[4,80,128]{2,1,0:T(8,128)(2,1)S(1)}, bf16[4,80,128]{2,1,0:T(8,128)(2,1)S(1)}, u32[]{:S(2)}, u32[]{:S(2)}) collective-permute-start(bf16[4,80,128]{2,1,0:T(8,128)(2,1)S(1)} %get-tuple-element.123), channel_id=1, source_target_pairs={{0,16},{4,20},{8,24},{12,28},{16,0},{20,4},{24,8},{28,12},{1,17},{... | collective-permute-start | bytes 245768 | tf_op jit(solution)/shard_map/ppermute | solution.py:614
  70.2 8.4 %collective-permute-start.25 = (bf16[4,80,128]{2,1,0:T(8,128)(2,1)S(1)}, bf16[4,80,128]{2,1,0:T(8,128)(2,1)S(1)}, u32[]{:S(2)}, u32[]{:S(2)}) collective-permute-start(bf16[4,80,128]{2,1,0:T(8,128)(2,1)S(1)} %get-tuple-element.124), channel_id=1, source_target_pairs={{0,24},{4,28},{8,16},{12,20},{16,8},{20,12},{24,0},{28,4},{1,25},{... | collective-permute-start | bytes 245768 | tf_op jit(solution)/shard_map/ppermute | solution.py:614
  72.5 6.2 %collective-permute-start.26 = (bf16[4,64,128]{2,1,0:T(8,128)(2,1)S(1)}, bf16[4,64,128]{2,1,0:T(8,128)(2,1)S(1)}, u32[]{:S(2)}, u32[]{:S(2)}) collective-permute-start(bf16[4,64,128]{2,1,0:T(8,128)(2,1)S(1)} %get-tuple-element.128), channel_id=1, source_target_pairs={{0,24},{4,28},{8,16},{12,20},{16,8},{20,12},{24,0},{28,4},{1,25},{... | collective-permute-start | bytes 196616 | tf_op jit(solution)/shard_map/ppermute | solution.py:614
  (22 other events, 126.8 us)

commit v14 on v12

--- a/solution.py
+++ b/solution.py
@@ -634,12 +634,6 @@
         return group, lax.bitwise_xor(tile // TILE_DEV, mine), tile % TILE_DEV
 
     half = groups // 2
-    group, part, tile = relative(ids_x)
-    spot_x = jnp.where(part == 0, ((group & 1) * half + (group >> 1)) * TILE_DEV + tile, -1)
-    group, part, tile = relative(ids_y)
-    here = ((group & 1) == 0) & ((part & 1) == 0)
-    spot_y = jnp.where(here, ((part >> 1) * half + (group >> 1)) * TILE_DEV + tile, -1)
-
     weights, masked = weights_of(weight_map, seam_mask)
     bit = 1
     while bit < groups:
@@ -651,7 +645,7 @@
             got, frames = tie((got, frames))
         if bit == half:
             colours = colours_of(frames)
-            got, far, near, spot_x, spot_y, colours = tie((got, far, near, spot_x, spot_y, colours))
+            got, far, near, ids_x, ids_y, colours = tie((got, far, near, ids_x, ids_y, colours))
         strips = jnp.where((mask & bit) != 0, got, strips)
         bit *= 2
 
@@ -662,7 +656,12 @@
         return [own] + [swap(part, "frames", 2 * (j + 1)) for j, part in enumerate(away)]
 
     first, second = blend(strip_cell, strips, colours, masked)
-    first, second, spot_x, spot_y, far = tie((first, second, spot_x, spot_y, far))
+    first, second, ids_x, ids_y, far = tie((first, second, ids_x, ids_y, far))
+    group, part, tile = relative(ids_x)
+    spot_x = jnp.where(part == 0, ((group & 1) * half + (group >> 1)) * TILE_DEV + tile, -1)
+    group, part, tile = relative(ids_y)
+    here = ((group & 1) == 0) & ((part & 1) == 0)
+    spot_y = jnp.where(here, ((part >> 1) * half + (group >> 1)) * TILE_DEV + tile, -1)
     far_first, near_first = swap(first, "tiles", 2), swap(first, "tiles", 1)
     far_second, near_second = swap(second, "frames", 1), swap(second, "tiles", 1)
     routes_x, routes_y = routes_of(spot_x), routes_of(spot_y)

time: 77.9 us -> 80 us (1.027)
  waiting for transfers between devices: 19.2 us -> 21 us
  starting transfers between devices: 28 us -> 26.4 us
  local copies, waits for them, and re-layouts: 8.84 us -> 9.89 us
    ppermute x24, waiting for transfers between devices: 19.2 us -> 21 us  [swap(): return lax.ppermute(value, axis, [(i, i ^ bit) for i in range(size)])]
    ppermute x24, starting transfers between devices: 28 us -> 26.4 us  [swap(): return lax.ppermute(value, axis, [(i, i ^ bit) for i in range(size)])]
    unnamed x38, local copies, waits for them, and re-layouts: 8.84 us -> 9.89 us
  transfers between devices with their start and end apart: 24 -> 24, of which waited for: 9 -> 10; matrix products, arithmetic and copies ran while one was open for 1% -> 2% of each run, Pallas kernels for 17% -> 17%
where the time goes in v14:
time: 80 us; the launch traced here: 79.5 us
  starting transfers between devices  26.4 us (33%)
  waiting for transfers between devices  21 us (26%)
  Pallas kernels  18.7 us (23%)
  local copies, waits for them, and re-layouts  9.89 us (12%)
  other arithmetic  1.95 us (2%)
  between operations  1.57 us (2%)
    ppermute x24, starting transfers between devices, swap(): return lax.ppermute(value, axis, [(i, i ^ bit) for i in range(size)])  26.4 us
    ppermute x24, waiting for transfers between devices, swap(): return lax.ppermute(value, axis, [(i, i ^ bit) for i in range(size)])  21 us
    unnamed x38, local copies, waits for them, and re-layouts  9.89 us
    pallas_call x3, Pallas kernels, gather_rows(): pl.pallas_call(gather_kernel, in_specs=[pl.BlockSpec(memory_space=pltpu.S...  4.16 us
    pallas_call x1, Pallas kernels, colours_of(): pl.pallas_call(functools.partial(colours_kernel, small_places, large_plac...  3.53 us
    pallas_call x2, Pallas kernels, routes_of(): pl.pallas_call(routes_kernel, in_specs=[smem], out_specs=[smem, smem], ou...  3.29 us
    pallas_call x1, Pallas kernels, weights_of(): pl.pallas_call(functools.partial(weights_kernel, small_places, large_plac...  2.22 us
    pallas_call x1, Pallas kernels, collapse(): pl.pallas_call(functools.partial(collapse_kernel, places, len(b)), out_sh...  2.17 us
  transfers between devices with their start and end apart: 24, of which 10 were waited for; matrix products, arithmetic and copies ran while one was open for 2% of the time, Pallas kernels for 17%

profile of v14, /device:TPU:0, one launch (start us, length us, event | category | flops | bytes accessed | tf_op | source)
XLA Modules:
  0.0 79.5 jit_solution(6793249623634021358)
XLA Ops:
  3.5 1.9 %strips.1 = bf16[288,128]{1,0:T(8,128)(2,1)S(1)} custom-call(s32[1]{0:T(128)S(6)} %copy.14.cell, bf16[1,3,128,1024]{3,2,1,0:T(8,128)(2,1)S(1)} %copy-done.10, bf16[1,3,128,1024]{3,2,1,0:T(8,128)(2,1)S(1)} %copy-done.10, bf16[512,512]{1,0:T(8,128)(2,1)S(1)} %copy-done.16), custom_call_target="tpu_custom_call" | custom-call | flops 2000000000 | bytes 1000000 | tf_op jit(solution)/shard_map/strips/pallas_call | solution.py:247
  5.9 2.6 %collective-permute-start = (bf16[288,128]{1,0:T(8,128)(2,1)S(1)}, bf16[288,128]{1,0:T(8,128)(2,1)S(1)}, u32[]{:S(2)}, u32[]{:S(2)}) collective-permute-start(bf16[288,128]{1,0:T(8,128)(2,1)S(1)} %strips.1), channel_id=1, source_target_pairs={{0,4},{4,0},{8,12},{12,8},{16,20},{20,16},{24,28},{28,24},{1,5},{5... | collective-permute-start | bytes 221192 | tf_op jit(solution)/shard_map/ppermute | solution.py:614
  10.2 2.2 %weights.1 = (bf16[32,32,128]{2,1,0:T(8,128)(2,1)S(1)}, f32[320,1024]{1,0:T(8,128)S(1)}) custom-call(bf16[1,128,1024]{2,1,0:T(8,128)(2,1)S(1)} %copy-done.12, s32[1,64,128]{2,1,0:T(8,128)S(1)} %bitcast.13, bf16[512,512]{1,0:T(8,128)(2,1)S(1)} %copy-done.17, bf16[512,640]{1,0:T(8,128)(2,1)S(1)} %copy-done.14), custom_call_target="tpu_custom_call" | custom-call | flops 4000000000 | bytes 2000000 | tf_op jit(solution)/shard_map/weights/pallas_call | solution.py:356
  12.6 2.0 %collective-permute-start.6 = (s32[2,32]{1,0:T(2,128)S(1)}, s32[2,32]{1,0:T(2,128)S(1)}, u32[]{:S(2)}, u32[]{:S(2)}) collective-permute-start(s32[2,32]{1,0:T(2,128)S(1)} %pad_add_fusion.3), channel_id=1, source_target_pairs={{0,2},{1,3},{2,0},{3,1},{4,6},{5,7},{6,4},{7,5},{8,10},{9,11},{10,... | collective-permute-start | bytes 776 | tf_op jit(solution)/shard_map/ppermute | solution.py:614
  14.6 1.6 %collective-permute-start.1 = (bf16[288,128]{1,0:T(8,128)(2,1)S(1)}, bf16[288,128]{1,0:T(8,128)(2,1)S(1)}, u32[]{:S(2)}, u32[]{:S(2)}) collective-permute-start(bf16[288,128]{1,0:T(8,128)(2,1)S(1)} %broadcast_select_fusion), channel_id=1, source_target_pairs={{0,8},{4,12},{8,0},{12,4},{16,24},{20,28},{24,16},{28,20},{1,9},{5... | collective-permute-start | bytes 221192 | tf_op jit(solution)/shard_map/ppermute | solution.py:614
  16.3 2.0 %collective-permute-start.3 = (bf16[32,32,128]{2,1,0:T(8,128)(2,1)S(1)}, bf16[32,32,128]{2,1,0:T(8,128)(2,1)S(1)}, u32[]{:S(2)}, u32[]{:S(2)}) collective-permute-start(bf16[32,32,128]{2,1,0:T(8,128)(2,1)S(1)} %get-tuple-element.61.refs_0_), channel_id=1, source_target_pairs={{0,2},{1,3},{2,0},{3,1},{4,6},{5,7},{6,4},{7,5},{8,10},{9,11},{10,... | collective-permute-start | bytes 786440 | tf_op jit(solution)/shard_map/ppermute | solution.py:614
  19.0 2.7 %collective-permute-start.2 = (bf16[288,128]{1,0:T(8,128)(2,1)S(1)}, bf16[288,128]{1,0:T(8,128)(2,1)S(1)}, u32[]{:S(2)}, u32[]{:S(2)}) collective-permute-start(bf16[288,128]{1,0:T(8,128)(2,1)S(1)} %broadcast_select_fusion.1), channel_id=1, source_target_pairs={{0,16},{4,20},{8,24},{12,28},{16,0},{20,4},{24,8},{28,12},{1,17},{... | collective-permute-start | bytes 221192 | tf_op jit(solution)/shard_map/ppermute | solution.py:614
  23.8 3.5 %colours.1 = f32[560,1024]{1,0:T(8,128)S(1)} custom-call(bf16[1,3,128,1024]{3,2,1,0:T(8,128)(2,1)S(1)} %copy-done.11, bf16[512,512]{1,0:T(8,128)(2,1)S(1)} %copy-done.18, bf16[512,640]{1,0:T(8,128)(2,1)S(1)} %copy-done.15), custom_call_target="tpu_custom_call" | custom-call | flops 6000000000 | bytes 4000000 | tf_op jit(solution)/shard_map/colours/pallas_call | solution.py:368
  27.4 1.4 %blend.1 = (bf16[32,80,128]{2,1,0:T(8,128)(2,1)S(1)}, bf16[32,64,128]{2,1,0:T(8,128)(2,1)S(1)}) custom-call(s32[1]{0:T(128)S(6)} %copy.14.cell, bf16[288,128]{1,0:T(8,128)(2,1)S(1)} %broadcast_select_fusion.2.strips, f32[560,1024]{1,0:T(8,128)S(1)} %colours.1, f32[320,1024]{1,0:T(8,128)S(1)} %get-tuple-element.66.masked), custom_call_target="tpu_custom_call" | custom-call | flops 1000000 | bytes 10000 | tf_op jit(solution)/shard_map/blend/pallas_call | solution.py:439
  28.8 1.6 %collective-permute-start.10 = (bf16[32,64,128]{2,1,0:T(8,128)(2,1)S(1)}, bf16[32,64,128]{2,1,0:T(8,128)(2,1)S(1)}, u32[]{:S(2)}, u32[]{:S(2)}) collective-permute-start(bf16[32,64,128]{2,1,0:T(8,128)(2,1)S(1)} %get-tuple-element.76.refs_0_), channel_id=1, source_target_pairs={{0,4},{4,0},{8,12},{12,8},{16,20},{20,16},{24,28},{28,24},{1,5},{5... | collective-permute-start | bytes 1572872 | tf_op jit(solution)/shard_map/ppermute | solution.py:614
  31.5 1.6 %routes.3 = (s32[4,33]{1,0:T(4,128)}, s32[4]{0:T(128)}) custom-call(s32[4,32]{1,0:T(4,128)} %fusion.8.spot), custom_call_target="tpu_custom_call" | custom-call | tf_op jit(solution)/shard_map/routes/pallas_call | solution.py:462
  34.4 1.6 %routes.2 = (s32[4,33]{1,0:T(4,128)}, s32[4]{0:T(128)}) custom-call(s32[4,32]{1,0:T(4,128)} %fusion.4.spot), custom_call_target="tpu_custom_call" | custom-call | tf_op jit(solution)/shard_map/routes/pallas_call | solution.py:462
  41.9 1.5 %collective-permute-start.14 = (bf16[16,32,128]{2,1,0:T(8,128)(2,1)S(1)}, bf16[16,32,128]{2,1,0:T(8,128)(2,1)S(1)}, u32[]{:S(2)}, u32[]{:S(2)}) collective-permute-start(bf16[16,32,128]{2,1,0:T(8,128)(2,1)S(1)} %get-tuple-element.87), channel_id=1, source_target_pairs={{0,4},{4,0},{8,12},{12,8},{16,20},{20,16},{24,28},{28,24},{1,5},{5... | collective-permute-start | bytes 393224 | tf_op jit(solution)/shard_map/ppermute | solution.py:614
  47.8 2.1 %collective-permute-done.9.refs_2_ = bf16[32,80,128]{2,1,0:T(8,128)(2,1)S(1)} collective-permute-done((bf16[32,80,128]{2,1,0:T(8,128)(2,1)S(1)}, bf16[32,80,128]{2,1,0:T(8,128)(2,1)S(1)}, u32[]{:S(2)}, u32[]{:S(2)}) %collective-permute-start.9) | collective-permute-done | bytes 655392 | tf_op jit(solution)/shard_map/ppermute | solution.py:614
  50.4 1.6 %collective-permute-done.15.refs_3_ = bf16[32,80,128]{2,1,0:T(8,128)(2,1)S(1)} collective-permute-done((bf16[32,80,128]{2,1,0:T(8,128)(2,1)S(1)}, bf16[32,80,128]{2,1,0:T(8,128)(2,1)S(1)}, u32[]{:S(2)}, u32[]{:S(2)}) %collective-permute-start.15) | collective-permute-done | bytes 655392 | tf_op jit(solution)/shard_map/ppermute | solution.py:614
  52.0 1.5 %gather_rows.5 = (f32[16,80,128]{2,1,0:T(8,128)S(1)}, bf16[16,80,128]{2,1,0:T(8,128)(2,1)S(1)}) custom-call(s32[4,33]{1,0:T(4,128)S(1)} %copy-done.6, s32[4]{0:T(128)S(1)} %copy-done.7, bf16[32,80,128]{2,1,0:T(8,128)(2,1)S(1)} %get-tuple-element.75.refs_0_, bf16[32,80,128]{2,1,0:T(8,128)(2,1)S(1)} %collective-permute-done.8.refs_1_, ...), custom_call_target="tpu_custom_call" | custom-call | flops 1000000 | bytes 10000 | tf_op jit(solution)/shard_map/gather_rows/pallas_call | solution.py:496
  53.9 4.7 %collective-permute-done.17.refs_2_ = bf16[16,64,128]{2,1,0:T(8,128)(2,1)S(1)} collective-permute-done((bf16[16,64,128]{2,1,0:T(8,128)(2,1)S(1)}, bf16[16,64,128]{2,1,0:T(8,128)(2,1)S(1)}, u32[]{:S(2)}, u32[]{:S(2)}) %collective-permute-start.17) | collective-permute-done | bytes 262176 | tf_op jit(solution)/shard_map/ppermute | solution.py:614
  58.7 1.6 %collective-permute-start.18 = (bf16[4,96,128]{2,1,0:T(8,128)(2,1)S(1)}, bf16[4,96,128]{2,1,0:T(8,128)(2,1)S(1)}, u32[]{:S(2)}, u32[]{:S(2)}) collective-permute-start(bf16[4,96,128]{2,1,0:T(8,128)(2,1)S(1)} %get-tuple-element.95), channel_id=1, source_target_pairs={{0,8},{4,12},{8,0},{12,4},{16,24},{20,28},{24,16},{28,20},{1,9},{5... | collective-permute-start | bytes 294920 | tf_op jit(solution)/shard_map/ppermute | solution.py:614
  61.0 2.2 %collective-permute-start.23 = (bf16[4,96,128]{2,1,0:T(8,128)(2,1)S(1)}, bf16[4,96,128]{2,1,0:T(8,128)(2,1)S(1)}, u32[]{:S(2)}, u32[]{:S(2)}) collective-permute-start(bf16[4,96,128]{2,1,0:T(8,128)(2,1)S(1)} %get-tuple-element.104), channel_id=1, source_target_pairs={{0,24},{4,28},{8,16},{12,20},{16,8},{20,12},{24,0},{28,4},{1,25},{... | collective-permute-start | bytes 294920 | tf_op jit(solution)/shard_map/ppermute | solution.py:614
  63.6 2.5 %collective-permute-start.19 = (bf16[4,80,128]{2,1,0:T(8,128)(2,1)S(1)}, bf16[4,80,128]{2,1,0:T(8,128)(2,1)S(1)}, u32[]{:S(2)}, u32[]{:S(2)}) collective-permute-start(bf16[4,80,128]{2,1,0:T(8,128)(2,1)S(1)} %get-tuple-element.98), channel_id=1, source_target_pairs={{0,8},{4,12},{8,0},{12,4},{16,24},{20,28},{24,16},{28,20},{1,9},{5... | collective-permute-start | bytes 245768 | tf_op jit(solution)/shard_map/ppermute | solution.py:614
  67.0 1.6 %collective-permute-start.21 = (bf16[4,80,128]{2,1,0:T(8,128)(2,1)S(1)}, bf16[4,80,128]{2,1,0:T(8,128)(2,1)S(1)}, u32[]{:S(2)}, u32[]{:S(2)}) collective-permute-start(bf16[4,80,128]{2,1,0:T(8,128)(2,1)S(1)} %get-tuple-element.100), channel_id=1, source_target_pairs={{0,24},{4,28},{8,16},{12,20},{16,8},{20,12},{24,0},{28,4},{1,25},{... | collective-permute-start | bytes 245768 | tf_op jit(solution)/shard_map/ppermute | solution.py:614
  68.6 4.8 %collective-permute-done.22.refs_6_ = bf16[4,96,128]{2,1,0:T(8,128)(2,1)S(1)} collective-permute-done((bf16[4,96,128]{2,1,0:T(8,128)(2,1)S(1)}, bf16[4,96,128]{2,1,0:T(8,128)(2,1)S(1)}, u32[]{:S(2)}, u32[]{:S(2)}) %collective-permute-start.22) | collective-permute-done | bytes 98336 | tf_op jit(solution)/shard_map/ppermute | solution.py:614
  73.4 3.9 %collective-permute-done.20.refs_2_ = bf16[4,80,128]{2,1,0:T(8,128)(2,1)S(1)} collective-permute-done((bf16[4,80,128]{2,1,0:T(8,128)(2,1)S(1)}, bf16[4,80,128]{2,1,0:T(8,128)(2,1)S(1)}, u32[]{:S(2)}, u32[]{:S(2)}) %collective-permute-start.20) | collective-permute-done | bytes 81952 | tf_op jit(solution)/shard_map/ppermute | solution.py:614
  77.3 2.2 %collapse.1 = f32[3,4,4096]{2,1,0:T(4,128)} custom-call(bf16[192,1280]{1,0:T(8,128)(2,1)S(1)} %copy-done, f32[4,80,128]{2,1,0:T(8,128)S(1)} %get-tuple-element.97.refs_0_, bf16[4,80,128]{2,1,0:T(8,128)(2,1)S(1)} %collective-permute-done.19.refs_1_, bf16[4,80,128]{2,1,0:T(8,128)(2,1)S(1)} %collective-permute-done.20.refs_2_, ...), custom_call_target="tpu_custom_call" | custom-call | flops 1000000 | bytes 10000 | tf_op jit(solution)/shard_map/collapse/pallas_call | solution.py:601
  (82 shorter events, 23.0 us)
Async XLA Ops:
  5.4 7.1 %collective-permute-start.5 = (s32[32]{0:T(128)S(1)}, s32[32]{0:T(128)S(1)}, u32[]{:S(2)}, u32[]{:S(2)}) collective-permute-start(s32[32]{0:T(128)S(1)} %bitcast_add_fusion), channel_id=1, source_target_pairs={{0,1},{1,0},{2,3},{3,2},{4,5},{5,4},{6,7},{7,6},{8,9},{9,8},{10,11... | collective-permute-start | bytes 392 | tf_op jit(solution)/shard_map/ppermute | solution.py:614
  5.9 8.7 %collective-permute-start = (bf16[288,128]{1,0:T(8,128)(2,1)S(1)}, bf16[288,128]{1,0:T(8,128)(2,1)S(1)}, u32[]{:S(2)}, u32[]{:S(2)}) collective-permute-start(bf16[288,128]{1,0:T(8,128)(2,1)S(1)} %strips.1), channel_id=1, source_target_pairs={{0,4},{4,0},{8,12},{12,8},{16,20},{20,16},{24,28},{28,24},{1,5},{5... | collective-permute-start | bytes 221192 | tf_op jit(solution)/shard_map/ppermute | solution.py:614
  12.5 3.7 %collective-permute-start.7 = (s32[2,32]{1,0:T(2,128)S(1)}, s32[2,32]{1,0:T(2,128)S(1)}, u32[]{:S(2)}, u32[]{:S(2)}) collective-permute-start(s32[2,32]{1,0:T(2,128)S(1)} %pad_add_fusion.3), channel_id=1, source_target_pairs={{0,4},{4,0},{8,12},{12,8},{16,20},{20,16},{24,28},{28,24},{1,5},{5... | collective-permute-start | bytes 776 | tf_op jit(solution)/shard_map/ppermute | solution.py:614
  12.6 3.6 %collective-permute-start.6 = (s32[2,32]{1,0:T(2,128)S(1)}, s32[2,32]{1,0:T(2,128)S(1)}, u32[]{:S(2)}, u32[]{:S(2)}) collective-permute-start(s32[2,32]{1,0:T(2,128)S(1)} %pad_add_fusion.3), channel_id=1, source_target_pairs={{0,2},{1,3},{2,0},{3,1},{4,6},{5,7},{6,4},{7,5},{8,10},{9,11},{10,... | collective-permute-start | bytes 776 | tf_op jit(solution)/shard_map/ppermute | solution.py:614
  14.6 4.4 %collective-permute-start.1 = (bf16[288,128]{1,0:T(8,128)(2,1)S(1)}, bf16[288,128]{1,0:T(8,128)(2,1)S(1)}, u32[]{:S(2)}, u32[]{:S(2)}) collective-permute-start(bf16[288,128]{1,0:T(8,128)(2,1)S(1)} %broadcast_select_fusion), channel_id=1, source_target_pairs={{0,8},{4,12},{8,0},{12,4},{16,24},{20,28},{24,16},{28,20},{1,9},{5... | collective-permute-start | bytes 221192 | tf_op jit(solution)/shard_map/ppermute | solution.py:614
  16.3 11.1 %collective-permute-start.4 = (bf16[32,32,128]{2,1,0:T(8,128)(2,1)S(1)}, bf16[32,32,128]{2,1,0:T(8,128)(2,1)S(1)}, u32[]{:S(2)}, u32[]{:S(2)}) collective-permute-start(bf16[32,32,128]{2,1,0:T(8,128)(2,1)S(1)} %get-tuple-element.61.refs_0_), channel_id=1, source_target_pairs={{0,1},{1,0},{2,3},{3,2},{4,5},{5,4},{6,7},{7,6},{8,9},{9,8},{10,11... | collective-permute-start | bytes 786440 | tf_op jit(solution)/shard_map/ppermute | solution.py:614
  16.3 11.1 %collective-permute-start.3 = (bf16[32,32,128]{2,1,0:T(8,128)(2,1)S(1)}, bf16[32,32,128]{2,1,0:T(8,128)(2,1)S(1)}, u32[]{:S(2)}, u32[]{:S(2)}) collective-permute-start(bf16[32,32,128]{2,1,0:T(8,128)(2,1)S(1)} %get-tuple-element.61.refs_0_), channel_id=1, source_target_pairs={{0,2},{1,3},{2,0},{3,1},{4,6},{5,7},{6,4},{7,5},{8,10},{9,11},{10,... | collective-permute-start | bytes 786440 | tf_op jit(solution)/shard_map/ppermute | solution.py:614
  19.0 8.3 %collective-permute-start.2 = (bf16[288,128]{1,0:T(8,128)(2,1)S(1)}, bf16[288,128]{1,0:T(8,128)(2,1)S(1)}, u32[]{:S(2)}, u32[]{:S(2)}) collective-permute-start(bf16[288,128]{1,0:T(8,128)(2,1)S(1)} %broadcast_select_fusion.1), channel_id=1, source_target_pairs={{0,16},{4,20},{8,24},{12,28},{16,0},{20,4},{24,8},{28,12},{1,17},{... | collective-permute-start | bytes 221192 | tf_op jit(solution)/shard_map/ppermute | solution.py:614
  28.8 13.1 %collective-permute-start.10 = (bf16[32,64,128]{2,1,0:T(8,128)(2,1)S(1)}, bf16[32,64,128]{2,1,0:T(8,128)(2,1)S(1)}, u32[]{:S(2)}, u32[]{:S(2)}) collective-permute-start(bf16[32,64,128]{2,1,0:T(8,128)(2,1)S(1)} %get-tuple-element.76.refs_0_), channel_id=1, source_target_pairs={{0,4},{4,0},{8,12},{12,8},{16,20},{20,16},{24,28},{28,24},{1,5},{5... | collective-permute-start | bytes 1572872 | tf_op jit(solution)/shard_map/ppermute | solution.py:614
  30.4 13.2 %collective-permute-start.12 = (bf16[32,64,128]{2,1,0:T(8,128)(2,1)S(1)}, bf16[32,64,128]{2,1,0:T(8,128)(2,1)S(1)}, u32[]{:S(2)}, u32[]{:S(2)}) collective-permute-start(bf16[32,64,128]{2,1,0:T(8,128)(2,1)S(1)} %get-tuple-element.76.refs_0_), channel_id=1, source_target_pairs={{0,1},{1,0},{2,3},{3,2},{4,5},{5,4},{6,7},{7,6},{8,9},{9,8},{10,11... | collective-permute-start | bytes 1572872 | tf_op jit(solution)/shard_map/ppermute | solution.py:614
  30.4 5.6 %collective-permute-start.11 = (bf16[32,32,128]{2,1,0:T(8,128)(2,1)S(1)}, bf16[32,32,128]{2,1,0:T(8,128)(2,1)S(1)}, u32[]{:S(2)}, u32[]{:S(2)}) collective-permute-start(bf16[32,32,128]{2,1,0:T(8,128)(2,1)S(1)} %collective-permute-done.3.refs_2_), channel_id=1, source_target_pairs={{0,1},{1,0},{2,3},{3,2},{4,5},{5,4},{6,7},{7,6},{8,9},{9,8},{10,11... | collective-permute-start | bytes 786440 | tf_op jit(solution)/shard_map/ppermute | solution.py:614
  33.2 16.7 %collective-permute-start.9 = (bf16[32,80,128]{2,1,0:T(8,128)(2,1)S(1)}, bf16[32,80,128]{2,1,0:T(8,128)(2,1)S(1)}, u32[]{:S(2)}, u32[]{:S(2)}) collective-permute-start(bf16[32,80,128]{2,1,0:T(8,128)(2,1)S(1)} %get-tuple-element.75.refs_0_), channel_id=1, source_target_pairs={{0,2},{1,3},{2,0},{3,1},{4,6},{5,7},{6,4},{7,5},{8,10},{9,11},{10,... | collective-permute-start | bytes 1966088 | tf_op jit(solution)/shard_map/ppermute | solution.py:614
  41.9 1.9 %collective-permute-start.13 = (bf16[32,64,128]{2,1,0:T(8,128)(2,1)S(1)}, bf16[32,64,128]{2,1,0:T(8,128)(2,1)S(1)}, u32[]{:S(2)}, u32[]{:S(2)}) collective-permute-start(bf16[32,64,128]{2,1,0:T(8,128)(2,1)S(1)} %collective-permute-done.10.refs_2_), channel_id=1, source_target_pairs={{0,1},{1,0},{2,3},{3,2},{4,5},{5,4},{6,7},{7,6},{8,9},{9,8},{10,11... | collective-permute-start | bytes 1572872 | tf_op jit(solution)/shard_map/ppermute | solution.py:614
  41.9 5.9 %collective-permute-start.14 = (bf16[16,32,128]{2,1,0:T(8,128)(2,1)S(1)}, bf16[16,32,128]{2,1,0:T(8,128)(2,1)S(1)}, u32[]{:S(2)}, u32[]{:S(2)}) collective-permute-start(bf16[16,32,128]{2,1,0:T(8,128)(2,1)S(1)} %get-tuple-element.87), channel_id=1, source_target_pairs={{0,4},{4,0},{8,12},{12,8},{16,20},{20,16},{24,28},{28,24},{1,5},{5... | collective-permute-start | bytes 393224 | tf_op jit(solution)/shard_map/ppermute | solution.py:614
  43.4 7.0 %collective-permute-start.8 = (bf16[32,80,128]{2,1,0:T(8,128)(2,1)S(1)}, bf16[32,80,128]{2,1,0:T(8,128)(2,1)S(1)}, u32[]{:S(2)}, u32[]{:S(2)}) collective-permute-start(bf16[32,80,128]{2,1,0:T(8,128)(2,1)S(1)} %get-tuple-element.75.refs_0_), channel_id=1, source_target_pairs={{0,1},{1,0},{2,3},{3,2},{4,5},{5,4},{6,7},{7,6},{8,9},{9,8},{10,11... | collective-permute-start | bytes 1966088 | tf_op jit(solution)/shard_map/ppermute | solution.py:614
  49.9 2.1 %collective-permute-start.15 = (bf16[32,80,128]{2,1,0:T(8,128)(2,1)S(1)}, bf16[32,80,128]{2,1,0:T(8,128)(2,1)S(1)}, u32[]{:S(2)}, u32[]{:S(2)}) collective-permute-start(bf16[32,80,128]{2,1,0:T(8,128)(2,1)S(1)} %collective-permute-done.9.refs_2_), channel_id=1, source_target_pairs={{0,1},{1,0},{2,3},{3,2},{4,5},{5,4},{6,7},{7,6},{8,9},{9,8},{10,11... | collective-permute-start | bytes 1966088 | tf_op jit(solution)/shard_map/ppermute | solution.py:614
  49.9 8.7 %collective-permute-start.17 = (bf16[16,64,128]{2,1,0:T(8,128)(2,1)S(1)}, bf16[16,64,128]{2,1,0:T(8,128)(2,1)S(1)}, u32[]{:S(2)}, u32[]{:S(2)}) collective-permute-start(bf16[16,64,128]{2,1,0:T(8,128)(2,1)S(1)} %get-tuple-element.93), channel_id=1, source_target_pairs={{0,2},{1,3},{2,0},{3,1},{4,6},{5,7},{6,4},{7,5},{8,10},{9,11},{10,... | collective-permute-start | bytes 786440 | tf_op jit(solution)/shard_map/ppermute | solution.py:614
  53.5 10.1 %collective-permute-start.16 = (bf16[16,80,128]{2,1,0:T(8,128)(2,1)S(1)}, bf16[16,80,128]{2,1,0:T(8,128)(2,1)S(1)}, u32[]{:S(2)}, u32[]{:S(2)}) collective-permute-start(bf16[16,80,128]{2,1,0:T(8,128)(2,1)S(1)} %get-tuple-element.90), channel_id=1, source_target_pairs={{0,4},{4,0},{8,12},{12,8},{16,20},{20,16},{24,28},{28,24},{1,5},{5... | collective-permute-start | bytes 983048 | tf_op jit(solution)/shard_map/ppermute | solution.py:614
  58.7 4.9 %collective-permute-start.18 = (bf16[4,96,128]{2,1,0:T(8,128)(2,1)S(1)}, bf16[4,96,128]{2,1,0:T(8,128)(2,1)S(1)}, u32[]{:S(2)}, u32[]{:S(2)}) collective-permute-start(bf16[4,96,128]{2,1,0:T(8,128)(2,1)S(1)} %get-tuple-element.95), channel_id=1, source_target_pairs={{0,8},{4,12},{8,0},{12,4},{16,24},{20,28},{24,16},{28,20},{1,9},{5... | collective-permute-start | bytes 294920 | tf_op jit(solution)/shard_map/ppermute | solution.py:614
  60.3 13.1 %collective-permute-start.22 = (bf16[4,96,128]{2,1,0:T(8,128)(2,1)S(1)}, bf16[4,96,128]{2,1,0:T(8,128)(2,1)S(1)}, u32[]{:S(2)}, u32[]{:S(2)}) collective-permute-start(bf16[4,96,128]{2,1,0:T(8,128)(2,1)S(1)} %get-tuple-element.103), channel_id=1, source_target_pairs={{0,16},{4,20},{8,24},{12,28},{16,0},{20,4},{24,8},{28,12},{1,17},{... | collective-permute-start | bytes 294920 | tf_op jit(solution)/shard_map/ppermute | solution.py:614
  61.0 12.5 %collective-permute-start.23 = (bf16[4,96,128]{2,1,0:T(8,128)(2,1)S(1)}, bf16[4,96,128]{2,1,0:T(8,128)(2,1)S(1)}, u32[]{:S(2)}, u32[]{:S(2)}) collective-permute-start(bf16[4,96,128]{2,1,0:T(8,128)(2,1)S(1)} %get-tuple-element.104), channel_id=1, source_target_pairs={{0,24},{4,28},{8,16},{12,20},{16,8},{20,12},{24,0},{28,4},{1,25},{... | collective-permute-start | bytes 294920 | tf_op jit(solution)/shard_map/ppermute | solution.py:614
  63.6 9.8 %collective-permute-start.19 = (bf16[4,80,128]{2,1,0:T(8,128)(2,1)S(1)}, bf16[4,80,128]{2,1,0:T(8,128)(2,1)S(1)}, u32[]{:S(2)}, u32[]{:S(2)}) collective-permute-start(bf16[4,80,128]{2,1,0:T(8,128)(2,1)S(1)} %get-tuple-element.98), channel_id=1, source_target_pairs={{0,8},{4,12},{8,0},{12,4},{16,24},{20,28},{24,16},{28,20},{1,9},{5... | collective-permute-start | bytes 245768 | tf_op jit(solution)/shard_map/ppermute | solution.py:614
  66.1 11.1 %collective-permute-start.20 = (bf16[4,80,128]{2,1,0:T(8,128)(2,1)S(1)}, bf16[4,80,128]{2,1,0:T(8,128)(2,1)S(1)}, u32[]{:S(2)}, u32[]{:S(2)}) collective-permute-start(bf16[4,80,128]{2,1,0:T(8,128)(2,1)S(1)} %get-tuple-element.99), channel_id=1, source_target_pairs={{0,16},{4,20},{8,24},{12,28},{16,0},{20,4},{24,8},{28,12},{1,17},{... | collective-permute-start | bytes 245768 | tf_op jit(solution)/shard_map/ppermute | solution.py:614
  67.0 10.3 %collective-permute-start.21 = (bf16[4,80,128]{2,1,0:T(8,128)(2,1)S(1)}, bf16[4,80,128]{2,1,0:T(8,128)(2,1)S(1)}, u32[]{:S(2)}, u32[]{:S(2)}) collective-permute-start(bf16[4,80,128]{2,1,0:T(8,128)(2,1)S(1)} %get-tuple-element.100), channel_id=1, source_target_pairs={{0,24},{4,28},{8,16},{12,20},{16,8},{20,12},{24,0},{28,4},{1,25},{... | collective-permute-start | bytes 245768 | tf_op jit(solution)/shard_map/ppermute | solution.py:614
  (19 other events, 98.0 us)
